TPU v7x, 32 devices: a whole 2x2x4 slice. The times are simulated.
32 devices in a mesh: row: 4 (over x, core), col: 2 (over y), mat: 4 (over z).
Axes of the slice: x: 2, y: 2, z: 4, core: 2. Of those that a mesh axis runs over, the one named last changes fastest.
Arguments:
- grads: float32 [4, 4096, 4096], P('mat', 'row', 'col'), may hold values from -6 to 6
- left_stats: float32 [4, 4096, 256], P('mat', 'row'), as said below
- right_stats: float32 [4, 4096, 256], P('mat', 'col'), as said below
Outputs:
- update: float32 [4, 4096, 4096], P('mat', ('row', 'col'))
Inputs may be any that keep to these rules, and one draw needn't show every extreme that they name: `left_stats`: each aligned block of 256 rows along the second dimension, taken as a 256 x 256 matrix, is symmetric positive definite. `right_stats`: each aligned block of 256 rows along the second dimension, taken as a 256 x 256 matrix, is symmetric positive definite.
All inputs are finite; a program needn't handle non-finite values.
Results may differ from a plain program's by a relative error of at most 0.00011.
Values sent between devices are 32-bit elements; how exact they have to be, the bound alone decides.
No kernel may reach another device: no remote copies, remote signals or barrier semaphores. Data moves between devices by JAX's collectives and lax.ppermute only.
A program may use at most 64 MiB of HBM per device.

v0:
```python
import functools

import jax
import jax.numpy as jnp
from jax import lax
from jax.experimental import pallas as pl
from jax.experimental.pallas import tpu as pltpu
from jax.sharding import PartitionSpec as P

ITERS = 3
beta_mix = 0.5
eps_shift = 0.001
PAD = 8
VMEM_LIMIT = 24 * 1024 * 1024
SMALL = pl.CostEstimate(flops=1, bytes_accessed=1, transcendentals=0)


def matmul(left, right):
    return jnp.einsum("...ij,...jk->...ik", left, right, precision=lax.Precision.HIGHEST)


def newton_root(factor):
    size = factor.shape[-1]
    ident = jnp.eye(size, dtype=jnp.float32)
    scale = jnp.sqrt(jnp.sum(factor * factor, axis=(-2, -1), keepdims=True))
    moving = factor / scale
    result = jnp.broadcast_to(ident, factor.shape)
    for count in range(ITERS):
        step_mat = (5.0 * ident - moving) * 0.25
        result = matmul(result, step_mat)
        squared = matmul(step_mat, step_mat)
        moving = matmul(matmul(squared, squared), moving)
    return result * jnp.power(scale, -0.25)


def general_device(full_dim, grads, left_stats, right_stats):
    mats, tile_rows, tile_cols = grads.shape
    blk = left_stats.shape[2]
    row_blocks = tile_rows // blk
    col_blocks = tile_cols // blk
    ident = jnp.eye(blk, dtype=jnp.float32)
    by_rows = grads.reshape(mats, row_blocks, blk, tile_cols)
    left_part = jnp.einsum("mibd,mied->mibe", by_rows, by_rows, precision=lax.Precision.HIGHEST) / full_dim
    by_cols = grads.reshape(mats, tile_rows, col_blocks, blk)
    right_part = (
        jnp.einsum("mdjb,mdje->mjbe", by_cols, by_cols, precision=lax.Precision.HIGHEST) / full_dim
    )
    left_gram = lax.psum(left_part, "col")
    right_gram = lax.psum(right_part, "row")
    left_factor = (
        beta_mix * left_stats.reshape(mats, row_blocks, blk, blk)
        + (1.0 - beta_mix) * left_gram
        + eps_shift * ident
    )
    right_factor = (
        beta_mix * right_stats.reshape(mats, col_blocks, blk, blk)
        + (1.0 - beta_mix) * right_gram
        + eps_shift * ident
    )
    left_root = newton_root(left_factor)
    right_root = newton_root(right_factor)
    half = jnp.einsum("mibe,mied->mibd", left_root, by_rows, precision=lax.Precision.HIGHEST)
    half = half.reshape(mats, tile_rows, col_blocks, blk)
    full = jnp.einsum("mdjb,mjbe->mdje", half, right_root, precision=lax.Precision.HIGHEST)
    full = full.reshape(mats, tile_rows, tile_cols)
    return lax.all_to_all(full, "col", split_axis=1, concat_axis=2, tiled=True)


def split(value):
    high = value.astype(jnp.bfloat16)
    low = (value - high.astype(jnp.float32)).astype(jnp.bfloat16)
    return high, low


def dot(left, right, dims=((1,), (0,))):
    return lax.dot_general(left, right, (dims, ((), ())), preferred_element_type=jnp.float32)


def product(left, right):
    lh, ll = left
    rh, rl = right
    return dot(lh, rh) + (dot(lh, rl) + dot(ll, rh))


def places(blk):
    rows = lax.broadcasted_iota(jnp.int32, (blk, blk), 0)
    cols = lax.broadcasted_iota(jnp.int32, (blk, blk), 1)
    return rows, cols


def pack(first, second):
    blk = first.shape[0]
    rows, cols = places(blk)
    body = jnp.where(rows <= cols, first, second)
    diag = jnp.sum(jnp.where(rows == cols, second, 0.0), axis=0, keepdims=True)
    return body, jnp.broadcast_to(diag, (PAD, blk))


def unpack(body, diag):
    blk = body.shape[0]
    rows, cols = places(blk)
    turned = body.T
    first = jnp.where(rows <= cols, body, turned)
    second = jnp.where(rows > cols, body, jnp.where(rows == cols, diag, turned))
    return first, second


def gram_kernel(place, g_ref, after_ref, send_ref, keep_ref, lsend_ref, lkeep_ref, lhh, lcross):
    step = pl.program_id(0)
    last = pl.num_programs(0) - 1
    col_at = place[1]
    rows, wide = g_ref.shape
    blk = wide // 2
    high, low = split(g_ref[...])

    grams = []
    for b in range(2):
        hb = high[:, b * blk : (b + 1) * blk]
        lb = low[:, b * blk : (b + 1) * blk]
        both = dot(hb, hb, ((0,), (0,)))
        cross = dot(hb, lb, ((0,), (0,)))
        grams.append(both + (cross + cross.T))
    body, diag = pack(*grams)

    @pl.when(step < 2)
    def _():
        send_ref[0, :blk, :] = body
        send_ref[0, blk:, :] = diag

    @pl.when(step >= 2)
    def _():
        keep_ref[0, :blk, :] = body
        keep_ref[0, blk:, :] = diag

    for i in range(rows // blk):
        hi = high[i * blk : (i + 1) * blk, :]
        lo = low[i * blk : (i + 1) * blk, :]
        both = dot(hi, hi, ((1,), (1,)))
        cross = dot(hi, lo, ((1,), (1,)))

        @pl.when(step == 0)
        def _():
            lhh[i] = both
            lcross[i] = cross

        @pl.when(step > 0)
        def _():
            lhh[i] += both
            lcross[i] += cross

    @pl.when(step == last)
    def _():
        for ref, owner in ((lsend_ref, 1 - col_at), (lkeep_ref, col_at)):
            pair = []
            for b in range(2):
                cross = lcross[owner * 2 + b]
                pair.append(lhh[owner * 2 + b] + (cross + cross.T))
            body, diag = pack(*pair)
            ref[:blk, :] = body
            ref[blk:, :] = diag


def grams(place, tile, blk, after):
    rows, width = tile.shape
    pairs = width // (2 * blk)
    tall = blk + PAD

    def pair_of(step, place):
        flip = jnp.where(step == 0, 3, jnp.where(step == 3, 0, step))
        return (0, place[0] ^ flip)

    shape = jax.ShapeDtypeStruct((2, tall, blk), jnp.float32)
    flat = jax.ShapeDtypeStruct((tall, blk), jnp.float32)
    return pl.pallas_call(
        gram_kernel,
        out_shape=(shape, shape, flat, flat),
        grid_spec=pltpu.PrefetchScalarGridSpec(
            num_scalar_prefetch=1,
            grid=(pairs,),
            in_specs=[pl.BlockSpec((rows, 2 * blk), pair_of), pl.BlockSpec(memory_space=pl.ANY)],
            out_specs=(
                pl.BlockSpec((1, tall, blk), lambda s, place: (jnp.minimum(s, 1), 0, 0)),
                pl.BlockSpec((1, tall, blk), lambda s, place: (jnp.maximum(s - 2, 0), 0, 0)),
                pl.BlockSpec((tall, blk), lambda s, place: (0, 0)),
                pl.BlockSpec((tall, blk), lambda s, place: (0, 0)),
            ),
            scratch_shapes=[
                pltpu.VMEM((rows // blk, blk, blk), jnp.float32),
                pltpu.VMEM((rows // blk, blk, blk), jnp.float32),
            ],
        ),
        compiler_params=pltpu.CompilerParams(vmem_limit_bytes=VMEM_LIMIT),
        cost_estimate=SMALL,
        name="grams",
    )(place, tile, after)


def take_kernel(place, g_ref, *rest):
    rest[-1][...] = g_ref[...]


def take(place, tile, blk, chunk, after):
    flip, at, blocks = chunk
    rows = tile.shape[0] // 2
    operands = [place, tile]
    in_specs = [pl.BlockSpec((rows, blk), lambda s, place: (1 - place[1], (place[0] ^ flip) * 2 + at + s))]
    for other in after:
        operands.append(other)
        in_specs.append(pl.BlockSpec(memory_space=pl.ANY))
    return pl.pallas_call(
        take_kernel,
        out_shape=jax.ShapeDtypeStruct((rows, blocks * blk), jnp.float32),
        grid_spec=pltpu.PrefetchScalarGridSpec(
            num_scalar_prefetch=1,
            grid=(blocks,),
            in_specs=in_specs,
            out_specs=pl.BlockSpec((rows, blk), lambda s, place: (0, s)),
        ),
        compiler_params=pltpu.CompilerParams(vmem_limit_bytes=VMEM_LIMIT),
        cost_estimate=SMALL,
        name="take",
    )(*operands)


def fold_kernel(a_ref, b_ref, after_ref, out_ref):
    out_ref[...] = a_ref[0] + b_ref[0]


def fold(kept, near, after):
    tall, blk = kept.shape[1:]
    return pl.pallas_call(
        fold_kernel,
        out_shape=jax.ShapeDtypeStruct((tall, blk), jnp.float32),
        grid=(1,),
        in_specs=[
            pl.BlockSpec((1, tall, blk), lambda s: (0, 0, 0)),
            pl.BlockSpec((1, tall, blk), lambda s: (0, 0, 0)),
            pl.BlockSpec(memory_space=pl.ANY),
        ],
        out_specs=pl.BlockSpec((tall, blk), lambda s: (0, 0)),
        compiler_params=pltpu.CompilerParams(vmem_limit_bytes=VMEM_LIMIT),
        cost_estimate=SMALL,
        name="fold",
    )(kept, near, after)


def pair_roots(full_dim, stats_ref, body, diag):
    blk = body.shape[0]
    rows, cols = places(blk)
    ident = jnp.where(rows == cols, 1.0, 0.0)
    moving, scales = [], []
    for b, gram in enumerate(unpack(body, diag)):
        factor = (
            beta_mix * stats_ref[b * blk : (b + 1) * blk, :]
            + (1.0 - beta_mix) * (gram / full_dim)
            + eps_shift * ident
        )
        scale = jnp.sqrt(jnp.sum(factor * factor, keepdims=True))
        moving.append(factor / scale)
        scales.append(scale)
    result = None
    for count in range(ITERS):
        steps = [(5.0 * ident - m) * 0.25 for m in moving]
        parts = [split(s) for s in steps]
        if result is None:
            result = steps
        else:
            result = [product(split(r), p) for r, p in zip(result, parts)]
        if count < ITERS - 1:
            squared = [split(product(p, p)) for p in parts]
            fourth = [split(product(s, s)) for s in squared]
            moving = [product(f, split(m)) for f, m in zip(fourth, moving)]
    return [r * jnp.exp(-0.25 * jnp.log(s)) for r, s in zip(result, scales)]


def right_kernel(full_dim, place, stats_ref, a_ref, b_ref, c_ref, out_ref):
    blk = stats_ref.shape[1]
    total = a_ref[0] + b_ref[0] + c_ref[...]
    body, diag = pack(*pair_roots(full_dim, stats_ref, total[:blk], total[blk : blk + 1]))
    out_ref[:blk, :] = body
    out_ref[blk:, :] = diag


def right_roots(full_dim, place, stats, kept, near, far):
    blk = stats.shape[1]
    tall = blk + PAD
    return pl.pallas_call(
        functools.partial(right_kernel, full_dim),
        out_shape=jax.ShapeDtypeStruct((tall, blk), jnp.float32),
        grid_spec=pltpu.PrefetchScalarGridSpec(
            num_scalar_prefetch=1,
            grid=(1,),
            in_specs=[
                pl.BlockSpec((2 * blk, blk), lambda s, place: (place[0], 0)),
                pl.BlockSpec((1, tall, blk), lambda s, place: (1, 0, 0)),
                pl.BlockSpec((1, tall, blk), lambda s, place: (1, 0, 0)),
                pl.BlockSpec((tall, blk), lambda s, place: (0, 0)),
            ],
            out_specs=pl.BlockSpec((tall, blk), lambda s, place: (0, 0)),
        ),
        compiler_params=pltpu.CompilerParams(vmem_limit_bytes=VMEM_LIMIT),
        cost_estimate=SMALL,
        name="right_roots",
    )(place, stats, kept, near, far)


def left_kernel(full_dim, place, stats_ref, a_ref, b_ref, out_ref):
    blk = stats_ref.shape[1]
    total = a_ref[...] + b_ref[...]
    for b, root in enumerate(pair_roots(full_dim, stats_ref, total[:blk], total[blk : blk + 1])):
        high, low = split(root)
        out_ref[b, 0] = high
        out_ref[b, 1] = low


def left_roots(full_dim, place, stats, kept, came):
    blk = stats.shape[1]
    tall = blk + PAD
    return pl.pallas_call(
        functools.partial(left_kernel, full_dim),
        out_shape=jax.ShapeDtypeStruct((2, 2, blk, blk), jnp.bfloat16),
        grid_spec=pltpu.PrefetchScalarGridSpec(
            num_scalar_prefetch=1,
            grid=(1,),
            in_specs=[
                pl.BlockSpec((2 * blk, blk), lambda s, place: (place[1], 0)),
                pl.BlockSpec((tall, blk), lambda s, place: (0, 0)),
                pl.BlockSpec((tall, blk), lambda s, place: (0, 0)),
            ],
            out_specs=pl.BlockSpec((2, 2, blk, blk), lambda s, place: (0, 0, 0, 0)),
        ),
        compiler_params=pltpu.CompilerParams(vmem_limit_bytes=VMEM_LIMIT),
        cost_estimate=SMALL,
        name="left_roots",
    )(place, stats, kept, came)


def spread_kernel(*refs):
    out_ref = refs[-1]
    blk = out_ref.shape[-1]
    for at, ref in enumerate(refs[:-1]):
        for b, root in enumerate(unpack(ref[:blk, :], ref[blk : blk + 1, :])):
            high, low = split(root)
            out_ref[2 * at + b, 0] = high
            out_ref[2 * at + b, 1] = low


def spread_roots(packed):
    blk = packed[0].shape[1]
    count = len(packed)
    return pl.pallas_call(
        spread_kernel,
        out_shape=jax.ShapeDtypeStruct((2 * count, 2, blk, blk), jnp.bfloat16),
        compiler_params=pltpu.CompilerParams(vmem_limit_bytes=VMEM_LIMIT),
        cost_estimate=SMALL,
        name="spread_roots",
    )(*packed)


def update_kernel(place, g_ref, left_ref, right_ref, *rest):
    out_ref = rest[-1]
    blk = right_ref.shape[-1]
    right = (right_ref[0, 0], right_ref[0, 1])
    half = product(split(g_ref[...]), right)
    for i in range(g_ref.shape[0] // blk):
        part = split(half[i * blk : (i + 1) * blk])
        out_ref[i * blk : (i + 1) * blk, :] = product((left_ref[i, 0], left_ref[i, 1]), part)


def update(place, source, left, right, out, out_shape, blocks, g_map, right_at, out_map):
    blk = right.shape[-1]
    rows = out_shape[0]
    in_specs = [
        pl.BlockSpec((rows, blk), g_map),
        pl.BlockSpec((2, 2, blk, blk), lambda s, place: (0, 0, 0, 0)),
        pl.BlockSpec((1, 2, blk, blk), lambda s, place: (right_at + s, 0, 0, 0)),
    ]
    operands = [source, left, right]
    aliases = {}
    if out is not None:
        in_specs.append(pl.BlockSpec(memory_space=pl.ANY))
        operands.append(out)
        aliases = {4: 0}
    return pl.pallas_call(
        update_kernel,
        out_shape=jax.ShapeDtypeStruct(out_shape, jnp.float32),
        grid_spec=pltpu.PrefetchScalarGridSpec(
            num_scalar_prefetch=1,
            grid=(blocks,),
            in_specs=in_specs,
            out_specs=pl.BlockSpec((rows, blk), out_map),
        ),
        input_output_aliases=aliases,
        compiler_params=pltpu.CompilerParams(vmem_limit_bytes=VMEM_LIMIT),
        cost_estimate=SMALL,
        name="update",
    )(place, *operands)


def exchange_device(full_dim, n_row, grads, left_stats, right_stats):
    tile_rows, tile_cols = grads.shape[1:]
    blk = left_stats.shape[2]
    tile = pltpu.with_memory_space_constraint(grads.reshape(tile_rows, tile_cols), pltpu.HBM)
    lstats = left_stats.reshape(tile_rows, blk)
    rstats = right_stats.reshape(tile_cols, blk)
    r = lax.axis_index("row")
    c = lax.axis_index("col")
    place = jnp.stack([r, c]).astype(jnp.int32)
    rows = tile_rows // 2
    halves = tile_cols // blk

    def over(axis, value):
        if axis == "col":
            return lax.ppermute(value, "col", [(0, 1), (1, 0)])
        flip = {"core": 1, "x": 2}[axis]
        return lax.ppermute(value, "row", [(i, i ^ flip) for i in range(n_row)])

    chunks = [(0, 0, 2), (1, 0, 2), (2, 0, 2), (3, 0, 1), (3, 1, 1)]
    first = take(place, tile, blk, chunks[0], ())
    came = [over("col", first)]

    send, keep, lsend, lkeep = grams(place, tile, blk, first)
    near = over("core", send)
    lcame = over("col", lsend)
    for k in (1,):
        came.append(over("col", take(place, tile, blk, chunks[k], (lsend,))))
    far = over("x", fold(keep, near, came[0]))
    own = right_roots(full_dim, place, rstats, keep, near, far)
    across = over("col", own)
    for k in (2, 3, 4):
        came.append(over("col", take(place, tile, blk, chunks[k], (own,))))
    left = left_roots(full_dim, place, lstats, lkeep, lcame)

    own_x = over("x", own)
    own_c = over("core", own)
    own_xc = over("core", own_x)
    mine = spread_roots([own, own_c, own_x, own_xc])
    across_x = over("x", across)
    across_c = over("core", across)
    across_xc = over("core", across_x)
    theirs = spread_roots([across, across_c, across_x, across_xc])

    def block_of(flip_block, place):
        return ((place[0] ^ (flip_block // 2)) * 2) + flip_block % 2

    shape = (rows, 2 * tile_cols)
    out = update(
        place, tile, left, mine, None, shape, halves,
        lambda s, place: (place[1], block_of(s, place)),
        0,
        lambda s, place: (0, place[1] * halves + block_of(s, place)),
    )
    for (flip, at, blocks), value in zip(chunks, came):
        base = 2 * flip + at
        out = update(
            place, value, left, theirs, out, shape, blocks,
            lambda s, place: (0, s),
            base,
            lambda s, place, base=base: (0, (1 - place[1]) * halves + block_of(base + s, place)),
        )
    return out.reshape(1, rows, 2 * tile_cols)


def per_device(n_row, n_col, grads, left_stats, right_stats):
    mats, tile_rows, tile_cols = grads.shape
    blk = left_stats.shape[2]
    full_dim = tile_cols * n_col
    if mats == 1 and n_col == 2 and n_row == 4 and tile_rows == 4 * blk and tile_cols == 8 * blk:
        return exchange_device(full_dim, n_row, grads, left_stats, right_stats)
    return general_device(full_dim, grads, left_stats, right_stats)


def solution(mesh):
    return jax.shard_map(
        functools.partial(per_device, mesh.shape["row"], mesh.shape["col"]),
        mesh=mesh,
        in_specs=(P("mat", "row", "col"), P("mat", "row", None), P("mat", "col", None)),
        out_specs=P("mat", ("row", "col"), None),
        check_vma=False,
    )
```

profile of v0, /device:TPU:0, one launch (start us, length us, event | category | flops | bytes accessed | tf_op | source)
XLA Modules:
  0.0 117.2 jit_solution(7475412889220702118)
XLA Ops:
  0.1 1.9 %take.5.after_ref = f32[512,512]{1,0:T(8,128)S(1)} custom-call(s32[2]{0:T(128)S(1)} %pad_add_fusion.place, f32[1024,2048]{1,0:T(8,128)} %bitcast.8), custom_call_target="tpu_custom_call" | custom-call | flops 1 | bytes 1 | tf_op jit(solution)/shard_map/take/pallas_call | solution.py:210
  2.0 3.0 %collective-permute-start.1 = (f32[512,512]{1,0:T(8,128)S(1)}, f32[512,512]{1,0:T(8,128)S(1)}, u32[]{:S(2)}, u32[]{:S(2)}) collective-permute-start(f32[512,512]{1,0:T(8,128)S(1)} %take.5.after_ref), channel_id=1, source_target_pairs={{0,4},{4,0},{1,5},{5,1},{2,6},{6,2},{3,7},{7,3},{8,12},{12,8},{9,1... | collective-permute-start | bytes 3145736 | tf_op jit(solution)/shard_map/ppermute | solution.py:414
  5.0 11.9 %grams.1 = (f32[2,264,256]{2,1,0:T(8,128)S(1)}, f32[2,264,256]{2,1,0:T(8,128)S(1)}, f32[264,256]{1,0:T(8,128)S(1)}, f32[264,256]{1,0:T(8,128)S(1)}) custom-call(s32[2]{0:T(128)S(1)} %pad_add_fusion.place, f32[1024,2048]{1,0:T(8,128)} %bitcast.9, f32[512,512]{1,0:T(8,128)S(1)} %take.5.after_ref), custom_call_target="tpu_custom_call" | custom-call | flops 1 | bytes 1 | tf_op jit(solution)/shard_map/grams/pallas_call | solution.py:174
  17.0 1.9 %collective-permute-done.b_ref = f32[2,264,256]{2,1,0:T(8,128)S(1)} collective-permute-done((f32[2,264,256]{2,1,0:T(8,128)S(1)}, f32[2,264,256]{2,1,0:T(8,128)S(1)}, u32[]{:S(2)}, u32[]{:S(2)}) %collective-permute-start) | collective-permute-done | bytes 540704 | tf_op jit(solution)/shard_map/ppermute | solution.py:416
  18.9 9.3 %collective-permute-done.1.after_ref.g_ref = f32[512,512]{1,0:T(8,128)S(1)} collective-permute-done((f32[512,512]{1,0:T(8,128)S(1)}, f32[512,512]{1,0:T(8,128)S(1)}, u32[]{:S(2)}, u32[]{:S(2)}) %collective-permute-start.1) | collective-permute-done | bytes 1048608 | tf_op jit(solution)/shard_map/ppermute | solution.py:414
  28.2 1.8 %collective-permute-start.2 = (f32[264,256]{1,0:T(8,128)S(1)}, f32[264,256]{1,0:T(8,128)S(1)}, u32[]{:S(2)}, u32[]{:S(2)}) collective-permute-start(f32[264,256]{1,0:T(8,128)S(1)} %fold.1), channel_id=1, source_target_pairs={{0,16},{8,24},{16,0},{24,8},{1,17},{9,25},{17,1},{25,9},{2,18},{10... | collective-permute-start | bytes 811016 | tf_op jit(solution)/shard_map/ppermute | solution.py:416
  31.5 4.4 %collective-permute-done.2.c_ref = f32[264,256]{1,0:T(8,128)S(1)} collective-permute-done((f32[264,256]{1,0:T(8,128)S(1)}, f32[264,256]{1,0:T(8,128)S(1)}, u32[]{:S(2)}, u32[]{:S(2)}) %collective-permute-start.2) | collective-permute-done | bytes 270368 | tf_op jit(solution)/shard_map/ppermute | solution.py:416
  36.0 3.6 %right_roots.1.rest_0_.refs_0_ = f32[264,256]{1,0:T(8,128)S(1)} custom-call(s32[2]{0:T(128)S(1)} %pad_add_fusion.place, f32[2048,256]{1,0:T(8,128)S(1)} %bitcast.6, f32[2,264,256]{2,1,0:T(8,128)S(1)} %get-tuple-element.9.a_ref, f32[2,264,256]{2,1,0:T(8,128)S(1)} %collective-permute-done.b_ref, f32[264,256]{1,0:T(8,128)S(1)} %collective-permute-done.2.c_ref), custom_call_target="tpu_custom_call" | custom-call | flops 1 | bytes 1 | tf_op jit(solution)/shard_map/right_roots/pallas_call | solution.py:287
  42.5 1.9 %take.9 = f32[512,512]{1,0:T(8,128)S(1)} custom-call(s32[2]{0:T(128)S(1)} %pad_add_fusion.place, f32[1024,2048]{1,0:T(8,128)} %bitcast.10, f32[264,256]{1,0:T(8,128)S(1)} %get-tuple-element.12.rest_0_), custom_call_target="tpu_custom_call" | custom-call | flops 1 | bytes 1 | tf_op jit(solution)/shard_map/take/pallas_call | solution.py:210
  45.0 1.9 %take.8 = f32[512,512]{1,0:T(8,128)S(1)} custom-call(s32[2]{0:T(128)S(1)} %pad_add_fusion.place, f32[1024,2048]{1,0:T(8,128)} %bitcast.11, f32[264,256]{1,0:T(8,128)S(1)} %right_roots.1.rest_0_.refs_0_), custom_call_target="tpu_custom_call" | custom-call | flops 1 | bytes 1 | tf_op jit(solution)/shard_map/take/pallas_call | solution.py:210
  46.8 1.6 %collective-permute-start.10 = (f32[512,512]{1,0:T(8,128)S(1)}, f32[512,512]{1,0:T(8,128)S(1)}, u32[]{:S(2)}, u32[]{:S(2)}) collective-permute-start(f32[512,512]{1,0:T(8,128)S(1)} %take.8), channel_id=1, source_target_pairs={{0,4},{4,0},{1,5},{5,1},{2,6},{6,2},{3,7},{7,3},{8,12},{12,8},{9,1... | collective-permute-start | bytes 3145736 | tf_op jit(solution)/shard_map/ppermute | solution.py:414
  51.1 1.6 %take.7 = f32[512,256]{1,0:T(8,128)S(1)} custom-call(s32[2]{0:T(128)S(1)} %pad_add_fusion.place, f32[1024,2048]{1,0:T(8,128)} %bitcast.12, f32[264,256]{1,0:T(8,128)S(1)} %right_roots.1.rest_0_.refs_0_), custom_call_target="tpu_custom_call" | custom-call | flops 1 | bytes 1 | tf_op jit(solution)/shard_map/take/pallas_call | solution.py:210
  52.7 1.6 %take.6 = f32[512,256]{1,0:T(8,128)S(1)} custom-call(s32[2]{0:T(128)S(1)} %pad_add_fusion.place, f32[1024,2048]{1,0:T(8,128)} %bitcast.13, f32[264,256]{1,0:T(8,128)S(1)} %right_roots.1.rest_0_.refs_0_), custom_call_target="tpu_custom_call" | custom-call | flops 1 | bytes 1 | tf_op jit(solution)/shard_map/take/pallas_call | solution.py:210
  55.8 1.6 %collective-permute-done.7.refs_2_ = f32[264,256]{1,0:T(8,128)S(1)} collective-permute-done((f32[264,256]{1,0:T(8,128)S(1)}, f32[264,256]{1,0:T(8,128)S(1)}, u32[]{:S(2)}, u32[]{:S(2)}) %collective-permute-start.7) | collective-permute-done | bytes 270368 | tf_op jit(solution)/shard_map/ppermute | solution.py:416
  58.4 3.6 %left_roots.1.left_ref = bf16[2,2,256,256]{3,2,1,0:T(8,128)(2,1)S(1)} custom-call(s32[2]{0:T(128)S(1)} %pad_add_fusion.place, f32[1024,256]{1,0:T(8,128)S(1)} %bitcast.7, f32[264,256]{1,0:T(8,128)S(1)} %get-tuple-element.11.a_ref, f32[264,256]{1,0:T(8,128)S(1)} %collective-permute-done.4.b_ref), custom_call_target="tpu_custom_call" | custom-call | flops 1 | bytes 1 | tf_op jit(solution)/shard_map/left_roots/pallas_call | solution.py:319
  62.4 11.4 %update.6.rest_0_ = f32[512,4096]{1,0:T(8,128)} custom-call(s32[2]{0:T(128)S(1)} %pad_add_fusion.place, f32[1024,2048]{1,0:T(8,128)} %bitcast.14, bf16[2,2,256,256]{3,2,1,0:T(8,128)(2,1)S(1)} %left_roots.1.left_ref, bf16[8,2,256,256]{3,2,1,0:T(8,128)(2,1)S(1)} %spread_roots.3.right_ref), custom_call_target="tpu_custom_call" | custom-call | flops 1 | bytes 1 | tf_op jit(solution)/shard_map/update/pallas_call | solution.py:384
  74.3 3.5 %update.7.rest_0_ = f32[512,4096]{1,0:T(8,128)} custom-call(s32[2]{0:T(128)S(1)} %pad_add_fusion.place, f32[512,512]{1,0:T(8,128)S(1)} %collective-permute-done.1.after_ref.g_ref, bf16[2,2,256,256]{3,2,1,0:T(8,128)(2,1)S(1)} %left_roots.1.left_ref, bf16[8,2,256,256]{3,2,1,0:T(8,128)(2,1)S(1)} %spread_roots.2.right_ref, ...), custom_call_target="tpu_custom_call", output_to_operand_aliasing={{}: (4, {})} | custom-call | flops 1 | bytes 1 | tf_op jit(solution)/shard_map/update/pallas_call | solution.py:384
  77.8 3.5 %update.8.rest_0_ = f32[512,4096]{1,0:T(8,128)} custom-call(s32[2]{0:T(128)S(1)} %pad_add_fusion.place, f32[512,512]{1,0:T(8,128)S(1)} %collective-permute-done.11.g_ref, bf16[2,2,256,256]{3,2,1,0:T(8,128)(2,1)S(1)} %left_roots.1.left_ref, bf16[8,2,256,256]{3,2,1,0:T(8,128)(2,1)S(1)} %spread_roots.2.right_ref, ...), custom_call_target="tpu_custom_call", output_to_operand_aliasing={{}: (4, {})} | custom-call | flops 1 | bytes 1 | tf_op jit(solution)/shard_map/update/pallas_call | solution.py:384
  81.3 14.0 %collective-permute-done.10.g_ref = f32[512,512]{1,0:T(8,128)S(1)} collective-permute-done((f32[512,512]{1,0:T(8,128)S(1)}, f32[512,512]{1,0:T(8,128)S(1)}, u32[]{:S(2)}, u32[]{:S(2)}) %collective-permute-start.10) | collective-permute-done | bytes 1048608 | tf_op jit(solution)/shard_map/ppermute | solution.py:414
  95.3 3.5 %update.9.rest_0_ = f32[512,4096]{1,0:T(8,128)} custom-call(s32[2]{0:T(128)S(1)} %pad_add_fusion.place, f32[512,512]{1,0:T(8,128)S(1)} %collective-permute-done.10.g_ref, bf16[2,2,256,256]{3,2,1,0:T(8,128)(2,1)S(1)} %left_roots.1.left_ref, bf16[8,2,256,256]{3,2,1,0:T(8,128)(2,1)S(1)} %spread_roots.2.right_ref, ...), custom_call_target="tpu_custom_call", output_to_operand_aliasing={{}: (4, {})} | custom-call | flops 1 | bytes 1 | tf_op jit(solution)/shard_map/update/pallas_call | solution.py:384
  98.8 7.7 %collective-permute-done.9.g_ref = f32[512,256]{1,0:T(8,128)S(1)} collective-permute-done((f32[512,256]{1,0:T(8,128)S(1)}, f32[512,256]{1,0:T(8,128)S(1)}, u32[]{:S(2)}, u32[]{:S(2)}) %collective-permute-start.9) | collective-permute-done | bytes 524320 | tf_op jit(solution)/shard_map/ppermute | solution.py:414
  106.5 2.3 %update.10.rest_0_ = f32[512,4096]{1,0:T(8,128)} custom-call(s32[2]{0:T(128)S(1)} %pad_add_fusion.place, f32[512,256]{1,0:T(8,128)S(1)} %collective-permute-done.9.g_ref, bf16[2,2,256,256]{3,2,1,0:T(8,128)(2,1)S(1)} %left_roots.1.left_ref, bf16[8,2,256,256]{3,2,1,0:T(8,128)(2,1)S(1)} %spread_roots.2.right_ref, ...), custom_call_target="tpu_custom_call", output_to_operand_aliasing={{}: (4, {})} | custom-call | flops 1 | bytes 1 | tf_op jit(solution)/shard_map/update/pallas_call | solution.py:384
  108.9 6.0 %collective-permute-done.3.g_ref = f32[512,256]{1,0:T(8,128)S(1)} collective-permute-done((f32[512,256]{1,0:T(8,128)S(1)}, f32[512,256]{1,0:T(8,128)S(1)}, u32[]{:S(2)}, u32[]{:S(2)}) %collective-permute-start.3) | collective-permute-done | bytes 524320 | tf_op jit(solution)/shard_map/ppermute | solution.py:414
  114.8 2.3 %update.11 = f32[512,4096]{1,0:T(8,128)} custom-call(s32[2]{0:T(128)S(1)} %pad_add_fusion.place, f32[512,256]{1,0:T(8,128)S(1)} %collective-permute-done.3.g_ref, bf16[2,2,256,256]{3,2,1,0:T(8,128)(2,1)S(1)} %left_roots.1.left_ref, bf16[8,2,256,256]{3,2,1,0:T(8,128)(2,1)S(1)} %spread_roots.2.right_ref, ...), custom_call_target="tpu_custom_call", output_to_operand_aliasing={{}: (4, {})} | custom-call | flops 1 | bytes 1 | tf_op jit(solution)/shard_map/update/pallas_call | solution.py:384
  (28 shorter events, 11.3 us)
Async XLA Ops:
  0.1 35.9 %copy-start = (f32[1,2048,256]{2,1,0:T(8,128)S(1)}, f32[1,2048,256]{2,1,0:T(8,128)}, u32[]{:S(2)}) copy-start(f32[1,2048,256]{2,1,0:T(8,128)} %param.5) | copy-start | bytes 6291460
  2.0 26.2 %collective-permute-start.1 = (f32[512,512]{1,0:T(8,128)S(1)}, f32[512,512]{1,0:T(8,128)S(1)}, u32[]{:S(2)}, u32[]{:S(2)}) collective-permute-start(f32[512,512]{1,0:T(8,128)S(1)} %take.5.after_ref), channel_id=1, source_target_pairs={{0,4},{4,0},{1,5},{5,1},{2,6},{6,2},{3,7},{7,3},{8,12},{12,8},{9,1... | collective-permute-start | bytes 3145736 | tf_op jit(solution)/shard_map/ppermute | solution.py:414
  16.9 2.0 %collective-permute-start = (f32[2,264,256]{2,1,0:T(8,128)S(1)}, f32[2,264,256]{2,1,0:T(8,128)S(1)}, u32[]{:S(2)}, u32[]{:S(2)}) collective-permute-start(f32[2,264,256]{2,1,0:T(8,128)S(1)} %get-tuple-element.10), channel_id=1, source_target_pairs={{0,8},{8,0},{16,24},{24,16},{1,9},{9,1},{17,25},{25,17},{2,10},{10... | collective-permute-start | bytes 1622024 | tf_op jit(solution)/shard_map/ppermute | solution.py:416
  28.2 7.7 %collective-permute-start.2 = (f32[264,256]{1,0:T(8,128)S(1)}, f32[264,256]{1,0:T(8,128)S(1)}, u32[]{:S(2)}, u32[]{:S(2)}) collective-permute-start(f32[264,256]{1,0:T(8,128)S(1)} %fold.1), channel_id=1, source_target_pairs={{0,16},{8,24},{16,0},{24,8},{1,17},{9,25},{17,1},{25,9},{2,18},{10... | collective-permute-start | bytes 811016 | tf_op jit(solution)/shard_map/ppermute | solution.py:416
  30.0 18.4 %collective-permute-start.4 = (f32[264,256]{1,0:T(8,128)S(1)}, f32[264,256]{1,0:T(8,128)S(1)}, u32[]{:S(2)}, u32[]{:S(2)}) collective-permute-start(f32[264,256]{1,0:T(8,128)S(1)} %get-tuple-element.12.rest_0_), channel_id=1, source_target_pairs={{0,4},{4,0},{1,5},{5,1},{2,6},{6,2},{3,7},{7,3},{8,12},{12,8},{9,1... | collective-permute-start | bytes 811016 | tf_op jit(solution)/shard_map/ppermute | solution.py:414
  39.5 8.9 %collective-permute-start.13 = (f32[264,256]{1,0:T(8,128)S(1)}, f32[264,256]{1,0:T(8,128)S(1)}, u32[]{:S(2)}, u32[]{:S(2)}) collective-permute-start(f32[264,256]{1,0:T(8,128)S(1)} %right_roots.1.rest_0_.refs_0_), channel_id=1, source_target_pairs={{0,16},{8,24},{16,0},{24,8},{1,17},{9,25},{17,1},{25,9},{2,18},{10... | collective-permute-start | bytes 811016 | tf_op jit(solution)/shard_map/ppermute | solution.py:416
  41.0 9.4 %collective-permute-start.5 = (f32[264,256]{1,0:T(8,128)S(1)}, f32[264,256]{1,0:T(8,128)S(1)}, u32[]{:S(2)}, u32[]{:S(2)}) collective-permute-start(f32[264,256]{1,0:T(8,128)S(1)} %right_roots.1.rest_0_.refs_0_), channel_id=1, source_target_pairs={{0,4},{4,0},{1,5},{5,1},{2,6},{6,2},{3,7},{7,3},{8,12},{12,8},{9,1... | collective-permute-start | bytes 811016 | tf_op jit(solution)/shard_map/ppermute | solution.py:414
  44.4 33.4 %collective-permute-start.11 = (f32[512,512]{1,0:T(8,128)S(1)}, f32[512,512]{1,0:T(8,128)S(1)}, u32[]{:S(2)}, u32[]{:S(2)}) collective-permute-start(f32[512,512]{1,0:T(8,128)S(1)} %take.9), channel_id=1, source_target_pairs={{0,4},{4,0},{1,5},{5,1},{2,6},{6,2},{3,7},{7,3},{8,12},{12,8},{9,1... | collective-permute-start | bytes 3145736 | tf_op jit(solution)/shard_map/ppermute | solution.py:414
  46.8 11.6 %copy-start.1 = (f32[1,1024,256]{2,1,0:T(8,128)S(1)}, f32[1,1024,256]{2,1,0:T(8,128)}, u32[]{:S(2)}) copy-start(f32[1,1024,256]{2,1,0:T(8,128)} %param.4) | copy-start | bytes 3145732
  46.8 48.5 %collective-permute-start.10 = (f32[512,512]{1,0:T(8,128)S(1)}, f32[512,512]{1,0:T(8,128)S(1)}, u32[]{:S(2)}, u32[]{:S(2)}) collective-permute-start(f32[512,512]{1,0:T(8,128)S(1)} %take.8), channel_id=1, source_target_pairs={{0,4},{4,0},{1,5},{5,1},{2,6},{6,2},{3,7},{7,3},{8,12},{12,8},{9,1... | collective-permute-start | bytes 3145736 | tf_op jit(solution)/shard_map/ppermute | solution.py:414
  48.4 2.6 %collective-permute-start.12 = (f32[264,256]{1,0:T(8,128)S(1)}, f32[264,256]{1,0:T(8,128)S(1)}, u32[]{:S(2)}, u32[]{:S(2)}) collective-permute-start(f32[264,256]{1,0:T(8,128)S(1)} %right_roots.1.rest_0_.refs_0_), channel_id=1, source_target_pairs={{0,8},{8,0},{16,24},{24,16},{1,9},{9,1},{17,25},{25,17},{2,10},{10... | collective-permute-start | bytes 811016 | tf_op jit(solution)/shard_map/ppermute | solution.py:416
  48.4 5.9 %collective-permute-start.14 = (f32[264,256]{1,0:T(8,128)S(1)}, f32[264,256]{1,0:T(8,128)S(1)}, u32[]{:S(2)}, u32[]{:S(2)}) collective-permute-start(f32[264,256]{1,0:T(8,128)S(1)} %collective-permute-done.13.refs_2_), channel_id=1, source_target_pairs={{0,8},{8,0},{16,24},{24,16},{1,9},{9,1},{17,25},{25,17},{2,10},{10... | collective-permute-start | bytes 811016 | tf_op jit(solution)/shard_map/ppermute | solution.py:416
  50.4 7.0 %collective-permute-start.7 = (f32[264,256]{1,0:T(8,128)S(1)}, f32[264,256]{1,0:T(8,128)S(1)}, u32[]{:S(2)}, u32[]{:S(2)}) collective-permute-start(f32[264,256]{1,0:T(8,128)S(1)} %collective-permute-done.5.refs_0_), channel_id=1, source_target_pairs={{0,16},{8,24},{16,0},{24,8},{1,17},{9,25},{17,1},{25,9},{2,18},{10... | collective-permute-start | bytes 811016 | tf_op jit(solution)/shard_map/ppermute | solution.py:416
  51.1 7.3 %collective-permute-start.6 = (f32[264,256]{1,0:T(8,128)S(1)}, f32[264,256]{1,0:T(8,128)S(1)}, u32[]{:S(2)}, u32[]{:S(2)}) collective-permute-start(f32[264,256]{1,0:T(8,128)S(1)} %collective-permute-done.5.refs_0_), channel_id=1, source_target_pairs={{0,8},{8,0},{16,24},{24,16},{1,9},{9,1},{17,25},{25,17},{2,10},{10... | collective-permute-start | bytes 811016 | tf_op jit(solution)/shard_map/ppermute | solution.py:416
  54.3 52.2 %collective-permute-start.9 = (f32[512,256]{1,0:T(8,128)S(1)}, f32[512,256]{1,0:T(8,128)S(1)}, u32[]{:S(2)}, u32[]{:S(2)}) collective-permute-start(f32[512,256]{1,0:T(8,128)S(1)} %take.7), channel_id=1, source_target_pairs={{0,4},{4,0},{1,5},{5,1},{2,6},{6,2},{3,7},{7,3},{8,12},{12,8},{9,1... | collective-permute-start | bytes 1572872 | tf_op jit(solution)/shard_map/ppermute | solution.py:414
  57.4 57.4 %collective-permute-start.3 = (f32[512,256]{1,0:T(8,128)S(1)}, f32[512,256]{1,0:T(8,128)S(1)}, u32[]{:S(2)}, u32[]{:S(2)}) collective-permute-start(f32[512,256]{1,0:T(8,128)S(1)} %take.6), channel_id=1, source_target_pairs={{0,4},{4,0},{1,5},{5,1},{2,6},{6,2},{3,7},{7,3},{8,12},{12,8},{9,1... | collective-permute-start | bytes 1572872 | tf_op jit(solution)/shard_map/ppermute | solution.py:414
  58.4 15.4 %collective-permute-start.8 = (f32[264,256]{1,0:T(8,128)S(1)}, f32[264,256]{1,0:T(8,128)S(1)}, u32[]{:S(2)}, u32[]{:S(2)}) collective-permute-start(f32[264,256]{1,0:T(8,128)S(1)} %collective-permute-done.7.refs_2_), channel_id=1, source_target_pairs={{0,8},{8,0},{16,24},{24,16},{1,9},{9,1},{17,25},{25,17},{2,10},{10... | collective-permute-start | bytes 811016 | tf_op jit(solution)/shard_map/ppermute | solution.py:416
where the time goes:
time: 118 us; the launch traced here: 117 us
  Pallas kernels  55.4 us (47%)
  waiting for transfers between devices  46.3 us (39%)
  starting transfers between devices  15.2 us (13%)
    ppermute x7, waiting for transfers between devices, over(): return lax.ppermute(value, 'col', [(0, 1), (1, 0)])  38.3 us
    pallas_call x6, Pallas kernels, update(): pl.pallas_call(update_kernel, out_shape=jax.ShapeDtypeStruct(out_shape, j...  26.6 us
    pallas_call x1, Pallas kernels, grams(): pl.pallas_call(gram_kernel, out_shape=(shape, shape, flat, flat), grid_sp...  11.9 us
    ppermute x7, starting transfers between devices, over(): return lax.ppermute(value, 'col', [(0, 1), (1, 0)])  10.7 us
    pallas_call x5, Pallas kernels, take(): pl.pallas_call(take_kernel, out_shape=jax.ShapeDtypeStruct((rows, blocks...  8.88 us
    ppermute x8, waiting for transfers between devices, over(): return lax.ppermute(value, 'row', [(i, i ^ flip) for i in range(n_row)])  7.96 us
    ppermute x8, starting transfers between devices, over(): return lax.ppermute(value, 'row', [(i, i ^ flip) for i in range(n_row)])  4.51 us
    pallas_call x1, Pallas kernels, right_roots(): pl.pallas_call(functools.partial(right_kernel, full_dim), out_shape=jax.S...  3.56 us
  transfers between devices with their start and end apart: 15, of which 8 were waited for; matrix products, arithmetic and copies ran while one was open for 0% of the time, Pallas kernels for 44%

commit v1 on v0

--- a/solution.py
+++ b/solution.py
@@ -105,14 +105,15 @@
     return first, second
 
 
-def gram_kernel(place, g_ref, after_ref, send_ref, keep_ref, lsend_ref, lkeep_ref, lhh, lcross):
+def pair_of(step, place):
+    flip = jnp.where(step == 0, 3, jnp.where(step == 3, 0, step))
+    return (0, place[0] ^ flip)
+
+
+def right_gram_kernel(place, g_ref, after_ref, *out_refs):
     step = pl.program_id(0)
-    last = pl.num_programs(0) - 1
-    col_at = place[1]
-    rows, wide = g_ref.shape
-    blk = wide // 2
+    blk = g_ref.shape[1] // 2
     high, low = split(g_ref[...])
-
     grams = []
     for b in range(2):
         hb = high[:, b * blk : (b + 1) * blk]
@@ -122,16 +123,40 @@
         grams.append(both + (cross + cross.T))
     body, diag = pack(*grams)
 
-    @pl.when(step < 2)
-    def _():
-        send_ref[0, :blk, :] = body
-        send_ref[0, blk:, :] = diag
-
-    @pl.when(step >= 2)
-    def _():
-        keep_ref[0, :blk, :] = body
-        keep_ref[0, blk:, :] = diag
-
+    for at, ref in enumerate(out_refs):
+
+        @pl.when(step == at)
+        def _():
+            ref[:blk, :] = body
+            ref[blk:, :] = diag
+
+
+def right_grams(place, tile, blk, after):
+    rows, width = tile.shape
+    tall = blk + PAD
+    pairs = width // (2 * blk)
+    return pl.pallas_call(
+        right_gram_kernel,
+        out_shape=(jax.ShapeDtypeStruct((tall, blk), jnp.float32),) * pairs,
+        grid_spec=pltpu.PrefetchScalarGridSpec(
+            num_scalar_prefetch=1,
+            grid=(pairs,),
+            in_specs=[pl.BlockSpec((rows, 2 * blk), pair_of), pl.BlockSpec(memory_space=pl.ANY)],
+            out_specs=(pl.BlockSpec((tall, blk), lambda s, place: (0, 0)),) * pairs,
+        ),
+        compiler_params=pltpu.CompilerParams(vmem_limit_bytes=VMEM_LIMIT),
+        cost_estimate=SMALL,
+        name="right_grams",
+    )(place, tile, after)
+
+
+def left_gram_kernel(place, g_ref, after_ref, lsend_ref, lkeep_ref, lhh, lcross):
+    step = pl.program_id(0)
+    last = pl.num_programs(0) - 1
+    col_at = place[1]
+    rows = g_ref.shape[0]
+    blk = lhh.shape[-1]
+    high, low = split(g_ref[...])
     for i in range(rows // blk):
         hi = high[i * blk : (i + 1) * blk, :]
         lo = low[i * blk : (i + 1) * blk, :]
@@ -160,27 +185,21 @@
             ref[blk:, :] = diag
 
 
-def grams(place, tile, blk, after):
+def left_grams(place, tile, blk, after):
     rows, width = tile.shape
-    pairs = width // (2 * blk)
     tall = blk + PAD
-
-    def pair_of(step, place):
-        flip = jnp.where(step == 0, 3, jnp.where(step == 3, 0, step))
-        return (0, place[0] ^ flip)
-
-    shape = jax.ShapeDtypeStruct((2, tall, blk), jnp.float32)
     flat = jax.ShapeDtypeStruct((tall, blk), jnp.float32)
     return pl.pallas_call(
-        gram_kernel,
-        out_shape=(shape, shape, flat, flat),
-        grid_spec=pltpu.PrefetchScalarGridSpec(
-            num_scalar_prefetch=1,
-            grid=(pairs,),
-            in_specs=[pl.BlockSpec((rows, 2 * blk), pair_of), pl.BlockSpec(memory_space=pl.ANY)],
+        left_gram_kernel,
+        out_shape=(flat, flat),
+        grid_spec=pltpu.PrefetchScalarGridSpec(
+            num_scalar_prefetch=1,
+            grid=(width // (2 * blk),),
+            in_specs=[
+                pl.BlockSpec((rows, 2 * blk), lambda s, place: (0, s)),
+                pl.BlockSpec(memory_space=pl.ANY),
+            ],
             out_specs=(
-                pl.BlockSpec((1, tall, blk), lambda s, place: (jnp.minimum(s, 1), 0, 0)),
-                pl.BlockSpec((1, tall, blk), lambda s, place: (jnp.maximum(s - 2, 0), 0, 0)),
                 pl.BlockSpec((tall, blk), lambda s, place: (0, 0)),
                 pl.BlockSpec((tall, blk), lambda s, place: (0, 0)),
             ),
@@ -191,57 +210,64 @@
         ),
         compiler_params=pltpu.CompilerParams(vmem_limit_bytes=VMEM_LIMIT),
         cost_estimate=SMALL,
-        name="grams",
+        name="left_grams",
     )(place, tile, after)
 
 
-def take_kernel(place, g_ref, *rest):
-    rest[-1][...] = g_ref[...]
-
-
-def take(place, tile, blk, chunk, after):
-    flip, at, blocks = chunk
-    rows = tile.shape[0] // 2
-    operands = [place, tile]
-    in_specs = [pl.BlockSpec((rows, blk), lambda s, place: (1 - place[1], (place[0] ^ flip) * 2 + at + s))]
-    for other in after:
-        operands.append(other)
-        in_specs.append(pl.BlockSpec(memory_space=pl.ANY))
+def take_kernel(place, g_ref, out_ref, sem):
+    rows, wide = out_ref.shape
+    top = pl.multiple_of((1 - place[1]) * rows, rows)
+    start = pl.multiple_of((place[0] ^ raw_flip(place)) * wide, wide)
+    copy = pltpu.make_async_copy(g_ref.at[pl.ds(top, rows), pl.ds(start, wide)], out_ref, sem)
+    copy.start()
+    copy.wait()
+
+
+def take(place, tile, blk):
     return pl.pallas_call(
         take_kernel,
-        out_shape=jax.ShapeDtypeStruct((rows, blocks * blk), jnp.float32),
-        grid_spec=pltpu.PrefetchScalarGridSpec(
-            num_scalar_prefetch=1,
-            grid=(blocks,),
-            in_specs=in_specs,
-            out_specs=pl.BlockSpec((rows, blk), lambda s, place: (0, s)),
+        out_shape=jax.ShapeDtypeStruct((tile.shape[0] // 2, 2 * blk), jnp.float32),
+        grid_spec=pltpu.PrefetchScalarGridSpec(
+            num_scalar_prefetch=1,
+            grid=(1,),
+            in_specs=[pl.BlockSpec(memory_space=pl.ANY)],
+            out_specs=pl.BlockSpec(memory_space=pl.ANY),
+            scratch_shapes=[pltpu.SemaphoreType.DMA],
         ),
         compiler_params=pltpu.CompilerParams(vmem_limit_bytes=VMEM_LIMIT),
         cost_estimate=SMALL,
         name="take",
-    )(*operands)
-
-
-def fold_kernel(a_ref, b_ref, after_ref, out_ref):
-    out_ref[...] = a_ref[0] + b_ref[0]
-
-
-def fold(kept, near, after):
-    tall, blk = kept.shape[1:]
+    )(place, tile)
+
+
+def fold_kernel(a_ref, b_ref, out_ref):
+    out_ref[...] = a_ref[...] + b_ref[...]
+
+
+def fold(kept, near):
     return pl.pallas_call(
         fold_kernel,
-        out_shape=jax.ShapeDtypeStruct((tall, blk), jnp.float32),
-        grid=(1,),
-        in_specs=[
-            pl.BlockSpec((1, tall, blk), lambda s: (0, 0, 0)),
-            pl.BlockSpec((1, tall, blk), lambda s: (0, 0, 0)),
-            pl.BlockSpec(memory_space=pl.ANY),
-        ],
-        out_specs=pl.BlockSpec((tall, blk), lambda s: (0, 0)),
+        out_shape=jax.ShapeDtypeStruct(kept.shape, jnp.float32),
         compiler_params=pltpu.CompilerParams(vmem_limit_bytes=VMEM_LIMIT),
         cost_estimate=SMALL,
         name="fold",
-    )(kept, near, after)
+    )(kept, near)
+
+
+def hold_kernel(a_ref, *rest):
+    out_ref = rest[-1]
+    out_ref[...] = a_ref[...]
+
+
+def hold(value, *after):
+    return pl.pallas_call(
+        hold_kernel,
+        out_shape=jax.ShapeDtypeStruct(value.shape, jnp.float32),
+        in_specs=[pl.BlockSpec(memory_space=pltpu.VMEM)] + [pl.BlockSpec(memory_space=pl.ANY)] * len(after),
+        compiler_params=pltpu.CompilerParams(vmem_limit_bytes=VMEM_LIMIT),
+        cost_estimate=SMALL,
+        name="hold",
+    )(value, *after)
 
 
 def pair_roots(full_dim, stats_ref, body, diag):
@@ -273,40 +299,52 @@
     return [r * jnp.exp(-0.25 * jnp.log(s)) for r, s in zip(result, scales)]
 
 
-def right_kernel(full_dim, place, stats_ref, a_ref, b_ref, c_ref, out_ref):
+def right_kernel(full_dim, place, stats_ref, a_ref, b_ref, c_ref, after_ref, out_ref, halves_ref):
     blk = stats_ref.shape[1]
-    total = a_ref[0] + b_ref[0] + c_ref[...]
-    body, diag = pack(*pair_roots(full_dim, stats_ref, total[:blk], total[blk : blk + 1]))
+    total = a_ref[...] + b_ref[...] + c_ref[...]
+    roots = pair_roots(full_dim, stats_ref, total[:blk], total[blk : blk + 1])
+    body, diag = pack(*roots)
     out_ref[:blk, :] = body
     out_ref[blk:, :] = diag
-
-
-def right_roots(full_dim, place, stats, kept, near, far):
+    for b, root in enumerate(roots):
+        high, low = split(root)
+        halves_ref[b, 0] = high
+        halves_ref[b, 1] = low
+
+
+def right_roots(full_dim, place, stats, kept, near, far, after):
     blk = stats.shape[1]
     tall = blk + PAD
     return pl.pallas_call(
         functools.partial(right_kernel, full_dim),
-        out_shape=jax.ShapeDtypeStruct((tall, blk), jnp.float32),
+        out_shape=(
+            jax.ShapeDtypeStruct((tall, blk), jnp.float32),
+            jax.ShapeDtypeStruct((2, 2, blk, blk), jnp.bfloat16),
+        ),
         grid_spec=pltpu.PrefetchScalarGridSpec(
             num_scalar_prefetch=1,
             grid=(1,),
             in_specs=[
                 pl.BlockSpec((2 * blk, blk), lambda s, place: (place[0], 0)),
-                pl.BlockSpec((1, tall, blk), lambda s, place: (1, 0, 0)),
-                pl.BlockSpec((1, tall, blk), lambda s, place: (1, 0, 0)),
                 pl.BlockSpec((tall, blk), lambda s, place: (0, 0)),
+                pl.BlockSpec((tall, blk), lambda s, place: (0, 0)),
+                pl.BlockSpec((tall, blk), lambda s, place: (0, 0)),
+                pl.BlockSpec(memory_space=pl.ANY),
             ],
-            out_specs=pl.BlockSpec((tall, blk), lambda s, place: (0, 0)),
+            out_specs=(
+                pl.BlockSpec((tall, blk), lambda s, place: (0, 0)),
+                pl.BlockSpec((2, 2, blk, blk), lambda s, place: (0, 0, 0, 0)),
+            ),
         ),
         compiler_params=pltpu.CompilerParams(vmem_limit_bytes=VMEM_LIMIT),
         cost_estimate=SMALL,
         name="right_roots",
-    )(place, stats, kept, near, far)
+    )(place, stats, kept, near, far, after)
 
 
 def left_kernel(full_dim, place, stats_ref, a_ref, b_ref, out_ref):
     blk = stats_ref.shape[1]
-    total = a_ref[...] + b_ref[...]
+    total = a_ref[...] + b_ref[b_ref.shape[0] - a_ref.shape[0] :, :]
     for b, root in enumerate(pair_roots(full_dim, stats_ref, total[:blk], total[blk : blk + 1])):
         high, low = split(root)
         out_ref[b, 0] = high
@@ -325,7 +363,7 @@
             in_specs=[
                 pl.BlockSpec((2 * blk, blk), lambda s, place: (place[1], 0)),
                 pl.BlockSpec((tall, blk), lambda s, place: (0, 0)),
-                pl.BlockSpec((tall, blk), lambda s, place: (0, 0)),
+                pl.BlockSpec(came.shape, lambda s, place: (0, 0)),
             ],
             out_specs=pl.BlockSpec((2, 2, blk, blk), lambda s, place: (0, 0, 0, 0)),
         ),
@@ -333,67 +371,204 @@
         cost_estimate=SMALL,
         name="left_roots",
     )(place, stats, kept, came)
+
+
+def raw_flip(place):
+    return 2 + (place[0] & 1)
+
+
+def put_roots(out_ref, at, body, diag):
+    for b, root in enumerate(unpack(body, diag)):
+        high, low = split(root)
+        out_ref[2 * at + b, 0] = high
+        out_ref[2 * at + b, 1] = low
 
 
 def spread_kernel(*refs):
     out_ref = refs[-1]
     blk = out_ref.shape[-1]
     for at, ref in enumerate(refs[:-1]):
-        for b, root in enumerate(unpack(ref[:blk, :], ref[blk : blk + 1, :])):
-            high, low = split(root)
-            out_ref[2 * at + b, 0] = high
-            out_ref[2 * at + b, 1] = low
-
-
-def spread_roots(packed):
+        put_roots(out_ref, at, ref[:blk, :], ref[blk : blk + 1, :])
+
+
+def spread_roots(*packed):
     blk = packed[0].shape[1]
-    count = len(packed)
     return pl.pallas_call(
         spread_kernel,
-        out_shape=jax.ShapeDtypeStruct((2 * count, 2, blk, blk), jnp.bfloat16),
+        out_shape=jax.ShapeDtypeStruct((2 * len(packed), 2, blk, blk), jnp.bfloat16),
         compiler_params=pltpu.CompilerParams(vmem_limit_bytes=VMEM_LIMIT),
         cost_estimate=SMALL,
         name="spread_roots",
     )(*packed)
 
 
+def cut_kernel(place, x_ref, xc_ref, out_ref):
+    half = out_ref.shape[0] - PAD
+
+    @pl.when((place[0] & 1) == 0)
+    def _():
+        out_ref[:half, :] = x_ref[:half, :]
+        out_ref[half:, :] = x_ref[2 * half :, :]
+
+    @pl.when((place[0] & 1) == 1)
+    def _():
+        out_ref[:half, :] = xc_ref[half : 2 * half, :]
+        out_ref[half:, :] = xc_ref[2 * half :, :]
+
+
+def cut(place, of_x, of_xc):
+    tall, blk = of_x.shape
+    whole = pl.BlockSpec((tall, blk), lambda s, place: (0, 0))
+    return pl.pallas_call(
+        cut_kernel,
+        out_shape=jax.ShapeDtypeStruct((blk // 2 + PAD, blk), jnp.float32),
+        grid_spec=pltpu.PrefetchScalarGridSpec(
+            num_scalar_prefetch=1,
+            grid=(1,),
+            in_specs=[whole, whole],
+            out_specs=pl.BlockSpec((blk // 2 + PAD, blk), lambda s, place: (0, 0)),
+        ),
+        compiler_params=pltpu.CompilerParams(vmem_limit_bytes=VMEM_LIMIT),
+        cost_estimate=SMALL,
+        name="cut",
+    )(place, of_x, of_xc)
+
+
+def rest_kernel(a_ref, out_ref):
+    out_ref[...] = a_ref[a_ref.shape[0] - out_ref.shape[0] :, :]
+
+
+def rest_of(value, rows):
+    return pl.pallas_call(
+        rest_kernel,
+        out_shape=jax.ShapeDtypeStruct((value.shape[0] - rows, value.shape[1]), jnp.float32),
+        compiler_params=pltpu.CompilerParams(vmem_limit_bytes=VMEM_LIMIT),
+        cost_estimate=SMALL,
+        name="rest_of",
+    )(value)
+
+
+def join_kernel(place, mine_ref, other_ref, out_ref, body):
+    half = mine_ref.shape[0] - PAD
+    core = place[0] & 1
+    body[pl.ds(pl.multiple_of(core * half, half), half), :] = mine_ref[:half, :]
+    body[pl.ds(pl.multiple_of((1 - core) * half, half), half), :] = other_ref[:half, :]
+    put_roots(out_ref, 0, body[...], mine_ref[half : half + 1, :])
+
+
+def join_roots(place, mine, other):
+    tall, blk = mine.shape
+    half = pl.BlockSpec((tall, blk), lambda s, place: (0, 0))
+    return pl.pallas_call(
+        join_kernel,
+        out_shape=jax.ShapeDtypeStruct((2, 2, blk, blk), jnp.bfloat16),
+        grid_spec=pltpu.PrefetchScalarGridSpec(
+            num_scalar_prefetch=1,
+            grid=(1,),
+            in_specs=[half, half],
+            out_specs=pl.BlockSpec((2, 2, blk, blk), lambda s, place: (0, 0, 0, 0)),
+            scratch_shapes=[pltpu.VMEM((blk, blk), jnp.float32)],
+        ),
+        compiler_params=pltpu.CompilerParams(vmem_limit_bytes=VMEM_LIMIT),
+        cost_estimate=SMALL,
+        name="join_roots",
+    )(place, mine, other)
+
+
+def right_apply_kernel(width, carries, place, g_ref, right_ref, *rest):
+    step = pl.program_id(0)
+    out_refs = rest[-len(width) :]
+    value = product(split(g_ref[...]), (right_ref[0, 0], right_ref[0, 1]))
+    blk = value.shape[1]
+    start = 0
+    for size, ref in zip(width, out_refs):
+        for b in range(start // blk, -(-(start + size) // blk)):
+            low, high = max(start, b * blk), min(start + size, (b + 1) * blk)
+
+            @pl.when(step == b)
+            def _():
+                ref[: value.shape[0], low - start : high - start] = value[:, low - b * blk : high - b * blk]
+
+        start += size
+    if carries:
+        out_refs[0][value.shape[0] :, :] = rest[0][...]
+
+
+def right_apply(place, tile, right, flip, right_at, first, width, under, after):
+    rows = tile.shape[0] // 2
+    blk = right.shape[-1]
+    in_specs = [
+        pl.BlockSpec((rows, blk), lambda s, place: (1 - place[1], (place[0] ^ flip(place)) * 2 + first + s)),
+        pl.BlockSpec((1, 2, blk, blk), lambda s, place: (right_at(place) + first + s, 0, 0, 0)),
+    ]
+    operands = [tile, right]
+    tall = rows
+    if under is not None:
+        tall += under.shape[0]
+        in_specs.append(pl.BlockSpec(under.shape, lambda s, place: (0, 0)))
+        operands.append(under)
+    return pl.pallas_call(
+        functools.partial(right_apply_kernel, width, under is not None),
+        out_shape=tuple(jax.ShapeDtypeStruct((tall, w), jnp.float32) for w in width),
+        grid_spec=pltpu.PrefetchScalarGridSpec(
+            num_scalar_prefetch=1,
+            grid=(sum(width) // blk,),
+            in_specs=in_specs + [pl.BlockSpec(memory_space=pl.ANY)] * len(after),
+            out_specs=tuple(pl.BlockSpec((tall, w), lambda s, place: (0, 0)) for w in width),
+        ),
+        compiler_params=pltpu.CompilerParams(vmem_limit_bytes=VMEM_LIMIT),
+        cost_estimate=SMALL,
+        name="right_apply",
+    )(place, *operands, *after)
+
+
+def left_product(left_ref, value, out_ref):
+    blk = left_ref.shape[-1]
+    for i in range(value.shape[0] // blk):
+        part = split(value[i * blk : (i + 1) * blk])
+        out_ref[i * blk : (i + 1) * blk, :] = product((left_ref[i, 0], left_ref[i, 1]), part)
+
+
 def update_kernel(place, g_ref, left_ref, right_ref, *rest):
-    out_ref = rest[-1]
-    blk = right_ref.shape[-1]
-    right = (right_ref[0, 0], right_ref[0, 1])
-    half = product(split(g_ref[...]), right)
-    for i in range(g_ref.shape[0] // blk):
-        part = split(half[i * blk : (i + 1) * blk])
-        out_ref[i * blk : (i + 1) * blk, :] = product((left_ref[i, 0], left_ref[i, 1]), part)
-
-
-def update(place, source, left, right, out, out_shape, blocks, g_map, right_at, out_map):
-    blk = right.shape[-1]
+    half = product(split(g_ref[...]), (right_ref[0, 0], right_ref[0, 1]))
+    left_product(left_ref, half, rest[-2])
+    rest[-1][...] = jnp.zeros_like(rest[-1])
+
+
+def finish_kernel(place, half_ref, left_ref, out_before, out_ref, done_ref):
+    left_product(left_ref, half_ref[...], out_ref)
+    done_ref[...] = jnp.zeros_like(done_ref)
+
+
+def into_output(kernel, name, place, source, left, right, out, out_shape, wide, steps, g_map, right_at, out_map):
     rows = out_shape[0]
+    blk = left.shape[-1]
     in_specs = [
-        pl.BlockSpec((rows, blk), g_map),
+        pl.BlockSpec((rows, wide), g_map),
         pl.BlockSpec((2, 2, blk, blk), lambda s, place: (0, 0, 0, 0)),
-        pl.BlockSpec((1, 2, blk, blk), lambda s, place: (right_at + s, 0, 0, 0)),
     ]
-    operands = [source, left, right]
+    operands = [source, left]
+    if right is not None:
+        in_specs.append(pl.BlockSpec((1, 2, blk, blk), lambda s, place: (right_at + s, 0, 0, 0)))
+        operands.append(right)
     aliases = {}
     if out is not None:
+        aliases = {1 + len(operands): 0}
         in_specs.append(pl.BlockSpec(memory_space=pl.ANY))
         operands.append(out)
-        aliases = {4: 0}
-    return pl.pallas_call(
-        update_kernel,
-        out_shape=jax.ShapeDtypeStruct(out_shape, jnp.float32),
-        grid_spec=pltpu.PrefetchScalarGridSpec(
-            num_scalar_prefetch=1,
-            grid=(blocks,),
+    return pl.pallas_call(
+        kernel,
+        out_shape=(jax.ShapeDtypeStruct(out_shape, jnp.float32), jax.ShapeDtypeStruct((8, 128), jnp.float32)),
+        grid_spec=pltpu.PrefetchScalarGridSpec(
+            num_scalar_prefetch=1,
+            grid=(steps,),
             in_specs=in_specs,
-            out_specs=pl.BlockSpec((rows, blk), out_map),
+            out_specs=(pl.BlockSpec((rows, wide), out_map), pl.BlockSpec((8, 128), lambda s, place: (0, 0))),
         ),
         input_output_aliases=aliases,
         compiler_params=pltpu.CompilerParams(vmem_limit_bytes=VMEM_LIMIT),
         cost_estimate=SMALL,
-        name="update",
+        name=name,
     )(place, *operands)
 
 
@@ -407,57 +582,87 @@
     c = lax.axis_index("col")
     place = jnp.stack([r, c]).astype(jnp.int32)
     rows = tile_rows // 2
+    shape = (rows, 2 * tile_cols)
     halves = tile_cols // blk
 
     def over(axis, value):
-        if axis == "col":
+        if axis == "y":
             return lax.ppermute(value, "col", [(0, 1), (1, 0)])
         flip = {"core": 1, "x": 2}[axis]
         return lax.ppermute(value, "row", [(i, i ^ flip) for i in range(n_row)])
 
-    chunks = [(0, 0, 2), (1, 0, 2), (2, 0, 2), (3, 0, 1), (3, 1, 1)]
-    first = take(place, tile, blk, chunks[0], ())
-    came = [over("col", first)]
-
-    send, keep, lsend, lkeep = grams(place, tile, blk, first)
+    first = take(place, tile, blk)
+    raw = over("y", first)
+
+    send_on, send, keep_on, keep = right_grams(place, tile, blk, first)
+    near_on = over("core", send_on)
     near = over("core", send)
-    lcame = over("col", lsend)
-    for k in (1,):
-        came.append(over("col", take(place, tile, blk, chunks[k], (lsend,))))
-    far = over("x", fold(keep, near, came[0]))
-    own = right_roots(full_dim, place, rstats, keep, near, far)
-    across = over("col", own)
-    for k in (2, 3, 4):
-        came.append(over("col", take(place, tile, blk, chunks[k], (own,))))
-    left = left_roots(full_dim, place, lstats, lkeep, lcame)
-
+    lsend, lkeep = left_grams(place, tile, blk, send)
+    far = over("x", fold(keep_on, near_on))
+    own, roots_own = right_roots(full_dim, place, rstats, keep, near, far, lsend)
+
+    own_pair, core_pair = (lambda place: 0), (lambda place: 1)
+    last_pair = lambda place: 3 - (place[0] & 1)
+    begin = lambda place: 0
+    last_at = lambda place: 2 * (1 - (place[0] & 1))
+    tail = (blk, blk // 2, blk // 2)
+
+    held = right_apply(place, tile, roots_own, own_pair, begin, 0, (blk,), lsend, ())
+    came_0a = over("y", held[0])
+    own = hold(own, raw, held[0])
+    own_c = over("core", own)
     own_x = over("x", own)
-    own_c = over("core", own)
     own_xc = over("core", own_x)
-    mine = spread_roots([own, own_c, own_x, own_xc])
-    across_x = over("x", across)
-    across_c = over("core", across)
-    across_xc = over("core", across_x)
-    theirs = spread_roots([across, across_c, across_x, across_xc])
-
-    def block_of(flip_block, place):
-        return ((place[0] ^ (flip_block // 2)) * 2) + flip_block % 2
-
-    shape = (rows, 2 * tile_cols)
-    out = update(
-        place, tile, left, mine, None, shape, halves,
-        lambda s, place: (place[1], block_of(s, place)),
-        0,
-        lambda s, place: (0, place[1] * halves + block_of(s, place)),
+    held = right_apply(place, tile, roots_own, own_pair, begin, 1, (blk,), None, (own,))
+    came_0b = over("y", held[0])
+    roots_core = spread_roots(own_c)
+    held = right_apply(place, tile, roots_core, core_pair, begin, 0, (2 * blk,), None, (came_0a, own_xc))
+    came_1 = over("y", held[0])
+    own_x = hold(own_x, came_0b)
+    roots_far = spread_roots(own_x, own_xc)
+    held = right_apply(place, tile, roots_far, last_pair, last_at, 0, tail[:1], cut(place, own_x, own_xc), ())
+    came_2 = [over("y", held[0])]
+    mine = rest_of(came_2[0], rows)
+    roots_raw = join_roots(place, mine, over("core", mine))
+
+    left = left_roots(full_dim, place, lstats, lkeep, came_0a)
+
+    def own_cols(base):
+        return lambda s, place: (place[1], (place[0] ^ (base + s // 2)) * 2 + s % 2)
+
+    out = None
+    for base, roots in ((0, roots_own), (1, roots_core), (2, roots_far)):
+        at = own_cols(base)
+        out, done = into_output(
+            update_kernel, "update", place, tile, left, roots, out, shape, blk, roots.shape[0], at, 0,
+            lambda s, place, at=at: (0, place[1] * halves + at(s, place)[1]),
+        )
+
+    def finish(out, value, wide, width, start, flip):
+        per_pair = 2 * blk // wide
+        return into_output(
+            finish_kernel, "finish", place, value, left, None, out, shape, wide, width // wide,
+            lambda s, place: (0, s), 0,
+            lambda s, place: (
+                0,
+                (1 - place[1]) * (tile_cols // wide) + (place[0] ^ flip(place)) * per_pair + start // wide + s,
+            ),
+        )
+
+    for b, value in enumerate((came_0a, came_0b)):
+        out, done = finish(out, value, blk, blk, b * blk, own_pair)
+    held = right_apply(place, tile, roots_far, last_pair, last_at, 1, tail[1:], None, (came_1, done))
+    came_2 += [over("y", half) for half in held]
+    out, done = finish(out, came_1, blk, 2 * blk, 0, core_pair)
+    out, done = into_output(
+        update_kernel, "update", place, raw, left, roots_raw, out, shape, blk, 2,
+        lambda s, place: (0, s), 0,
+        lambda s, place: (0, (1 - place[1]) * halves + (place[0] ^ raw_flip(place)) * 2 + s),
     )
-    for (flip, at, blocks), value in zip(chunks, came):
-        base = 2 * flip + at
-        out = update(
-            place, value, left, theirs, out, shape, blocks,
-            lambda s, place: (0, s),
-            base,
-            lambda s, place, base=base: (0, (1 - place[1]) * halves + block_of(base + s, place)),
-        )
+    start = 0
+    for wide, value in zip(tail, came_2):
+        out, done = finish(out, value, wide, wide, start, last_pair)
+        start += wide
     return out.reshape(1, rows, 2 * tile_cols)
 
 

time: 118 us -> 112 us (0.949)
  waiting for transfers between devices: 46.3 us -> 33.1 us
  Pallas kernels: 55.4 us -> 67.1 us
  starting transfers between devices: 15.2 us -> 10.8 us
    ppermute x7, waiting for transfers between devices: 38.3 us -> 22.8 us  [over(): return lax.ppermute(value, 'col', [(0, 1), (1, 0)])]
    pallas_call x16 -> x27, Pallas kernels: 51.9 us -> 63.5 us  [the longest x10 29.8 us: into_output(): pl.pallas_call(kernel, out_shape=(jax.ShapeDtypeStruct(out_shape, jnp.flo...]
    ppermute x8 -> x7, waiting for transfers between devices: 7.96 us -> 10.3 us  [over(): return lax.ppermute(value, 'row', [(i, i ^ flip) for i in range(n_row)])]
    ppermute x7, starting transfers between devices: 10.7 us -> 8.43 us  [over(): return lax.ppermute(value, 'col', [(0, 1), (1, 0)])]
    ppermute x8 -> x7, starting transfers between devices: 4.51 us -> 2.34 us  [over(): return lax.ppermute(value, 'row', [(i, i ^ flip) for i in range(n_row)])]
  transfers between devices with their start and end apart: 15 -> 14, of which waited for: 8 -> 6; matrix products, arithmetic and copies ran while one was open for 0% -> 0% of each run, Pallas kernels for 44% -> 57%
where the time goes in v1:
time: 112 us; the launch traced here: 111 us
  Pallas kernels  67.1 us (60%)
  waiting for transfers between devices  33.1 us (30%)
  starting transfers between devices  10.8 us (10%)
    pallas_call x10, Pallas kernels, into_output(): pl.pallas_call(kernel, out_shape=(jax.ShapeDtypeStruct(out_shape, jnp.flo...  29.8 us
    ppermute x7, waiting for transfers between devices, over(): return lax.ppermute(value, 'col', [(0, 1), (1, 0)])  22.8 us
    pallas_call x5, Pallas kernels, right_apply(): pl.pallas_call(functools.partial(right_apply_kernel, width, under is not...  10.3 us
    ppermute x7, waiting for transfers between devices, over(): return lax.ppermute(value, 'row', [(i, i ^ flip) for i in range(n_row)])  10.3 us
    pallas_call x1, Pallas kernels, left_grams(): pl.pallas_call(left_gram_kernel, out_shape=(flat, flat), grid_spec=pltpu....  9.52 us
    ppermute x7, starting transfers between devices, over(): return lax.ppermute(value, 'col', [(0, 1), (1, 0)])  8.43 us
    pallas_call x1, Pallas kernels, right_grams(): pl.pallas_call(right_gram_kernel, out_shape=(jax.ShapeDtypeStruct((tall,...  6.53 us
    pallas_call x1, Pallas kernels, right_roots(): pl.pallas_call(functools.partial(right_kernel, full_dim), out_shape=(jax....  3.57 us
  transfers between devices with their start and end apart: 14, of which 6 were waited for; matrix products, arithmetic and copies ran while one was open for 0% of the time, Pallas kernels for 57%

profile of v1, /device:TPU:0, one launch (start us, length us, event | category | flops | bytes accessed | tf_op | source)
XLA Modules:
  0.0 111.2 jit_solution(13318998569733388162)
XLA Ops:
  0.1 1.8 %take.1.after_ref = f32[512,512]{1,0:T(8,128)S(1)} custom-call(s32[2]{0:T(128)S(1)} %pad_add_fusion.place, f32[1024,2048]{1,0:T(8,128)} %bitcast.8), custom_call_target="tpu_custom_call" | custom-call | flops 1 | bytes 1 | tf_op jit(solution)/shard_map/take/pallas_call | solution.py:227
  1.9 3.0 %collective-permute-start.3 = (f32[512,512]{1,0:T(8,128)S(1)}, f32[512,512]{1,0:T(8,128)S(1)}, u32[]{:S(2)}, u32[]{:S(2)}) collective-permute-start(f32[512,512]{1,0:T(8,128)S(1)} %take.1.after_ref), channel_id=1, source_target_pairs={{0,4},{4,0},{1,5},{5,1},{2,6},{6,2},{3,7},{7,3},{8,12},{12,8},{9,1... | collective-permute-start | bytes 3145736 | tf_op jit(solution)/shard_map/ppermute | solution.py:590
  4.9 6.5 %right_grams.1 = (f32[264,256]{1,0:T(8,128)S(1)}, f32[264,256]{1,0:T(8,128)S(1)}, f32[264,256]{1,0:T(8,128)S(1)}, f32[264,256]{1,0:T(8,128)S(1)}) custom-call(s32[2]{0:T(128)S(1)} %pad_add_fusion.place, f32[1024,2048]{1,0:T(8,128)} %bitcast.9, f32[512,512]{1,0:T(8,128)S(1)} %take.1.after_ref), custom_call_target="tpu_custom_call" | custom-call | flops 1 | bytes 1 | tf_op jit(solution)/shard_map/right_grams/pallas_call | solution.py:138
  14.6 9.5 %left_grams.1 = (f32[264,256]{1,0:T(8,128)S(1)}, f32[264,256]{1,0:T(8,128)S(1)}) custom-call(s32[2]{0:T(128)S(1)} %pad_add_fusion.place, f32[1024,2048]{1,0:T(8,128)} %bitcast.10, f32[264,256]{1,0:T(8,128)S(1)} %get-tuple-element.27.after_ref), custom_call_target="tpu_custom_call" | custom-call | flops 1 | bytes 1 | tf_op jit(solution)/shard_map/left_grams/pallas_call | solution.py:192
  24.2 3.6 %right_roots.1 = (f32[264,256]{1,0:T(8,128)S(1)}, bf16[2,2,256,256]{3,2,1,0:T(8,128)(2,1)S(1)}) custom-call(s32[2]{0:T(128)S(1)} %pad_add_fusion.place, f32[2048,256]{1,0:T(8,128)S(1)} %bitcast.6, f32[264,256]{1,0:T(8,128)S(1)} %get-tuple-element.26.a_ref, f32[264,256]{1,0:T(8,128)S(1)} %collective-permute-done.b_ref, ...), custom_call_target="tpu_custom_call" | custom-call | flops 1 | bytes 1 | tf_op jit(solution)/shard_map/right_roots/pallas_call | solution.py:318
  27.8 2.0 %right_apply.5.rest_1_ = f32[776,256]{1,0:T(8,128)S(1)} custom-call(s32[2]{0:T(128)S(1)} %pad_add_fusion.place, f32[1024,2048]{1,0:T(8,128)} %bitcast.11, bf16[2,2,256,256]{3,2,1,0:T(8,128)(2,1)S(1)} %get-tuple-element.32.right_ref, f32[264,256]{1,0:T(8,128)S(1)} %get-tuple-element.30.after_ref.rest_0_), custom_call_target="tpu_custom_call" | custom-call | flops 1 | bytes 1 | tf_op jit(solution)/shard_map/right_apply/pallas_call | solution.py:510
  30.5 7.9 %collective-permute-done.4.a_ref = f32[264,256]{1,0:T(8,128)S(1)} collective-permute-done((f32[264,256]{1,0:T(8,128)S(1)}, f32[264,256]{1,0:T(8,128)S(1)}, u32[]{:S(2)}, u32[]{:S(2)}) %collective-permute-start.4) | collective-permute-done | bytes 270368 | tf_op jit(solution)/shard_map/ppermute | solution.py:592
  38.4 2.0 %right_apply.6 = f32[512,256]{1,0:T(8,128)S(1)} custom-call(s32[2]{0:T(128)S(1)} %pad_add_fusion.place, f32[1024,2048]{1,0:T(8,128)} %bitcast.12, bf16[2,2,256,256]{3,2,1,0:T(8,128)(2,1)S(1)} %get-tuple-element.32.right_ref, f32[264,256]{1,0:T(8,128)S(1)} %hold.2.rest_0_), custom_call_target="tpu_custom_call" | custom-call | flops 1 | bytes 1 | tf_op jit(solution)/shard_map/right_apply/pallas_call | solution.py:510
  42.1 8.3 %collective-permute-done.8.rest_0_.b_ref.half_ref = f32[776,256]{1,0:T(8,128)S(1)} collective-permute-done((f32[776,256]{1,0:T(8,128)S(1)}, f32[776,256]{1,0:T(8,128)S(1)}, u32[]{:S(2)}, u32[]{:S(2)}) %collective-permute-start.8) | collective-permute-done | bytes 794656 | tf_op jit(solution)/shard_map/ppermute | solution.py:590
  50.4 2.4 %right_apply.7 = f32[512,512]{1,0:T(8,128)S(1)} custom-call(s32[2]{0:T(128)S(1)} %pad_add_fusion.place, f32[1024,2048]{1,0:T(8,128)} %bitcast.13, bf16[2,2,256,256]{3,2,1,0:T(8,128)(2,1)S(1)} %spread_roots.3.right_ref, f32[776,256]{1,0:T(8,128)S(1)} %collective-permute-done.8.rest_0_.b_ref.half_ref, f32[264,256]{1,0:T(8,128)S(1)} %collective-permute-done.6.refs_1_.rest_1_.xc_ref), custom_call_target="tpu_custom_call" | custom-call | flops 1 | bytes 1 | tf_op jit(solution)/shard_map/right_apply/pallas_call | solution.py:510
  53.5 8.2 %collective-permute-done.5.rest_0_.half_ref = f32[512,256]{1,0:T(8,128)S(1)} collective-permute-done((f32[512,256]{1,0:T(8,128)S(1)}, f32[512,256]{1,0:T(8,128)S(1)}, u32[]{:S(2)}, u32[]{:S(2)}) %collective-permute-start.5) | collective-permute-done | bytes 524320 | tf_op jit(solution)/shard_map/ppermute | solution.py:590
  62.7 2.0 %right_apply.9 = f32[648,256]{1,0:T(8,128)S(1)} custom-call(s32[2]{0:T(128)S(1)} %pad_add_fusion.place, f32[1024,2048]{1,0:T(8,128)} %bitcast.14, bf16[4,2,256,256]{3,2,1,0:T(8,128)(2,1)S(1)} %spread_roots.2.right_ref, f32[136,256]{1,0:T(8,128)S(1)} %cut.1.rest_0_), custom_call_target="tpu_custom_call" | custom-call | flops 1 | bytes 1 | tf_op jit(solution)/shard_map/right_apply/pallas_call | solution.py:510
  65.3 3.5 %left_roots.1.left_ref = bf16[2,2,256,256]{3,2,1,0:T(8,128)(2,1)S(1)} custom-call(s32[2]{0:T(128)S(1)} %pad_add_fusion.place, f32[1024,256]{1,0:T(8,128)S(1)} %bitcast.7, f32[264,256]{1,0:T(8,128)S(1)} %get-tuple-element.33.a_ref, f32[776,256]{1,0:T(8,128)S(1)} %collective-permute-done.8.rest_0_.b_ref.half_ref), custom_call_target="tpu_custom_call" | custom-call | flops 1 | bytes 1 | tf_op jit(solution)/shard_map/left_roots/pallas_call | solution.py:357
  68.8 4.5 %update.4 = (f32[512,4096]{1,0:T(8,128)}, f32[8,128]{1,0:T(8,128)}) custom-call(s32[2]{0:T(128)S(1)} %pad_add_fusion.place, f32[1024,2048]{1,0:T(8,128)} %bitcast.15, bf16[2,2,256,256]{3,2,1,0:T(8,128)(2,1)S(1)} %left_roots.1.left_ref, bf16[2,2,256,256]{3,2,1,0:T(8,128)(2,1)S(1)} %get-tuple-element.32.right_ref), custom_call_target="tpu_custom_call" | custom-call | flops 1 | bytes 1 | tf_op jit(solution)/shard_map/update/pallas_call | solution.py:559
  73.3 4.5 %update.5 = (f32[512,4096]{1,0:T(8,128)}, f32[8,128]{1,0:T(8,128)}) custom-call(s32[2]{0:T(128)S(1)} %pad_add_fusion.place, f32[1024,2048]{1,0:T(8,128)} %bitcast.16, bf16[2,2,256,256]{3,2,1,0:T(8,128)(2,1)S(1)} %left_roots.1.left_ref, bf16[2,2,256,256]{3,2,1,0:T(8,128)(2,1)S(1)} %spread_roots.3.right_ref, ...), custom_call_target="tpu_custom_call", output_to_operand_aliasing={{0}: (4, {})} | custom-call | flops 1 | bytes 1 | tf_op jit(solution)/shard_map/update/pallas_call | solution.py:559
  77.7 6.8 %update.6 = (f32[512,4096]{1,0:T(8,128)}, f32[8,128]{1,0:T(8,128)}) custom-call(s32[2]{0:T(128)S(1)} %pad_add_fusion.place, f32[1024,2048]{1,0:T(8,128)} %bitcast.17, bf16[2,2,256,256]{3,2,1,0:T(8,128)(2,1)S(1)} %left_roots.1.left_ref, bf16[4,2,256,256]{3,2,1,0:T(8,128)(2,1)S(1)} %spread_roots.2.right_ref, ...), custom_call_target="tpu_custom_call", output_to_operand_aliasing={{0}: (4, {})} | custom-call | flops 1 | bytes 1 | tf_op jit(solution)/shard_map/update/pallas_call | solution.py:559
  84.5 1.7 %finish.6 = (f32[512,4096]{1,0:T(8,128)}, f32[8,128]{1,0:T(8,128)}) custom-call(s32[2]{0:T(128)S(1)} %pad_add_fusion.place, f32[776,256]{1,0:T(8,128)S(1)} %collective-permute-done.8.rest_0_.b_ref.half_ref, bf16[2,2,256,256]{3,2,1,0:T(8,128)(2,1)S(1)} %left_roots.1.left_ref, f32[512,4096]{1,0:T(8,128)} %get-tuple-element.36.out_before), custom_call_target="tpu_custom_call", output_to_operand_aliasing={{0}: (3, {})} | custom-call | flops 1 | bytes 1 | tf_op jit(solution)/shard_map/finish/pallas_call | solution.py:559
  86.3 1.7 %finish.7 = (f32[512,4096]{1,0:T(8,128)}, f32[8,128]{1,0:T(8,128)S(1)}) custom-call(s32[2]{0:T(128)S(1)} %pad_add_fusion.place, f32[512,256]{1,0:T(8,128)S(1)} %collective-permute-done.5.rest_0_.half_ref, bf16[2,2,256,256]{3,2,1,0:T(8,128)(2,1)S(1)} %left_roots.1.left_ref, f32[512,4096]{1,0:T(8,128)} %get-tuple-element.37.out_before), custom_call_target="tpu_custom_call", output_to_operand_aliasing={{0}: (3, {})} | custom-call | flops 1 | bytes 1 | tf_op jit(solution)/shard_map/finish/pallas_call | solution.py:559
  88.0 2.0 %right_apply.8 = (f32[512,128]{1,0:T(8,128)S(1)}, f32[512,128]{1,0:T(8,128)S(1)}) custom-call(s32[2]{0:T(128)S(1)} %pad_add_fusion.place, f32[1024,2048]{1,0:T(8,128)} %bitcast.18, bf16[4,2,256,256]{3,2,1,0:T(8,128)(2,1)S(1)} %spread_roots.2.right_ref, f32[512,512]{1,0:T(8,128)S(1)} %collective-permute-done.9.rest_0_.half_ref, ...), custom_call_target="tpu_custom_call" | custom-call | flops 1 | bytes 1 | tf_op jit(solution)/shard_map/right_apply/pallas_call | solution.py:510
  92.0 6.3 %collective-permute-done.12.a_ref.half_ref = f32[648,256]{1,0:T(8,128)S(1)} collective-permute-done((f32[648,256]{1,0:T(8,128)S(1)}, f32[648,256]{1,0:T(8,128)S(1)}, u32[]{:S(2)}, u32[]{:S(2)}) %collective-permute-start.12) | collective-permute-done | bytes 663584 | tf_op jit(solution)/shard_map/ppermute | solution.py:590
  100.5 2.2 %finish.8 = (f32[512,4096]{1,0:T(8,128)}, f32[8,128]{1,0:T(8,128)}) custom-call(s32[2]{0:T(128)S(1)} %pad_add_fusion.place, f32[512,512]{1,0:T(8,128)S(1)} %collective-permute-done.9.rest_0_.half_ref, bf16[2,2,256,256]{3,2,1,0:T(8,128)(2,1)S(1)} %left_roots.1.left_ref, f32[512,4096]{1,0:T(8,128)} %get-tuple-element.41.out_before), custom_call_target="tpu_custom_call", output_to_operand_aliasing={{0}: (3, {})} | custom-call | flops 1 | bytes 1 | tf_op jit(solution)/shard_map/finish/pallas_call | solution.py:559
  102.8 3.5 %update.7 = (f32[512,4096]{1,0:T(8,128)}, f32[8,128]{1,0:T(8,128)}) custom-call(s32[2]{0:T(128)S(1)} %pad_add_fusion.place, f32[512,512]{1,0:T(8,128)S(1)} %collective-permute-done.3.rest_0_.g_ref, bf16[2,2,256,256]{3,2,1,0:T(8,128)(2,1)S(1)} %left_roots.1.left_ref, ...), custom_call_target="tpu_custom_call", output_to_operand_aliasing={{0}: (4, {})} | custom-call | flops 1 | bytes 1 | tf_op jit(solution)/shard_map/update/pallas_call | solution.py:559
  106.3 1.7 %finish.9 = (f32[512,4096]{1,0:T(8,128)}, f32[8,128]{1,0:T(8,128)}) custom-call(s32[2]{0:T(128)S(1)} %pad_add_fusion.place, f32[648,256]{1,0:T(8,128)S(1)} %collective-permute-done.12.a_ref.half_ref, bf16[2,2,256,256]{3,2,1,0:T(8,128)(2,1)S(1)} %left_roots.1.left_ref, f32[512,4096]{1,0:T(8,128)} %get-tuple-element.43.out_before), custom_call_target="tpu_custom_call", output_to_operand_aliasing={{0}: (3, {})} | custom-call | flops 1 | bytes 1 | tf_op jit(solution)/shard_map/finish/pallas_call | solution.py:559
  109.6 1.6 %finish.11 = (f32[512,4096]{1,0:T(8,128)}, f32[8,128]{1,0:T(8,128)}) custom-call(s32[2]{0:T(128)S(1)} %pad_add_fusion.place, f32[512,128]{1,0:T(8,128)S(1)} %collective-permute-done.10.half_ref, bf16[2,2,256,256]{3,2,1,0:T(8,128)(2,1)S(1)} %left_roots.1.left_ref, f32[512,4096]{1,0:T(8,128)} %get-tuple-element.45.out_before), custom_call_target="tpu_custom_call", output_to_operand_aliasing={{0}: (3, {})} | custom-call | flops 1 | bytes 1 | tf_op jit(solution)/shard_map/finish/pallas_call | solution.py:559
  (37 shorter events, 13.8 us)
Async XLA Ops:
  1.9 22.3 %copy-start = (f32[1,2048,256]{2,1,0:T(8,128)S(1)}, f32[1,2048,256]{2,1,0:T(8,128)}, u32[]{:S(2)}) copy-start(f32[1,2048,256]{2,1,0:T(8,128)} %param.5) | copy-start | bytes 6291460
  1.9 28.5 %collective-permute-start.3 = (f32[512,512]{1,0:T(8,128)S(1)}, f32[512,512]{1,0:T(8,128)S(1)}, u32[]{:S(2)}, u32[]{:S(2)}) collective-permute-start(f32[512,512]{1,0:T(8,128)S(1)} %take.1.after_ref), channel_id=1, source_target_pairs={{0,4},{4,0},{1,5},{5,1},{2,6},{6,2},{3,7},{7,3},{8,12},{12,8},{9,1... | collective-permute-start | bytes 3145736 | tf_op jit(solution)/shard_map/ppermute | solution.py:590
  11.4 1.6 %collective-permute-start.1 = (f32[264,256]{1,0:T(8,128)S(1)}, f32[264,256]{1,0:T(8,128)S(1)}, u32[]{:S(2)}, u32[]{:S(2)}) collective-permute-start(f32[264,256]{1,0:T(8,128)S(1)} %get-tuple-element.29), channel_id=1, source_target_pairs={{0,8},{8,0},{16,24},{24,16},{1,9},{9,1},{17,25},{25,17},{2,10},{10... | collective-permute-start | bytes 811016 | tf_op jit(solution)/shard_map/ppermute | solution.py:592
  11.5 12.6 %collective-permute-start = (f32[264,256]{1,0:T(8,128)S(1)}, f32[264,256]{1,0:T(8,128)S(1)}, u32[]{:S(2)}, u32[]{:S(2)}) collective-permute-start(f32[264,256]{1,0:T(8,128)S(1)} %get-tuple-element.27.after_ref), channel_id=1, source_target_pairs={{0,8},{8,0},{16,24},{24,16},{1,9},{9,1},{17,25},{25,17},{2,10},{10... | collective-permute-start | bytes 811016 | tf_op jit(solution)/shard_map/ppermute | solution.py:592
  13.1 11.1 %collective-permute-start.2 = (f32[264,256]{1,0:T(8,128)S(1)}, f32[264,256]{1,0:T(8,128)S(1)}, u32[]{:S(2)}, u32[]{:S(2)}) collective-permute-start(f32[264,256]{1,0:T(8,128)S(1)} %fold.1), channel_id=1, source_target_pairs={{0,16},{8,24},{16,0},{24,8},{1,17},{9,25},{17,1},{25,9},{2,18},{10... | collective-permute-start | bytes 811016 | tf_op jit(solution)/shard_map/ppermute | solution.py:592
  29.8 20.7 %collective-permute-start.8 = (f32[776,256]{1,0:T(8,128)S(1)}, f32[776,256]{1,0:T(8,128)S(1)}, u32[]{:S(2)}, u32[]{:S(2)}) collective-permute-start(f32[776,256]{1,0:T(8,128)S(1)} %right_apply.5.rest_1_), channel_id=1, source_target_pairs={{0,4},{4,0},{1,5},{5,1},{2,6},{6,2},{3,7},{7,3},{8,12},{12,8},{9,1... | collective-permute-start | bytes 2383880 | tf_op jit(solution)/shard_map/ppermute | solution.py:590
  30.4 8.0 %collective-permute-start.4 = (f32[264,256]{1,0:T(8,128)S(1)}, f32[264,256]{1,0:T(8,128)S(1)}, u32[]{:S(2)}, u32[]{:S(2)}) collective-permute-start(f32[264,256]{1,0:T(8,128)S(1)} %hold.2.rest_0_), channel_id=1, source_target_pairs={{0,16},{8,24},{16,0},{24,8},{1,17},{9,25},{17,1},{25,9},{2,18},{10... | collective-permute-start | bytes 811016 | tf_op jit(solution)/shard_map/ppermute | solution.py:592
  30.5 11.4 %collective-permute-start.7 = (f32[264,256]{1,0:T(8,128)S(1)}, f32[264,256]{1,0:T(8,128)S(1)}, u32[]{:S(2)}, u32[]{:S(2)}) collective-permute-start(f32[264,256]{1,0:T(8,128)S(1)} %hold.2.rest_0_), channel_id=1, source_target_pairs={{0,8},{8,0},{16,24},{24,16},{1,9},{9,1},{17,25},{25,17},{2,10},{10... | collective-permute-start | bytes 811016 | tf_op jit(solution)/shard_map/ppermute | solution.py:592
  38.4 12.0 %collective-permute-start.6 = (f32[264,256]{1,0:T(8,128)S(1)}, f32[264,256]{1,0:T(8,128)S(1)}, u32[]{:S(2)}, u32[]{:S(2)}) collective-permute-start(f32[264,256]{1,0:T(8,128)S(1)} %collective-permute-done.4.a_ref), channel_id=1, source_target_pairs={{0,8},{8,0},{16,24},{24,16},{1,9},{9,1},{17,25},{25,17},{2,10},{10... | collective-permute-start | bytes 811016 | tf_op jit(solution)/shard_map/ppermute | solution.py:592
  40.4 21.3 %collective-permute-start.5 = (f32[512,256]{1,0:T(8,128)S(1)}, f32[512,256]{1,0:T(8,128)S(1)}, u32[]{:S(2)}, u32[]{:S(2)}) collective-permute-start(f32[512,256]{1,0:T(8,128)S(1)} %right_apply.6), channel_id=1, source_target_pairs={{0,4},{4,0},{1,5},{5,1},{2,6},{6,2},{3,7},{7,3},{8,12},{12,8},{9,1... | collective-permute-start | bytes 1572872 | tf_op jit(solution)/shard_map/ppermute | solution.py:590
  52.9 12.4 %copy-start.1 = (f32[1,1024,256]{2,1,0:T(8,128)S(1)}, f32[1,1024,256]{2,1,0:T(8,128)}, u32[]{:S(2)}) copy-start(f32[1,1024,256]{2,1,0:T(8,128)} %param.4) | copy-start | bytes 3145732
  52.9 35.1 %collective-permute-start.9 = (f32[512,512]{1,0:T(8,128)S(1)}, f32[512,512]{1,0:T(8,128)S(1)}, u32[]{:S(2)}, u32[]{:S(2)}) collective-permute-start(f32[512,512]{1,0:T(8,128)S(1)} %right_apply.7), channel_id=1, source_target_pairs={{0,4},{4,0},{1,5},{5,1},{2,6},{6,2},{3,7},{7,3},{8,12},{12,8},{9,1... | collective-permute-start | bytes 3145736 | tf_op jit(solution)/shard_map/ppermute | solution.py:590
  64.7 33.7 %collective-permute-start.12 = (f32[648,256]{1,0:T(8,128)S(1)}, f32[648,256]{1,0:T(8,128)S(1)}, u32[]{:S(2)}, u32[]{:S(2)}) collective-permute-start(f32[648,256]{1,0:T(8,128)S(1)} %right_apply.9), channel_id=1, source_target_pairs={{0,4},{4,0},{1,5},{5,1},{2,6},{6,2},{3,7},{7,3},{8,12},{12,8},{9,1... | collective-permute-start | bytes 1990664 | tf_op jit(solution)/shard_map/ppermute | solution.py:590
  90.0 18.0 %collective-permute-start.11 = (f32[512,128]{1,0:T(8,128)S(1)}, f32[512,128]{1,0:T(8,128)S(1)}, u32[]{:S(2)}, u32[]{:S(2)}) collective-permute-start(f32[512,128]{1,0:T(8,128)S(1)} %get-tuple-element.40), channel_id=1, source_target_pairs={{0,4},{4,0},{1,5},{5,1},{2,6},{6,2},{3,7},{7,3},{8,12},{12,8},{9,1... | collective-permute-start | bytes 786440 | tf_op jit(solution)/shard_map/ppermute | solution.py:590
  91.5 18.1 %collective-permute-start.10 = (f32[512,128]{1,0:T(8,128)S(1)}, f32[512,128]{1,0:T(8,128)S(1)}, u32[]{:S(2)}, u32[]{:S(2)}) collective-permute-start(f32[512,128]{1,0:T(8,128)S(1)} %get-tuple-element.39), channel_id=1, source_target_pairs={{0,4},{4,0},{1,5},{5,1},{2,6},{6,2},{3,7},{7,3},{8,12},{12,8},{9,1... | collective-permute-start | bytes 786440 | tf_op jit(solution)/shard_map/ppermute | solution.py:590
  98.4 1.4 %collective-permute-start.13 = (f32[136,256]{1,0:T(8,128)S(1)}, f32[136,256]{1,0:T(8,128)S(1)}, u32[]{:S(2)}, u32[]{:S(2)}) collective-permute-start(f32[136,256]{1,0:T(8,128)S(1)} %rest_of.1.mine_ref), channel_id=1, source_target_pairs={{0,8},{8,0},{16,24},{24,16},{1,9},{9,1},{17,25},{25,17},{2,10},{10... | collective-permute-start | bytes 417800 | tf_op jit(solution)/shard_map/ppermute | solution.py:592

commit v2 on v1

--- a/solution.py
+++ b/solution.py
@@ -105,11 +105,6 @@
     return first, second
 
 
-def pair_of(step, place):
-    flip = jnp.where(step == 0, 3, jnp.where(step == 3, 0, step))
-    return (0, place[0] ^ flip)
-
-
 def right_gram_kernel(place, g_ref, after_ref, *out_refs):
     step = pl.program_id(0)
     blk = g_ref.shape[1] // 2
@@ -131,18 +126,21 @@
             ref[blk:, :] = diag
 
 
-def right_grams(place, tile, blk, after):
-    rows, width = tile.shape
+def right_grams(place, tile, blk, flips, after):
+    rows = tile.shape[0]
     tall = blk + PAD
-    pairs = width // (2 * blk)
+    flip = lambda s: jnp.where(s == 0, flips[0], flips[1])
     return pl.pallas_call(
         right_gram_kernel,
-        out_shape=(jax.ShapeDtypeStruct((tall, blk), jnp.float32),) * pairs,
-        grid_spec=pltpu.PrefetchScalarGridSpec(
-            num_scalar_prefetch=1,
-            grid=(pairs,),
-            in_specs=[pl.BlockSpec((rows, 2 * blk), pair_of), pl.BlockSpec(memory_space=pl.ANY)],
-            out_specs=(pl.BlockSpec((tall, blk), lambda s, place: (0, 0)),) * pairs,
+        out_shape=(jax.ShapeDtypeStruct((tall, blk), jnp.float32),) * 2,
+        grid_spec=pltpu.PrefetchScalarGridSpec(
+            num_scalar_prefetch=1,
+            grid=(2,),
+            in_specs=[
+                pl.BlockSpec((rows, 2 * blk), lambda s, place: (0, place[0] ^ flip(s))),
+                pl.BlockSpec(memory_space=pl.ANY),
+            ],
+            out_specs=(pl.BlockSpec((tall, blk), lambda s, place: (0, 0)),) * 2,
         ),
         compiler_params=pltpu.CompilerParams(vmem_limit_bytes=VMEM_LIMIT),
         cost_estimate=SMALL,
@@ -150,18 +148,16 @@
     )(place, tile, after)
 
 
-def left_gram_kernel(place, g_ref, after_ref, lsend_ref, lkeep_ref, lhh, lcross):
+def left_gram_kernel(place, g_ref, after_ref, out_ref, lhh, lcross):
     step = pl.program_id(0)
     last = pl.num_programs(0) - 1
-    col_at = place[1]
-    rows = g_ref.shape[0]
     blk = lhh.shape[-1]
     high, low = split(g_ref[...])
-    for i in range(rows // blk):
+    for i in range(2):
         hi = high[i * blk : (i + 1) * blk, :]
         lo = low[i * blk : (i + 1) * blk, :]
         both = dot(hi, hi, ((1,), (1,)))
-        cross = dot(hi, lo, ((1,), (1,)))
+        cross = dot(lo, hi, ((1,), (1,)))
 
         @pl.when(step == 0)
         def _():
@@ -175,37 +171,28 @@
 
     @pl.when(step == last)
     def _():
-        for ref, owner in ((lsend_ref, 1 - col_at), (lkeep_ref, col_at)):
-            pair = []
-            for b in range(2):
-                cross = lcross[owner * 2 + b]
-                pair.append(lhh[owner * 2 + b] + (cross + cross.T))
-            body, diag = pack(*pair)
-            ref[:blk, :] = body
-            ref[blk:, :] = diag
-
-
-def left_grams(place, tile, blk, after):
-    rows, width = tile.shape
+        body, diag = pack(*(lhh[b] + (lcross[b] + lcross[b].T) for b in range(2)))
+        out_ref[:blk, :] = body
+        out_ref[blk:, :] = diag
+
+
+def left_grams(place, tile, blk, at, after):
+    width = tile.shape[1]
     tall = blk + PAD
-    flat = jax.ShapeDtypeStruct((tall, blk), jnp.float32)
     return pl.pallas_call(
         left_gram_kernel,
-        out_shape=(flat, flat),
-        grid_spec=pltpu.PrefetchScalarGridSpec(
-            num_scalar_prefetch=1,
-            grid=(width // (2 * blk),),
+        out_shape=jax.ShapeDtypeStruct((tall, blk), jnp.float32),
+        grid_spec=pltpu.PrefetchScalarGridSpec(
+            num_scalar_prefetch=1,
+            grid=(width // (4 * blk),),
             in_specs=[
-                pl.BlockSpec((rows, 2 * blk), lambda s, place: (0, s)),
+                pl.BlockSpec((2 * blk, 4 * blk), lambda s, place: (at(place), s)),
                 pl.BlockSpec(memory_space=pl.ANY),
             ],
-            out_specs=(
-                pl.BlockSpec((tall, blk), lambda s, place: (0, 0)),
-                pl.BlockSpec((tall, blk), lambda s, place: (0, 0)),
-            ),
+            out_specs=pl.BlockSpec((tall, blk), lambda s, place: (0, 0)),
             scratch_shapes=[
-                pltpu.VMEM((rows // blk, blk, blk), jnp.float32),
-                pltpu.VMEM((rows // blk, blk, blk), jnp.float32),
+                pltpu.VMEM((2, blk, blk), jnp.float32),
+                pltpu.VMEM((2, blk, blk), jnp.float32),
             ],
         ),
         compiler_params=pltpu.CompilerParams(vmem_limit_bytes=VMEM_LIMIT),
@@ -214,13 +201,23 @@
     )(place, tile, after)
 
 
-def take_kernel(place, g_ref, out_ref, sem):
+def take_kernel(place, g_ref, out_ref, sems):
     rows, wide = out_ref.shape
-    top = pl.multiple_of((1 - place[1]) * rows, rows)
+    count = sems.shape[0]
+    part = rows // count
     start = pl.multiple_of((place[0] ^ raw_flip(place)) * wide, wide)
-    copy = pltpu.make_async_copy(g_ref.at[pl.ds(top, rows), pl.ds(start, wide)], out_ref, sem)
-    copy.start()
-    copy.wait()
+    copies = []
+    for k in range(count):
+        top = pl.multiple_of((1 - place[1]) * rows + k * part, part)
+        copies.append(
+            pltpu.make_async_copy(
+                g_ref.at[pl.ds(top, part), pl.ds(start, wide)], out_ref.at[pl.ds(k * part, part), :], sems.at[k]
+            )
+        )
+    for copy in copies:
+        copy.start()
+    for copy in copies:
+        copy.wait()
 
 
 def take(place, tile, blk):
@@ -232,7 +229,7 @@
             grid=(1,),
             in_specs=[pl.BlockSpec(memory_space=pl.ANY)],
             out_specs=pl.BlockSpec(memory_space=pl.ANY),
-            scratch_shapes=[pltpu.SemaphoreType.DMA],
+            scratch_shapes=[pltpu.SemaphoreType.DMA((8,))],
         ),
         compiler_params=pltpu.CompilerParams(vmem_limit_bytes=VMEM_LIMIT),
         cost_estimate=SMALL,
@@ -299,10 +296,13 @@
     return [r * jnp.exp(-0.25 * jnp.log(s)) for r, s in zip(result, scales)]
 
 
-def right_kernel(full_dim, place, stats_ref, a_ref, b_ref, c_ref, after_ref, out_ref, halves_ref):
+def right_kernel(full_dim, place, stats_ref, a_ref, b_ref, c_ref, g_ref, under_ref, out_ref, halves_ref, half_ref):
     blk = stats_ref.shape[1]
+    rows = g_ref.shape[0]
     total = a_ref[...] + b_ref[...] + c_ref[...]
     roots = pair_roots(full_dim, stats_ref, total[:blk], total[blk : blk + 1])
+    half_ref[:rows, :] = product(split(g_ref[...]), split(roots[0]))
+    half_ref[rows:, :] = under_ref[...]
     body, diag = pack(*roots)
     out_ref[:blk, :] = body
     out_ref[blk:, :] = diag
@@ -312,34 +312,39 @@
         halves_ref[b, 1] = low
 
 
-def right_roots(full_dim, place, stats, kept, near, far, after):
+def right_roots(full_dim, place, stats, kept, near, far, tile, under):
     blk = stats.shape[1]
     tall = blk + PAD
+    rows = tile.shape[0] // 2
+    flat = pl.BlockSpec((tall, blk), lambda s, place: (0, 0))
     return pl.pallas_call(
         functools.partial(right_kernel, full_dim),
         out_shape=(
             jax.ShapeDtypeStruct((tall, blk), jnp.float32),
             jax.ShapeDtypeStruct((2, 2, blk, blk), jnp.bfloat16),
+            jax.ShapeDtypeStruct((rows + tall, blk), jnp.float32),
         ),
         grid_spec=pltpu.PrefetchScalarGridSpec(
             num_scalar_prefetch=1,
             grid=(1,),
             in_specs=[
                 pl.BlockSpec((2 * blk, blk), lambda s, place: (place[0], 0)),
-                pl.BlockSpec((tall, blk), lambda s, place: (0, 0)),
-                pl.BlockSpec((tall, blk), lambda s, place: (0, 0)),
-                pl.BlockSpec((tall, blk), lambda s, place: (0, 0)),
-                pl.BlockSpec(memory_space=pl.ANY),
+                flat,
+                flat,
+                flat,
+                pl.BlockSpec((rows, blk), lambda s, place: (1 - place[1], place[0] * 2)),
+                flat,
             ],
             out_specs=(
-                pl.BlockSpec((tall, blk), lambda s, place: (0, 0)),
+                flat,
                 pl.BlockSpec((2, 2, blk, blk), lambda s, place: (0, 0, 0, 0)),
+                pl.BlockSpec((rows + tall, blk), lambda s, place: (0, 0)),
             ),
         ),
         compiler_params=pltpu.CompilerParams(vmem_limit_bytes=VMEM_LIMIT),
         cost_estimate=SMALL,
         name="right_roots",
-    )(place, stats, kept, near, far, after)
+    )(place, stats, kept, near, far, tile, under)
 
 
 def left_kernel(full_dim, place, stats_ref, a_ref, b_ref, out_ref):
@@ -535,40 +540,68 @@
     rest[-1][...] = jnp.zeros_like(rest[-1])
 
 
-def finish_kernel(place, half_ref, left_ref, out_before, out_ref, done_ref):
-    left_product(left_ref, half_ref[...], out_ref)
+def finish_kernel(column, width, place, half_ref, left_ref, out_before, out_ref, done_ref, stage, sems):
+    blk = left_ref.shape[-1]
+    start = pl.multiple_of(column(place), width)
+    copies = []
+    for i in range(left_ref.shape[0]):
+        rows = pl.ds(i * blk, blk)
+        for b in range(0, width, blk):
+            cols = pl.ds(b, min(blk, width))
+            stage[rows, cols] = product((left_ref[i, 0], left_ref[i, 1]), split(half_ref[rows, cols]))
+        copies.append(
+            pltpu.make_async_copy(stage.at[rows, :], out_ref.at[rows, pl.ds(start, width)], sems.at[i])
+        )
+        copies[i].start()
     done_ref[...] = jnp.zeros_like(done_ref)
-
-
-def into_output(kernel, name, place, source, left, right, out, out_shape, wide, steps, g_map, right_at, out_map):
+    for copy in copies:
+        copy.wait()
+
+
+def finish(place, half, left, out, column):
+    width = half.shape[1]
+    rows = out.shape[0]
+    vmem = pl.BlockSpec(memory_space=pltpu.VMEM)
+    return pl.pallas_call(
+        functools.partial(finish_kernel, column, width),
+        out_shape=(jax.ShapeDtypeStruct(out.shape, jnp.float32), jax.ShapeDtypeStruct((8, 128), jnp.float32)),
+        in_specs=[pl.BlockSpec(memory_space=pltpu.SMEM), vmem, vmem, pl.BlockSpec(memory_space=pl.ANY)],
+        out_specs=(pl.BlockSpec(memory_space=pl.ANY), vmem),
+        scratch_shapes=[pltpu.VMEM((rows, width), jnp.float32), pltpu.SemaphoreType.DMA((left.shape[0],))],
+        input_output_aliases={3: 0},
+        compiler_params=pltpu.CompilerParams(vmem_limit_bytes=VMEM_LIMIT),
+        cost_estimate=SMALL,
+        name="finish",
+    )(place, half, left, out)
+
+
+def update(place, source, left, right, out, out_shape, g_map, out_map):
     rows = out_shape[0]
     blk = left.shape[-1]
     in_specs = [
-        pl.BlockSpec((rows, wide), g_map),
+        pl.BlockSpec((rows, blk), g_map),
         pl.BlockSpec((2, 2, blk, blk), lambda s, place: (0, 0, 0, 0)),
+        pl.BlockSpec((1, 2, blk, blk), lambda s, place: (s, 0, 0, 0)),
     ]
-    operands = [source, left]
-    if right is not None:
-        in_specs.append(pl.BlockSpec((1, 2, blk, blk), lambda s, place: (right_at + s, 0, 0, 0)))
-        operands.append(right)
+    operands = [source, left, right]
     aliases = {}
     if out is not None:
         aliases = {1 + len(operands): 0}
         in_specs.append(pl.BlockSpec(memory_space=pl.ANY))
         operands.append(out)
     return pl.pallas_call(
-        kernel,
+        update_kernel,
         out_shape=(jax.ShapeDtypeStruct(out_shape, jnp.float32), jax.ShapeDtypeStruct((8, 128), jnp.float32)),
         grid_spec=pltpu.PrefetchScalarGridSpec(
             num_scalar_prefetch=1,
-            grid=(steps,),
+            grid=(right.shape[0],),
             in_specs=in_specs,
-            out_specs=(pl.BlockSpec((rows, wide), out_map), pl.BlockSpec((8, 128), lambda s, place: (0, 0))),
+            out_specs=(pl.BlockSpec((rows, blk), out_map), pl.BlockSpec((8, 128), lambda s, place: (0, 0))),
         ),
         input_output_aliases=aliases,
         compiler_params=pltpu.CompilerParams(vmem_limit_bytes=VMEM_LIMIT),
         cost_estimate=SMALL,
-        name=name,
+        name="update",
     )(place, *operands)
 
 
@@ -594,12 +627,12 @@
     first = take(place, tile, blk)
     raw = over("y", first)
 
-    send_on, send, keep_on, keep = right_grams(place, tile, blk, first)
+    send_on, keep_on = right_grams(place, tile, blk, (3, 2), first)
     near_on = over("core", send_on)
+    send, keep = right_grams(place, tile, blk, (1, 0), keep_on)
     near = over("core", send)
-    lsend, lkeep = left_grams(place, tile, blk, send)
     far = over("x", fold(keep_on, near_on))
-    own, roots_own = right_roots(full_dim, place, rstats, keep, near, far, lsend)
+    lsend = left_grams(place, tile, blk, lambda place: 1 - place[1], send)
 
     own_pair, core_pair = (lambda place: 0), (lambda place: 1)
     last_pair = lambda place: 3 - (place[0] & 1)
@@ -607,13 +640,14 @@
     last_at = lambda place: 2 * (1 - (place[0] & 1))
     tail = (blk, blk // 2, blk // 2)
 
-    held = right_apply(place, tile, roots_own, own_pair, begin, 0, (blk,), lsend, ())
-    came_0a = over("y", held[0])
-    own = hold(own, raw, held[0])
+    own, roots_own, half = right_roots(full_dim, place, rstats, keep, near, far, tile, lsend)
+    came_0a = over("y", half)
+    own = hold(own, raw, half)
+    lkeep = left_grams(place, tile, blk, lambda place: place[1], own)
     own_c = over("core", own)
     own_x = over("x", own)
     own_xc = over("core", own_x)
-    held = right_apply(place, tile, roots_own, own_pair, begin, 1, (blk,), None, (own,))
+    held = right_apply(place, tile, roots_own, own_pair, begin, 1, (blk,), None, (lkeep,))
     came_0b = over("y", held[0])
     roots_core = spread_roots(own_c)
     held = right_apply(place, tile, roots_core, core_pair, begin, 0, (2 * blk,), None, (came_0a, own_xc))
@@ -633,35 +667,27 @@
     out = None
     for base, roots in ((0, roots_own), (1, roots_core), (2, roots_far)):
         at = own_cols(base)
-        out, done = into_output(
-            update_kernel, "update", place, tile, left, roots, out, shape, blk, roots.shape[0], at, 0,
+        out, done = update(
+            place, tile, left, roots, out, shape, at,
             lambda s, place, at=at: (0, place[1] * halves + at(s, place)[1]),
         )
 
-    def finish(out, value, wide, width, start, flip):
-        per_pair = 2 * blk // wide
-        return into_output(
-            finish_kernel, "finish", place, value, left, None, out, shape, wide, width // wide,
-            lambda s, place: (0, s), 0,
-            lambda s, place: (
-                0,
-                (1 - place[1]) * (tile_cols // wide) + (place[0] ^ flip(place)) * per_pair + start // wide + s,
-            ),
-        )
+    def crossed(start, flip):
+        return lambda place: (1 - place[1]) * tile_cols + (place[0] ^ flip(place)) * 2 * blk + start
 
     for b, value in enumerate((came_0a, came_0b)):
-        out, done = finish(out, value, blk, blk, b * blk, own_pair)
+        out, done = finish(place, value, left, out, crossed(b * blk, own_pair))
+    out, done = finish(place, came_1, left, out, crossed(0, core_pair))
     held = right_apply(place, tile, roots_far, last_pair, last_at, 1, tail[1:], None, (came_1, done))
     came_2 += [over("y", half) for half in held]
-    out, done = finish(out, came_1, blk, 2 * blk, 0, core_pair)
-    out, done = into_output(
-        update_kernel, "update", place, raw, left, roots_raw, out, shape, blk, 2,
-        lambda s, place: (0, s), 0,
+    out, done = update(
+        place, raw, left, roots_raw, out, shape,
+        lambda s, place: (0, s),
         lambda s, place: (0, (1 - place[1]) * halves + (place[0] ^ raw_flip(place)) * 2 + s),
     )
     start = 0
     for wide, value in zip(tail, came_2):
-        out, done = finish(out, value, wide, wide, start, last_pair)
+        out, done = finish(place, value, left, out, crossed(start, last_pair))
         start += wide
     return out.reshape(1, rows, 2 * tile_cols)
 

time: 112 us -> 108 us (0.964)
  waiting for transfers between devices: 33.1 us -> 22.6 us
  Pallas kernels: 67.1 us -> 70.3 us
  starting transfers between devices: 10.8 us -> 13.9 us
    ppermute x7, waiting for transfers between devices: 22.8 us -> 13.1 us  [over(): return lax.ppermute(value, 'col', [(0, 1), (1, 0)])]
    pallas_call x11 -> x12, Pallas kernels: 39.3 us -> 41.9 us  [the longest x4 19.2 us: update(): pl.pallas_call(update_kernel, out_shape=(jax.ShapeDtypeStruct(out_shape,...]
    pallas_call x5 -> x4, Pallas kernels: 10.3 us -> 8.35 us  [right_apply(): pl.pallas_call(functools.partial(right_apply_kernel, width, under is not...]
    ppermute x7, starting transfers between devices: 2.34 us -> 4.07 us  [over(): return lax.ppermute(value, 'row', [(i, i ^ flip) for i in range(n_row)])]
    ppermute x7, starting transfers between devices: 8.43 us -> 9.82 us  [over(): return lax.ppermute(value, 'col', [(0, 1), (1, 0)])]
    pallas_call x1 -> x2, Pallas kernels: 6.53 us -> 7.82 us  [right_grams(): pl.pallas_call(right_gram_kernel, out_shape=(jax.ShapeDtypeStruct((tall,...]
    pallas_call x1, Pallas kernels: 3.57 us -> 4.8 us  [right_roots(): pl.pallas_call(functools.partial(right_kernel, full_dim), out_shape=(jax....]
  transfers between devices with their start and end apart: 14 -> 14, of which waited for: 6 -> 8; matrix products, arithmetic and copies ran while one was open for 0% -> 0% of each run, Pallas kernels for 57% -> 62%
where the time goes in v2:
time: 108 us; the launch traced here: 107 us
  Pallas kernels  70.3 us (65%)
  waiting for transfers between devices  22.6 us (21%)
  starting transfers between devices  13.9 us (13%)
    pallas_call x4, Pallas kernels, update(): pl.pallas_call(update_kernel, out_shape=(jax.ShapeDtypeStruct(out_shape,...  19.2 us
    pallas_call x6, Pallas kernels, finish(): pl.pallas_call(functools.partial(finish_kernel, column, width), out_shape...  13.3 us
    ppermute x7, waiting for transfers between devices, over(): return lax.ppermute(value, 'col', [(0, 1), (1, 0)])  13.1 us
    ppermute x7, starting transfers between devices, over(): return lax.ppermute(value, 'col', [(0, 1), (1, 0)])  9.82 us
    pallas_call x2, Pallas kernels, left_grams(): pl.pallas_call(left_gram_kernel, out_shape=jax.ShapeDtypeStruct((tall, bl...  9.47 us
    ppermute x7, waiting for transfers between devices, over(): return lax.ppermute(value, 'row', [(i, i ^ flip) for i in range(n_row)])  9.45 us
    pallas_call x4, Pallas kernels, right_apply(): pl.pallas_call(functools.partial(right_apply_kernel, width, under is not...  8.35 us
    pallas_call x2, Pallas kernels, right_grams(): pl.pallas_call(right_gram_kernel, out_shape=(jax.ShapeDtypeStruct((tall,...  7.82 us
  transfers between devices with their start and end apart: 14, of which 8 were waited for; matrix products, arithmetic and copies ran while one was open for 0% of the time, Pallas kernels for 62%

profile of v2, /device:TPU:0, one launch (start us, length us, event | category | flops | bytes accessed | tf_op | source)
XLA Modules:
  0.0 107.3 jit_solution(1500977506379820651)
XLA Ops:
  2.0 3.0 %collective-permute-start.3 = (f32[512,512]{1,0:T(8,128)S(1)}, f32[512,512]{1,0:T(8,128)S(1)}, u32[]{:S(2)}, u32[]{:S(2)}) collective-permute-start(f32[512,512]{1,0:T(8,128)S(1)} %take.1.after_ref), channel_id=1, source_target_pairs={{0,4},{4,0},{1,5},{5,1},{2,6},{6,2},{3,7},{7,3},{8,12},{12,8},{9,1... | collective-permute-start | bytes 3145736 | tf_op jit(solution)/shard_map/ppermute | solution.py:623
  5.0 3.9 %right_grams.2 = (f32[264,256]{1,0:T(8,128)S(1)}, f32[264,256]{1,0:T(8,128)S(1)}) custom-call(s32[2]{0:T(128)S(1)} %pad_add_fusion.place, f32[1024,2048]{1,0:T(8,128)} %bitcast.9, f32[512,512]{1,0:T(8,128)S(1)} %take.1.after_ref), custom_call_target="tpu_custom_call" | custom-call | flops 1 | bytes 1 | tf_op jit(solution)/shard_map/right_grams/pallas_call | solution.py:133
  9.0 3.9 %right_grams.3 = (f32[264,256]{1,0:T(8,128)S(1)}, f32[264,256]{1,0:T(8,128)S(1)}) custom-call(s32[2]{0:T(128)S(1)} %pad_add_fusion.place, f32[1024,2048]{1,0:T(8,128)} %bitcast.10, f32[264,256]{1,0:T(8,128)S(1)} %get-tuple-element.25.after_ref.a_ref), custom_call_target="tpu_custom_call" | custom-call | flops 1 | bytes 1 | tf_op jit(solution)/shard_map/right_grams/pallas_call | solution.py:133
  15.1 4.7 %left_grams.2.under_ref = f32[264,256]{1,0:T(8,128)S(1)} custom-call(s32[2]{0:T(128)S(1)} %pad_add_fusion.place, f32[1024,2048]{1,0:T(8,128)} %bitcast.11, f32[264,256]{1,0:T(8,128)S(1)} %get-tuple-element.27.after_ref), custom_call_target="tpu_custom_call" | custom-call | flops 1 | bytes 1 | tf_op jit(solution)/shard_map/left_grams/pallas_call | solution.py:182
  19.9 2.1 %collective-permute-done.2.c_ref = f32[264,256]{1,0:T(8,128)S(1)} collective-permute-done((f32[264,256]{1,0:T(8,128)S(1)}, f32[264,256]{1,0:T(8,128)S(1)}, u32[]{:S(2)}, u32[]{:S(2)}) %collective-permute-start.2) | collective-permute-done | bytes 270368 | tf_op jit(solution)/shard_map/ppermute | solution.py:625
  22.0 4.8 %right_roots.1 = (f32[264,256]{1,0:T(8,128)S(1)}, bf16[2,2,256,256]{3,2,1,0:T(8,128)(2,1)S(1)}, f32[776,256]{1,0:T(8,128)S(1)}) custom-call(s32[2]{0:T(128)S(1)} %pad_add_fusion.place, f32[2048,256]{1,0:T(8,128)S(1)} %bitcast.6, f32[264,256]{1,0:T(8,128)S(1)} %get-tuple-element.26.a_ref, f32[264,256]{1,0:T(8,128)S(1)} %collective-permute-done.b_ref, ...), custom_call_target="tpu_custom_call" | custom-call | flops 1 | bytes 1 | tf_op jit(solution)/shard_map/right_roots/pallas_call | solution.py:320
  30.0 6.0 %collective-permute-done.4.a_ref = f32[264,256]{1,0:T(8,128)S(1)} collective-permute-done((f32[264,256]{1,0:T(8,128)S(1)}, f32[264,256]{1,0:T(8,128)S(1)}, u32[]{:S(2)}, u32[]{:S(2)}) %collective-permute-start.4) | collective-permute-done | bytes 270368 | tf_op jit(solution)/shard_map/ppermute | solution.py:625
  35.9 4.7 %left_grams.3.rest_0_.a_ref = f32[264,256]{1,0:T(8,128)S(1)} custom-call(s32[2]{0:T(128)S(1)} %pad_add_fusion.place, f32[1024,2048]{1,0:T(8,128)} %bitcast.13, f32[264,256]{1,0:T(8,128)S(1)} %hold.2.after_ref), custom_call_target="tpu_custom_call" | custom-call | flops 1 | bytes 1 | tf_op jit(solution)/shard_map/left_grams/pallas_call | solution.py:182
  40.7 2.0 %right_apply.4 = f32[512,256]{1,0:T(8,128)S(1)} custom-call(s32[2]{0:T(128)S(1)} %pad_add_fusion.place, f32[1024,2048]{1,0:T(8,128)} %bitcast.14, bf16[2,2,256,256]{3,2,1,0:T(8,128)(2,1)S(1)} %get-tuple-element.31.right_ref, f32[264,256]{1,0:T(8,128)S(1)} %left_grams.3.rest_0_.a_ref), custom_call_target="tpu_custom_call" | custom-call | flops 1 | bytes 1 | tf_op jit(solution)/shard_map/right_apply/pallas_call | solution.py:515
  45.7 2.4 %right_apply.5 = f32[512,512]{1,0:T(8,128)S(1)} custom-call(s32[2]{0:T(128)S(1)} %pad_add_fusion.place, f32[1024,2048]{1,0:T(8,128)} %bitcast.15, bf16[2,2,256,256]{3,2,1,0:T(8,128)(2,1)S(1)} %spread_roots.3.right_ref, f32[776,256]{1,0:T(8,128)S(1)} %collective-permute-done.8.rest_0_.b_ref.half_ref, f32[264,256]{1,0:T(8,128)S(1)} %collective-permute-done.6.refs_1_.rest_1_.xc_ref), custom_call_target="tpu_custom_call" | custom-call | flops 1 | bytes 1 | tf_op jit(solution)/shard_map/right_apply/pallas_call | solution.py:515
  49.5 8.0 %collective-permute-done.5.rest_0_.half_ref = f32[512,256]{1,0:T(8,128)S(1)} collective-permute-done((f32[512,256]{1,0:T(8,128)S(1)}, f32[512,256]{1,0:T(8,128)S(1)}, u32[]{:S(2)}, u32[]{:S(2)}) %collective-permute-start.5) | collective-permute-done | bytes 524320 | tf_op jit(solution)/shard_map/ppermute | solution.py:623
  58.5 2.0 %right_apply.7 = f32[648,256]{1,0:T(8,128)S(1)} custom-call(s32[2]{0:T(128)S(1)} %pad_add_fusion.place, f32[1024,2048]{1,0:T(8,128)} %bitcast.16, bf16[4,2,256,256]{3,2,1,0:T(8,128)(2,1)S(1)} %spread_roots.2.right_ref, f32[136,256]{1,0:T(8,128)S(1)} %cut.1.rest_0_), custom_call_target="tpu_custom_call" | custom-call | flops 1 | bytes 1 | tf_op jit(solution)/shard_map/right_apply/pallas_call | solution.py:515
  62.0 3.5 %left_roots.1.left_ref = bf16[2,2,256,256]{3,2,1,0:T(8,128)(2,1)S(1)} custom-call(s32[2]{0:T(128)S(1)} %pad_add_fusion.place, f32[1024,256]{1,0:T(8,128)S(1)} %bitcast.7, f32[264,256]{1,0:T(8,128)S(1)} %left_grams.3.rest_0_.a_ref, f32[776,256]{1,0:T(8,128)S(1)} %collective-permute-done.8.rest_0_.b_ref.half_ref), custom_call_target="tpu_custom_call" | custom-call | flops 1 | bytes 1 | tf_op jit(solution)/shard_map/left_roots/pallas_call | solution.py:362
  65.5 4.5 %update.4 = (f32[512,4096]{1,0:T(8,128)}, f32[8,128]{1,0:T(8,128)}) custom-call(s32[2]{0:T(128)S(1)} %pad_add_fusion.place, f32[1024,2048]{1,0:T(8,128)} %bitcast.17, bf16[2,2,256,256]{3,2,1,0:T(8,128)(2,1)S(1)} %left_roots.1.left_ref, bf16[2,2,256,256]{3,2,1,0:T(8,128)(2,1)S(1)} %get-tuple-element.31.right_ref), custom_call_target="tpu_custom_call" | custom-call | flops 1 | bytes 1 | tf_op jit(solution)/shard_map/update/pallas_call | solution.py:592
  70.0 4.5 %update.5 = (f32[512,4096]{1,0:T(8,128)}, f32[8,128]{1,0:T(8,128)}) custom-call(s32[2]{0:T(128)S(1)} %pad_add_fusion.place, f32[1024,2048]{1,0:T(8,128)} %bitcast.18, bf16[2,2,256,256]{3,2,1,0:T(8,128)(2,1)S(1)} %left_roots.1.left_ref, bf16[2,2,256,256]{3,2,1,0:T(8,128)(2,1)S(1)} %spread_roots.3.right_ref, ...), custom_call_target="tpu_custom_call", output_to_operand_aliasing={{0}: (4, {})} | custom-call | flops 1 | bytes 1 | tf_op jit(solution)/shard_map/update/pallas_call | solution.py:592
  74.4 6.8 %update.6 = (f32[512,4096]{1,0:T(8,128)}, f32[8,128]{1,0:T(8,128)}) custom-call(s32[2]{0:T(128)S(1)} %pad_add_fusion.place, f32[1024,2048]{1,0:T(8,128)} %bitcast.19, bf16[2,2,256,256]{3,2,1,0:T(8,128)(2,1)S(1)} %left_roots.1.left_ref, bf16[4,2,256,256]{3,2,1,0:T(8,128)(2,1)S(1)} %spread_roots.2.right_ref, ...), custom_call_target="tpu_custom_call", output_to_operand_aliasing={{0}: (4, {})} | custom-call | flops 1 | bytes 1 | tf_op jit(solution)/shard_map/update/pallas_call | solution.py:592
  81.2 2.3 %finish.6 = (f32[512,4096]{1,0:T(8,128)}, f32[8,128]{1,0:T(8,128)}) custom-call(s32[2]{0:T(128)S(1)} %pad_add_fusion.place, f32[776,256]{1,0:T(8,128)S(1)} %collective-permute-done.8.rest_0_.b_ref.half_ref, bf16[2,2,256,256]{3,2,1,0:T(8,128)(2,1)S(1)} %left_roots.1.left_ref, f32[512,4096]{1,0:T(8,128)} %get-tuple-element.34.out_before), custom_call_target="tpu_custom_call", output_to_operand_aliasing={{0}: (3, {})} | custom-call | flops 1 | bytes 1 | tf_op jit(solution)/shard_map/finish/pallas_call | solution.py:565
  83.6 2.3 %finish.7 = (f32[512,4096]{1,0:T(8,128)}, f32[8,128]{1,0:T(8,128)}) custom-call(s32[2]{0:T(128)S(1)} %pad_add_fusion.place, f32[512,256]{1,0:T(8,128)S(1)} %collective-permute-done.5.rest_0_.half_ref, bf16[2,2,256,256]{3,2,1,0:T(8,128)(2,1)S(1)} %left_roots.1.left_ref, f32[512,4096]{1,0:T(8,128)} %get-tuple-element.35.out_before), custom_call_target="tpu_custom_call", output_to_operand_aliasing={{0}: (3, {})} | custom-call | flops 1 | bytes 1 | tf_op jit(solution)/shard_map/finish/pallas_call | solution.py:565
  87.9 2.0 %right_apply.6 = (f32[512,128]{1,0:T(8,128)S(1)}, f32[512,128]{1,0:T(8,128)S(1)}) custom-call(s32[2]{0:T(128)S(1)} %pad_add_fusion.place, f32[1024,2048]{1,0:T(8,128)} %bitcast.20, bf16[4,2,256,256]{3,2,1,0:T(8,128)(2,1)S(1)} %spread_roots.2.right_ref, f32[512,512]{1,0:T(8,128)S(1)} %collective-permute-done.9.half_ref.rest_0_, ...), custom_call_target="tpu_custom_call" | custom-call | flops 1 | bytes 1 | tf_op jit(solution)/shard_map/right_apply/pallas_call | solution.py:515
  91.9 2.2 %collective-permute-done.12.a_ref.half_ref = f32[648,256]{1,0:T(8,128)S(1)} collective-permute-done((f32[648,256]{1,0:T(8,128)S(1)}, f32[648,256]{1,0:T(8,128)S(1)}, u32[]{:S(2)}, u32[]{:S(2)}) %collective-permute-start.12) | collective-permute-done | bytes 663584 | tf_op jit(solution)/shard_map/ppermute | solution.py:623
  96.3 3.5 %update.7 = (f32[512,4096]{1,0:T(8,128)}, f32[8,128]{1,0:T(8,128)}) custom-call(s32[2]{0:T(128)S(1)} %pad_add_fusion.place, f32[512,512]{1,0:T(8,128)S(1)} %collective-permute-done.3.rest_0_.g_ref, bf16[2,2,256,256]{3,2,1,0:T(8,128)(2,1)S(1)} %left_roots.1.left_ref, ...), custom_call_target="tpu_custom_call", output_to_operand_aliasing={{0}: (4, {})} | custom-call | flops 1 | bytes 1 | tf_op jit(solution)/shard_map/update/pallas_call | solution.py:592
  99.8 2.3 %finish.9 = (f32[512,4096]{1,0:T(8,128)}, f32[8,128]{1,0:T(8,128)}) custom-call(s32[2]{0:T(128)S(1)} %pad_add_fusion.place, f32[648,256]{1,0:T(8,128)S(1)} %collective-permute-done.12.a_ref.half_ref, bf16[2,2,256,256]{3,2,1,0:T(8,128)(2,1)S(1)} %left_roots.1.left_ref, f32[512,4096]{1,0:T(8,128)} %get-tuple-element.41.out_before), custom_call_target="tpu_custom_call", output_to_operand_aliasing={{0}: (3, {})} | custom-call | flops 1 | bytes 1 | tf_op jit(solution)/shard_map/finish/pallas_call | solution.py:565
  102.1 2.2 %finish.10 = (f32[512,4096]{1,0:T(8,128)}, f32[8,128]{1,0:T(8,128)}) custom-call(s32[2]{0:T(128)S(1)} %pad_add_fusion.place, f32[512,128]{1,0:T(8,128)S(1)} %collective-permute-done.11.half_ref, bf16[2,2,256,256]{3,2,1,0:T(8,128)(2,1)S(1)} %left_roots.1.left_ref, f32[512,4096]{1,0:T(8,128)} %get-tuple-element.42.out_before), custom_call_target="tpu_custom_call", output_to_operand_aliasing={{0}: (3, {})} | custom-call | flops 1 | bytes 1 | tf_op jit(solution)/shard_map/finish/pallas_call | solution.py:565
  105.0 2.2 %finish.11 = (f32[512,4096]{1,0:T(8,128)}, f32[8,128]{1,0:T(8,128)}) custom-call(s32[2]{0:T(128)S(1)} %pad_add_fusion.place, f32[512,128]{1,0:T(8,128)S(1)} %collective-permute-done.10.half_ref, bf16[2,2,256,256]{3,2,1,0:T(8,128)(2,1)S(1)} %left_roots.1.left_ref, f32[512,4096]{1,0:T(8,128)} %get-tuple-element.43.out_before), custom_call_target="tpu_custom_call", output_to_operand_aliasing={{0}: (3, {})} | custom-call | flops 1 | bytes 1 | tf_op jit(solution)/shard_map/finish/pallas_call | solution.py:565
  (38 shorter events, 21.1 us)
Async XLA Ops:
  2.0 26.2 %collective-permute-start.3 = (f32[512,512]{1,0:T(8,128)S(1)}, f32[512,512]{1,0:T(8,128)S(1)}, u32[]{:S(2)}, u32[]{:S(2)}) collective-permute-start(f32[512,512]{1,0:T(8,128)S(1)} %take.1.after_ref), channel_id=1, source_target_pairs={{0,4},{4,0},{1,5},{5,1},{2,6},{6,2},{3,7},{7,3},{8,12},{12,8},{9,1... | collective-permute-start | bytes 3145736 | tf_op jit(solution)/shard_map/ppermute | solution.py:623
  8.9 4.6 %collective-permute-start.1 = (f32[264,256]{1,0:T(8,128)S(1)}, f32[264,256]{1,0:T(8,128)S(1)}, u32[]{:S(2)}, u32[]{:S(2)}) collective-permute-start(f32[264,256]{1,0:T(8,128)S(1)} %get-tuple-element.28), channel_id=1, source_target_pairs={{0,8},{8,0},{16,24},{24,16},{1,9},{9,1},{17,25},{25,17},{2,10},{10... | collective-permute-start | bytes 811016 | tf_op jit(solution)/shard_map/ppermute | solution.py:625
  9.0 13.0 %copy-start = (f32[1,2048,256]{2,1,0:T(8,128)S(1)}, f32[1,2048,256]{2,1,0:T(8,128)}, u32[]{:S(2)}) copy-start(f32[1,2048,256]{2,1,0:T(8,128)} %param.5) | copy-start | bytes 6291460
  12.9 6.9 %collective-permute-start = (f32[264,256]{1,0:T(8,128)S(1)}, f32[264,256]{1,0:T(8,128)S(1)}, u32[]{:S(2)}, u32[]{:S(2)}) collective-permute-start(f32[264,256]{1,0:T(8,128)S(1)} %get-tuple-element.27.after_ref), channel_id=1, source_target_pairs={{0,8},{8,0},{16,24},{24,16},{1,9},{9,1},{17,25},{25,17},{2,10},{10... | collective-permute-start | bytes 811016 | tf_op jit(solution)/shard_map/ppermute | solution.py:625
  13.5 8.5 %collective-permute-start.2 = (f32[264,256]{1,0:T(8,128)S(1)}, f32[264,256]{1,0:T(8,128)S(1)}, u32[]{:S(2)}, u32[]{:S(2)}) collective-permute-start(f32[264,256]{1,0:T(8,128)S(1)} %fold.1), channel_id=1, source_target_pairs={{0,16},{8,24},{16,0},{24,8},{1,17},{9,25},{17,1},{25,9},{2,18},{10... | collective-permute-start | bytes 811016 | tf_op jit(solution)/shard_map/ppermute | solution.py:625
  26.8 18.9 %collective-permute-start.8 = (f32[776,256]{1,0:T(8,128)S(1)}, f32[776,256]{1,0:T(8,128)S(1)}, u32[]{:S(2)}, u32[]{:S(2)}) collective-permute-start(f32[776,256]{1,0:T(8,128)S(1)} %get-tuple-element.30.rest_1_), channel_id=1, source_target_pairs={{0,4},{4,0},{1,5},{5,1},{2,6},{6,2},{3,7},{7,3},{8,12},{12,8},{9,1... | collective-permute-start | bytes 2383880 | tf_op jit(solution)/shard_map/ppermute | solution.py:623
  28.2 7.7 %collective-permute-start.4 = (f32[264,256]{1,0:T(8,128)S(1)}, f32[264,256]{1,0:T(8,128)S(1)}, u32[]{:S(2)}, u32[]{:S(2)}) collective-permute-start(f32[264,256]{1,0:T(8,128)S(1)} %hold.2.after_ref), channel_id=1, source_target_pairs={{0,16},{8,24},{16,0},{24,8},{1,17},{9,25},{17,1},{25,9},{2,18},{10... | collective-permute-start | bytes 811016 | tf_op jit(solution)/shard_map/ppermute | solution.py:625
  30.0 14.2 %collective-permute-start.7 = (f32[264,256]{1,0:T(8,128)S(1)}, f32[264,256]{1,0:T(8,128)S(1)}, u32[]{:S(2)}, u32[]{:S(2)}) collective-permute-start(f32[264,256]{1,0:T(8,128)S(1)} %hold.2.after_ref), channel_id=1, source_target_pairs={{0,8},{8,0},{16,24},{24,16},{1,9},{9,1},{17,25},{25,17},{2,10},{10... | collective-permute-start | bytes 811016 | tf_op jit(solution)/shard_map/ppermute | solution.py:625
  35.9 9.8 %collective-permute-start.6 = (f32[264,256]{1,0:T(8,128)S(1)}, f32[264,256]{1,0:T(8,128)S(1)}, u32[]{:S(2)}, u32[]{:S(2)}) collective-permute-start(f32[264,256]{1,0:T(8,128)S(1)} %collective-permute-done.4.a_ref), channel_id=1, source_target_pairs={{0,8},{8,0},{16,24},{24,16},{1,9},{9,1},{17,25},{25,17},{2,10},{10... | collective-permute-start | bytes 811016 | tf_op jit(solution)/shard_map/ppermute | solution.py:625
  42.6 14.8 %collective-permute-start.5 = (f32[512,256]{1,0:T(8,128)S(1)}, f32[512,256]{1,0:T(8,128)S(1)}, u32[]{:S(2)}, u32[]{:S(2)}) collective-permute-start(f32[512,256]{1,0:T(8,128)S(1)} %right_apply.4), channel_id=1, source_target_pairs={{0,4},{4,0},{1,5},{5,1},{2,6},{6,2},{3,7},{7,3},{8,12},{12,8},{9,1... | collective-permute-start | bytes 1572872 | tf_op jit(solution)/shard_map/ppermute | solution.py:623
  48.1 13.8 %copy-start.1 = (f32[1,1024,256]{2,1,0:T(8,128)S(1)}, f32[1,1024,256]{2,1,0:T(8,128)}, u32[]{:S(2)}) copy-start(f32[1,1024,256]{2,1,0:T(8,128)} %param.4) | copy-start | bytes 3145732
  48.2 37.7 %collective-permute-start.9 = (f32[512,512]{1,0:T(8,128)S(1)}, f32[512,512]{1,0:T(8,128)S(1)}, u32[]{:S(2)}, u32[]{:S(2)}) collective-permute-start(f32[512,512]{1,0:T(8,128)S(1)} %right_apply.5), channel_id=1, source_target_pairs={{0,4},{4,0},{1,5},{5,1},{2,6},{6,2},{3,7},{7,3},{8,12},{12,8},{9,1... | collective-permute-start | bytes 3145736 | tf_op jit(solution)/shard_map/ppermute | solution.py:623
  60.5 33.7 %collective-permute-start.12 = (f32[648,256]{1,0:T(8,128)S(1)}, f32[648,256]{1,0:T(8,128)S(1)}, u32[]{:S(2)}, u32[]{:S(2)}) collective-permute-start(f32[648,256]{1,0:T(8,128)S(1)} %right_apply.7), channel_id=1, source_target_pairs={{0,4},{4,0},{1,5},{5,1},{2,6},{6,2},{3,7},{7,3},{8,12},{12,8},{9,1... | collective-permute-start | bytes 1990664 | tf_op jit(solution)/shard_map/ppermute | solution.py:623
  89.8 12.3 %collective-permute-start.11 = (f32[512,128]{1,0:T(8,128)S(1)}, f32[512,128]{1,0:T(8,128)S(1)}, u32[]{:S(2)}, u32[]{:S(2)}) collective-permute-start(f32[512,128]{1,0:T(8,128)S(1)} %get-tuple-element.39), channel_id=1, source_target_pairs={{0,4},{4,0},{1,5},{5,1},{2,6},{6,2},{3,7},{7,3},{8,12},{12,8},{9,1... | collective-permute-start | bytes 786440 | tf_op jit(solution)/shard_map/ppermute | solution.py:623
  90.5 14.5 %collective-permute-start.10 = (f32[512,128]{1,0:T(8,128)S(1)}, f32[512,128]{1,0:T(8,128)S(1)}, u32[]{:S(2)}, u32[]{:S(2)}) collective-permute-start(f32[512,128]{1,0:T(8,128)S(1)} %get-tuple-element.38), channel_id=1, source_target_pairs={{0,4},{4,0},{1,5},{5,1},{2,6},{6,2},{3,7},{7,3},{8,12},{12,8},{9,1... | collective-permute-start | bytes 786440 | tf_op jit(solution)/shard_map/ppermute | solution.py:623
  94.1 1.4 %collective-permute-start.13 = (f32[136,256]{1,0:T(8,128)S(1)}, f32[136,256]{1,0:T(8,128)S(1)}, u32[]{:S(2)}, u32[]{:S(2)}) collective-permute-start(f32[136,256]{1,0:T(8,128)S(1)} %rest_of.1.mine_ref), channel_id=1, source_target_pairs={{0,8},{8,0},{16,24},{24,16},{1,9},{9,1},{17,25},{25,17},{2,10},{10... | collective-permute-start | bytes 417800 | tf_op jit(solution)/shard_map/ppermute | solution.py:625

commit v3 on v2

--- a/solution.py
+++ b/solution.py
@@ -201,40 +201,31 @@
     )(place, tile, after)
 
 
-def take_kernel(place, g_ref, out_ref, sems):
+def here():
+    return lax.axis_index("row"), lax.axis_index("col")
+
+
+def take_kernel(g_ref, out_ref, sem):
     rows, wide = out_ref.shape
-    count = sems.shape[0]
-    part = rows // count
+    place = here()
     start = pl.multiple_of((place[0] ^ raw_flip(place)) * wide, wide)
-    copies = []
-    for k in range(count):
-        top = pl.multiple_of((1 - place[1]) * rows + k * part, part)
-        copies.append(
-            pltpu.make_async_copy(
-                g_ref.at[pl.ds(top, part), pl.ds(start, wide)], out_ref.at[pl.ds(k * part, part), :], sems.at[k]
-            )
-        )
-    for copy in copies:
-        copy.start()
-    for copy in copies:
-        copy.wait()
-
-
-def take(place, tile, blk):
+    top = pl.multiple_of((1 - place[1]) * rows, rows)
+    copy = pltpu.make_async_copy(g_ref.at[pl.ds(top, rows), pl.ds(start, wide)], out_ref, sem)
+    copy.start()
+    copy.wait()
+
+
+def take(tile, blk):
     return pl.pallas_call(
         take_kernel,
         out_shape=jax.ShapeDtypeStruct((tile.shape[0] // 2, 2 * blk), jnp.float32),
-        grid_spec=pltpu.PrefetchScalarGridSpec(
-            num_scalar_prefetch=1,
-            grid=(1,),
-            in_specs=[pl.BlockSpec(memory_space=pl.ANY)],
-            out_specs=pl.BlockSpec(memory_space=pl.ANY),
-            scratch_shapes=[pltpu.SemaphoreType.DMA((8,))],
-        ),
+        in_specs=[pl.BlockSpec(memory_space=pl.ANY)],
+        out_specs=pl.BlockSpec(memory_space=pl.ANY),
+        scratch_shapes=[pltpu.SemaphoreType.DMA],
         compiler_params=pltpu.CompilerParams(vmem_limit_bytes=VMEM_LIMIT),
         cost_estimate=SMALL,
         name="take",
-    )(place, tile)
+    )(tile)
 
 
 def fold_kernel(a_ref, b_ref, out_ref):
@@ -540,9 +531,10 @@
     rest[-1][...] = jnp.zeros_like(rest[-1])
 
 
-def finish_kernel(column, width, place, half_ref, left_ref, out_before, out_ref, done_ref, stage, sems):
+def finish_kernel(column, width, half_ref, left_ref, out_before, out_ref, *rest):
+    stage, sems = rest[-2:]
     blk = left_ref.shape[-1]
-    start = pl.multiple_of(column(place), width)
+    start = pl.multiple_of(column(here()), width)
     copies = []
     for i in range(left_ref.shape[0]):
         rows = pl.ds(i * blk, blk)
@@ -553,26 +545,29 @@
             pltpu.make_async_copy(stage.at[rows, :], out_ref.at[rows, pl.ds(start, width)], sems.at[i])
         )
         copies[i].start()
-    done_ref[...] = jnp.zeros_like(done_ref)
+    for done_ref in rest[:-2]:
+        done_ref[...] = jnp.zeros_like(done_ref)
     for copy in copies:
         copy.wait()
 
 
-def finish(place, half, left, out, column):
+def finish(half, left, out, column, mark=False):
     width = half.shape[1]
     rows = out.shape[0]
     vmem = pl.BlockSpec(memory_space=pltpu.VMEM)
+    anywhere = pl.BlockSpec(memory_space=pl.ANY)
+    shapes = (jax.ShapeDtypeStruct(out.shape, jnp.float32), jax.ShapeDtypeStruct((8, 128), jnp.float32))
     return pl.pallas_call(
         functools.partial(finish_kernel, column, width),
-        out_shape=(jax.ShapeDtypeStruct(out.shape, jnp.float32), jax.ShapeDtypeStruct((8, 128), jnp.float32)),
-        in_specs=[pl.BlockSpec(memory_space=pltpu.SMEM), vmem, vmem, pl.BlockSpec(memory_space=pl.ANY)],
-        out_specs=(pl.BlockSpec(memory_space=pl.ANY), vmem),
+        out_shape=shapes if mark else shapes[:1],
+        in_specs=[vmem, vmem, anywhere],
+        out_specs=(anywhere, vmem) if mark else (anywhere,),
         scratch_shapes=[pltpu.VMEM((rows, width), jnp.float32), pltpu.SemaphoreType.DMA((left.shape[0],))],
-        input_output_aliases={3: 0},
+        input_output_aliases={2: 0},
         compiler_params=pltpu.CompilerParams(vmem_limit_bytes=VMEM_LIMIT),
         cost_estimate=SMALL,
         name="finish",
-    )(place, half, left, out)
+    )(half, left, out)
 
 
 def update(place, source, left, right, out, out_shape, g_map, out_map):
@@ -624,7 +619,7 @@
         flip = {"core": 1, "x": 2}[axis]
         return lax.ppermute(value, "row", [(i, i ^ flip) for i in range(n_row)])
 
-    first = take(place, tile, blk)
+    first = take(tile, blk)
     raw = over("y", first)
 
     send_on, keep_on = right_grams(place, tile, blk, (3, 2), first)
@@ -676,8 +671,8 @@
         return lambda place: (1 - place[1]) * tile_cols + (place[0] ^ flip(place)) * 2 * blk + start
 
     for b, value in enumerate((came_0a, came_0b)):
-        out, done = finish(place, value, left, out, crossed(b * blk, own_pair))
-    out, done = finish(place, came_1, left, out, crossed(0, core_pair))
+        (out,) = finish(value, left, out, crossed(b * blk, own_pair))
+    out, done = finish(came_1, left, out, crossed(0, core_pair), mark=True)
     held = right_apply(place, tile, roots_far, last_pair, last_at, 1, tail[1:], None, (came_1, done))
     came_2 += [over("y", half) for half in held]
     out, done = update(
@@ -687,7 +682,7 @@
     )
     start = 0
     for wide, value in zip(tail, came_2):
-        out, done = finish(place, value, left, out, crossed(start, last_pair))
+        (out,) = finish(value, left, out, crossed(start, last_pair))
         start += wide
     return out.reshape(1, rows, 2 * tile_cols)
 

time: 108 us -> 106 us (0.981)
  Pallas kernels: 70.3 us -> 63.4 us
  waiting for transfers between devices: 22.6 us -> 27.8 us
    pallas_call x6, Pallas kernels: 13.3 us -> 7.09 us  [finish(): pl.pallas_call(functools.partial(finish_kernel, column, width), out_shape...]
    ppermute x7, waiting for transfers between devices: 13.1 us -> 18.3 us  [over(): return lax.ppermute(value, 'col', [(0, 1), (1, 0)])]
  transfers between devices with their start and end apart: 14 -> 14, of which waited for: 8 -> 8; matrix products, arithmetic and copies ran while one was open for 0% -> 0% of each run, Pallas kernels for 62% -> 58%
where the time goes in v3:
time: 106 us; the launch traced here: 105 us
  Pallas kernels  63.4 us (60%)
  waiting for transfers between devices  27.8 us (26%)
  starting transfers between devices  13.7 us (13%)
    pallas_call x4, Pallas kernels, update(): pl.pallas_call(update_kernel, out_shape=(jax.ShapeDtypeStruct(out_shape,...  19.2 us
    ppermute x7, waiting for transfers between devices, over(): return lax.ppermute(value, 'col', [(0, 1), (1, 0)])  18.3 us
    ppermute x7, starting transfers between devices, over(): return lax.ppermute(value, 'col', [(0, 1), (1, 0)])  9.64 us
    ppermute x7, waiting for transfers between devices, over(): return lax.ppermute(value, 'row', [(i, i ^ flip) for i in range(n_row)])  9.5 us
    pallas_call x2, Pallas kernels, left_grams(): pl.pallas_call(left_gram_kernel, out_shape=jax.ShapeDtypeStruct((tall, bl...  9.43 us
    pallas_call x4, Pallas kernels, right_apply(): pl.pallas_call(functools.partial(right_apply_kernel, width, under is not...  8.35 us
    pallas_call x2, Pallas kernels, right_grams(): pl.pallas_call(right_gram_kernel, out_shape=(jax.ShapeDtypeStruct((tall,...  7.83 us
    pallas_call x6, Pallas kernels, finish(): pl.pallas_call(functools.partial(finish_kernel, column, width), out_shape...  7.09 us
  transfers between devices with their start and end apart: 14, of which 8 were waited for; matrix products, arithmetic and copies ran while one was open for 0% of the time, Pallas kernels for 58%

profile of v3, /device:TPU:0, one launch (start us, length us, event | category | flops | bytes accessed | tf_op | source)
XLA Modules:
  0.0 105.4 jit_solution(9036319711695049430)
XLA Ops:
  1.2 3.0 %collective-permute-start.3 = (f32[512,512]{1,0:T(8,128)S(1)}, f32[512,512]{1,0:T(8,128)S(1)}, u32[]{:S(2)}, u32[]{:S(2)}) collective-permute-start(f32[512,512]{1,0:T(8,128)S(1)} %take.1.after_ref), channel_id=1, source_target_pairs={{0,4},{4,0},{1,5},{5,1},{2,6},{6,2},{3,7},{7,3},{8,12},{12,8},{9,1... | collective-permute-start | bytes 3145736 | tf_op jit(solution)/shard_map/ppermute | solution.py:618
  4.3 3.9 %right_grams.2 = (f32[264,256]{1,0:T(8,128)S(1)}, f32[264,256]{1,0:T(8,128)S(1)}) custom-call(s32[2]{0:T(128)S(1)} %pad_add_fusion.place, f32[1024,2048]{1,0:T(8,128)} %bitcast.9, f32[512,512]{1,0:T(8,128)S(1)} %take.1.after_ref), custom_call_target="tpu_custom_call" | custom-call | flops 1 | bytes 1 | tf_op jit(solution)/shard_map/right_grams/pallas_call | solution.py:133
  8.3 4.0 %right_grams.3 = (f32[264,256]{1,0:T(8,128)S(1)}, f32[264,256]{1,0:T(8,128)S(1)}) custom-call(s32[2]{0:T(128)S(1)} %pad_add_fusion.place, f32[1024,2048]{1,0:T(8,128)} %bitcast.10, f32[264,256]{1,0:T(8,128)S(1)} %get-tuple-element.20.after_ref.a_ref), custom_call_target="tpu_custom_call" | custom-call | flops 1 | bytes 1 | tf_op jit(solution)/shard_map/right_grams/pallas_call | solution.py:133
  12.9 1.6 %collective-permute-start.2 = (f32[264,256]{1,0:T(8,128)S(1)}, f32[264,256]{1,0:T(8,128)S(1)}, u32[]{:S(2)}, u32[]{:S(2)}) collective-permute-start(f32[264,256]{1,0:T(8,128)S(1)} %fold.1), channel_id=1, source_target_pairs={{0,16},{8,24},{16,0},{24,8},{1,17},{9,25},{17,1},{25,9},{2,18},{10... | collective-permute-start | bytes 811016 | tf_op jit(solution)/shard_map/ppermute | solution.py:620
  14.4 4.7 %left_grams.2.under_ref = f32[264,256]{1,0:T(8,128)S(1)} custom-call(s32[2]{0:T(128)S(1)} %pad_add_fusion.place, f32[1024,2048]{1,0:T(8,128)} %bitcast.11, f32[264,256]{1,0:T(8,128)S(1)} %get-tuple-element.22.after_ref), custom_call_target="tpu_custom_call" | custom-call | flops 1 | bytes 1 | tf_op jit(solution)/shard_map/left_grams/pallas_call | solution.py:182
  19.2 2.2 %collective-permute-done.2.c_ref = f32[264,256]{1,0:T(8,128)S(1)} collective-permute-done((f32[264,256]{1,0:T(8,128)S(1)}, f32[264,256]{1,0:T(8,128)S(1)}, u32[]{:S(2)}, u32[]{:S(2)}) %collective-permute-start.2) | collective-permute-done | bytes 270368 | tf_op jit(solution)/shard_map/ppermute | solution.py:620
  21.4 4.8 %right_roots.1 = (f32[264,256]{1,0:T(8,128)S(1)}, bf16[2,2,256,256]{3,2,1,0:T(8,128)(2,1)S(1)}, f32[776,256]{1,0:T(8,128)S(1)}) custom-call(s32[2]{0:T(128)S(1)} %pad_add_fusion.place, f32[2048,256]{1,0:T(8,128)S(1)} %bitcast.6, f32[264,256]{1,0:T(8,128)S(1)} %get-tuple-element.21.a_ref, f32[264,256]{1,0:T(8,128)S(1)} %collective-permute-done.b_ref, ...), custom_call_target="tpu_custom_call" | custom-call | flops 1 | bytes 1 | tf_op jit(solution)/shard_map/right_roots/pallas_call | solution.py:311
  27.5 1.8 %collective-permute-start.4 = (f32[264,256]{1,0:T(8,128)S(1)}, f32[264,256]{1,0:T(8,128)S(1)}, u32[]{:S(2)}, u32[]{:S(2)}) collective-permute-start(f32[264,256]{1,0:T(8,128)S(1)} %hold.2.after_ref), channel_id=1, source_target_pairs={{0,16},{8,24},{16,0},{24,8},{1,17},{9,25},{17,1},{25,9},{2,18},{10... | collective-permute-start | bytes 811016 | tf_op jit(solution)/shard_map/ppermute | solution.py:620
  29.2 6.0 %collective-permute-done.4.a_ref = f32[264,256]{1,0:T(8,128)S(1)} collective-permute-done((f32[264,256]{1,0:T(8,128)S(1)}, f32[264,256]{1,0:T(8,128)S(1)}, u32[]{:S(2)}, u32[]{:S(2)}) %collective-permute-start.4) | collective-permute-done | bytes 270368 | tf_op jit(solution)/shard_map/ppermute | solution.py:620
  35.2 4.7 %left_grams.3.rest_0_.a_ref = f32[264,256]{1,0:T(8,128)S(1)} custom-call(s32[2]{0:T(128)S(1)} %pad_add_fusion.place, f32[1024,2048]{1,0:T(8,128)} %bitcast.13, f32[264,256]{1,0:T(8,128)S(1)} %hold.2.after_ref), custom_call_target="tpu_custom_call" | custom-call | flops 1 | bytes 1 | tf_op jit(solution)/shard_map/left_grams/pallas_call | solution.py:182
  39.9 2.0 %right_apply.4 = f32[512,256]{1,0:T(8,128)S(1)} custom-call(s32[2]{0:T(128)S(1)} %pad_add_fusion.place, f32[1024,2048]{1,0:T(8,128)} %bitcast.14, bf16[2,2,256,256]{3,2,1,0:T(8,128)(2,1)S(1)} %get-tuple-element.26.right_ref, f32[264,256]{1,0:T(8,128)S(1)} %left_grams.3.rest_0_.a_ref), custom_call_target="tpu_custom_call" | custom-call | flops 1 | bytes 1 | tf_op jit(solution)/shard_map/right_apply/pallas_call | solution.py:506
  43.5 1.5 %collective-permute-done.8.rest_0_.b_ref.half_ref = f32[776,256]{1,0:T(8,128)S(1)} collective-permute-done((f32[776,256]{1,0:T(8,128)S(1)}, f32[776,256]{1,0:T(8,128)S(1)}, u32[]{:S(2)}, u32[]{:S(2)}) %collective-permute-start.8) | collective-permute-done | bytes 794656 | tf_op jit(solution)/shard_map/ppermute | solution.py:618
  45.0 2.4 %right_apply.5 = f32[512,512]{1,0:T(8,128)S(1)} custom-call(s32[2]{0:T(128)S(1)} %pad_add_fusion.place, f32[1024,2048]{1,0:T(8,128)} %bitcast.15, bf16[2,2,256,256]{3,2,1,0:T(8,128)(2,1)S(1)} %spread_roots.3.right_ref, f32[776,256]{1,0:T(8,128)S(1)} %collective-permute-done.8.rest_0_.b_ref.half_ref, f32[264,256]{1,0:T(8,128)S(1)} %collective-permute-done.6.refs_1_.rest_1_.xc_ref), custom_call_target="tpu_custom_call" | custom-call | flops 1 | bytes 1 | tf_op jit(solution)/shard_map/right_apply/pallas_call | solution.py:506
  48.7 7.9 %collective-permute-done.5.rest_0_.half_ref = f32[512,256]{1,0:T(8,128)S(1)} collective-permute-done((f32[512,256]{1,0:T(8,128)S(1)}, f32[512,256]{1,0:T(8,128)S(1)}, u32[]{:S(2)}, u32[]{:S(2)}) %collective-permute-start.5) | collective-permute-done | bytes 524320 | tf_op jit(solution)/shard_map/ppermute | solution.py:618
  57.7 2.0 %right_apply.7 = f32[648,256]{1,0:T(8,128)S(1)} custom-call(s32[2]{0:T(128)S(1)} %pad_add_fusion.place, f32[1024,2048]{1,0:T(8,128)} %bitcast.16, bf16[4,2,256,256]{3,2,1,0:T(8,128)(2,1)S(1)} %spread_roots.2.right_ref, f32[136,256]{1,0:T(8,128)S(1)} %cut.1.rest_0_), custom_call_target="tpu_custom_call" | custom-call | flops 1 | bytes 1 | tf_op jit(solution)/shard_map/right_apply/pallas_call | solution.py:506
  59.7 1.5 %collective-permute-start.12 = (f32[648,256]{1,0:T(8,128)S(1)}, f32[648,256]{1,0:T(8,128)S(1)}, u32[]{:S(2)}, u32[]{:S(2)}) collective-permute-start(f32[648,256]{1,0:T(8,128)S(1)} %right_apply.7), channel_id=1, source_target_pairs={{0,4},{4,0},{1,5},{5,1},{2,6},{6,2},{3,7},{7,3},{8,12},{12,8},{9,1... | collective-permute-start | bytes 1990664 | tf_op jit(solution)/shard_map/ppermute | solution.py:618
  61.2 3.5 %left_roots.1.left_ref = bf16[2,2,256,256]{3,2,1,0:T(8,128)(2,1)S(1)} custom-call(s32[2]{0:T(128)S(1)} %pad_add_fusion.place, f32[1024,256]{1,0:T(8,128)S(1)} %bitcast.7, f32[264,256]{1,0:T(8,128)S(1)} %left_grams.3.rest_0_.a_ref, f32[776,256]{1,0:T(8,128)S(1)} %collective-permute-done.8.rest_0_.b_ref.half_ref), custom_call_target="tpu_custom_call" | custom-call | flops 1 | bytes 1 | tf_op jit(solution)/shard_map/left_roots/pallas_call | solution.py:353
  64.7 4.5 %update.4 = (f32[512,4096]{1,0:T(8,128)}, f32[8,128]{1,0:T(8,128)}) custom-call(s32[2]{0:T(128)S(1)} %pad_add_fusion.place, f32[1024,2048]{1,0:T(8,128)} %bitcast.17, bf16[2,2,256,256]{3,2,1,0:T(8,128)(2,1)S(1)} %left_roots.1.left_ref, bf16[2,2,256,256]{3,2,1,0:T(8,128)(2,1)S(1)} %get-tuple-element.26.right_ref), custom_call_target="tpu_custom_call" | custom-call | flops 1 | bytes 1 | tf_op jit(solution)/shard_map/update/pallas_call | solution.py:587
  69.2 4.5 %update.5 = (f32[512,4096]{1,0:T(8,128)}, f32[8,128]{1,0:T(8,128)}) custom-call(s32[2]{0:T(128)S(1)} %pad_add_fusion.place, f32[1024,2048]{1,0:T(8,128)} %bitcast.18, bf16[2,2,256,256]{3,2,1,0:T(8,128)(2,1)S(1)} %left_roots.1.left_ref, bf16[2,2,256,256]{3,2,1,0:T(8,128)(2,1)S(1)} %spread_roots.3.right_ref, ...), custom_call_target="tpu_custom_call", output_to_operand_aliasing={{0}: (4, {})} | custom-call | flops 1 | bytes 1 | tf_op jit(solution)/shard_map/update/pallas_call | solution.py:587
  73.7 6.8 %update.6 = (f32[512,4096]{1,0:T(8,128)}, f32[8,128]{1,0:T(8,128)}) custom-call(s32[2]{0:T(128)S(1)} %pad_add_fusion.place, f32[1024,2048]{1,0:T(8,128)} %bitcast.19, bf16[2,2,256,256]{3,2,1,0:T(8,128)(2,1)S(1)} %left_roots.1.left_ref, bf16[4,2,256,256]{3,2,1,0:T(8,128)(2,1)S(1)} %spread_roots.2.right_ref, ...), custom_call_target="tpu_custom_call", output_to_operand_aliasing={{0}: (4, {})} | custom-call | flops 1 | bytes 1 | tf_op jit(solution)/shard_map/update/pallas_call | solution.py:587
  84.3 2.0 %right_apply.6 = (f32[512,128]{1,0:T(8,128)S(1)}, f32[512,128]{1,0:T(8,128)S(1)}) custom-call(s32[2]{0:T(128)S(1)} %pad_add_fusion.place, f32[1024,2048]{1,0:T(8,128)} %bitcast.20, bf16[4,2,256,256]{3,2,1,0:T(8,128)(2,1)S(1)} %spread_roots.2.right_ref, f32[512,512]{1,0:T(8,128)S(1)} %collective-permute-done.9.half_ref.rest_0_, ...), custom_call_target="tpu_custom_call" | custom-call | flops 1 | bytes 1 | tf_op jit(solution)/shard_map/right_apply/pallas_call | solution.py:506
  88.4 5.0 %collective-permute-done.12.a_ref.half_ref = f32[648,256]{1,0:T(8,128)S(1)} collective-permute-done((f32[648,256]{1,0:T(8,128)S(1)}, f32[648,256]{1,0:T(8,128)S(1)}, u32[]{:S(2)}, u32[]{:S(2)}) %collective-permute-start.12) | collective-permute-done | bytes 663584 | tf_op jit(solution)/shard_map/ppermute | solution.py:618
  95.5 3.5 %update.7 = (f32[512,4096]{1,0:T(8,128)}, f32[8,128]{1,0:T(8,128)}) custom-call(s32[2]{0:T(128)S(1)} %pad_add_fusion.place, f32[512,512]{1,0:T(8,128)S(1)} %collective-permute-done.3.rest_0_.g_ref, bf16[2,2,256,256]{3,2,1,0:T(8,128)(2,1)S(1)} %left_roots.1.left_ref, ...), custom_call_target="tpu_custom_call", output_to_operand_aliasing={{0}: (4, {})} | custom-call | flops 1 | bytes 1 | tf_op jit(solution)/shard_map/update/pallas_call | solution.py:587
  101.3 2.9 %collective-permute-done.10.half_ref = f32[512,128]{1,0:T(8,128)S(1)} collective-permute-done((f32[512,128]{1,0:T(8,128)S(1)}, f32[512,128]{1,0:T(8,128)S(1)}, u32[]{:S(2)}, u32[]{:S(2)}) %collective-permute-start.10) | collective-permute-done | bytes 262176 | tf_op jit(solution)/shard_map/ppermute | solution.py:618
  (38 shorter events, 18.5 us)
Async XLA Ops:
  1.2 26.2 %collective-permute-start.3 = (f32[512,512]{1,0:T(8,128)S(1)}, f32[512,512]{1,0:T(8,128)S(1)}, u32[]{:S(2)}, u32[]{:S(2)}) collective-permute-start(f32[512,512]{1,0:T(8,128)S(1)} %take.1.after_ref), channel_id=1, source_target_pairs={{0,4},{4,0},{1,5},{5,1},{2,6},{6,2},{3,7},{7,3},{8,12},{12,8},{9,1... | collective-permute-start | bytes 3145736 | tf_op jit(solution)/shard_map/ppermute | solution.py:618
  8.2 4.6 %collective-permute-start.1 = (f32[264,256]{1,0:T(8,128)S(1)}, f32[264,256]{1,0:T(8,128)S(1)}, u32[]{:S(2)}, u32[]{:S(2)}) collective-permute-start(f32[264,256]{1,0:T(8,128)S(1)} %get-tuple-element.23), channel_id=1, source_target_pairs={{0,8},{8,0},{16,24},{24,16},{1,9},{9,1},{17,25},{25,17},{2,10},{10... | collective-permute-start | bytes 811016 | tf_op jit(solution)/shard_map/ppermute | solution.py:620
  8.3 13.0 %copy-start = (f32[1,2048,256]{2,1,0:T(8,128)S(1)}, f32[1,2048,256]{2,1,0:T(8,128)}, u32[]{:S(2)}) copy-start(f32[1,2048,256]{2,1,0:T(8,128)} %param.5) | copy-start | bytes 6291460
  12.3 6.9 %collective-permute-start = (f32[264,256]{1,0:T(8,128)S(1)}, f32[264,256]{1,0:T(8,128)S(1)}, u32[]{:S(2)}, u32[]{:S(2)}) collective-permute-start(f32[264,256]{1,0:T(8,128)S(1)} %get-tuple-element.22.after_ref), channel_id=1, source_target_pairs={{0,8},{8,0},{16,24},{24,16},{1,9},{9,1},{17,25},{25,17},{2,10},{10... | collective-permute-start | bytes 811016 | tf_op jit(solution)/shard_map/ppermute | solution.py:620
  12.9 8.5 %collective-permute-start.2 = (f32[264,256]{1,0:T(8,128)S(1)}, f32[264,256]{1,0:T(8,128)S(1)}, u32[]{:S(2)}, u32[]{:S(2)}) collective-permute-start(f32[264,256]{1,0:T(8,128)S(1)} %fold.1), channel_id=1, source_target_pairs={{0,16},{8,24},{16,0},{24,8},{1,17},{9,25},{17,1},{25,9},{2,18},{10... | collective-permute-start | bytes 811016 | tf_op jit(solution)/shard_map/ppermute | solution.py:620
  26.2 18.9 %collective-permute-start.8 = (f32[776,256]{1,0:T(8,128)S(1)}, f32[776,256]{1,0:T(8,128)S(1)}, u32[]{:S(2)}, u32[]{:S(2)}) collective-permute-start(f32[776,256]{1,0:T(8,128)S(1)} %get-tuple-element.25.rest_1_), channel_id=1, source_target_pairs={{0,4},{4,0},{1,5},{5,1},{2,6},{6,2},{3,7},{7,3},{8,12},{12,8},{9,1... | collective-permute-start | bytes 2383880 | tf_op jit(solution)/shard_map/ppermute | solution.py:618
  27.5 7.7 %collective-permute-start.4 = (f32[264,256]{1,0:T(8,128)S(1)}, f32[264,256]{1,0:T(8,128)S(1)}, u32[]{:S(2)}, u32[]{:S(2)}) collective-permute-start(f32[264,256]{1,0:T(8,128)S(1)} %hold.2.after_ref), channel_id=1, source_target_pairs={{0,16},{8,24},{16,0},{24,8},{1,17},{9,25},{17,1},{25,9},{2,18},{10... | collective-permute-start | bytes 811016 | tf_op jit(solution)/shard_map/ppermute | solution.py:620
  29.2 14.1 %collective-permute-start.7 = (f32[264,256]{1,0:T(8,128)S(1)}, f32[264,256]{1,0:T(8,128)S(1)}, u32[]{:S(2)}, u32[]{:S(2)}) collective-permute-start(f32[264,256]{1,0:T(8,128)S(1)} %hold.2.after_ref), channel_id=1, source_target_pairs={{0,8},{8,0},{16,24},{24,16},{1,9},{9,1},{17,25},{25,17},{2,10},{10... | collective-permute-start | bytes 811016 | tf_op jit(solution)/shard_map/ppermute | solution.py:620
  35.2 9.9 %collective-permute-start.6 = (f32[264,256]{1,0:T(8,128)S(1)}, f32[264,256]{1,0:T(8,128)S(1)}, u32[]{:S(2)}, u32[]{:S(2)}) collective-permute-start(f32[264,256]{1,0:T(8,128)S(1)} %collective-permute-done.4.a_ref), channel_id=1, source_target_pairs={{0,8},{8,0},{16,24},{24,16},{1,9},{9,1},{17,25},{25,17},{2,10},{10... | collective-permute-start | bytes 811016 | tf_op jit(solution)/shard_map/ppermute | solution.py:620
  41.9 14.8 %collective-permute-start.5 = (f32[512,256]{1,0:T(8,128)S(1)}, f32[512,256]{1,0:T(8,128)S(1)}, u32[]{:S(2)}, u32[]{:S(2)}) collective-permute-start(f32[512,256]{1,0:T(8,128)S(1)} %right_apply.4), channel_id=1, source_target_pairs={{0,4},{4,0},{1,5},{5,1},{2,6},{6,2},{3,7},{7,3},{8,12},{12,8},{9,1... | collective-permute-start | bytes 1572872 | tf_op jit(solution)/shard_map/ppermute | solution.py:618
  47.5 13.7 %copy-start.1 = (f32[1,1024,256]{2,1,0:T(8,128)S(1)}, f32[1,1024,256]{2,1,0:T(8,128)}, u32[]{:S(2)}) copy-start(f32[1,1024,256]{2,1,0:T(8,128)} %param.4) | copy-start | bytes 3145732
  47.5 35.3 %collective-permute-start.9 = (f32[512,512]{1,0:T(8,128)S(1)}, f32[512,512]{1,0:T(8,128)S(1)}, u32[]{:S(2)}, u32[]{:S(2)}) collective-permute-start(f32[512,512]{1,0:T(8,128)S(1)} %right_apply.5), channel_id=1, source_target_pairs={{0,4},{4,0},{1,5},{5,1},{2,6},{6,2},{3,7},{7,3},{8,12},{12,8},{9,1... | collective-permute-start | bytes 3145736 | tf_op jit(solution)/shard_map/ppermute | solution.py:618
  59.7 33.7 %collective-permute-start.12 = (f32[648,256]{1,0:T(8,128)S(1)}, f32[648,256]{1,0:T(8,128)S(1)}, u32[]{:S(2)}, u32[]{:S(2)}) collective-permute-start(f32[648,256]{1,0:T(8,128)S(1)} %right_apply.7), channel_id=1, source_target_pairs={{0,4},{4,0},{1,5},{5,1},{2,6},{6,2},{3,7},{7,3},{8,12},{12,8},{9,1... | collective-permute-start | bytes 1990664 | tf_op jit(solution)/shard_map/ppermute | solution.py:618
  86.3 14.0 %collective-permute-start.11 = (f32[512,128]{1,0:T(8,128)S(1)}, f32[512,128]{1,0:T(8,128)S(1)}, u32[]{:S(2)}, u32[]{:S(2)}) collective-permute-start(f32[512,128]{1,0:T(8,128)S(1)} %get-tuple-element.32), channel_id=1, source_target_pairs={{0,4},{4,0},{1,5},{5,1},{2,6},{6,2},{3,7},{7,3},{8,12},{12,8},{9,1... | collective-permute-start | bytes 786440 | tf_op jit(solution)/shard_map/ppermute | solution.py:618
  86.9 17.3 %collective-permute-start.10 = (f32[512,128]{1,0:T(8,128)S(1)}, f32[512,128]{1,0:T(8,128)S(1)}, u32[]{:S(2)}, u32[]{:S(2)}) collective-permute-start(f32[512,128]{1,0:T(8,128)S(1)} %get-tuple-element.31), channel_id=1, source_target_pairs={{0,4},{4,0},{1,5},{5,1},{2,6},{6,2},{3,7},{7,3},{8,12},{12,8},{9,1... | collective-permute-start | bytes 786440 | tf_op jit(solution)/shard_map/ppermute | solution.py:618
  93.4 1.4 %collective-permute-start.13 = (f32[136,256]{1,0:T(8,128)S(1)}, f32[136,256]{1,0:T(8,128)S(1)}, u32[]{:S(2)}, u32[]{:S(2)}) collective-permute-start(f32[136,256]{1,0:T(8,128)S(1)} %rest_of.1.mine_ref), channel_id=1, source_target_pairs={{0,8},{8,0},{16,24},{24,16},{1,9},{9,1},{17,25},{25,17},{2,10},{10... | collective-permute-start | bytes 417800 | tf_op jit(solution)/shard_map/ppermute | solution.py:620

commit v4 on v3

--- a/solution.py
+++ b/solution.py
@@ -201,27 +201,48 @@
     )(place, tile, after)
 
 
+RAW = (1, 3)
+
+
 def here():
     return lax.axis_index("row"), lax.axis_index("col")
 
 
-def take_kernel(g_ref, out_ref, sem):
+def own_first(place):
+    return place[0] * 2
+
+
+def core_first(place):
+    return (place[0] ^ 1) * 2
+
+
+def later(k, place):
+    return jnp.where(place[0] < 2, 4 + k, jnp.where(k < 2, 2 * k, 2 * k + 1))
+
+
+def take_kernel(g_ref, out_ref, sems):
     rows, wide = out_ref.shape
-    place = here()
-    start = pl.multiple_of((place[0] ^ raw_flip(place)) * wide, wide)
-    top = pl.multiple_of((1 - place[1]) * rows, rows)
-    copy = pltpu.make_async_copy(g_ref.at[pl.ds(top, rows), pl.ds(start, wide)], out_ref, sem)
-    copy.start()
-    copy.wait()
+    blk = wide // len(RAW)
+    top = pl.multiple_of((1 - here()[1]) * rows, rows)
+    copies = [
+        pltpu.make_async_copy(
+            g_ref.at[pl.ds(top, rows), pl.ds(block * blk, blk)], out_ref.at[:, pl.ds(k * blk, blk)], sems.at[k]
+        )
+        for k, block in enumerate(RAW)
+    ]
+    for copy in copies:
+        copy.start()
+    for copy in copies:
+        copy.wait()
 
 
 def take(tile, blk):
     return pl.pallas_call(
         take_kernel,
-        out_shape=jax.ShapeDtypeStruct((tile.shape[0] // 2, 2 * blk), jnp.float32),
+        out_shape=jax.ShapeDtypeStruct((tile.shape[0] // 2, len(RAW) * blk), jnp.float32),
         in_specs=[pl.BlockSpec(memory_space=pl.ANY)],
         out_specs=pl.BlockSpec(memory_space=pl.ANY),
-        scratch_shapes=[pltpu.SemaphoreType.DMA],
+        scratch_shapes=[pltpu.SemaphoreType.DMA((len(RAW),))],
         compiler_params=pltpu.CompilerParams(vmem_limit_bytes=VMEM_LIMIT),
         cost_estimate=SMALL,
         name="take",
@@ -287,7 +308,7 @@
     return [r * jnp.exp(-0.25 * jnp.log(s)) for r, s in zip(result, scales)]
 
 
-def right_kernel(full_dim, place, stats_ref, a_ref, b_ref, c_ref, g_ref, under_ref, out_ref, halves_ref, half_ref):
+def right_kernel(full_dim, place, stats_ref, a_ref, b_ref, c_ref, g_ref, under_ref, out_ref, half_ref):
     blk = stats_ref.shape[1]
     rows = g_ref.shape[0]
     total = a_ref[...] + b_ref[...] + c_ref[...]
@@ -297,10 +318,6 @@
     body, diag = pack(*roots)
     out_ref[:blk, :] = body
     out_ref[blk:, :] = diag
-    for b, root in enumerate(roots):
-        high, low = split(root)
-        halves_ref[b, 0] = high
-        halves_ref[b, 1] = low
 
 
 def right_roots(full_dim, place, stats, kept, near, far, tile, under):
@@ -312,7 +329,6 @@
         functools.partial(right_kernel, full_dim),
         out_shape=(
             jax.ShapeDtypeStruct((tall, blk), jnp.float32),
-            jax.ShapeDtypeStruct((2, 2, blk, blk), jnp.bfloat16),
             jax.ShapeDtypeStruct((rows + tall, blk), jnp.float32),
         ),
         grid_spec=pltpu.PrefetchScalarGridSpec(
@@ -323,12 +339,11 @@
                 flat,
                 flat,
                 flat,
-                pl.BlockSpec((rows, blk), lambda s, place: (1 - place[1], place[0] * 2)),
+                pl.BlockSpec((rows, blk), lambda s, place: (1 - place[1], own_first(place))),
                 flat,
             ],
             out_specs=(
                 flat,
-                pl.BlockSpec((2, 2, blk, blk), lambda s, place: (0, 0, 0, 0)),
                 pl.BlockSpec((rows + tall, blk), lambda s, place: (0, 0)),
             ),
         ),
@@ -369,106 +384,101 @@
     )(place, stats, kept, came)
 
 
-def raw_flip(place):
-    return 2 + (place[0] & 1)
-
-
-def put_roots(out_ref, at, body, diag):
-    for b, root in enumerate(unpack(body, diag)):
+def put_roots(out_ref, at, roots):
+    for b, root in enumerate(roots):
         high, low = split(root)
-        out_ref[2 * at + b, 0] = high
-        out_ref[2 * at + b, 1] = low
-
-
-def spread_kernel(*refs):
-    out_ref = refs[-1]
+        out_ref[at + b, 0] = high
+        out_ref[at + b, 1] = low
+
+
+def spread_kernel(own_ref, c_ref, x_ref, xc_ref, out_ref, cut_ref, seconds, body):
     blk = out_ref.shape[-1]
-    for at, ref in enumerate(refs[:-1]):
-        put_roots(out_ref, at, ref[:blk, :], ref[blk : blk + 1, :])
+    r = here()[0]
+    for flip, ref in enumerate((own_ref, c_ref, x_ref, xc_ref)):
+        roots = unpack(ref[:blk, :], ref[blk : blk + 1, :])
+        put_roots(out_ref, 2 * (r ^ flip), roots)
+        seconds[r ^ flip] = roots[1]
+    part = cut_ref.shape[0] - PAD
+    body[...], diag = pack(seconds[RAW[0] // 2], seconds[RAW[1] // 2])
+    cut_ref[:part, :] = body[pl.ds(pl.multiple_of(r * part, part), part), :]
+    cut_ref[part:, :] = diag
 
 
 def spread_roots(*packed):
     blk = packed[0].shape[1]
+    count = len(packed)
     return pl.pallas_call(
         spread_kernel,
-        out_shape=jax.ShapeDtypeStruct((2 * len(packed), 2, blk, blk), jnp.bfloat16),
+        out_shape=(
+            jax.ShapeDtypeStruct((2 * count, 2, blk, blk), jnp.bfloat16),
+            jax.ShapeDtypeStruct((blk // count + PAD, blk), jnp.float32),
+        ),
+        scratch_shapes=[pltpu.VMEM((count, blk, blk), jnp.float32), pltpu.VMEM((blk, blk), jnp.float32)],
         compiler_params=pltpu.CompilerParams(vmem_limit_bytes=VMEM_LIMIT),
         cost_estimate=SMALL,
         name="spread_roots",
     )(*packed)
 
 
-def cut_kernel(place, x_ref, xc_ref, out_ref):
-    half = out_ref.shape[0] - PAD
-
-    @pl.when((place[0] & 1) == 0)
-    def _():
-        out_ref[:half, :] = x_ref[:half, :]
-        out_ref[half:, :] = x_ref[2 * half :, :]
-
-    @pl.when((place[0] & 1) == 1)
-    def _():
-        out_ref[:half, :] = xc_ref[half : 2 * half, :]
-        out_ref[half:, :] = xc_ref[2 * half :, :]
-
-
-def cut(place, of_x, of_xc):
-    tall, blk = of_x.shape
-    whole = pl.BlockSpec((tall, blk), lambda s, place: (0, 0))
-    return pl.pallas_call(
-        cut_kernel,
-        out_shape=jax.ShapeDtypeStruct((blk // 2 + PAD, blk), jnp.float32),
+def rest_kernel(a_ref, out_ref):
+    out_ref[...] = a_ref[a_ref.shape[0] - out_ref.shape[0] :, :]
+
+
+def rest_of(value, rows):
+    return pl.pallas_call(
+        rest_kernel,
+        out_shape=jax.ShapeDtypeStruct((value.shape[0] - rows, value.shape[1]), jnp.float32),
+        compiler_params=pltpu.CompilerParams(vmem_limit_bytes=VMEM_LIMIT),
+        cost_estimate=SMALL,
+        name="rest_of",
+    )(value)
+
+
+def join_kernel(own_ref, c_ref, x_ref, xc_ref, out_ref, body):
+    part = own_ref.shape[0] - PAD
+    r = here()[0]
+    for flip, ref in enumerate((own_ref, c_ref, x_ref, xc_ref)):
+        body[pl.ds(pl.multiple_of((r ^ flip) * part, part), part), :] = ref[:part, :]
+    put_roots(out_ref, 0, unpack(body[...], own_ref[part : part + 1, :]))
+
+
+def join_roots(*parts):
+    blk = parts[0].shape[1]
+    return pl.pallas_call(
+        join_kernel,
+        out_shape=jax.ShapeDtypeStruct((2, 2, blk, blk), jnp.bfloat16),
+        scratch_shapes=[pltpu.VMEM((blk, blk), jnp.float32)],
+        compiler_params=pltpu.CompilerParams(vmem_limit_bytes=VMEM_LIMIT),
+        cost_estimate=SMALL,
+        name="join_roots",
+    )(*parts)
+
+
+def core_apply_kernel(place, g_ref, packed_ref, out_ref):
+    blk = g_ref.shape[1]
+    root = unpack(packed_ref[:blk, :], packed_ref[blk : blk + 1, :])[0]
+    out_ref[...] = product(split(g_ref[...]), split(root))
+
+
+def core_apply(place, tile, packed):
+    rows = tile.shape[0] // 2
+    tall, blk = packed.shape
+    return pl.pallas_call(
+        core_apply_kernel,
+        out_shape=jax.ShapeDtypeStruct((rows, blk), jnp.float32),
         grid_spec=pltpu.PrefetchScalarGridSpec(
             num_scalar_prefetch=1,
             grid=(1,),
-            in_specs=[whole, whole],
-            out_specs=pl.BlockSpec((blk // 2 + PAD, blk), lambda s, place: (0, 0)),
-        ),
-        compiler_params=pltpu.CompilerParams(vmem_limit_bytes=VMEM_LIMIT),
-        cost_estimate=SMALL,
-        name="cut",
-    )(place, of_x, of_xc)
-
-
-def rest_kernel(a_ref, out_ref):
-    out_ref[...] = a_ref[a_ref.shape[0] - out_ref.shape[0] :, :]
-
-
-def rest_of(value, rows):
-    return pl.pallas_call(
-        rest_kernel,
-        out_shape=jax.ShapeDtypeStruct((value.shape[0] - rows, value.shape[1]), jnp.float32),
-        compiler_params=pltpu.CompilerParams(vmem_limit_bytes=VMEM_LIMIT),
-        cost_estimate=SMALL,
-        name="rest_of",
-    )(value)
-
-
-def join_kernel(place, mine_ref, other_ref, out_ref, body):
-    half = mine_ref.shape[0] - PAD
-    core = place[0] & 1
-    body[pl.ds(pl.multiple_of(core * half, half), half), :] = mine_ref[:half, :]
-    body[pl.ds(pl.multiple_of((1 - core) * half, half), half), :] = other_ref[:half, :]
-    put_roots(out_ref, 0, body[...], mine_ref[half : half + 1, :])
-
-
-def join_roots(place, mine, other):
-    tall, blk = mine.shape
-    half = pl.BlockSpec((tall, blk), lambda s, place: (0, 0))
-    return pl.pallas_call(
-        join_kernel,
-        out_shape=jax.ShapeDtypeStruct((2, 2, blk, blk), jnp.bfloat16),
-        grid_spec=pltpu.PrefetchScalarGridSpec(
-            num_scalar_prefetch=1,
-            grid=(1,),
-            in_specs=[half, half],
-            out_specs=pl.BlockSpec((2, 2, blk, blk), lambda s, place: (0, 0, 0, 0)),
-            scratch_shapes=[pltpu.VMEM((blk, blk), jnp.float32)],
-        ),
-        compiler_params=pltpu.CompilerParams(vmem_limit_bytes=VMEM_LIMIT),
-        cost_estimate=SMALL,
-        name="join_roots",
-    )(place, mine, other)
+            in_specs=[
+                pl.BlockSpec((rows, blk), lambda s, place: (1 - place[1], core_first(place))),
+                pl.BlockSpec((tall, blk), lambda s, place: (0, 0)),
+            ],
+            out_specs=pl.BlockSpec((rows, blk), lambda s, place: (0, 0)),
+        ),
+        compiler_params=pltpu.CompilerParams(vmem_limit_bytes=VMEM_LIMIT),
+        cost_estimate=SMALL,
+        name="core_apply",
+    )(place, tile, packed)
 
 
 def right_apply_kernel(width, carries, place, g_ref, right_ref, *rest):
@@ -490,12 +500,12 @@
         out_refs[0][value.shape[0] :, :] = rest[0][...]
 
 
-def right_apply(place, tile, right, flip, right_at, first, width, under, after):
+def right_apply(place, tile, right, first, width, under, after):
     rows = tile.shape[0] // 2
     blk = right.shape[-1]
     in_specs = [
-        pl.BlockSpec((rows, blk), lambda s, place: (1 - place[1], (place[0] ^ flip(place)) * 2 + first + s)),
-        pl.BlockSpec((1, 2, blk, blk), lambda s, place: (right_at(place) + first + s, 0, 0, 0)),
+        pl.BlockSpec((rows, blk), lambda s, place: (1 - place[1], later(first + s, place))),
+        pl.BlockSpec((1, 2, blk, blk), lambda s, place: (later(first + s, place), 0, 0, 0)),
     ]
     operands = [tile, right]
     tall = rows
@@ -531,38 +541,42 @@
     rest[-1][...] = jnp.zeros_like(rest[-1])
 
 
-def finish_kernel(column, width, half_ref, left_ref, out_before, out_ref, *rest):
+def finish_kernel(columns, half_ref, left_ref, out_before, out_ref, *rest):
     stage, sems = rest[-2:]
     blk = left_ref.shape[-1]
-    start = pl.multiple_of(column(here()), width)
+    size = stage.shape[1] // len(columns)
     copies = []
-    for i in range(left_ref.shape[0]):
-        rows = pl.ds(i * blk, blk)
-        for b in range(0, width, blk):
-            cols = pl.ds(b, min(blk, width))
+    for b, column in enumerate(columns):
+        start = pl.multiple_of(column(here()), size)
+        cols = pl.ds(b * size, size)
+        for i in range(left_ref.shape[0]):
+            rows = pl.ds(i * blk, blk)
             stage[rows, cols] = product((left_ref[i, 0], left_ref[i, 1]), split(half_ref[rows, cols]))
-        copies.append(
-            pltpu.make_async_copy(stage.at[rows, :], out_ref.at[rows, pl.ds(start, width)], sems.at[i])
-        )
-        copies[i].start()
+            copies.append(
+                pltpu.make_async_copy(stage.at[rows, cols], out_ref.at[rows, pl.ds(start, size)], sems.at[len(copies)])
+            )
+            copies[-1].start()
     for done_ref in rest[:-2]:
         done_ref[...] = jnp.zeros_like(done_ref)
     for copy in copies:
         copy.wait()
 
 
-def finish(half, left, out, column, mark=False):
+def finish(half, left, out, columns, mark=False):
     width = half.shape[1]
     rows = out.shape[0]
     vmem = pl.BlockSpec(memory_space=pltpu.VMEM)
     anywhere = pl.BlockSpec(memory_space=pl.ANY)
     shapes = (jax.ShapeDtypeStruct(out.shape, jnp.float32), jax.ShapeDtypeStruct((8, 128), jnp.float32))
     return pl.pallas_call(
-        functools.partial(finish_kernel, column, width),
+        functools.partial(finish_kernel, columns),
         out_shape=shapes if mark else shapes[:1],
         in_specs=[vmem, vmem, anywhere],
         out_specs=(anywhere, vmem) if mark else (anywhere,),
-        scratch_shapes=[pltpu.VMEM((rows, width), jnp.float32), pltpu.SemaphoreType.DMA((left.shape[0],))],
+        scratch_shapes=[
+            pltpu.VMEM((rows, width), jnp.float32),
+            pltpu.SemaphoreType.DMA((left.shape[0] * len(columns),)),
+        ],
         input_output_aliases={2: 0},
         compiler_params=pltpu.CompilerParams(vmem_limit_bytes=VMEM_LIMIT),
         cost_estimate=SMALL,
@@ -629,61 +643,48 @@
     far = over("x", fold(keep_on, near_on))
     lsend = left_grams(place, tile, blk, lambda place: 1 - place[1], send)
 
-    own_pair, core_pair = (lambda place: 0), (lambda place: 1)
-    last_pair = lambda place: 3 - (place[0] & 1)
-    begin = lambda place: 0
-    last_at = lambda place: 2 * (1 - (place[0] & 1))
-    tail = (blk, blk // 2, blk // 2)
-
-    own, roots_own, half = right_roots(full_dim, place, rstats, keep, near, far, tile, lsend)
-    came_0a = over("y", half)
+    own, half = right_roots(full_dim, place, rstats, keep, near, far, tile, lsend)
+    came_a = over("y", half)
     own = hold(own, raw, half)
-    lkeep = left_grams(place, tile, blk, lambda place: place[1], own)
     own_c = over("core", own)
     own_x = over("x", own)
-    own_xc = over("core", own_x)
-    held = right_apply(place, tile, roots_own, own_pair, begin, 1, (blk,), None, (lkeep,))
-    came_0b = over("y", held[0])
-    roots_core = spread_roots(own_c)
-    held = right_apply(place, tile, roots_core, core_pair, begin, 0, (2 * blk,), None, (came_0a, own_xc))
-    came_1 = over("y", held[0])
-    own_x = hold(own_x, came_0b)
-    roots_far = spread_roots(own_x, own_xc)
-    held = right_apply(place, tile, roots_far, last_pair, last_at, 0, tail[:1], cut(place, own_x, own_xc), ())
-    came_2 = [over("y", held[0])]
-    mine = rest_of(came_2[0], rows)
-    roots_raw = join_roots(place, mine, over("core", mine))
-
-    left = left_roots(full_dim, place, lstats, lkeep, came_0a)
-
-    def own_cols(base):
-        return lambda s, place: (place[1], (place[0] ^ (base + s // 2)) * 2 + s % 2)
-
-    out = None
-    for base, roots in ((0, roots_own), (1, roots_core), (2, roots_far)):
-        at = own_cols(base)
-        out, done = update(
-            place, tile, left, roots, out, shape, at,
-            lambda s, place, at=at: (0, place[1] * halves + at(s, place)[1]),
-        )
-
-    def crossed(start, flip):
-        return lambda place: (1 - place[1]) * tile_cols + (place[0] ^ flip(place)) * 2 * blk + start
-
-    for b, value in enumerate((came_0a, came_0b)):
-        (out,) = finish(value, left, out, crossed(b * blk, own_pair))
-    out, done = finish(came_1, left, out, crossed(0, core_pair), mark=True)
-    held = right_apply(place, tile, roots_far, last_pair, last_at, 1, tail[1:], None, (came_1, done))
-    came_2 += [over("y", half) for half in held]
+    lkeep = left_grams(place, tile, blk, lambda place: place[1], own)
+    came_b = over("y", core_apply(place, tile, own_c))
+    own_x = hold(own_x, lkeep)
+    roots, part = spread_roots(own, own_c, own_x, over("core", own_x))
+
+    (half,) = right_apply(place, tile, roots, 0, (blk,), part, (came_a,))
+    came_c = over("y", half)
+    left = left_roots(full_dim, place, lstats, lkeep, came_a)
+    (half,) = right_apply(place, tile, roots, 1, (blk,), None, (came_b, left))
+    came_d = over("y", half)
+
+    def crossed(block, start=0):
+        return (lambda place: (1 - place[1]) * tile_cols + block(place) * blk + start,)
+
+    out, done = update(
+        place, tile, left, roots, None, shape,
+        lambda s, place: (place[1], s),
+        lambda s, place: (0, place[1] * halves + s),
+    )
+    (half,) = right_apply(place, tile, roots, 2, (blk,), None, (came_c, done))
+    came_e = over("y", half)
+    (out,) = finish(came_a, left, out, crossed(own_first))
+    (out,) = finish(came_b, left, out, crossed(core_first))
+    part = rest_of(came_c, rows)
+    part_x = over("x", part)
+    roots_raw = join_roots(part, over("core", part), part_x, over("core", part_x))
     out, done = update(
         place, raw, left, roots_raw, out, shape,
         lambda s, place: (0, s),
-        lambda s, place: (0, (1 - place[1]) * halves + (place[0] ^ raw_flip(place)) * 2 + s),
+        lambda s, place: (0, (1 - place[1]) * halves + jnp.where(s == 0, RAW[0], RAW[1])),
     )
-    start = 0
-    for wide, value in zip(tail, came_2):
-        (out,) = finish(value, left, out, crossed(start, last_pair))
-        start += wide
+    last = (blk // 2, blk // 2)
+    came_last = [over("y", half) for half in right_apply(place, tile, roots, 3, last, None, (came_d, done))]
+    for k, value in enumerate((came_c, came_d, came_e)):
+        (out,) = finish(value, left, out, crossed(functools.partial(later, k)))
+    for k, value in enumerate(came_last):
+        (out,) = finish(value, left, out, crossed(functools.partial(later, 3), k * last[0]))
     return out.reshape(1, rows, 2 * tile_cols)
 
 

time: 106 us -> 105 us (level)
  Pallas kernels: 63.4 us -> 60.4 us
  starting transfers between devices: 13.7 us -> 15 us
    pallas_call x4 -> x2, Pallas kernels: 19.2 us -> 14.8 us  [update(): pl.pallas_call(update_kernel, out_shape=(jax.ShapeDtypeStruct(out_shape,...]
    ppermute x7 -> x8, waiting for transfers between devices: 18.3 us -> 21.8 us  [over(): return lax.ppermute(value, 'col', [(0, 1), (1, 0)])]
    ppermute x7 -> x9, waiting for transfers between devices: 9.5 us -> 6.28 us  [over(): return lax.ppermute(value, 'row', [(i, i ^ flip) for i in range(n_row)])]
    pallas_call x9, Pallas kernels: 8.26 us -> 10.7 us  [the longest x7 8.08 us: finish(): pl.pallas_call(functools.partial(finish_kernel, columns), out_shape=shape...]
    ppermute x7 -> x9, starting transfers between devices: 4.03 us -> 5.54 us  [over(): return lax.ppermute(value, 'row', [(i, i ^ flip) for i in range(n_row)])]
    ppermute x7 -> x8, starting transfers between devices: 9.64 us -> 9.47 us  [over(): return lax.ppermute(value, 'col', [(0, 1), (1, 0)])]
  transfers between devices with their start and end apart: 14 -> 17, of which waited for: 8 -> 8; matrix products, arithmetic and copies ran while one was open for 0% -> 0% of each run, Pallas kernels for 58% -> 56%
where the time goes in v4:
time: 105 us; the launch traced here: 104 us
  Pallas kernels  60.4 us (58%)
  waiting for transfers between devices  28 us (27%)
  starting transfers between devices  15 us (14%)
    ppermute x8, waiting for transfers between devices, over(): return lax.ppermute(value, 'col', [(0, 1), (1, 0)])  21.8 us
    pallas_call x2, Pallas kernels, update(): pl.pallas_call(update_kernel, out_shape=(jax.ShapeDtypeStruct(out_shape,...  14.8 us
    ppermute x8, starting transfers between devices, over(): return lax.ppermute(value, 'col', [(0, 1), (1, 0)])  9.47 us
    pallas_call x2, Pallas kernels, left_grams(): pl.pallas_call(left_gram_kernel, out_shape=jax.ShapeDtypeStruct((tall, bl...  9.43 us
    pallas_call x7, Pallas kernels, finish(): pl.pallas_call(functools.partial(finish_kernel, columns), out_shape=shape...  8.08 us
    pallas_call x4, Pallas kernels, right_apply(): pl.pallas_call(functools.partial(right_apply_kernel, width, under is not...  7.85 us
    pallas_call x2, Pallas kernels, right_grams(): pl.pallas_call(right_gram_kernel, out_shape=(jax.ShapeDtypeStruct((tall,...  7.81 us
    ppermute x9, waiting for transfers between devices, over(): return lax.ppermute(value, 'row', [(i, i ^ flip) for i in range(n_row)])  6.28 us
  transfers between devices with their start and end apart: 17, of which 8 were waited for; matrix products, arithmetic and copies ran while one was open for 0% of the time, Pallas kernels for 56%

profile of v4, /device:TPU:0, one launch (start us, length us, event | category | flops | bytes accessed | tf_op | source)
XLA Modules:
  0.0 104.0 jit_solution(4501455143881517386)
XLA Ops:
  1.2 3.0 %collective-permute-start.3 = (f32[512,512]{1,0:T(8,128)S(1)}, f32[512,512]{1,0:T(8,128)S(1)}, u32[]{:S(2)}, u32[]{:S(2)}) collective-permute-start(f32[512,512]{1,0:T(8,128)S(1)} %take.1.after_ref), channel_id=1, source_target_pairs={{0,4},{4,0},{1,5},{5,1},{2,6},{6,2},{3,7},{7,3},{8,12},{12,8},{9,1... | collective-permute-start | bytes 3145736 | tf_op jit(solution)/shard_map/ppermute | solution.py:632
  4.3 3.9 %right_grams.2 = (f32[264,256]{1,0:T(8,128)S(1)}, f32[264,256]{1,0:T(8,128)S(1)}) custom-call(s32[2]{0:T(128)S(1)} %pad_add_fusion.place, f32[1024,2048]{1,0:T(8,128)} %bitcast.9, f32[512,512]{1,0:T(8,128)S(1)} %take.1.after_ref), custom_call_target="tpu_custom_call" | custom-call | flops 1 | bytes 1 | tf_op jit(solution)/shard_map/right_grams/pallas_call | solution.py:133
  8.3 4.0 %right_grams.3 = (f32[264,256]{1,0:T(8,128)S(1)}, f32[264,256]{1,0:T(8,128)S(1)}) custom-call(s32[2]{0:T(128)S(1)} %pad_add_fusion.place, f32[1024,2048]{1,0:T(8,128)} %bitcast.10, f32[264,256]{1,0:T(8,128)S(1)} %get-tuple-element.19.after_ref.a_ref), custom_call_target="tpu_custom_call" | custom-call | flops 1 | bytes 1 | tf_op jit(solution)/shard_map/right_grams/pallas_call | solution.py:133
  12.9 1.6 %collective-permute-start.2 = (f32[264,256]{1,0:T(8,128)S(1)}, f32[264,256]{1,0:T(8,128)S(1)}, u32[]{:S(2)}, u32[]{:S(2)}) collective-permute-start(f32[264,256]{1,0:T(8,128)S(1)} %fold.1), channel_id=1, source_target_pairs={{0,16},{8,24},{16,0},{24,8},{1,17},{9,25},{17,1},{25,9},{2,18},{10... | collective-permute-start | bytes 811016 | tf_op jit(solution)/shard_map/ppermute | solution.py:634
  14.4 4.7 %left_grams.2.under_ref = f32[264,256]{1,0:T(8,128)S(1)} custom-call(s32[2]{0:T(128)S(1)} %pad_add_fusion.place, f32[1024,2048]{1,0:T(8,128)} %bitcast.11, f32[264,256]{1,0:T(8,128)S(1)} %get-tuple-element.21.after_ref), custom_call_target="tpu_custom_call" | custom-call | flops 1 | bytes 1 | tf_op jit(solution)/shard_map/left_grams/pallas_call | solution.py:182
  19.1 2.2 %collective-permute-done.2.c_ref = f32[264,256]{1,0:T(8,128)S(1)} collective-permute-done((f32[264,256]{1,0:T(8,128)S(1)}, f32[264,256]{1,0:T(8,128)S(1)}, u32[]{:S(2)}, u32[]{:S(2)}) %collective-permute-start.2) | collective-permute-done | bytes 270368 | tf_op jit(solution)/shard_map/ppermute | solution.py:634
  21.3 4.8 %right_roots.1 = (f32[264,256]{1,0:T(8,128)S(1)}, f32[776,256]{1,0:T(8,128)S(1)}) custom-call(s32[2]{0:T(128)S(1)} %pad_add_fusion.place, f32[2048,256]{1,0:T(8,128)S(1)} %bitcast.6, f32[264,256]{1,0:T(8,128)S(1)} %get-tuple-element.20.a_ref, f32[264,256]{1,0:T(8,128)S(1)} %collective-permute-done.b_ref, f32[264,256]{1,0:T(8,128)S(1)} %collective-permute-done.2.c_ref, ...), custom_call_target="tpu_custom_call" | custom-call | flops 1 | bytes 1 | tf_op jit(solution)/shard_map/right_roots/pallas_call | solution.py:328
  27.4 1.8 %collective-permute-start.5 = (f32[264,256]{1,0:T(8,128)S(1)}, f32[264,256]{1,0:T(8,128)S(1)}, u32[]{:S(2)}, u32[]{:S(2)}) collective-permute-start(f32[264,256]{1,0:T(8,128)S(1)} %hold.2.after_ref.own_ref), channel_id=1, source_target_pairs={{0,16},{8,24},{16,0},{24,8},{1,17},{9,25},{17,1},{25,9},{2,18},{10... | collective-permute-start | bytes 811016 | tf_op jit(solution)/shard_map/ppermute | solution.py:634
  29.2 4.7 %left_grams.3.rest_0_.a_ref = f32[264,256]{1,0:T(8,128)S(1)} custom-call(s32[2]{0:T(128)S(1)} %pad_add_fusion.place, f32[1024,2048]{1,0:T(8,128)} %bitcast.13, f32[264,256]{1,0:T(8,128)S(1)} %hold.2.after_ref.own_ref), custom_call_target="tpu_custom_call" | custom-call | flops 1 | bytes 1 | tf_op jit(solution)/shard_map/left_grams/pallas_call | solution.py:182
  35.3 2.1 %core_apply.1 = f32[512,256]{1,0:T(8,128)S(1)} custom-call(s32[2]{0:T(128)S(1)} %pad_add_fusion.place, f32[1024,2048]{1,0:T(8,128)} %bitcast.14, f32[264,256]{1,0:T(8,128)S(1)} %collective-permute-done.4.c_ref.packed_ref), custom_call_target="tpu_custom_call" | custom-call | flops 1 | bytes 1 | tf_op jit(solution)/shard_map/core_apply/pallas_call | solution.py:466
  39.4 7.5 %collective-permute-done.8.b_ref.rest_1_.half_ref = f32[776,256]{1,0:T(8,128)S(1)} collective-permute-done((f32[776,256]{1,0:T(8,128)S(1)}, f32[776,256]{1,0:T(8,128)S(1)}, u32[]{:S(2)}, u32[]{:S(2)}) %collective-permute-start.8) | collective-permute-done | bytes 794656 | tf_op jit(solution)/shard_map/ppermute | solution.py:632
  46.9 2.0 %right_apply.5 = f32[584,256]{1,0:T(8,128)S(1)} custom-call(s32[2]{0:T(128)S(1)} %pad_add_fusion.place, f32[1024,2048]{1,0:T(8,128)} %bitcast.15, bf16[8,2,256,256]{3,2,1,0:T(8,128)(2,1)S(1)} %get-tuple-element.25.right_ref, f32[72,256]{1,0:T(8,128)S(1)} %get-tuple-element.26.rest_0_, f32[776,256]{1,0:T(8,128)S(1)} %collective-permute-done.8.b_ref.rest_1_.half_ref), custom_call_target="tpu_custom_call" | custom-call | flops 1 | bytes 1 | tf_op jit(solution)/shard_map/right_apply/pallas_call | solution.py:516
  49.2 3.5 %left_roots.1.rest_1_.left_ref = bf16[2,2,256,256]{3,2,1,0:T(8,128)(2,1)S(1)} custom-call(s32[2]{0:T(128)S(1)} %pad_add_fusion.place, f32[1024,256]{1,0:T(8,128)S(1)} %bitcast.7, f32[264,256]{1,0:T(8,128)S(1)} %left_grams.3.rest_0_.a_ref, f32[776,256]{1,0:T(8,128)S(1)} %collective-permute-done.8.b_ref.rest_1_.half_ref), custom_call_target="tpu_custom_call" | custom-call | flops 1 | bytes 1 | tf_op jit(solution)/shard_map/left_roots/pallas_call | solution.py:368
  52.7 5.4 %collective-permute-done.7.rest_0_.half_ref = f32[512,256]{1,0:T(8,128)S(1)} collective-permute-done((f32[512,256]{1,0:T(8,128)S(1)}, f32[512,256]{1,0:T(8,128)S(1)}, u32[]{:S(2)}, u32[]{:S(2)}) %collective-permute-start.7) | collective-permute-done | bytes 524320 | tf_op jit(solution)/shard_map/ppermute | solution.py:632
  58.1 2.0 %right_apply.4 = f32[512,256]{1,0:T(8,128)S(1)} custom-call(s32[2]{0:T(128)S(1)} %pad_add_fusion.place, f32[1024,2048]{1,0:T(8,128)} %bitcast.16, bf16[8,2,256,256]{3,2,1,0:T(8,128)(2,1)S(1)} %get-tuple-element.25.right_ref, f32[512,256]{1,0:T(8,128)S(1)} %collective-permute-done.7.rest_0_.half_ref, bf16[2,2,256,256]{3,2,1,0:T(8,128)(2,1)S(1)} %left_roots.1.rest_1_.left_ref), custom_call_target="tpu_custom_call" | custom-call | flops 1 | bytes 1 | tf_op jit(solution)/shard_map/right_apply/pallas_call | solution.py:516
  60.4 11.3 %update.2 = (f32[512,4096]{1,0:T(8,128)}, f32[8,128]{1,0:T(8,128)S(1)}) custom-call(s32[2]{0:T(128)S(1)} %pad_add_fusion.place, f32[1024,2048]{1,0:T(8,128)} %bitcast.17, bf16[2,2,256,256]{3,2,1,0:T(8,128)(2,1)S(1)} %left_roots.1.rest_1_.left_ref, bf16[8,2,256,256]{3,2,1,0:T(8,128)(2,1)S(1)} %get-tuple-element.25.right_ref), custom_call_target="tpu_custom_call" | custom-call | flops 1 | bytes 1 | tf_op jit(solution)/shard_map/update/pallas_call | solution.py:601
  71.7 2.0 %right_apply.7 = f32[512,256]{1,0:T(8,128)S(1)} custom-call(s32[2]{0:T(128)S(1)} %pad_add_fusion.place, f32[1024,2048]{1,0:T(8,128)} %bitcast.18, bf16[8,2,256,256]{3,2,1,0:T(8,128)(2,1)S(1)} %get-tuple-element.25.right_ref, f32[584,256]{1,0:T(8,128)S(1)} %collective-permute-done.10.a_ref.rest_0_.half_ref, f32[8,128]{1,0:T(8,128)S(1)} %get-tuple-element.31.rest_1_), custom_call_target="tpu_custom_call" | custom-call | flops 1 | bytes 1 | tf_op jit(solution)/shard_map/right_apply/pallas_call | solution.py:516
  73.7 1.8 %collective-permute-start.16 = (f32[512,256]{1,0:T(8,128)S(1)}, f32[512,256]{1,0:T(8,128)S(1)}, u32[]{:S(2)}, u32[]{:S(2)}) collective-permute-start(f32[512,256]{1,0:T(8,128)S(1)} %right_apply.7), channel_id=1, source_target_pairs={{0,4},{4,0},{1,5},{5,1},{2,6},{6,2},{3,7},{7,3},{8,12},{12,8},{9,1... | collective-permute-start | bytes 1572872 | tf_op jit(solution)/shard_map/ppermute | solution.py:632
  77.0 2.9 %collective-permute-done.12.x_ref = f32[72,256]{1,0:T(8,128)S(1)} collective-permute-done((f32[72,256]{1,0:T(8,128)S(1)}, f32[72,256]{1,0:T(8,128)S(1)}, u32[]{:S(2)}, u32[]{:S(2)}) %collective-permute-start.12) | collective-permute-done | bytes 73760 | tf_op jit(solution)/shard_map/ppermute | solution.py:634
  82.5 3.5 %update.3 = (f32[512,4096]{1,0:T(8,128)}, f32[8,128]{1,0:T(8,128)S(1)}) custom-call(s32[2]{0:T(128)S(1)} %pad_add_fusion.place, f32[512,512]{1,0:T(8,128)S(1)} %collective-permute-done.3.rest_0_.g_ref, bf16[2,2,256,256]{3,2,1,0:T(8,128)(2,1)S(1)} %left_roots.1.rest_1_.left_ref, ...), custom_call_target="tpu_custom_call", output_to_operand_aliasing={{0}: (4, {})} | custom-call | flops 1 | bytes 1 | tf_op jit(solution)/shard_map/update/pallas_call | solution.py:601
  86.0 2.0 %right_apply.6 = (f32[512,128]{1,0:T(8,128)S(1)}, f32[512,128]{1,0:T(8,128)S(1)}) custom-call(s32[2]{0:T(128)S(1)} %pad_add_fusion.place, f32[1024,2048]{1,0:T(8,128)} %bitcast.19, bf16[8,2,256,256]{3,2,1,0:T(8,128)(2,1)S(1)} %get-tuple-element.25.right_ref, f32[512,256]{1,0:T(8,128)S(1)} %collective-permute-done.9.rest_0_.half_ref, ...), custom_call_target="tpu_custom_call" | custom-call | flops 1 | bytes 1 | tf_op jit(solution)/shard_map/right_apply/pallas_call | solution.py:516
  88.3 1.7 %collective-permute-start.14 = (f32[512,128]{1,0:T(8,128)S(1)}, f32[512,128]{1,0:T(8,128)S(1)}, u32[]{:S(2)}, u32[]{:S(2)}) collective-permute-start(f32[512,128]{1,0:T(8,128)S(1)} %get-tuple-element.29), channel_id=1, source_target_pairs={{0,4},{4,0},{1,5},{5,1},{2,6},{6,2},{3,7},{7,3},{8,12},{12,8},{9,1... | collective-permute-start | bytes 786440 | tf_op jit(solution)/shard_map/ppermute | solution.py:632
  93.7 3.7 %collective-permute-done.15.half_ref = f32[512,128]{1,0:T(8,128)S(1)} collective-permute-done((f32[512,128]{1,0:T(8,128)S(1)}, f32[512,128]{1,0:T(8,128)S(1)}, u32[]{:S(2)}, u32[]{:S(2)}) %collective-permute-start.15) | collective-permute-done | bytes 262176 | tf_op jit(solution)/shard_map/ppermute | solution.py:632
  98.5 4.3 %collective-permute-done.14.half_ref = f32[512,128]{1,0:T(8,128)S(1)} collective-permute-done((f32[512,128]{1,0:T(8,128)S(1)}, f32[512,128]{1,0:T(8,128)S(1)}, u32[]{:S(2)}, u32[]{:S(2)}) %collective-permute-start.14) | collective-permute-done | bytes 262176 | tf_op jit(solution)/shard_map/ppermute | solution.py:632
  (42 shorter events, 17.5 us)
Async XLA Ops:
  1.2 26.2 %collective-permute-start.3 = (f32[512,512]{1,0:T(8,128)S(1)}, f32[512,512]{1,0:T(8,128)S(1)}, u32[]{:S(2)}, u32[]{:S(2)}) collective-permute-start(f32[512,512]{1,0:T(8,128)S(1)} %take.1.after_ref), channel_id=1, source_target_pairs={{0,4},{4,0},{1,5},{5,1},{2,6},{6,2},{3,7},{7,3},{8,12},{12,8},{9,1... | collective-permute-start | bytes 3145736 | tf_op jit(solution)/shard_map/ppermute | solution.py:632
  8.2 4.6 %collective-permute-start.1 = (f32[264,256]{1,0:T(8,128)S(1)}, f32[264,256]{1,0:T(8,128)S(1)}, u32[]{:S(2)}, u32[]{:S(2)}) collective-permute-start(f32[264,256]{1,0:T(8,128)S(1)} %get-tuple-element.22), channel_id=1, source_target_pairs={{0,8},{8,0},{16,24},{24,16},{1,9},{9,1},{17,25},{25,17},{2,10},{10... | collective-permute-start | bytes 811016 | tf_op jit(solution)/shard_map/ppermute | solution.py:634
  8.3 13.0 %copy-start = (f32[1,2048,256]{2,1,0:T(8,128)S(1)}, f32[1,2048,256]{2,1,0:T(8,128)}, u32[]{:S(2)}) copy-start(f32[1,2048,256]{2,1,0:T(8,128)} %param.5) | copy-start | bytes 6291460
  12.3 6.9 %collective-permute-start = (f32[264,256]{1,0:T(8,128)S(1)}, f32[264,256]{1,0:T(8,128)S(1)}, u32[]{:S(2)}, u32[]{:S(2)}) collective-permute-start(f32[264,256]{1,0:T(8,128)S(1)} %get-tuple-element.21.after_ref), channel_id=1, source_target_pairs={{0,8},{8,0},{16,24},{24,16},{1,9},{9,1},{17,25},{25,17},{2,10},{10... | collective-permute-start | bytes 811016 | tf_op jit(solution)/shard_map/ppermute | solution.py:634
  12.9 8.5 %collective-permute-start.2 = (f32[264,256]{1,0:T(8,128)S(1)}, f32[264,256]{1,0:T(8,128)S(1)}, u32[]{:S(2)}, u32[]{:S(2)}) collective-permute-start(f32[264,256]{1,0:T(8,128)S(1)} %fold.1), channel_id=1, source_target_pairs={{0,16},{8,24},{16,0},{24,8},{1,17},{9,25},{17,1},{25,9},{2,18},{10... | collective-permute-start | bytes 811016 | tf_op jit(solution)/shard_map/ppermute | solution.py:634
  26.1 20.7 %collective-permute-start.8 = (f32[776,256]{1,0:T(8,128)S(1)}, f32[776,256]{1,0:T(8,128)S(1)}, u32[]{:S(2)}, u32[]{:S(2)}) collective-permute-start(f32[776,256]{1,0:T(8,128)S(1)} %get-tuple-element.24.rest_1_), channel_id=1, source_target_pairs={{0,4},{4,0},{1,5},{5,1},{2,6},{6,2},{3,7},{7,3},{8,12},{12,8},{9,1... | collective-permute-start | bytes 2383880 | tf_op jit(solution)/shard_map/ppermute | solution.py:632
  27.4 7.7 %collective-permute-start.5 = (f32[264,256]{1,0:T(8,128)S(1)}, f32[264,256]{1,0:T(8,128)S(1)}, u32[]{:S(2)}, u32[]{:S(2)}) collective-permute-start(f32[264,256]{1,0:T(8,128)S(1)} %hold.2.after_ref.own_ref), channel_id=1, source_target_pairs={{0,16},{8,24},{16,0},{24,8},{1,17},{9,25},{17,1},{25,9},{2,18},{10... | collective-permute-start | bytes 811016 | tf_op jit(solution)/shard_map/ppermute | solution.py:634
  29.2 6.1 %collective-permute-start.4 = (f32[264,256]{1,0:T(8,128)S(1)}, f32[264,256]{1,0:T(8,128)S(1)}, u32[]{:S(2)}, u32[]{:S(2)}) collective-permute-start(f32[264,256]{1,0:T(8,128)S(1)} %hold.2.after_ref.own_ref), channel_id=1, source_target_pairs={{0,8},{8,0},{16,24},{24,16},{1,9},{9,1},{17,25},{25,17},{2,10},{10... | collective-permute-start | bytes 811016 | tf_op jit(solution)/shard_map/ppermute | solution.py:634
  35.2 3.7 %collective-permute-start.6 = (f32[264,256]{1,0:T(8,128)S(1)}, f32[264,256]{1,0:T(8,128)S(1)}, u32[]{:S(2)}, u32[]{:S(2)}) collective-permute-start(f32[264,256]{1,0:T(8,128)S(1)} %hold.3.x_ref), channel_id=1, source_target_pairs={{0,8},{8,0},{16,24},{24,16},{1,9},{9,1},{17,25},{25,17},{2,10},{10... | collective-permute-start | bytes 811016 | tf_op jit(solution)/shard_map/ppermute | solution.py:634
  37.4 11.8 %copy-start.1 = (f32[1,1024,256]{2,1,0:T(8,128)S(1)}, f32[1,1024,256]{2,1,0:T(8,128)}, u32[]{:S(2)}) copy-start(f32[1,1024,256]{2,1,0:T(8,128)} %param.4) | copy-start | bytes 3145732
  37.4 20.7 %collective-permute-start.7 = (f32[512,256]{1,0:T(8,128)S(1)}, f32[512,256]{1,0:T(8,128)S(1)}, u32[]{:S(2)}, u32[]{:S(2)}) collective-permute-start(f32[512,256]{1,0:T(8,128)S(1)} %core_apply.1), channel_id=1, source_target_pairs={{0,4},{4,0},{1,5},{5,1},{2,6},{6,2},{3,7},{7,3},{8,12},{12,8},{9,1... | collective-permute-start | bytes 1572872 | tf_op jit(solution)/shard_map/ppermute | solution.py:632
  48.8 22.9 %collective-permute-start.10 = (f32[584,256]{1,0:T(8,128)S(1)}, f32[584,256]{1,0:T(8,128)S(1)}, u32[]{:S(2)}, u32[]{:S(2)}) collective-permute-start(f32[584,256]{1,0:T(8,128)S(1)} %right_apply.5), channel_id=1, source_target_pairs={{0,4},{4,0},{1,5},{5,1},{2,6},{6,2},{3,7},{7,3},{8,12},{12,8},{9,1... | collective-permute-start | bytes 1794056 | tf_op jit(solution)/shard_map/ppermute | solution.py:632
  60.1 26.0 %collective-permute-start.9 = (f32[512,256]{1,0:T(8,128)S(1)}, f32[512,256]{1,0:T(8,128)S(1)}, u32[]{:S(2)}, u32[]{:S(2)}) collective-permute-start(f32[512,256]{1,0:T(8,128)S(1)} %right_apply.4), channel_id=1, source_target_pairs={{0,4},{4,0},{1,5},{5,1},{2,6},{6,2},{3,7},{7,3},{8,12},{12,8},{9,1... | collective-permute-start | bytes 1572872 | tf_op jit(solution)/shard_map/ppermute | solution.py:632
  73.7 18.8 %collective-permute-start.16 = (f32[512,256]{1,0:T(8,128)S(1)}, f32[512,256]{1,0:T(8,128)S(1)}, u32[]{:S(2)}, u32[]{:S(2)}) collective-permute-start(f32[512,256]{1,0:T(8,128)S(1)} %right_apply.7), channel_id=1, source_target_pairs={{0,4},{4,0},{1,5},{5,1},{2,6},{6,2},{3,7},{7,3},{8,12},{12,8},{9,1... | collective-permute-start | bytes 1572872 | tf_op jit(solution)/shard_map/ppermute | solution.py:632
  75.5 4.4 %collective-permute-start.12 = (f32[72,256]{1,0:T(8,128)S(1)}, f32[72,256]{1,0:T(8,128)S(1)}, u32[]{:S(2)}, u32[]{:S(2)}) collective-permute-start(f32[72,256]{1,0:T(8,128)S(1)} %rest_of.1.own_ref), channel_id=1, source_target_pairs={{0,16},{8,24},{16,0},{24,8},{1,17},{9,25},{17,1},{25,9},{2,18},{10... | collective-permute-start | bytes 221192 | tf_op jit(solution)/shard_map/ppermute | solution.py:634
  77.0 5.3 %collective-permute-start.11 = (f32[72,256]{1,0:T(8,128)S(1)}, f32[72,256]{1,0:T(8,128)S(1)}, u32[]{:S(2)}, u32[]{:S(2)}) collective-permute-start(f32[72,256]{1,0:T(8,128)S(1)} %rest_of.1.own_ref), channel_id=1, source_target_pairs={{0,8},{8,0},{16,24},{24,16},{1,9},{9,1},{17,25},{25,17},{2,10},{10... | collective-permute-start | bytes 221192 | tf_op jit(solution)/shard_map/ppermute | solution.py:634
  79.9 2.4 %collective-permute-start.13 = (f32[72,256]{1,0:T(8,128)S(1)}, f32[72,256]{1,0:T(8,128)S(1)}, u32[]{:S(2)}, u32[]{:S(2)}) collective-permute-start(f32[72,256]{1,0:T(8,128)S(1)} %collective-permute-done.12.x_ref), channel_id=1, source_target_pairs={{0,8},{8,0},{16,24},{24,16},{1,9},{9,1},{17,25},{25,17},{2,10},{10... | collective-permute-start | bytes 221192 | tf_op jit(solution)/shard_map/ppermute | solution.py:634
  88.0 9.5 %collective-permute-start.15 = (f32[512,128]{1,0:T(8,128)S(1)}, f32[512,128]{1,0:T(8,128)S(1)}, u32[]{:S(2)}, u32[]{:S(2)}) collective-permute-start(f32[512,128]{1,0:T(8,128)S(1)} %get-tuple-element.30), channel_id=1, source_target_pairs={{0,4},{4,0},{1,5},{5,1},{2,6},{6,2},{3,7},{7,3},{8,12},{12,8},{9,1... | collective-permute-start | bytes 786440 | tf_op jit(solution)/shard_map/ppermute | solution.py:632
  88.3 14.4 %collective-permute-start.14 = (f32[512,128]{1,0:T(8,128)S(1)}, f32[512,128]{1,0:T(8,128)S(1)}, u32[]{:S(2)}, u32[]{:S(2)}) collective-permute-start(f32[512,128]{1,0:T(8,128)S(1)} %get-tuple-element.29), channel_id=1, source_target_pairs={{0,4},{4,0},{1,5},{5,1},{2,6},{6,2},{3,7},{7,3},{8,12},{12,8},{9,1... | collective-permute-start | bytes 786440 | tf_op jit(solution)/shard_map/ppermute | solution.py:632

commit v5 on v4

--- a/solution.py
+++ b/solution.py
@@ -66,6 +66,14 @@
     return lax.all_to_all(full, "col", split_axis=1, concat_axis=2, tiled=True)
 
 
+def here():
+    return lax.axis_index("row"), lax.axis_index("col")
+
+
+def placed(index_map):
+    return lambda s: index_map(s, here())
+
+
 def split(value):
     high = value.astype(jnp.bfloat16)
     low = (value - high.astype(jnp.float32)).astype(jnp.bfloat16)
@@ -105,7 +113,7 @@
     return first, second
 
 
-def right_gram_kernel(place, g_ref, after_ref, *out_refs):
+def right_gram_kernel(g_ref, after_ref, *out_refs):
     step = pl.program_id(0)
     blk = g_ref.shape[1] // 2
     high, low = split(g_ref[...])
@@ -126,7 +134,7 @@
             ref[blk:, :] = diag
 
 
-def right_grams(place, tile, blk, flips, after):
+def right_grams(tile, blk, flips, after):
     rows = tile.shape[0]
     tall = blk + PAD
     flip = lambda s: jnp.where(s == 0, flips[0], flips[1])
@@ -134,21 +142,21 @@
         right_gram_kernel,
         out_shape=(jax.ShapeDtypeStruct((tall, blk), jnp.float32),) * 2,
         grid_spec=pltpu.PrefetchScalarGridSpec(
-            num_scalar_prefetch=1,
+            num_scalar_prefetch=0,
             grid=(2,),
             in_specs=[
-                pl.BlockSpec((rows, 2 * blk), lambda s, place: (0, place[0] ^ flip(s))),
+                pl.BlockSpec((rows, 2 * blk), placed(lambda s, place: (0, place[0] ^ flip(s)))),
                 pl.BlockSpec(memory_space=pl.ANY),
             ],
-            out_specs=(pl.BlockSpec((tall, blk), lambda s, place: (0, 0)),) * 2,
+            out_specs=(pl.BlockSpec((tall, blk), lambda s: (0, 0)),) * 2,
         ),
         compiler_params=pltpu.CompilerParams(vmem_limit_bytes=VMEM_LIMIT),
         cost_estimate=SMALL,
         name="right_grams",
-    )(place, tile, after)
-
-
-def left_gram_kernel(place, g_ref, after_ref, out_ref, lhh, lcross):
+    )(tile, after)
+
+
+def left_gram_kernel(g_ref, after_ref, out_ref, lhh, lcross):
     step = pl.program_id(0)
     last = pl.num_programs(0) - 1
     blk = lhh.shape[-1]
@@ -176,20 +184,20 @@
         out_ref[blk:, :] = diag
 
 
-def left_grams(place, tile, blk, at, after):
+def left_grams(tile, blk, at, after):
     width = tile.shape[1]
     tall = blk + PAD
     return pl.pallas_call(
         left_gram_kernel,
         out_shape=jax.ShapeDtypeStruct((tall, blk), jnp.float32),
         grid_spec=pltpu.PrefetchScalarGridSpec(
-            num_scalar_prefetch=1,
+            num_scalar_prefetch=0,
             grid=(width // (4 * blk),),
             in_specs=[
-                pl.BlockSpec((2 * blk, 4 * blk), lambda s, place: (at(place), s)),
+                pl.BlockSpec((2 * blk, 4 * blk), placed(lambda s, place: (at(place), s))),
                 pl.BlockSpec(memory_space=pl.ANY),
             ],
-            out_specs=pl.BlockSpec((tall, blk), lambda s, place: (0, 0)),
+            out_specs=pl.BlockSpec((tall, blk), lambda s: (0, 0)),
             scratch_shapes=[
                 pltpu.VMEM((2, blk, blk), jnp.float32),
                 pltpu.VMEM((2, blk, blk), jnp.float32),
@@ -198,14 +206,10 @@
         compiler_params=pltpu.CompilerParams(vmem_limit_bytes=VMEM_LIMIT),
         cost_estimate=SMALL,
         name="left_grams",
-    )(place, tile, after)
+    )(tile, after)
 
 
 RAW = (1, 3)
-
-
-def here():
-    return lax.axis_index("row"), lax.axis_index("col")
 
 
 def own_first(place):
@@ -308,52 +312,49 @@
     return [r * jnp.exp(-0.25 * jnp.log(s)) for r, s in zip(result, scales)]
 
 
-def right_kernel(full_dim, place, stats_ref, a_ref, b_ref, c_ref, g_ref, under_ref, out_ref, half_ref):
+def right_kernel(full_dim, stats_ref, a_ref, b_ref, c_ref, g_ref, out_ref, half_ref):
     blk = stats_ref.shape[1]
-    rows = g_ref.shape[0]
     total = a_ref[...] + b_ref[...] + c_ref[...]
     roots = pair_roots(full_dim, stats_ref, total[:blk], total[blk : blk + 1])
-    half_ref[:rows, :] = product(split(g_ref[...]), split(roots[0]))
-    half_ref[rows:, :] = under_ref[...]
+    half_ref[...] = product(split(g_ref[...]), split(roots[0]))
     body, diag = pack(*roots)
     out_ref[:blk, :] = body
     out_ref[blk:, :] = diag
 
 
-def right_roots(full_dim, place, stats, kept, near, far, tile, under):
+def right_roots(full_dim, stats, kept, near, far, tile):
     blk = stats.shape[1]
     tall = blk + PAD
     rows = tile.shape[0] // 2
-    flat = pl.BlockSpec((tall, blk), lambda s, place: (0, 0))
+    flat = pl.BlockSpec((tall, blk), lambda s: (0, 0))
     return pl.pallas_call(
         functools.partial(right_kernel, full_dim),
         out_shape=(
             jax.ShapeDtypeStruct((tall, blk), jnp.float32),
-            jax.ShapeDtypeStruct((rows + tall, blk), jnp.float32),
+            jax.ShapeDtypeStruct((rows, blk), jnp.float32),
         ),
         grid_spec=pltpu.PrefetchScalarGridSpec(
-            num_scalar_prefetch=1,
+            num_scalar_prefetch=0,
             grid=(1,),
             in_specs=[
-                pl.BlockSpec((2 * blk, blk), lambda s, place: (place[0], 0)),
+                pl.BlockSpec((2 * blk, blk), placed(lambda s, place: (place[0], 0))),
                 flat,
                 flat,
                 flat,
-                pl.BlockSpec((rows, blk), lambda s, place: (1 - place[1], own_first(place))),
-                flat,
+                pl.BlockSpec((rows, blk), placed(lambda s, place: (1 - place[1], own_first(place)))),
             ],
             out_specs=(
                 flat,
-                pl.BlockSpec((rows + tall, blk), lambda s, place: (0, 0)),
+                pl.BlockSpec((rows, blk), lambda s: (0, 0)),
             ),
         ),
         compiler_params=pltpu.CompilerParams(vmem_limit_bytes=VMEM_LIMIT),
         cost_estimate=SMALL,
         name="right_roots",
-    )(place, stats, kept, near, far, tile, under)
-
-
-def left_kernel(full_dim, place, stats_ref, a_ref, b_ref, out_ref):
+    )(stats, kept, near, far, tile)
+
+
+def left_kernel(full_dim, stats_ref, a_ref, b_ref, out_ref):
     blk = stats_ref.shape[1]
     total = a_ref[...] + b_ref[b_ref.shape[0] - a_ref.shape[0] :, :]
     for b, root in enumerate(pair_roots(full_dim, stats_ref, total[:blk], total[blk : blk + 1])):
@@ -362,26 +363,26 @@
         out_ref[b, 1] = low
 
 
-def left_roots(full_dim, place, stats, kept, came):
+def left_roots(full_dim, stats, kept, came):
     blk = stats.shape[1]
     tall = blk + PAD
     return pl.pallas_call(
         functools.partial(left_kernel, full_dim),
         out_shape=jax.ShapeDtypeStruct((2, 2, blk, blk), jnp.bfloat16),
         grid_spec=pltpu.PrefetchScalarGridSpec(
-            num_scalar_prefetch=1,
+            num_scalar_prefetch=0,
             grid=(1,),
             in_specs=[
-                pl.BlockSpec((2 * blk, blk), lambda s, place: (place[1], 0)),
-                pl.BlockSpec((tall, blk), lambda s, place: (0, 0)),
-                pl.BlockSpec(came.shape, lambda s, place: (0, 0)),
+                pl.BlockSpec((2 * blk, blk), placed(lambda s, place: (place[1], 0))),
+                pl.BlockSpec((tall, blk), lambda s: (0, 0)),
+                pl.BlockSpec(came.shape, lambda s: (0, 0)),
             ],
-            out_specs=pl.BlockSpec((2, 2, blk, blk), lambda s, place: (0, 0, 0, 0)),
+            out_specs=pl.BlockSpec((2, 2, blk, blk), lambda s: (0, 0, 0, 0)),
         ),
         compiler_params=pltpu.CompilerParams(vmem_limit_bytes=VMEM_LIMIT),
         cost_estimate=SMALL,
         name="left_roots",
-    )(place, stats, kept, came)
+    )(stats, kept, came)
 
 
 def put_roots(out_ref, at, roots):
@@ -454,34 +455,36 @@
     )(*parts)
 
 
-def core_apply_kernel(place, g_ref, packed_ref, out_ref):
-    blk = g_ref.shape[1]
+def core_apply_kernel(g_ref, packed_ref, under_ref, out_ref):
+    rows, blk = g_ref.shape
     root = unpack(packed_ref[:blk, :], packed_ref[blk : blk + 1, :])[0]
-    out_ref[...] = product(split(g_ref[...]), split(root))
-
-
-def core_apply(place, tile, packed):
+    out_ref[:rows, :] = product(split(g_ref[...]), split(root))
+    out_ref[rows:, :] = under_ref[...]
+
+
+def core_apply(tile, packed, under):
     rows = tile.shape[0] // 2
     tall, blk = packed.shape
     return pl.pallas_call(
         core_apply_kernel,
-        out_shape=jax.ShapeDtypeStruct((rows, blk), jnp.float32),
+        out_shape=jax.ShapeDtypeStruct((rows + tall, blk), jnp.float32),
         grid_spec=pltpu.PrefetchScalarGridSpec(
-            num_scalar_prefetch=1,
+            num_scalar_prefetch=0,
             grid=(1,),
             in_specs=[
-                pl.BlockSpec((rows, blk), lambda s, place: (1 - place[1], core_first(place))),
-                pl.BlockSpec((tall, blk), lambda s, place: (0, 0)),
+                pl.BlockSpec((rows, blk), placed(lambda s, place: (1 - place[1], core_first(place)))),
+                pl.BlockSpec((tall, blk), lambda s: (0, 0)),
+                pl.BlockSpec((tall, blk), lambda s: (0, 0)),
             ],
-            out_specs=pl.BlockSpec((rows, blk), lambda s, place: (0, 0)),
+            out_specs=pl.BlockSpec((rows + tall, blk), lambda s: (0, 0)),
         ),
         compiler_params=pltpu.CompilerParams(vmem_limit_bytes=VMEM_LIMIT),
         cost_estimate=SMALL,
         name="core_apply",
-    )(place, tile, packed)
-
-
-def right_apply_kernel(width, carries, place, g_ref, right_ref, *rest):
+    )(tile, packed, under)
+
+
+def right_apply_kernel(width, carries, g_ref, right_ref, *rest):
     step = pl.program_id(0)
     out_refs = rest[-len(width) :]
     value = product(split(g_ref[...]), (right_ref[0, 0], right_ref[0, 1]))
@@ -500,32 +503,32 @@
         out_refs[0][value.shape[0] :, :] = rest[0][...]
 
 
-def right_apply(place, tile, right, first, width, under, after):
+def right_apply(tile, right, first, width, under, after):
     rows = tile.shape[0] // 2
     blk = right.shape[-1]
     in_specs = [
-        pl.BlockSpec((rows, blk), lambda s, place: (1 - place[1], later(first + s, place))),
-        pl.BlockSpec((1, 2, blk, blk), lambda s, place: (later(first + s, place), 0, 0, 0)),
+        pl.BlockSpec((rows, blk), placed(lambda s, place: (1 - place[1], later(first + s, place)))),
+        pl.BlockSpec((1, 2, blk, blk), placed(lambda s, place: (later(first + s, place), 0, 0, 0))),
     ]
     operands = [tile, right]
     tall = rows
     if under is not None:
         tall += under.shape[0]
-        in_specs.append(pl.BlockSpec(under.shape, lambda s, place: (0, 0)))
+        in_specs.append(pl.BlockSpec(under.shape, lambda s: (0, 0)))
         operands.append(under)
     return pl.pallas_call(
         functools.partial(right_apply_kernel, width, under is not None),
         out_shape=tuple(jax.ShapeDtypeStruct((tall, w), jnp.float32) for w in width),
         grid_spec=pltpu.PrefetchScalarGridSpec(
-            num_scalar_prefetch=1,
+            num_scalar_prefetch=0,
             grid=(sum(width) // blk,),
             in_specs=in_specs + [pl.BlockSpec(memory_space=pl.ANY)] * len(after),
-            out_specs=tuple(pl.BlockSpec((tall, w), lambda s, place: (0, 0)) for w in width),
+            out_specs=tuple(pl.BlockSpec((tall, w), lambda s: (0, 0)) for w in width),
         ),
         compiler_params=pltpu.CompilerParams(vmem_limit_bytes=VMEM_LIMIT),
         cost_estimate=SMALL,
         name="right_apply",
-    )(place, *operands, *after)
+    )(*operands, *after)
 
 
 def left_product(left_ref, value, out_ref):
@@ -535,7 +538,7 @@
         out_ref[i * blk : (i + 1) * blk, :] = product((left_ref[i, 0], left_ref[i, 1]), part)
 
 
-def update_kernel(place, g_ref, left_ref, right_ref, *rest):
+def update_kernel(g_ref, left_ref, right_ref, *rest):
     half = product(split(g_ref[...]), (right_ref[0, 0], right_ref[0, 1]))
     left_product(left_ref, half, rest[-2])
     rest[-1][...] = jnp.zeros_like(rest[-1])
@@ -584,34 +587,35 @@
     )(half, left, out)
 
 
-def update(place, source, left, right, out, out_shape, g_map, out_map):
+def update(source, left, right, out, out_shape, g_map, out_map, after=()):
     rows = out_shape[0]
     blk = left.shape[-1]
     in_specs = [
-        pl.BlockSpec((rows, blk), g_map),
-        pl.BlockSpec((2, 2, blk, blk), lambda s, place: (0, 0, 0, 0)),
-        pl.BlockSpec((1, 2, blk, blk), lambda s, place: (s, 0, 0, 0)),
+        pl.BlockSpec((rows, blk), placed(g_map)),
+        pl.BlockSpec((2, 2, blk, blk), lambda s: (0, 0, 0, 0)),
+        pl.BlockSpec((1, 2, blk, blk), lambda s: (s, 0, 0, 0)),
     ]
     operands = [source, left, right]
     aliases = {}
     if out is not None:
-        aliases = {1 + len(operands): 0}
+        aliases = {len(operands): 0}
         in_specs.append(pl.BlockSpec(memory_space=pl.ANY))
         operands.append(out)
+    in_specs += [pl.BlockSpec(memory_space=pl.ANY)] * len(after)
     return pl.pallas_call(
         update_kernel,
         out_shape=(jax.ShapeDtypeStruct(out_shape, jnp.float32), jax.ShapeDtypeStruct((8, 128), jnp.float32)),
         grid_spec=pltpu.PrefetchScalarGridSpec(
-            num_scalar_prefetch=1,
+            num_scalar_prefetch=0,
             grid=(right.shape[0],),
             in_specs=in_specs,
-            out_specs=(pl.BlockSpec((rows, blk), out_map), pl.BlockSpec((8, 128), lambda s, place: (0, 0))),
+            out_specs=(pl.BlockSpec((rows, blk), placed(out_map)), pl.BlockSpec((8, 128), lambda s: (0, 0))),
         ),
         input_output_aliases=aliases,
         compiler_params=pltpu.CompilerParams(vmem_limit_bytes=VMEM_LIMIT),
         cost_estimate=SMALL,
         name="update",
-    )(place, *operands)
+    )(*operands, *after)
 
 
 def exchange_device(full_dim, n_row, grads, left_stats, right_stats):
@@ -620,9 +624,6 @@
     tile = pltpu.with_memory_space_constraint(grads.reshape(tile_rows, tile_cols), pltpu.HBM)
     lstats = left_stats.reshape(tile_rows, blk)
     rstats = right_stats.reshape(tile_cols, blk)
-    r = lax.axis_index("row")
-    c = lax.axis_index("col")
-    place = jnp.stack([r, c]).astype(jnp.int32)
     rows = tile_rows // 2
     shape = (rows, 2 * tile_cols)
     halves = tile_cols // blk
@@ -636,51 +637,54 @@
     first = take(tile, blk)
     raw = over("y", first)
 
-    send_on, keep_on = right_grams(place, tile, blk, (3, 2), first)
-    near_on = over("core", send_on)
-    send, keep = right_grams(place, tile, blk, (1, 0), keep_on)
+    send_on, keep_on = right_grams(tile, blk, (3, 2), first)
+    far = fold(keep_on, over("core", send_on))
+    send, keep = right_grams(tile, blk, (1, 0), far)
     near = over("core", send)
-    far = over("x", fold(keep_on, near_on))
-    lsend = left_grams(place, tile, blk, lambda place: 1 - place[1], send)
-
-    own, half = right_roots(full_dim, place, rstats, keep, near, far, tile, lsend)
+    far = over("x", far)
+
+    own, half = right_roots(full_dim, rstats, keep, near, far, tile)
     came_a = over("y", half)
-    own = hold(own, raw, half)
+    lsend = left_grams(tile, blk, lambda place: 1 - place[1], half)
+    own = hold(own, raw, lsend)
     own_c = over("core", own)
     own_x = over("x", own)
-    lkeep = left_grams(place, tile, blk, lambda place: place[1], own)
-    came_b = over("y", core_apply(place, tile, own_c))
-    own_x = hold(own_x, lkeep)
+    half = core_apply(tile, own_c, lsend)
+    came_b = over("y", half)
+    own_x = hold(own_x, half, came_a)
+    lkeep = left_grams(tile, blk, lambda place: place[1], half)
     roots, part = spread_roots(own, own_c, own_x, over("core", own_x))
 
-    (half,) = right_apply(place, tile, roots, 0, (blk,), part, (came_a,))
+    (half,) = right_apply(tile, roots, 0, (blk,), part, (lkeep,))
     came_c = over("y", half)
-    left = left_roots(full_dim, place, lstats, lkeep, came_a)
-    (half,) = right_apply(place, tile, roots, 1, (blk,), None, (came_b, left))
+    (half,) = right_apply(tile, roots, 1, (blk,), None, (came_b,))
     came_d = over("y", half)
 
     def crossed(block, start=0):
         return (lambda place: (1 - place[1]) * tile_cols + block(place) * blk + start,)
 
+    left = left_roots(full_dim, lstats, lkeep, came_b)
     out, done = update(
-        place, tile, left, roots, None, shape,
+        tile, left, roots, None, shape,
         lambda s, place: (place[1], s),
         lambda s, place: (0, place[1] * halves + s),
     )
-    (half,) = right_apply(place, tile, roots, 2, (blk,), None, (came_c, done))
+    (half,) = right_apply(tile, roots, 2, (blk,), None, (came_c, done))
     came_e = over("y", half)
+    last = (blk // 2, blk // 2)
+    held = right_apply(tile, roots, 3, last, None, (came_d,))
+    came_last = [over("y", half) for half in held]
     (out,) = finish(came_a, left, out, crossed(own_first))
     (out,) = finish(came_b, left, out, crossed(core_first))
     part = rest_of(came_c, rows)
     part_x = over("x", part)
     roots_raw = join_roots(part, over("core", part), part_x, over("core", part_x))
     out, done = update(
-        place, raw, left, roots_raw, out, shape,
+        raw, left, roots_raw, out, shape,
         lambda s, place: (0, s),
         lambda s, place: (0, (1 - place[1]) * halves + jnp.where(s == 0, RAW[0], RAW[1])),
+        held[:1],
     )
-    last = (blk // 2, blk // 2)
-    came_last = [over("y", half) for half in right_apply(place, tile, roots, 3, last, None, (came_d, done))]
     for k, value in enumerate((came_c, came_d, came_e)):
         (out,) = finish(value, left, out, crossed(functools.partial(later, k)))
     for k, value in enumerate(came_last):

time: 105 us -> 104 us (level)
  Pallas kernels: 60.4 us -> 53.5 us
  waiting for transfers between devices: 28 us -> 32.1 us
  starting transfers between devices: 15 us -> 17.4 us
    ppermute x8, waiting for transfers between devices: 21.8 us -> 24.5 us  [over(): return lax.ppermute(value, 'col', [(0, 1), (1, 0)])]
    pallas_call x4, Pallas kernels: 7.85 us -> 5.69 us  [right_apply(): pl.pallas_call(functools.partial(right_apply_kernel, width, under is not...]
    ppermute x8, starting transfers between devices: 9.47 us -> 11.5 us  [over(): return lax.ppermute(value, 'col', [(0, 1), (1, 0)])]
    ppermute x9, waiting for transfers between devices: 6.28 us -> 7.59 us  [over(): return lax.ppermute(value, 'row', [(i, i ^ flip) for i in range(n_row)])]
    pallas_call x2, Pallas kernels: 7.81 us -> 6.7 us  [right_grams(): pl.pallas_call(right_gram_kernel, out_shape=(jax.ShapeDtypeStruct((tall,...]
  transfers between devices with their start and end apart: 17 -> 17, of which waited for: 8 -> 8; matrix products, arithmetic and copies ran while one was open for 0% -> 0% of each run, Pallas kernels for 56% -> 50%
where the time goes in v5:
time: 104 us; the launch traced here: 103 us
  Pallas kernels  53.5 us (51%)
  waiting for transfers between devices  32.1 us (31%)
  starting transfers between devices  17.4 us (17%)
    ppermute x8, waiting for transfers between devices, over(): return lax.ppermute(value, 'col', [(0, 1), (1, 0)])  24.5 us
    pallas_call x2, Pallas kernels, update(): pl.pallas_call(update_kernel, out_shape=(jax.ShapeDtypeStruct(out_shape,...  13.8 us
    ppermute x8, starting transfers between devices, over(): return lax.ppermute(value, 'col', [(0, 1), (1, 0)])  11.5 us
    pallas_call x2, Pallas kernels, left_grams(): pl.pallas_call(left_gram_kernel, out_shape=jax.ShapeDtypeStruct((tall, bl...  8.45 us
    pallas_call x7, Pallas kernels, finish(): pl.pallas_call(functools.partial(finish_kernel, columns), out_shape=shape...  8.08 us
    ppermute x9, waiting for transfers between devices, over(): return lax.ppermute(value, 'row', [(i, i ^ flip) for i in range(n_row)])  7.59 us
    pallas_call x2, Pallas kernels, right_grams(): pl.pallas_call(right_gram_kernel, out_shape=(jax.ShapeDtypeStruct((tall,...  6.7 us
    ppermute x9, starting transfers between devices, over(): return lax.ppermute(value, 'row', [(i, i ^ flip) for i in range(n_row)])  5.86 us
  transfers between devices with their start and end apart: 17, of which 8 were waited for; matrix products, arithmetic and copies ran while one was open for 0% of the time, Pallas kernels for 50%

profile of v5, /device:TPU:0, one launch (start us, length us, event | category | flops | bytes accessed | tf_op | source)
XLA Modules:
  0.0 103.4 jit_solution(4195295195936458082)
XLA Ops:
  1.2 3.0 %collective-permute-start.3 = (f32[512,512]{1,0:T(8,128)S(1)}, f32[512,512]{1,0:T(8,128)S(1)}, u32[]{:S(2)}, u32[]{:S(2)}) collective-permute-start(f32[512,512]{1,0:T(8,128)S(1)} %take.1.after_ref), channel_id=1, source_target_pairs={{0,4},{4,0},{1,5},{5,1},{2,6},{6,2},{3,7},{7,3},{8,12},{12,8},{9,1... | collective-permute-start | bytes 3145736 | tf_op jit(solution)/shard_map/ppermute | solution.py:633
  4.3 3.3 %right_grams.2 = (f32[264,256]{1,0:T(8,128)S(1)}, f32[264,256]{1,0:T(8,128)S(1)}) custom-call(f32[1024,2048]{1,0:T(8,128)} %bitcast.7, f32[512,512]{1,0:T(8,128)S(1)} %take.1.after_ref), custom_call_target="tpu_custom_call" | custom-call | flops 1 | bytes 1 | tf_op jit(solution)/shard_map/right_grams/pallas_call | solution.py:141
  9.3 1.6 %collective-permute-start.2 = (f32[264,256]{1,0:T(8,128)S(1)}, f32[264,256]{1,0:T(8,128)S(1)}, u32[]{:S(2)}, u32[]{:S(2)}) collective-permute-start(f32[264,256]{1,0:T(8,128)S(1)} %fold.1.after_ref), channel_id=1, source_target_pairs={{0,16},{8,24},{16,0},{24,8},{1,17},{9,25},{17,1},{25,9},{2,18},{10... | collective-permute-start | bytes 811016 | tf_op jit(solution)/shard_map/ppermute | solution.py:635
  10.8 3.4 %right_grams.3 = (f32[264,256]{1,0:T(8,128)S(1)}, f32[264,256]{1,0:T(8,128)S(1)}) custom-call(f32[1024,2048]{1,0:T(8,128)} %bitcast.8, f32[264,256]{1,0:T(8,128)S(1)} %fold.1.after_ref), custom_call_target="tpu_custom_call" | custom-call | flops 1 | bytes 1 | tf_op jit(solution)/shard_map/right_grams/pallas_call | solution.py:141
  14.3 3.6 %collective-permute-done.2.c_ref = f32[264,256]{1,0:T(8,128)S(1)} collective-permute-done((f32[264,256]{1,0:T(8,128)S(1)}, f32[264,256]{1,0:T(8,128)S(1)}, u32[]{:S(2)}, u32[]{:S(2)}) %collective-permute-start.2) | collective-permute-done | bytes 270368 | tf_op jit(solution)/shard_map/ppermute | solution.py:635
  17.9 4.2 %right_roots.1 = (f32[264,256]{1,0:T(8,128)S(1)}, f32[512,256]{1,0:T(8,128)S(1)}) custom-call(f32[2048,256]{1,0:T(8,128)S(1)} %bitcast.4, f32[264,256]{1,0:T(8,128)S(1)} %get-tuple-element.20.a_ref, f32[264,256]{1,0:T(8,128)S(1)} %collective-permute-done.1.b_ref, f32[264,256]{1,0:T(8,128)S(1)} %collective-permute-done.2.c_ref, f32[1024,2048]{1,0:T(8,128)} %bitcast.9), custom_call_target="tpu_custom_call" | custom-call | flops 1 | bytes 1 | tf_op jit(solution)/shard_map/right_roots/pallas_call | solution.py:330
  22.5 4.2 %left_grams.2.rest_1_.under_ref = f32[264,256]{1,0:T(8,128)S(1)} custom-call(f32[1024,2048]{1,0:T(8,128)} %bitcast.10, f32[512,256]{1,0:T(8,128)S(1)} %get-tuple-element.23.after_ref), custom_call_target="tpu_custom_call" | custom-call | flops 1 | bytes 1 | tf_op jit(solution)/shard_map/left_grams/pallas_call | solution.py:190
  26.7 1.6 %collective-permute-done.3.rest_0_.g_ref = f32[512,512]{1,0:T(8,128)S(1)} collective-permute-done((f32[512,512]{1,0:T(8,128)S(1)}, f32[512,512]{1,0:T(8,128)S(1)}, u32[]{:S(2)}, u32[]{:S(2)}) %collective-permute-start.3) | collective-permute-done | bytes 1048608 | tf_op jit(solution)/shard_map/ppermute | solution.py:633
  28.4 2.1 %collective-permute-start.5 = (f32[264,256]{1,0:T(8,128)S(1)}, f32[264,256]{1,0:T(8,128)S(1)}, u32[]{:S(2)}, u32[]{:S(2)}) collective-permute-start(f32[264,256]{1,0:T(8,128)S(1)} %hold.2.own_ref), channel_id=1, source_target_pairs={{0,16},{8,24},{16,0},{24,8},{1,17},{9,25},{17,1},{25,9},{2,18},{10... | collective-permute-start | bytes 811016 | tf_op jit(solution)/shard_map/ppermute | solution.py:635
  30.5 1.5 %core_apply.1.rest_0_.after_ref = f32[776,256]{1,0:T(8,128)S(1)} custom-call(f32[1024,2048]{1,0:T(8,128)} %bitcast.11, f32[264,256]{1,0:T(8,128)S(1)} %collective-permute-done.4.packed_ref.c_ref, f32[264,256]{1,0:T(8,128)S(1)} %left_grams.2.rest_1_.under_ref), custom_call_target="tpu_custom_call" | custom-call | flops 1 | bytes 1 | tf_op jit(solution)/shard_map/core_apply/pallas_call | solution.py:468
  32.0 1.6 %collective-permute-start.8 = (f32[776,256]{1,0:T(8,128)S(1)}, f32[776,256]{1,0:T(8,128)S(1)}, u32[]{:S(2)}, u32[]{:S(2)}) collective-permute-start(f32[776,256]{1,0:T(8,128)S(1)} %core_apply.1.rest_0_.after_ref), channel_id=1, source_target_pairs={{0,4},{4,0},{1,5},{5,1},{2,6},{6,2},{3,7},{7,3},{8,12},{12,8},{9,1... | collective-permute-start | bytes 2383880 | tf_op jit(solution)/shard_map/ppermute | solution.py:633
  33.6 5.9 %collective-permute-done.6.rest_1_.half_ref = f32[512,256]{1,0:T(8,128)S(1)} collective-permute-done((f32[512,256]{1,0:T(8,128)S(1)}, f32[512,256]{1,0:T(8,128)S(1)}, u32[]{:S(2)}, u32[]{:S(2)}) %collective-permute-start.6) | collective-permute-done | bytes 524320 | tf_op jit(solution)/shard_map/ppermute | solution.py:633
  39.6 4.2 %left_grams.3.a_ref.rest_1_ = f32[264,256]{1,0:T(8,128)S(1)} custom-call(f32[1024,2048]{1,0:T(8,128)} %bitcast.12, f32[776,256]{1,0:T(8,128)S(1)} %core_apply.1.rest_0_.after_ref), custom_call_target="tpu_custom_call" | custom-call | flops 1 | bytes 1 | tf_op jit(solution)/shard_map/left_grams/pallas_call | solution.py:190
  45.8 2.1 %collective-permute-start.12 = (f32[584,256]{1,0:T(8,128)S(1)}, f32[584,256]{1,0:T(8,128)S(1)}, u32[]{:S(2)}, u32[]{:S(2)}) collective-permute-start(f32[584,256]{1,0:T(8,128)S(1)} %right_apply.6), channel_id=1, source_target_pairs={{0,4},{4,0},{1,5},{5,1},{2,6},{6,2},{3,7},{7,3},{8,12},{12,8},{9,1... | collective-permute-start | bytes 1794056 | tf_op jit(solution)/shard_map/ppermute | solution.py:633
  47.9 8.6 %collective-permute-done.8.rest_0_.b_ref.half_ref = f32[776,256]{1,0:T(8,128)S(1)} collective-permute-done((f32[776,256]{1,0:T(8,128)S(1)}, f32[776,256]{1,0:T(8,128)S(1)}, u32[]{:S(2)}, u32[]{:S(2)}) %collective-permute-start.8) | collective-permute-done | bytes 794656 | tf_op jit(solution)/shard_map/ppermute | solution.py:633
  57.9 2.1 %collective-permute-start.9 = (f32[512,256]{1,0:T(8,128)S(1)}, f32[512,256]{1,0:T(8,128)S(1)}, u32[]{:S(2)}, u32[]{:S(2)}) collective-permute-start(f32[512,256]{1,0:T(8,128)S(1)} %right_apply.4), channel_id=1, source_target_pairs={{0,4},{4,0},{1,5},{5,1},{2,6},{6,2},{3,7},{7,3},{8,12},{12,8},{9,1... | collective-permute-start | bytes 1572872 | tf_op jit(solution)/shard_map/ppermute | solution.py:633
  60.1 3.0 %left_roots.1.left_ref = bf16[2,2,256,256]{3,2,1,0:T(8,128)(2,1)S(1)} custom-call(f32[1024,256]{1,0:T(8,128)S(1)} %bitcast.5, f32[264,256]{1,0:T(8,128)S(1)} %left_grams.3.a_ref.rest_1_, f32[776,256]{1,0:T(8,128)S(1)} %collective-permute-done.8.rest_0_.b_ref.half_ref), custom_call_target="tpu_custom_call" | custom-call | flops 1 | bytes 1 | tf_op jit(solution)/shard_map/left_roots/pallas_call | solution.py:369
  63.1 10.8 %update.2 = (f32[512,4096]{1,0:T(8,128)}, f32[8,128]{1,0:T(8,128)S(1)}) custom-call(f32[1024,2048]{1,0:T(8,128)} %bitcast.15, bf16[2,2,256,256]{3,2,1,0:T(8,128)(2,1)S(1)} %left_roots.1.left_ref, bf16[8,2,256,256]{3,2,1,0:T(8,128)(2,1)S(1)} %get-tuple-element.24.right_ref), custom_call_target="tpu_custom_call" | custom-call | flops 1 | bytes 1 | tf_op jit(solution)/shard_map/update/pallas_call | solution.py:605
  75.4 5.1 %collective-permute-done.9.rest_0_.half_ref = f32[512,256]{1,0:T(8,128)S(1)} collective-permute-done((f32[512,256]{1,0:T(8,128)S(1)}, f32[512,256]{1,0:T(8,128)S(1)}, u32[]{:S(2)}, u32[]{:S(2)}) %collective-permute-start.9) | collective-permute-done | bytes 524320 | tf_op jit(solution)/shard_map/ppermute | solution.py:633
  82.0 2.1 %collective-permute-start.11 = (f32[512,128]{1,0:T(8,128)S(1)}, f32[512,128]{1,0:T(8,128)S(1)}, u32[]{:S(2)}, u32[]{:S(2)}) collective-permute-start(f32[512,128]{1,0:T(8,128)S(1)} %get-tuple-element.26.rest_1_), channel_id=1, source_target_pairs={{0,4},{4,0},{1,5},{5,1},{2,6},{6,2},{3,7},{7,3},{8,12},{12,8},{9,1... | collective-permute-start | bytes 786440 | tf_op jit(solution)/shard_map/ppermute | solution.py:633
  84.2 1.9 %collective-permute-start.15 = (f32[72,256]{1,0:T(8,128)S(1)}, f32[72,256]{1,0:T(8,128)S(1)}, u32[]{:S(2)}, u32[]{:S(2)}) collective-permute-start(f32[72,256]{1,0:T(8,128)S(1)} %rest_of.1.own_ref), channel_id=1, source_target_pairs={{0,16},{8,24},{16,0},{24,8},{1,17},{9,25},{17,1},{25,9},{2,18},{10... | collective-permute-start | bytes 221192 | tf_op jit(solution)/shard_map/ppermute | solution.py:635
  86.1 2.4 %collective-permute-done.15.x_ref = f32[72,256]{1,0:T(8,128)S(1)} collective-permute-done((f32[72,256]{1,0:T(8,128)S(1)}, f32[72,256]{1,0:T(8,128)S(1)}, u32[]{:S(2)}, u32[]{:S(2)}) %collective-permute-start.15) | collective-permute-done | bytes 73760 | tf_op jit(solution)/shard_map/ppermute | solution.py:635
  91.2 3.0 %update.3 = (f32[512,4096]{1,0:T(8,128)}, f32[8,128]{1,0:T(8,128)}) custom-call(f32[512,512]{1,0:T(8,128)S(1)} %collective-permute-done.3.rest_0_.g_ref, bf16[2,2,256,256]{3,2,1,0:T(8,128)(2,1)S(1)} %left_roots.1.left_ref, bf16[2,2,256,256]{3,2,1,0:T(8,128)(2,1)S(1)} %join_roots.1.right_ref, ...), custom_call_target="tpu_custom_call", output_to_operand_aliasing={{0}: (3, {})} | custom-call | flops 1 | bytes 1 | tf_op jit(solution)/shard_map/update/pallas_call | solution.py:605
  98.9 3.3 %collective-permute-done.10.half_ref = f32[512,128]{1,0:T(8,128)S(1)} collective-permute-done((f32[512,128]{1,0:T(8,128)S(1)}, f32[512,128]{1,0:T(8,128)S(1)}, u32[]{:S(2)}, u32[]{:S(2)}) %collective-permute-start.10) | collective-permute-done | bytes 262176 | tf_op jit(solution)/shard_map/ppermute | solution.py:633
  (41 shorter events, 18.2 us)
Async XLA Ops:
  1.2 16.6 %copy-start = (f32[1,2048,256]{2,1,0:T(8,128)S(1)}, f32[1,2048,256]{2,1,0:T(8,128)}, u32[]{:S(2)}) copy-start(f32[1,2048,256]{2,1,0:T(8,128)} %param.5) | copy-start | bytes 6291460
  1.2 27.0 %collective-permute-start.3 = (f32[512,512]{1,0:T(8,128)S(1)}, f32[512,512]{1,0:T(8,128)S(1)}, u32[]{:S(2)}, u32[]{:S(2)}) collective-permute-start(f32[512,512]{1,0:T(8,128)S(1)} %take.1.after_ref), channel_id=1, source_target_pairs={{0,4},{4,0},{1,5},{5,1},{2,6},{6,2},{3,7},{7,3},{8,12},{12,8},{9,1... | collective-permute-start | bytes 3145736 | tf_op jit(solution)/shard_map/ppermute | solution.py:633
  7.6 1.6 %collective-permute-start = (f32[264,256]{1,0:T(8,128)S(1)}, f32[264,256]{1,0:T(8,128)S(1)}, u32[]{:S(2)}, u32[]{:S(2)}) collective-permute-start(f32[264,256]{1,0:T(8,128)S(1)} %get-tuple-element.19), channel_id=1, source_target_pairs={{0,8},{8,0},{16,24},{24,16},{1,9},{9,1},{17,25},{25,17},{2,10},{10... | collective-permute-start | bytes 811016 | tf_op jit(solution)/shard_map/ppermute | solution.py:635
  9.3 8.6 %collective-permute-start.2 = (f32[264,256]{1,0:T(8,128)S(1)}, f32[264,256]{1,0:T(8,128)S(1)}, u32[]{:S(2)}, u32[]{:S(2)}) collective-permute-start(f32[264,256]{1,0:T(8,128)S(1)} %fold.1.after_ref), channel_id=1, source_target_pairs={{0,16},{8,24},{16,0},{24,8},{1,17},{9,25},{17,1},{25,9},{2,18},{10... | collective-permute-start | bytes 811016 | tf_op jit(solution)/shard_map/ppermute | solution.py:635
  14.2 3.7 %collective-permute-start.1 = (f32[264,256]{1,0:T(8,128)S(1)}, f32[264,256]{1,0:T(8,128)S(1)}, u32[]{:S(2)}, u32[]{:S(2)}) collective-permute-start(f32[264,256]{1,0:T(8,128)S(1)} %get-tuple-element.21), channel_id=1, source_target_pairs={{0,8},{8,0},{16,24},{24,16},{1,9},{9,1},{17,25},{25,17},{2,10},{10... | collective-permute-start | bytes 811016 | tf_op jit(solution)/shard_map/ppermute | solution.py:635
  22.1 17.4 %collective-permute-start.6 = (f32[512,256]{1,0:T(8,128)S(1)}, f32[512,256]{1,0:T(8,128)S(1)}, u32[]{:S(2)}, u32[]{:S(2)}) collective-permute-start(f32[512,256]{1,0:T(8,128)S(1)} %get-tuple-element.23.after_ref), channel_id=1, source_target_pairs={{0,4},{4,0},{1,5},{5,1},{2,6},{6,2},{3,7},{7,3},{8,12},{12,8},{9,1... | collective-permute-start | bytes 1572872 | tf_op jit(solution)/shard_map/ppermute | solution.py:633
  28.3 2.2 %collective-permute-start.4 = (f32[264,256]{1,0:T(8,128)S(1)}, f32[264,256]{1,0:T(8,128)S(1)}, u32[]{:S(2)}, u32[]{:S(2)}) collective-permute-start(f32[264,256]{1,0:T(8,128)S(1)} %hold.2.own_ref), channel_id=1, source_target_pairs={{0,8},{8,0},{16,24},{24,16},{1,9},{9,1},{17,25},{25,17},{2,10},{10... | collective-permute-start | bytes 811016 | tf_op jit(solution)/shard_map/ppermute | solution.py:635
  28.4 11.1 %collective-permute-start.5 = (f32[264,256]{1,0:T(8,128)S(1)}, f32[264,256]{1,0:T(8,128)S(1)}, u32[]{:S(2)}, u32[]{:S(2)}) collective-permute-start(f32[264,256]{1,0:T(8,128)S(1)} %hold.2.own_ref), channel_id=1, source_target_pairs={{0,16},{8,24},{16,0},{24,8},{1,17},{9,25},{17,1},{25,9},{2,18},{10... | collective-permute-start | bytes 811016 | tf_op jit(solution)/shard_map/ppermute | solution.py:635
  32.0 24.5 %collective-permute-start.8 = (f32[776,256]{1,0:T(8,128)S(1)}, f32[776,256]{1,0:T(8,128)S(1)}, u32[]{:S(2)}, u32[]{:S(2)}) collective-permute-start(f32[776,256]{1,0:T(8,128)S(1)} %core_apply.1.rest_0_.after_ref), channel_id=1, source_target_pairs={{0,4},{4,0},{1,5},{5,1},{2,6},{6,2},{3,7},{7,3},{8,12},{12,8},{9,1... | collective-permute-start | bytes 2383880 | tf_op jit(solution)/shard_map/ppermute | solution.py:633
  39.5 4.3 %collective-permute-start.7 = (f32[264,256]{1,0:T(8,128)S(1)}, f32[264,256]{1,0:T(8,128)S(1)}, u32[]{:S(2)}, u32[]{:S(2)}) collective-permute-start(f32[264,256]{1,0:T(8,128)S(1)} %hold.3.x_ref), channel_id=1, source_target_pairs={{0,8},{8,0},{16,24},{24,16},{1,9},{9,1},{17,25},{25,17},{2,10},{10... | collective-permute-start | bytes 811016 | tf_op jit(solution)/shard_map/ppermute | solution.py:635
  45.8 14.2 %copy-start.1 = (f32[1,1024,256]{2,1,0:T(8,128)S(1)}, f32[1,1024,256]{2,1,0:T(8,128)}, u32[]{:S(2)}) copy-start(f32[1,1024,256]{2,1,0:T(8,128)} %param.4) | copy-start | bytes 3145732
  45.8 28.1 %collective-permute-start.12 = (f32[584,256]{1,0:T(8,128)S(1)}, f32[584,256]{1,0:T(8,128)S(1)}, u32[]{:S(2)}, u32[]{:S(2)}) collective-permute-start(f32[584,256]{1,0:T(8,128)S(1)} %right_apply.6), channel_id=1, source_target_pairs={{0,4},{4,0},{1,5},{5,1},{2,6},{6,2},{3,7},{7,3},{8,12},{12,8},{9,1... | collective-permute-start | bytes 1794056 | tf_op jit(solution)/shard_map/ppermute | solution.py:633
  57.9 22.6 %collective-permute-start.9 = (f32[512,256]{1,0:T(8,128)S(1)}, f32[512,256]{1,0:T(8,128)S(1)}, u32[]{:S(2)}, u32[]{:S(2)}) collective-permute-start(f32[512,256]{1,0:T(8,128)S(1)} %right_apply.4), channel_id=1, source_target_pairs={{0,4},{4,0},{1,5},{5,1},{2,6},{6,2},{3,7},{7,3},{8,12},{12,8},{9,1... | collective-permute-start | bytes 1572872 | tf_op jit(solution)/shard_map/ppermute | solution.py:633
  75.4 21.2 %collective-permute-start.13 = (f32[512,256]{1,0:T(8,128)S(1)}, f32[512,256]{1,0:T(8,128)S(1)}, u32[]{:S(2)}, u32[]{:S(2)}) collective-permute-start(f32[512,256]{1,0:T(8,128)S(1)} %right_apply.7), channel_id=1, source_target_pairs={{0,4},{4,0},{1,5},{5,1},{2,6},{6,2},{3,7},{7,3},{8,12},{12,8},{9,1... | collective-permute-start | bytes 1572872 | tf_op jit(solution)/shard_map/ppermute | solution.py:633
  82.0 15.8 %collective-permute-start.11 = (f32[512,128]{1,0:T(8,128)S(1)}, f32[512,128]{1,0:T(8,128)S(1)}, u32[]{:S(2)}, u32[]{:S(2)}) collective-permute-start(f32[512,128]{1,0:T(8,128)S(1)} %get-tuple-element.26.rest_1_), channel_id=1, source_target_pairs={{0,4},{4,0},{1,5},{5,1},{2,6},{6,2},{3,7},{7,3},{8,12},{12,8},{9,1... | collective-permute-start | bytes 786440 | tf_op jit(solution)/shard_map/ppermute | solution.py:633
  84.1 18.1 %collective-permute-start.10 = (f32[512,128]{1,0:T(8,128)S(1)}, f32[512,128]{1,0:T(8,128)S(1)}, u32[]{:S(2)}, u32[]{:S(2)}) collective-permute-start(f32[512,128]{1,0:T(8,128)S(1)} %get-tuple-element.25), channel_id=1, source_target_pairs={{0,4},{4,0},{1,5},{5,1},{2,6},{6,2},{3,7},{7,3},{8,12},{12,8},{9,1... | collective-permute-start | bytes 786440 | tf_op jit(solution)/shard_map/ppermute | solution.py:633
  84.2 4.4 %collective-permute-start.15 = (f32[72,256]{1,0:T(8,128)S(1)}, f32[72,256]{1,0:T(8,128)S(1)}, u32[]{:S(2)}, u32[]{:S(2)}) collective-permute-start(f32[72,256]{1,0:T(8,128)S(1)} %rest_of.1.own_ref), channel_id=1, source_target_pairs={{0,16},{8,24},{16,0},{24,8},{1,17},{9,25},{17,1},{25,9},{2,18},{10... | collective-permute-start | bytes 221192 | tf_op jit(solution)/shard_map/ppermute | solution.py:635
  86.1 4.9 %collective-permute-start.14 = (f32[72,256]{1,0:T(8,128)S(1)}, f32[72,256]{1,0:T(8,128)S(1)}, u32[]{:S(2)}, u32[]{:S(2)}) collective-permute-start(f32[72,256]{1,0:T(8,128)S(1)} %rest_of.1.own_ref), channel_id=1, source_target_pairs={{0,8},{8,0},{16,24},{24,16},{1,9},{9,1},{17,25},{25,17},{2,10},{10... | collective-permute-start | bytes 221192 | tf_op jit(solution)/shard_map/ppermute | solution.py:635
  88.6 2.4 %collective-permute-start.16 = (f32[72,256]{1,0:T(8,128)S(1)}, f32[72,256]{1,0:T(8,128)S(1)}, u32[]{:S(2)}, u32[]{:S(2)}) collective-permute-start(f32[72,256]{1,0:T(8,128)S(1)} %collective-permute-done.15.x_ref), channel_id=1, source_target_pairs={{0,8},{8,0},{16,24},{24,16},{1,9},{9,1},{17,25},{25,17},{2,10},{10... | collective-permute-start | bytes 221192 | tf_op jit(solution)/shard_map/ppermute | solution.py:635

commit v6 on v5

--- a/solution.py
+++ b/solution.py
@@ -484,46 +484,38 @@
     )(tile, packed, under)
 
 
-def right_apply_kernel(width, carries, g_ref, right_ref, *rest):
-    step = pl.program_id(0)
-    out_refs = rest[-len(width) :]
+def right_apply_kernel(pieces, carries, g_ref, right_ref, *rest):
+    out_refs = rest[-len(pieces) :]
     value = product(split(g_ref[...]), (right_ref[0, 0], right_ref[0, 1]))
-    blk = value.shape[1]
-    start = 0
-    for size, ref in zip(width, out_refs):
-        for b in range(start // blk, -(-(start + size) // blk)):
-            low, high = max(start, b * blk), min(start + size, (b + 1) * blk)
-
-            @pl.when(step == b)
-            def _():
-                ref[: value.shape[0], low - start : high - start] = value[:, low - b * blk : high - b * blk]
-
-        start += size
+    for (top, rows, start, width), ref in zip(pieces, out_refs):
+        ref[:rows, :] = value[top : top + rows, start : start + width]
     if carries:
         out_refs[0][value.shape[0] :, :] = rest[0][...]
 
 
-def right_apply(tile, right, first, width, under, after):
+def right_apply(tile, right, k, pieces, under, after):
     rows = tile.shape[0] // 2
     blk = right.shape[-1]
+    pieces = pieces or ((0, rows, 0, blk),)
     in_specs = [
-        pl.BlockSpec((rows, blk), placed(lambda s, place: (1 - place[1], later(first + s, place)))),
-        pl.BlockSpec((1, 2, blk, blk), placed(lambda s, place: (later(first + s, place), 0, 0, 0))),
+        pl.BlockSpec((rows, blk), placed(lambda s, place: (1 - place[1], later(k, place)))),
+        pl.BlockSpec((1, 2, blk, blk), placed(lambda s, place: (later(k, place), 0, 0, 0))),
     ]
     operands = [tile, right]
-    tall = rows
+    more = 0
     if under is not None:
-        tall += under.shape[0]
+        more = under.shape[0]
         in_specs.append(pl.BlockSpec(under.shape, lambda s: (0, 0)))
         operands.append(under)
-    return pl.pallas_call(
-        functools.partial(right_apply_kernel, width, under is not None),
-        out_shape=tuple(jax.ShapeDtypeStruct((tall, w), jnp.float32) for w in width),
+    shapes = [(tall + more, width) for _, tall, _, width in pieces]
+    return pl.pallas_call(
+        functools.partial(right_apply_kernel, pieces, under is not None),
+        out_shape=tuple(jax.ShapeDtypeStruct(shape, jnp.float32) for shape in shapes),
         grid_spec=pltpu.PrefetchScalarGridSpec(
             num_scalar_prefetch=0,
-            grid=(sum(width) // blk,),
+            grid=(1,),
             in_specs=in_specs + [pl.BlockSpec(memory_space=pl.ANY)] * len(after),
-            out_specs=tuple(pl.BlockSpec((tall, w), lambda s: (0, 0)) for w in width),
+            out_specs=tuple(pl.BlockSpec(shape, lambda s: (0, 0)) for shape in shapes),
         ),
         compiler_params=pltpu.CompilerParams(vmem_limit_bytes=VMEM_LIMIT),
         cost_estimate=SMALL,
@@ -544,42 +536,34 @@
     rest[-1][...] = jnp.zeros_like(rest[-1])
 
 
-def finish_kernel(columns, half_ref, left_ref, out_before, out_ref, *rest):
-    stage, sems = rest[-2:]
+def finish_kernel(column, first, half_ref, left_ref, out_before, out_ref, stage, sems):
     blk = left_ref.shape[-1]
-    size = stage.shape[1] // len(columns)
+    width = stage.shape[1]
+    cols = pl.ds(pl.multiple_of(column(here()), width), width)
     copies = []
-    for b, column in enumerate(columns):
-        start = pl.multiple_of(column(here()), size)
-        cols = pl.ds(b * size, size)
-        for i in range(left_ref.shape[0]):
-            rows = pl.ds(i * blk, blk)
-            stage[rows, cols] = product((left_ref[i, 0], left_ref[i, 1]), split(half_ref[rows, cols]))
-            copies.append(
-                pltpu.make_async_copy(stage.at[rows, cols], out_ref.at[rows, pl.ds(start, size)], sems.at[len(copies)])
-            )
-            copies[-1].start()
-    for done_ref in rest[:-2]:
-        done_ref[...] = jnp.zeros_like(done_ref)
+    for i in range(stage.shape[0] // blk):
+        rows = pl.ds(i * blk, blk)
+        root = (left_ref[first + i, 0], left_ref[first + i, 1])
+        stage[rows, :] = product(root, split(half_ref[rows, :]))
+        copies.append(
+            pltpu.make_async_copy(stage.at[rows, :], out_ref.at[pl.ds((first + i) * blk, blk), cols], sems.at[i])
+        )
+        copies[i].start()
     for copy in copies:
         copy.wait()
 
 
-def finish(half, left, out, columns, mark=False):
+def finish(half, left, out, column, first=0, count=2):
     width = half.shape[1]
-    rows = out.shape[0]
+    blk = left.shape[-1]
     vmem = pl.BlockSpec(memory_space=pltpu.VMEM)
     anywhere = pl.BlockSpec(memory_space=pl.ANY)
-    shapes = (jax.ShapeDtypeStruct(out.shape, jnp.float32), jax.ShapeDtypeStruct((8, 128), jnp.float32))
-    return pl.pallas_call(
-        functools.partial(finish_kernel, columns),
-        out_shape=shapes if mark else shapes[:1],
+    return pl.pallas_call(
+        functools.partial(finish_kernel, column, first),
+        out_shape=jax.ShapeDtypeStruct(out.shape, jnp.float32),
         in_specs=[vmem, vmem, anywhere],
-        out_specs=(anywhere, vmem) if mark else (anywhere,),
-        scratch_shapes=[
-            pltpu.VMEM((rows, width), jnp.float32),
-            pltpu.SemaphoreType.DMA((left.shape[0] * len(columns),)),
-        ],
+        out_specs=anywhere,
+        scratch_shapes=[pltpu.VMEM((count * blk, width), jnp.float32), pltpu.SemaphoreType.DMA((count,))],
         input_output_aliases={2: 0},
         compiler_params=pltpu.CompilerParams(vmem_limit_bytes=VMEM_LIMIT),
         cost_estimate=SMALL,
@@ -655,13 +639,13 @@
     lkeep = left_grams(tile, blk, lambda place: place[1], half)
     roots, part = spread_roots(own, own_c, own_x, over("core", own_x))
 
-    (half,) = right_apply(tile, roots, 0, (blk,), part, (lkeep,))
+    (half,) = right_apply(tile, roots, 0, None, part, (lkeep,))
     came_c = over("y", half)
-    (half,) = right_apply(tile, roots, 1, (blk,), None, (came_b,))
+    (half,) = right_apply(tile, roots, 1, None, None, (came_b,))
     came_d = over("y", half)
 
     def crossed(block, start=0):
-        return (lambda place: (1 - place[1]) * tile_cols + block(place) * blk + start,)
+        return lambda place: (1 - place[1]) * tile_cols + block(place) * blk + start
 
     left = left_roots(full_dim, lstats, lkeep, came_b)
     out, done = update(
@@ -669,13 +653,14 @@
         lambda s, place: (place[1], s),
         lambda s, place: (0, place[1] * halves + s),
     )
-    (half,) = right_apply(tile, roots, 2, (blk,), None, (came_c, done))
+    (half,) = right_apply(tile, roots, 2, None, None, (came_c, done))
     came_e = over("y", half)
-    last = (blk // 2, blk // 2)
+    wide = blk // 2
+    last = ((0, rows, 0, wide), (0, blk, wide, wide), (blk, blk, wide, wide))
     held = right_apply(tile, roots, 3, last, None, (came_d,))
     came_last = [over("y", half) for half in held]
-    (out,) = finish(came_a, left, out, crossed(own_first))
-    (out,) = finish(came_b, left, out, crossed(core_first))
+    out = finish(came_a, left, out, crossed(own_first))
+    out = finish(came_b, left, out, crossed(core_first))
     part = rest_of(came_c, rows)
     part_x = over("x", part)
     roots_raw = join_roots(part, over("core", part), part_x, over("core", part_x))
@@ -686,9 +671,9 @@
         held[:1],
     )
     for k, value in enumerate((came_c, came_d, came_e)):
-        (out,) = finish(value, left, out, crossed(functools.partial(later, k)))
-    for k, value in enumerate(came_last):
-        (out,) = finish(value, left, out, crossed(functools.partial(later, 3), k * last[0]))
+        out = finish(value, left, out, crossed(functools.partial(later, k)))
+    for (top, tall, start, _), value in zip(last, came_last):
+        out = finish(value, left, out, crossed(functools.partial(later, 3), start), top // blk, tall // blk)
     return out.reshape(1, rows, 2 * tile_cols)
 
 

time: 104 us -> 104 us (level)
    ppermute x8 -> x9, waiting for transfers between devices: 24.5 us -> 23.6 us  [over(): return lax.ppermute(value, 'col', [(0, 1), (1, 0)])]
    pallas_call x11 -> x12, Pallas kernels: 13.8 us -> 14.6 us  [the longest x8 8.88 us: finish(): pl.pallas_call(functools.partial(finish_kernel, column, first), out_shape...]
    ppermute x8 -> x9, starting transfers between devices: 11.5 us -> 12 us  [over(): return lax.ppermute(value, 'col', [(0, 1), (1, 0)])]
  transfers between devices with their start and end apart: 17 -> 18, of which waited for: 8 -> 9; matrix products, arithmetic and copies ran while one was open for 0% -> 0% of each run, Pallas kernels for 50% -> 50%
where the time goes in v6:
time: 104 us; the launch traced here: 103 us
  Pallas kernels  54.3 us (52%)
  waiting for transfers between devices  31.1 us (30%)
  starting transfers between devices  17.4 us (17%)
    ppermute x9, waiting for transfers between devices, over(): return lax.ppermute(value, 'col', [(0, 1), (1, 0)])  23.6 us
    pallas_call x2, Pallas kernels, update(): pl.pallas_call(update_kernel, out_shape=(jax.ShapeDtypeStruct(out_shape,...  13.8 us
    ppermute x9, starting transfers between devices, over(): return lax.ppermute(value, 'col', [(0, 1), (1, 0)])  12 us
    pallas_call x8, Pallas kernels, finish(): pl.pallas_call(functools.partial(finish_kernel, column, first), out_shape...  8.88 us
    pallas_call x2, Pallas kernels, left_grams(): pl.pallas_call(left_gram_kernel, out_shape=jax.ShapeDtypeStruct((tall, bl...  8.45 us
    ppermute x9, waiting for transfers between devices, over(): return lax.ppermute(value, 'row', [(i, i ^ flip) for i in range(n_row)])  7.5 us
    pallas_call x2, Pallas kernels, right_grams(): pl.pallas_call(right_gram_kernel, out_shape=(jax.ShapeDtypeStruct((tall,...  6.7 us
    pallas_call x4, Pallas kernels, right_apply(): pl.pallas_call(functools.partial(right_apply_kernel, pieces, under is not...  5.69 us
  transfers between devices with their start and end apart: 18, of which 9 were waited for; matrix products, arithmetic and copies ran while one was open for 0% of the time, Pallas kernels for 50%

profile of v6, /device:TPU:0, one launch (start us, length us, event | category | flops | bytes accessed | tf_op | source)
XLA Modules:
  0.0 103.3 jit_solution(15942427918979058178)
XLA Ops:
  1.2 3.0 %collective-permute-start.3 = (f32[512,512]{1,0:T(8,128)S(1)}, f32[512,512]{1,0:T(8,128)S(1)}, u32[]{:S(2)}, u32[]{:S(2)}) collective-permute-start(f32[512,512]{1,0:T(8,128)S(1)} %take.1.after_ref), channel_id=1, source_target_pairs={{0,4},{4,0},{1,5},{5,1},{2,6},{6,2},{3,7},{7,3},{8,12},{12,8},{9,1... | collective-permute-start | bytes 3145736 | tf_op jit(solution)/shard_map/ppermute | solution.py:617
  4.3 3.3 %right_grams.2 = (f32[264,256]{1,0:T(8,128)S(1)}, f32[264,256]{1,0:T(8,128)S(1)}) custom-call(f32[1024,2048]{1,0:T(8,128)} %bitcast.7, f32[512,512]{1,0:T(8,128)S(1)} %take.1.after_ref), custom_call_target="tpu_custom_call" | custom-call | flops 1 | bytes 1 | tf_op jit(solution)/shard_map/right_grams/pallas_call | solution.py:141
  7.7 1.5 %collective-permute-done.b_ref = f32[264,256]{1,0:T(8,128)S(1)} collective-permute-done((f32[264,256]{1,0:T(8,128)S(1)}, f32[264,256]{1,0:T(8,128)S(1)}, u32[]{:S(2)}, u32[]{:S(2)}) %collective-permute-start) | collective-permute-done | bytes 270368 | tf_op jit(solution)/shard_map/ppermute | solution.py:619
  9.3 1.6 %collective-permute-start.2 = (f32[264,256]{1,0:T(8,128)S(1)}, f32[264,256]{1,0:T(8,128)S(1)}, u32[]{:S(2)}, u32[]{:S(2)}) collective-permute-start(f32[264,256]{1,0:T(8,128)S(1)} %fold.1.after_ref), channel_id=1, source_target_pairs={{0,16},{8,24},{16,0},{24,8},{1,17},{9,25},{17,1},{25,9},{2,18},{10... | collective-permute-start | bytes 811016 | tf_op jit(solution)/shard_map/ppermute | solution.py:619
  10.8 3.4 %right_grams.3 = (f32[264,256]{1,0:T(8,128)S(1)}, f32[264,256]{1,0:T(8,128)S(1)}) custom-call(f32[1024,2048]{1,0:T(8,128)} %bitcast.8, f32[264,256]{1,0:T(8,128)S(1)} %fold.1.after_ref), custom_call_target="tpu_custom_call" | custom-call | flops 1 | bytes 1 | tf_op jit(solution)/shard_map/right_grams/pallas_call | solution.py:141
  14.3 3.6 %collective-permute-done.2.c_ref = f32[264,256]{1,0:T(8,128)S(1)} collective-permute-done((f32[264,256]{1,0:T(8,128)S(1)}, f32[264,256]{1,0:T(8,128)S(1)}, u32[]{:S(2)}, u32[]{:S(2)}) %collective-permute-start.2) | collective-permute-done | bytes 270368 | tf_op jit(solution)/shard_map/ppermute | solution.py:619
  17.9 4.2 %right_roots.1 = (f32[264,256]{1,0:T(8,128)S(1)}, f32[512,256]{1,0:T(8,128)S(1)}) custom-call(f32[2048,256]{1,0:T(8,128)S(1)} %bitcast.4, f32[264,256]{1,0:T(8,128)S(1)} %get-tuple-element.21.a_ref, f32[264,256]{1,0:T(8,128)S(1)} %collective-permute-done.1.b_ref, f32[264,256]{1,0:T(8,128)S(1)} %collective-permute-done.2.c_ref, f32[1024,2048]{1,0:T(8,128)} %bitcast.9), custom_call_target="tpu_custom_call" | custom-call | flops 1 | bytes 1 | tf_op jit(solution)/shard_map/right_roots/pallas_call | solution.py:330
  22.5 4.2 %left_grams.2.rest_1_.under_ref = f32[264,256]{1,0:T(8,128)S(1)} custom-call(f32[1024,2048]{1,0:T(8,128)} %bitcast.10, f32[512,256]{1,0:T(8,128)S(1)} %get-tuple-element.24.after_ref), custom_call_target="tpu_custom_call" | custom-call | flops 1 | bytes 1 | tf_op jit(solution)/shard_map/left_grams/pallas_call | solution.py:190
  26.7 1.6 %collective-permute-done.3.rest_0_.g_ref = f32[512,512]{1,0:T(8,128)S(1)} collective-permute-done((f32[512,512]{1,0:T(8,128)S(1)}, f32[512,512]{1,0:T(8,128)S(1)}, u32[]{:S(2)}, u32[]{:S(2)}) %collective-permute-start.3) | collective-permute-done | bytes 1048608 | tf_op jit(solution)/shard_map/ppermute | solution.py:617
  28.4 2.1 %collective-permute-start.5 = (f32[264,256]{1,0:T(8,128)S(1)}, f32[264,256]{1,0:T(8,128)S(1)}, u32[]{:S(2)}, u32[]{:S(2)}) collective-permute-start(f32[264,256]{1,0:T(8,128)S(1)} %hold.2.own_ref), channel_id=1, source_target_pairs={{0,16},{8,24},{16,0},{24,8},{1,17},{9,25},{17,1},{25,9},{2,18},{10... | collective-permute-start | bytes 811016 | tf_op jit(solution)/shard_map/ppermute | solution.py:619
  30.5 1.5 %core_apply.1.rest_0_.after_ref = f32[776,256]{1,0:T(8,128)S(1)} custom-call(f32[1024,2048]{1,0:T(8,128)} %bitcast.11, f32[264,256]{1,0:T(8,128)S(1)} %collective-permute-done.4.packed_ref.c_ref, f32[264,256]{1,0:T(8,128)S(1)} %left_grams.2.rest_1_.under_ref), custom_call_target="tpu_custom_call" | custom-call | flops 1 | bytes 1 | tf_op jit(solution)/shard_map/core_apply/pallas_call | solution.py:468
  32.0 1.6 %collective-permute-start.8 = (f32[776,256]{1,0:T(8,128)S(1)}, f32[776,256]{1,0:T(8,128)S(1)}, u32[]{:S(2)}, u32[]{:S(2)}) collective-permute-start(f32[776,256]{1,0:T(8,128)S(1)} %core_apply.1.rest_0_.after_ref), channel_id=1, source_target_pairs={{0,4},{4,0},{1,5},{5,1},{2,6},{6,2},{3,7},{7,3},{8,12},{12,8},{9,1... | collective-permute-start | bytes 2383880 | tf_op jit(solution)/shard_map/ppermute | solution.py:617
  33.6 5.9 %collective-permute-done.6.rest_1_.half_ref = f32[512,256]{1,0:T(8,128)S(1)} collective-permute-done((f32[512,256]{1,0:T(8,128)S(1)}, f32[512,256]{1,0:T(8,128)S(1)}, u32[]{:S(2)}, u32[]{:S(2)}) %collective-permute-start.6) | collective-permute-done | bytes 524320 | tf_op jit(solution)/shard_map/ppermute | solution.py:617
  39.6 4.2 %left_grams.3.a_ref.rest_1_ = f32[264,256]{1,0:T(8,128)S(1)} custom-call(f32[1024,2048]{1,0:T(8,128)} %bitcast.12, f32[776,256]{1,0:T(8,128)S(1)} %core_apply.1.rest_0_.after_ref), custom_call_target="tpu_custom_call" | custom-call | flops 1 | bytes 1 | tf_op jit(solution)/shard_map/left_grams/pallas_call | solution.py:190
  45.9 2.1 %collective-permute-start.13 = (f32[584,256]{1,0:T(8,128)S(1)}, f32[584,256]{1,0:T(8,128)S(1)}, u32[]{:S(2)}, u32[]{:S(2)}) collective-permute-start(f32[584,256]{1,0:T(8,128)S(1)} %right_apply.6), channel_id=1, source_target_pairs={{0,4},{4,0},{1,5},{5,1},{2,6},{6,2},{3,7},{7,3},{8,12},{12,8},{9,1... | collective-permute-start | bytes 1794056 | tf_op jit(solution)/shard_map/ppermute | solution.py:617
  48.0 8.6 %collective-permute-done.8.rest_0_.b_ref.half_ref = f32[776,256]{1,0:T(8,128)S(1)} collective-permute-done((f32[776,256]{1,0:T(8,128)S(1)}, f32[776,256]{1,0:T(8,128)S(1)}, u32[]{:S(2)}, u32[]{:S(2)}) %collective-permute-start.8) | collective-permute-done | bytes 794656 | tf_op jit(solution)/shard_map/ppermute | solution.py:617
  57.9 2.1 %collective-permute-start.9 = (f32[512,256]{1,0:T(8,128)S(1)}, f32[512,256]{1,0:T(8,128)S(1)}, u32[]{:S(2)}, u32[]{:S(2)}) collective-permute-start(f32[512,256]{1,0:T(8,128)S(1)} %right_apply.4), channel_id=1, source_target_pairs={{0,4},{4,0},{1,5},{5,1},{2,6},{6,2},{3,7},{7,3},{8,12},{12,8},{9,1... | collective-permute-start | bytes 1572872 | tf_op jit(solution)/shard_map/ppermute | solution.py:617
  60.1 3.0 %left_roots.1.left_ref = bf16[2,2,256,256]{3,2,1,0:T(8,128)(2,1)S(1)} custom-call(f32[1024,256]{1,0:T(8,128)S(1)} %bitcast.5, f32[264,256]{1,0:T(8,128)S(1)} %left_grams.3.a_ref.rest_1_, f32[776,256]{1,0:T(8,128)S(1)} %collective-permute-done.8.rest_0_.b_ref.half_ref), custom_call_target="tpu_custom_call" | custom-call | flops 1 | bytes 1 | tf_op jit(solution)/shard_map/left_roots/pallas_call | solution.py:369
  63.1 10.8 %update.2 = (f32[512,4096]{1,0:T(8,128)}, f32[8,128]{1,0:T(8,128)S(1)}) custom-call(f32[1024,2048]{1,0:T(8,128)} %bitcast.15, bf16[2,2,256,256]{3,2,1,0:T(8,128)(2,1)S(1)} %left_roots.1.left_ref, bf16[8,2,256,256]{3,2,1,0:T(8,128)(2,1)S(1)} %get-tuple-element.25.right_ref), custom_call_target="tpu_custom_call" | custom-call | flops 1 | bytes 1 | tf_op jit(solution)/shard_map/update/pallas_call | solution.py:589
  75.4 5.2 %collective-permute-done.9.rest_0_.half_ref = f32[512,256]{1,0:T(8,128)S(1)} collective-permute-done((f32[512,256]{1,0:T(8,128)S(1)}, f32[512,256]{1,0:T(8,128)S(1)}, u32[]{:S(2)}, u32[]{:S(2)}) %collective-permute-start.9) | collective-permute-done | bytes 524320 | tf_op jit(solution)/shard_map/ppermute | solution.py:617
  82.0 2.1 %collective-permute-start.12 = (f32[512,128]{1,0:T(8,128)S(1)}, f32[512,128]{1,0:T(8,128)S(1)}, u32[]{:S(2)}, u32[]{:S(2)}) collective-permute-start(f32[512,128]{1,0:T(8,128)S(1)} %get-tuple-element.28.rest_1_), channel_id=1, source_target_pairs={{0,4},{4,0},{1,5},{5,1},{2,6},{6,2},{3,7},{7,3},{8,12},{12,8},{9,1... | collective-permute-start | bytes 786440 | tf_op jit(solution)/shard_map/ppermute | solution.py:617
  84.1 1.5 %collective-permute-start.16 = (f32[72,256]{1,0:T(8,128)S(1)}, f32[72,256]{1,0:T(8,128)S(1)}, u32[]{:S(2)}, u32[]{:S(2)}) collective-permute-start(f32[72,256]{1,0:T(8,128)S(1)} %rest_of.1.own_ref), channel_id=1, source_target_pairs={{0,16},{8,24},{16,0},{24,8},{1,17},{9,25},{17,1},{25,9},{2,18},{10... | collective-permute-start | bytes 221192 | tf_op jit(solution)/shard_map/ppermute | solution.py:619
  86.1 2.4 %collective-permute-done.16.x_ref = f32[72,256]{1,0:T(8,128)S(1)} collective-permute-done((f32[72,256]{1,0:T(8,128)S(1)}, f32[72,256]{1,0:T(8,128)S(1)}, u32[]{:S(2)}, u32[]{:S(2)}) %collective-permute-start.16) | collective-permute-done | bytes 73760 | tf_op jit(solution)/shard_map/ppermute | solution.py:619
  91.2 3.0 %update.3 = (f32[512,4096]{1,0:T(8,128)}, f32[8,128]{1,0:T(8,128)}) custom-call(f32[512,512]{1,0:T(8,128)S(1)} %collective-permute-done.3.rest_0_.g_ref, bf16[2,2,256,256]{3,2,1,0:T(8,128)(2,1)S(1)} %left_roots.1.left_ref, bf16[2,2,256,256]{3,2,1,0:T(8,128)(2,1)S(1)} %join_roots.1.right_ref, ...), custom_call_target="tpu_custom_call", output_to_operand_aliasing={{0}: (3, {})} | custom-call | flops 1 | bytes 1 | tf_op jit(solution)/shard_map/update/pallas_call | solution.py:589
  (44 shorter events, 20.4 us)
Async XLA Ops:
  1.2 16.6 %copy-start = (f32[1,2048,256]{2,1,0:T(8,128)S(1)}, f32[1,2048,256]{2,1,0:T(8,128)}, u32[]{:S(2)}) copy-start(f32[1,2048,256]{2,1,0:T(8,128)} %param.5) | copy-start | bytes 6291460
  1.2 27.0 %collective-permute-start.3 = (f32[512,512]{1,0:T(8,128)S(1)}, f32[512,512]{1,0:T(8,128)S(1)}, u32[]{:S(2)}, u32[]{:S(2)}) collective-permute-start(f32[512,512]{1,0:T(8,128)S(1)} %take.1.after_ref), channel_id=1, source_target_pairs={{0,4},{4,0},{1,5},{5,1},{2,6},{6,2},{3,7},{7,3},{8,12},{12,8},{9,1... | collective-permute-start | bytes 3145736 | tf_op jit(solution)/shard_map/ppermute | solution.py:617
  7.6 1.6 %collective-permute-start = (f32[264,256]{1,0:T(8,128)S(1)}, f32[264,256]{1,0:T(8,128)S(1)}, u32[]{:S(2)}, u32[]{:S(2)}) collective-permute-start(f32[264,256]{1,0:T(8,128)S(1)} %get-tuple-element.20), channel_id=1, source_target_pairs={{0,8},{8,0},{16,24},{24,16},{1,9},{9,1},{17,25},{25,17},{2,10},{10... | collective-permute-start | bytes 811016 | tf_op jit(solution)/shard_map/ppermute | solution.py:619
  9.3 8.6 %collective-permute-start.2 = (f32[264,256]{1,0:T(8,128)S(1)}, f32[264,256]{1,0:T(8,128)S(1)}, u32[]{:S(2)}, u32[]{:S(2)}) collective-permute-start(f32[264,256]{1,0:T(8,128)S(1)} %fold.1.after_ref), channel_id=1, source_target_pairs={{0,16},{8,24},{16,0},{24,8},{1,17},{9,25},{17,1},{25,9},{2,18},{10... | collective-permute-start | bytes 811016 | tf_op jit(solution)/shard_map/ppermute | solution.py:619
  14.2 3.7 %collective-permute-start.1 = (f32[264,256]{1,0:T(8,128)S(1)}, f32[264,256]{1,0:T(8,128)S(1)}, u32[]{:S(2)}, u32[]{:S(2)}) collective-permute-start(f32[264,256]{1,0:T(8,128)S(1)} %get-tuple-element.22), channel_id=1, source_target_pairs={{0,8},{8,0},{16,24},{24,16},{1,9},{9,1},{17,25},{25,17},{2,10},{10... | collective-permute-start | bytes 811016 | tf_op jit(solution)/shard_map/ppermute | solution.py:619
  22.1 17.4 %collective-permute-start.6 = (f32[512,256]{1,0:T(8,128)S(1)}, f32[512,256]{1,0:T(8,128)S(1)}, u32[]{:S(2)}, u32[]{:S(2)}) collective-permute-start(f32[512,256]{1,0:T(8,128)S(1)} %get-tuple-element.24.after_ref), channel_id=1, source_target_pairs={{0,4},{4,0},{1,5},{5,1},{2,6},{6,2},{3,7},{7,3},{8,12},{12,8},{9,1... | collective-permute-start | bytes 1572872 | tf_op jit(solution)/shard_map/ppermute | solution.py:617
  28.3 2.2 %collective-permute-start.4 = (f32[264,256]{1,0:T(8,128)S(1)}, f32[264,256]{1,0:T(8,128)S(1)}, u32[]{:S(2)}, u32[]{:S(2)}) collective-permute-start(f32[264,256]{1,0:T(8,128)S(1)} %hold.2.own_ref), channel_id=1, source_target_pairs={{0,8},{8,0},{16,24},{24,16},{1,9},{9,1},{17,25},{25,17},{2,10},{10... | collective-permute-start | bytes 811016 | tf_op jit(solution)/shard_map/ppermute | solution.py:619
  28.4 11.1 %collective-permute-start.5 = (f32[264,256]{1,0:T(8,128)S(1)}, f32[264,256]{1,0:T(8,128)S(1)}, u32[]{:S(2)}, u32[]{:S(2)}) collective-permute-start(f32[264,256]{1,0:T(8,128)S(1)} %hold.2.own_ref), channel_id=1, source_target_pairs={{0,16},{8,24},{16,0},{24,8},{1,17},{9,25},{17,1},{25,9},{2,18},{10... | collective-permute-start | bytes 811016 | tf_op jit(solution)/shard_map/ppermute | solution.py:619
  32.0 24.5 %collective-permute-start.8 = (f32[776,256]{1,0:T(8,128)S(1)}, f32[776,256]{1,0:T(8,128)S(1)}, u32[]{:S(2)}, u32[]{:S(2)}) collective-permute-start(f32[776,256]{1,0:T(8,128)S(1)} %core_apply.1.rest_0_.after_ref), channel_id=1, source_target_pairs={{0,4},{4,0},{1,5},{5,1},{2,6},{6,2},{3,7},{7,3},{8,12},{12,8},{9,1... | collective-permute-start | bytes 2383880 | tf_op jit(solution)/shard_map/ppermute | solution.py:617
  39.5 4.3 %collective-permute-start.7 = (f32[264,256]{1,0:T(8,128)S(1)}, f32[264,256]{1,0:T(8,128)S(1)}, u32[]{:S(2)}, u32[]{:S(2)}) collective-permute-start(f32[264,256]{1,0:T(8,128)S(1)} %hold.3.x_ref), channel_id=1, source_target_pairs={{0,8},{8,0},{16,24},{24,16},{1,9},{9,1},{17,25},{25,17},{2,10},{10... | collective-permute-start | bytes 811016 | tf_op jit(solution)/shard_map/ppermute | solution.py:619
  45.8 14.2 %copy-start.1 = (f32[1,1024,256]{2,1,0:T(8,128)S(1)}, f32[1,1024,256]{2,1,0:T(8,128)}, u32[]{:S(2)}) copy-start(f32[1,1024,256]{2,1,0:T(8,128)} %param.4) | copy-start | bytes 3145732
  45.9 28.1 %collective-permute-start.13 = (f32[584,256]{1,0:T(8,128)S(1)}, f32[584,256]{1,0:T(8,128)S(1)}, u32[]{:S(2)}, u32[]{:S(2)}) collective-permute-start(f32[584,256]{1,0:T(8,128)S(1)} %right_apply.6), channel_id=1, source_target_pairs={{0,4},{4,0},{1,5},{5,1},{2,6},{6,2},{3,7},{7,3},{8,12},{12,8},{9,1... | collective-permute-start | bytes 1794056 | tf_op jit(solution)/shard_map/ppermute | solution.py:617
  57.9 22.6 %collective-permute-start.9 = (f32[512,256]{1,0:T(8,128)S(1)}, f32[512,256]{1,0:T(8,128)S(1)}, u32[]{:S(2)}, u32[]{:S(2)}) collective-permute-start(f32[512,256]{1,0:T(8,128)S(1)} %right_apply.4), channel_id=1, source_target_pairs={{0,4},{4,0},{1,5},{5,1},{2,6},{6,2},{3,7},{7,3},{8,12},{12,8},{9,1... | collective-permute-start | bytes 1572872 | tf_op jit(solution)/shard_map/ppermute | solution.py:617
  75.3 21.2 %collective-permute-start.14 = (f32[512,256]{1,0:T(8,128)S(1)}, f32[512,256]{1,0:T(8,128)S(1)}, u32[]{:S(2)}, u32[]{:S(2)}) collective-permute-start(f32[512,256]{1,0:T(8,128)S(1)} %right_apply.7), channel_id=1, source_target_pairs={{0,4},{4,0},{1,5},{5,1},{2,6},{6,2},{3,7},{7,3},{8,12},{12,8},{9,1... | collective-permute-start | bytes 1572872 | tf_op jit(solution)/shard_map/ppermute | solution.py:617
  82.0 15.8 %collective-permute-start.12 = (f32[512,128]{1,0:T(8,128)S(1)}, f32[512,128]{1,0:T(8,128)S(1)}, u32[]{:S(2)}, u32[]{:S(2)}) collective-permute-start(f32[512,128]{1,0:T(8,128)S(1)} %get-tuple-element.28.rest_1_), channel_id=1, source_target_pairs={{0,4},{4,0},{1,5},{5,1},{2,6},{6,2},{3,7},{7,3},{8,12},{12,8},{9,1... | collective-permute-start | bytes 786440 | tf_op jit(solution)/shard_map/ppermute | solution.py:617
  84.1 4.4 %collective-permute-start.16 = (f32[72,256]{1,0:T(8,128)S(1)}, f32[72,256]{1,0:T(8,128)S(1)}, u32[]{:S(2)}, u32[]{:S(2)}) collective-permute-start(f32[72,256]{1,0:T(8,128)S(1)} %rest_of.1.own_ref), channel_id=1, source_target_pairs={{0,16},{8,24},{16,0},{24,8},{1,17},{9,25},{17,1},{25,9},{2,18},{10... | collective-permute-start | bytes 221192 | tf_op jit(solution)/shard_map/ppermute | solution.py:619
  85.6 3.0 %collective-permute-start.15 = (f32[72,256]{1,0:T(8,128)S(1)}, f32[72,256]{1,0:T(8,128)S(1)}, u32[]{:S(2)}, u32[]{:S(2)}) collective-permute-start(f32[72,256]{1,0:T(8,128)S(1)} %rest_of.1.own_ref), channel_id=1, source_target_pairs={{0,8},{8,0},{16,24},{24,16},{1,9},{9,1},{17,25},{25,17},{2,10},{10... | collective-permute-start | bytes 221192 | tf_op jit(solution)/shard_map/ppermute | solution.py:619
  85.6 14.6 %collective-permute-start.11 = (f32[256,128]{1,0:T(8,128)S(1)}, f32[256,128]{1,0:T(8,128)S(1)}, u32[]{:S(2)}, u32[]{:S(2)}) collective-permute-start(f32[256,128]{1,0:T(8,128)S(1)} %get-tuple-element.27), channel_id=1, source_target_pairs={{0,4},{4,0},{1,5},{5,1},{2,6},{6,2},{3,7},{7,3},{8,12},{12,8},{9,1... | collective-permute-start | bytes 393224 | tf_op jit(solution)/shard_map/ppermute | solution.py:617
  88.5 13.7 %collective-permute-start.10 = (f32[256,128]{1,0:T(8,128)S(1)}, f32[256,128]{1,0:T(8,128)S(1)}, u32[]{:S(2)}, u32[]{:S(2)}) collective-permute-start(f32[256,128]{1,0:T(8,128)S(1)} %get-tuple-element.26), channel_id=1, source_target_pairs={{0,4},{4,0},{1,5},{5,1},{2,6},{6,2},{3,7},{7,3},{8,12},{12,8},{9,1... | collective-permute-start | bytes 393224 | tf_op jit(solution)/shard_map/ppermute | solution.py:617
  88.6 2.4 %collective-permute-start.17 = (f32[72,256]{1,0:T(8,128)S(1)}, f32[72,256]{1,0:T(8,128)S(1)}, u32[]{:S(2)}, u32[]{:S(2)}) collective-permute-start(f32[72,256]{1,0:T(8,128)S(1)} %collective-permute-done.16.x_ref), channel_id=1, source_target_pairs={{0,8},{8,0},{16,24},{24,16},{1,9},{9,1},{17,25},{25,17},{2,10},{10... | collective-permute-start | bytes 221192 | tf_op jit(solution)/shard_map/ppermute | solution.py:619

commit v7 on v6

--- a/solution.py
+++ b/solution.py
@@ -113,7 +113,8 @@
     return first, second
 
 
-def right_gram_kernel(g_ref, after_ref, *out_refs):
+def right_gram_kernel(g_ref, *rest):
+    out_refs = rest[-2:]
     step = pl.program_id(0)
     blk = g_ref.shape[1] // 2
     high, low = split(g_ref[...])
@@ -134,7 +135,7 @@
             ref[blk:, :] = diag
 
 
-def right_grams(tile, blk, flips, after):
+def right_grams(tile, blk, flips, *after):
     rows = tile.shape[0]
     tall = blk + PAD
     flip = lambda s: jnp.where(s == 0, flips[0], flips[1])
@@ -146,14 +147,14 @@
             grid=(2,),
             in_specs=[
                 pl.BlockSpec((rows, 2 * blk), placed(lambda s, place: (0, place[0] ^ flip(s)))),
-                pl.BlockSpec(memory_space=pl.ANY),
-            ],
+            ]
+            + [pl.BlockSpec(memory_space=pl.ANY)] * len(after),
             out_specs=(pl.BlockSpec((tall, blk), lambda s: (0, 0)),) * 2,
         ),
         compiler_params=pltpu.CompilerParams(vmem_limit_bytes=VMEM_LIMIT),
         cost_estimate=SMALL,
         name="right_grams",
-    )(tile, after)
+    )(tile, *after)
 
 
 def left_gram_kernel(g_ref, after_ref, out_ref, lhh, lcross):
@@ -224,33 +225,27 @@
     return jnp.where(place[0] < 2, 4 + k, jnp.where(k < 2, 2 * k, 2 * k + 1))
 
 
-def take_kernel(g_ref, out_ref, sems):
-    rows, wide = out_ref.shape
-    blk = wide // len(RAW)
+def take_kernel(block, g_ref, *rest):
+    out_ref, sem = rest[-2:]
+    rows, blk = out_ref.shape
     top = pl.multiple_of((1 - here()[1]) * rows, rows)
-    copies = [
-        pltpu.make_async_copy(
-            g_ref.at[pl.ds(top, rows), pl.ds(block * blk, blk)], out_ref.at[:, pl.ds(k * blk, blk)], sems.at[k]
-        )
-        for k, block in enumerate(RAW)
-    ]
-    for copy in copies:
-        copy.start()
-    for copy in copies:
-        copy.wait()
-
-
-def take(tile, blk):
-    return pl.pallas_call(
-        take_kernel,
-        out_shape=jax.ShapeDtypeStruct((tile.shape[0] // 2, len(RAW) * blk), jnp.float32),
-        in_specs=[pl.BlockSpec(memory_space=pl.ANY)],
-        out_specs=pl.BlockSpec(memory_space=pl.ANY),
-        scratch_shapes=[pltpu.SemaphoreType.DMA((len(RAW),))],
+    copy = pltpu.make_async_copy(g_ref.at[pl.ds(top, rows), pl.ds(block * blk, blk)], out_ref, sem)
+    copy.start()
+    copy.wait()
+
+
+def take(tile, blk, block, *after):
+    anywhere = pl.BlockSpec(memory_space=pl.ANY)
+    return pl.pallas_call(
+        functools.partial(take_kernel, block),
+        out_shape=jax.ShapeDtypeStruct((tile.shape[0] // 2, blk), jnp.float32),
+        in_specs=[anywhere] * (1 + len(after)),
+        out_specs=anywhere,
+        scratch_shapes=[pltpu.SemaphoreType.DMA],
         compiler_params=pltpu.CompilerParams(vmem_limit_bytes=VMEM_LIMIT),
         cost_estimate=SMALL,
         name="take",
-    )(tile)
+    )(tile, *after)
 
 
 def fold_kernel(a_ref, b_ref, out_ref):
@@ -571,13 +566,13 @@
     )(half, left, out)
 
 
-def update(source, left, right, out, out_shape, g_map, out_map, after=()):
+def update(source, left, right, out, out_shape, g_map, out_map, first=0, count=None, after=()):
     rows = out_shape[0]
     blk = left.shape[-1]
     in_specs = [
         pl.BlockSpec((rows, blk), placed(g_map)),
         pl.BlockSpec((2, 2, blk, blk), lambda s: (0, 0, 0, 0)),
-        pl.BlockSpec((1, 2, blk, blk), lambda s: (s, 0, 0, 0)),
+        pl.BlockSpec((1, 2, blk, blk), lambda s: (first + s, 0, 0, 0)),
     ]
     operands = [source, left, right]
     aliases = {}
@@ -591,7 +586,7 @@
         out_shape=(jax.ShapeDtypeStruct(out_shape, jnp.float32), jax.ShapeDtypeStruct((8, 128), jnp.float32)),
         grid_spec=pltpu.PrefetchScalarGridSpec(
             num_scalar_prefetch=0,
-            grid=(right.shape[0],),
+            grid=(count or right.shape[0],),
             in_specs=in_specs,
             out_specs=(pl.BlockSpec((rows, blk), placed(out_map)), pl.BlockSpec((8, 128), lambda s: (0, 0))),
         ),
@@ -605,7 +600,7 @@
 def exchange_device(full_dim, n_row, grads, left_stats, right_stats):
     tile_rows, tile_cols = grads.shape[1:]
     blk = left_stats.shape[2]
-    tile = pltpu.with_memory_space_constraint(grads.reshape(tile_rows, tile_cols), pltpu.HBM)
+    tile = grads.reshape(tile_rows, tile_cols)
     lstats = left_stats.reshape(tile_rows, blk)
     rstats = right_stats.reshape(tile_cols, blk)
     rows = tile_rows // 2
@@ -618,19 +613,20 @@
         flip = {"core": 1, "x": 2}[axis]
         return lax.ppermute(value, "row", [(i, i ^ flip) for i in range(n_row)])
 
-    first = take(tile, blk)
-    raw = over("y", first)
+    first = take(pltpu.with_memory_space_constraint(tile, pltpu.HBM), blk, RAW[0])
+    raw = [over("y", first)]
 
     send_on, keep_on = right_grams(tile, blk, (3, 2), first)
     far = fold(keep_on, over("core", send_on))
-    send, keep = right_grams(tile, blk, (1, 0), far)
+    raw.append(over("y", take(tile, blk, RAW[1], send_on)))
+    send, keep = right_grams(tile, blk, (1, 0), far, raw[0])
     near = over("core", send)
     far = over("x", far)
 
     own, half = right_roots(full_dim, rstats, keep, near, far, tile)
     came_a = over("y", half)
     lsend = left_grams(tile, blk, lambda place: 1 - place[1], half)
-    own = hold(own, raw, lsend)
+    own = hold(own, raw[1], lsend)
     own_c = over("core", own)
     own_x = over("x", own)
     half = core_apply(tile, own_c, lsend)
@@ -664,12 +660,13 @@
     part = rest_of(came_c, rows)
     part_x = over("x", part)
     roots_raw = join_roots(part, over("core", part), part_x, over("core", part_x))
-    out, done = update(
-        raw, left, roots_raw, out, shape,
-        lambda s, place: (0, s),
-        lambda s, place: (0, (1 - place[1]) * halves + jnp.where(s == 0, RAW[0], RAW[1])),
-        held[:1],
-    )
+    for k, (block, value) in enumerate(zip(RAW, raw)):
+        out, done = update(
+            value, left, roots_raw, out, shape,
+            lambda s, place: (0, 0),
+            lambda s, place, block=block: (0, (1 - place[1]) * halves + block),
+            k, 1, held[:1],
+        )
     for k, value in enumerate((came_c, came_d, came_e)):
         out = finish(value, left, out, crossed(functools.partial(later, k)))
     for (top, tall, start, _), value in zip(last, came_last):

time: 104 us -> 103 us (level)
  Pallas kernels: 54.3 us -> 42.3 us
  waiting for transfers between devices: 31.1 us -> 40.9 us
  starting transfers between devices: 17.4 us -> 19.7 us
    ppermute x9 -> x10, waiting for transfers between devices: 23.6 us -> 30.8 us  [over(): return lax.ppermute(value, 'col', [(0, 1), (1, 0)])]
    pallas_call x4, Pallas kernels: 5.69 us -> 1.52 us  [right_apply(): pl.pallas_call(functools.partial(right_apply_kernel, pieces, under is not...]
    ppermute x9 -> x10, starting transfers between devices: 12 us -> 14.8 us  [over(): return lax.ppermute(value, 'col', [(0, 1), (1, 0)])]
    pallas_call x2, Pallas kernels: 8.45 us -> 5.77 us  [left_grams(): pl.pallas_call(left_gram_kernel, out_shape=jax.ShapeDtypeStruct((tall, bl...]
    pallas_call x2, Pallas kernels: 6.7 us -> 4.08 us  [right_grams(): pl.pallas_call(right_gram_kernel, out_shape=(jax.ShapeDtypeStruct((tall,...]
    ppermute x9, waiting for transfers between devices: 7.5 us -> 10.1 us  [over(): return lax.ppermute(value, 'row', [(i, i ^ flip) for i in range(n_row)])]
    pallas_call x1, Pallas kernels: 1.53 us -> 0.48 us  [core_apply(): pl.pallas_call(core_apply_kernel, out_shape=jax.ShapeDtypeStruct((rows +...]
    pallas_call x2 -> x3, Pallas kernels: 13.8 us -> 13.3 us  [update(): pl.pallas_call(update_kernel, out_shape=(jax.ShapeDtypeStruct(out_shape,...]
  transfers between devices with their start and end apart: 18 -> 19, of which waited for: 9 -> 10; matrix products, arithmetic and copies ran while one was open for 0% -> 0% of each run, Pallas kernels for 50% -> 39%
where the time goes in v7:
time: 103 us
  Pallas kernels  42.3 us (41%)
  waiting for transfers between devices  40.9 us (40%)
  starting transfers between devices  19.7 us (19%)
    ppermute x10, waiting for transfers between devices, over(): return lax.ppermute(value, 'col', [(0, 1), (1, 0)])  30.8 us
    ppermute x10, starting transfers between devices, over(): return lax.ppermute(value, 'col', [(0, 1), (1, 0)])  14.8 us
    pallas_call x3, Pallas kernels, update(): pl.pallas_call(update_kernel, out_shape=(jax.ShapeDtypeStruct(out_shape,...  13.3 us
    ppermute x9, waiting for transfers between devices, over(): return lax.ppermute(value, 'row', [(i, i ^ flip) for i in range(n_row)])  10.1 us
    pallas_call x8, Pallas kernels, finish(): pl.pallas_call(functools.partial(finish_kernel, column, first), out_shape...  8.84 us
    pallas_call x2, Pallas kernels, left_grams(): pl.pallas_call(left_gram_kernel, out_shape=jax.ShapeDtypeStruct((tall, bl...  5.77 us
    ppermute x9, starting transfers between devices, over(): return lax.ppermute(value, 'row', [(i, i ^ flip) for i in range(n_row)])  4.89 us
    pallas_call x2, Pallas kernels, right_grams(): pl.pallas_call(right_gram_kernel, out_shape=(jax.ShapeDtypeStruct((tall,...  4.08 us
  transfers between devices with their start and end apart: 19, of which 10 were waited for; matrix products, arithmetic and copies ran while one was open for 0% of the time, Pallas kernels for 39%

profile of v7, /device:TPU:0, one launch (start us, length us, event | category | flops | bytes accessed | tf_op | source)
XLA Modules:
  0.0 103.3 jit_solution(17652339792585275694)
XLA Ops:
  1.2 3.0 %collective-permute-start.1 = (f32[512,256]{1,0:T(8,128)S(1)}, f32[512,256]{1,0:T(8,128)S(1)}, u32[]{:S(2)}, u32[]{:S(2)}) collective-permute-start(f32[512,256]{1,0:T(8,128)S(1)} %take.2.rest_0_), channel_id=1, source_target_pairs={{0,4},{4,0},{1,5},{5,1},{2,6},{6,2},{3,7},{7,3},{8,12},{12,8},{9,1... | collective-permute-start | bytes 1572872 | tf_op jit(solution)/shard_map/ppermute | solution.py:612
  4.2 2.0 %right_grams.2 = (f32[264,256]{1,0:T(8,128)S(1)}, f32[264,256]{1,0:T(8,128)S(1)}) custom-call(f32[1024,2048]{1,0:T(8,128)S(1)} %bitcast.5, f32[512,256]{1,0:T(8,128)S(1)} %take.2.rest_0_), custom_call_target="tpu_custom_call" | custom-call | flops 1 | bytes 1 | tf_op jit(solution)/shard_map/right_grams/pallas_call | solution.py:142
  6.5 2.3 %collective-permute-start.4 = (f32[512,256]{1,0:T(8,128)S(1)}, f32[512,256]{1,0:T(8,128)S(1)}, u32[]{:S(2)}, u32[]{:S(2)}) collective-permute-start(f32[512,256]{1,0:T(8,128)S(1)} %take.3), channel_id=1, source_target_pairs={{0,4},{4,0},{1,5},{5,1},{2,6},{6,2},{3,7},{7,3},{8,12},{12,8},{9,1... | collective-permute-start | bytes 1572872 | tf_op jit(solution)/shard_map/ppermute | solution.py:612
  8.9 1.6 %collective-permute-start.3 = (f32[264,256]{1,0:T(8,128)S(1)}, f32[264,256]{1,0:T(8,128)S(1)}, u32[]{:S(2)}, u32[]{:S(2)}) collective-permute-start(f32[264,256]{1,0:T(8,128)S(1)} %fold.1.rest_0_), channel_id=1, source_target_pairs={{0,16},{8,24},{16,0},{24,8},{1,17},{9,25},{17,1},{25,9},{2,18},{10... | collective-permute-start | bytes 811016 | tf_op jit(solution)/shard_map/ppermute | solution.py:614
  10.4 6.6 %collective-permute-done.1.rest_1_.g_ref = f32[512,256]{1,0:T(8,128)S(1)} collective-permute-done((f32[512,256]{1,0:T(8,128)S(1)}, f32[512,256]{1,0:T(8,128)S(1)}, u32[]{:S(2)}, u32[]{:S(2)}) %collective-permute-start.1) | collective-permute-done | bytes 524320 | tf_op jit(solution)/shard_map/ppermute | solution.py:612
  17.0 2.0 %right_grams.3 = (f32[264,256]{1,0:T(8,128)S(1)}, f32[264,256]{1,0:T(8,128)S(1)}) custom-call(f32[1024,2048]{1,0:T(8,128)S(1)} %bitcast.7, f32[264,256]{1,0:T(8,128)S(1)} %fold.1.rest_0_, f32[512,256]{1,0:T(8,128)S(1)} %collective-permute-done.1.rest_1_.g_ref), custom_call_target="tpu_custom_call" | custom-call | flops 1 | bytes 1 | tf_op jit(solution)/shard_map/right_grams/pallas_call | solution.py:142
  20.7 3.2 %right_roots.1 = (f32[264,256]{1,0:T(8,128)S(1)}, f32[512,256]{1,0:T(8,128)S(1)}) custom-call(f32[2048,256]{1,0:T(8,128)S(1)} %bitcast.17, f32[264,256]{1,0:T(8,128)S(1)} %get-tuple-element.22.a_ref, f32[264,256]{1,0:T(8,128)S(1)} %collective-permute-done.2.b_ref, f32[264,256]{1,0:T(8,128)S(1)} %collective-permute-done.3.c_ref, f32[1024,2048]{1,0:T(8,128)S(1)} %bitcast.8), custom_call_target="tpu_custom_call" | custom-call | flops 1 | bytes 1 | tf_op jit(solution)/shard_map/right_roots/pallas_call | solution.py:325
  23.9 2.1 %collective-permute-start.7 = (f32[512,256]{1,0:T(8,128)S(1)}, f32[512,256]{1,0:T(8,128)S(1)}, u32[]{:S(2)}, u32[]{:S(2)}) collective-permute-start(f32[512,256]{1,0:T(8,128)S(1)} %get-tuple-element.25.after_ref), channel_id=1, source_target_pairs={{0,4},{4,0},{1,5},{5,1},{2,6},{6,2},{3,7},{7,3},{8,12},{12,8},{9,1... | collective-permute-start | bytes 1572872 | tf_op jit(solution)/shard_map/ppermute | solution.py:612
  26.0 2.9 %left_grams.2.rest_1_.under_ref = f32[264,256]{1,0:T(8,128)S(1)} custom-call(f32[1024,2048]{1,0:T(8,128)S(1)} %bitcast.9, f32[512,256]{1,0:T(8,128)S(1)} %get-tuple-element.25.after_ref), custom_call_target="tpu_custom_call" | custom-call | flops 1 | bytes 1 | tf_op jit(solution)/shard_map/left_grams/pallas_call | solution.py:191
  29.0 1.6 %collective-permute-start.6 = (f32[264,256]{1,0:T(8,128)S(1)}, f32[264,256]{1,0:T(8,128)S(1)}, u32[]{:S(2)}, u32[]{:S(2)}) collective-permute-start(f32[264,256]{1,0:T(8,128)S(1)} %hold.2.own_ref), channel_id=1, source_target_pairs={{0,16},{8,24},{16,0},{24,8},{1,17},{9,25},{17,1},{25,9},{2,18},{10... | collective-permute-start | bytes 811016 | tf_op jit(solution)/shard_map/ppermute | solution.py:614
  31.7 6.2 %collective-permute-done.6.a_ref = f32[264,256]{1,0:T(8,128)S(1)} collective-permute-done((f32[264,256]{1,0:T(8,128)S(1)}, f32[264,256]{1,0:T(8,128)S(1)}, u32[]{:S(2)}, u32[]{:S(2)}) %collective-permute-start.6) | collective-permute-done | bytes 270368 | tf_op jit(solution)/shard_map/ppermute | solution.py:614
  39.1 2.9 %left_grams.3.a_ref.rest_1_ = f32[264,256]{1,0:T(8,128)S(1)} custom-call(f32[1024,2048]{1,0:T(8,128)S(1)} %bitcast.11, f32[776,256]{1,0:T(8,128)S(1)} %core_apply.1.rest_0_.after_ref), custom_call_target="tpu_custom_call" | custom-call | flops 1 | bytes 1 | tf_op jit(solution)/shard_map/left_grams/pallas_call | solution.py:191
  42.9 1.9 %collective-permute-start.14 = (f32[584,256]{1,0:T(8,128)S(1)}, f32[584,256]{1,0:T(8,128)S(1)}, u32[]{:S(2)}, u32[]{:S(2)}) collective-permute-start(f32[584,256]{1,0:T(8,128)S(1)} %right_apply.6), channel_id=1, source_target_pairs={{0,4},{4,0},{1,5},{5,1},{2,6},{6,2},{3,7},{7,3},{8,12},{12,8},{9,1... | collective-permute-start | bytes 1794056 | tf_op jit(solution)/shard_map/ppermute | solution.py:612
  44.8 11.2 %collective-permute-done.9.rest_0_.b_ref.half_ref = f32[776,256]{1,0:T(8,128)S(1)} collective-permute-done((f32[776,256]{1,0:T(8,128)S(1)}, f32[776,256]{1,0:T(8,128)S(1)}, u32[]{:S(2)}, u32[]{:S(2)}) %collective-permute-start.9) | collective-permute-done | bytes 794656 | tf_op jit(solution)/shard_map/ppermute | solution.py:612
  56.4 1.8 %collective-permute-start.10 = (f32[512,256]{1,0:T(8,128)S(1)}, f32[512,256]{1,0:T(8,128)S(1)}, u32[]{:S(2)}, u32[]{:S(2)}) collective-permute-start(f32[512,256]{1,0:T(8,128)S(1)} %right_apply.4), channel_id=1, source_target_pairs={{0,4},{4,0},{1,5},{5,1},{2,6},{6,2},{3,7},{7,3},{8,12},{12,8},{9,1... | collective-permute-start | bytes 1572872 | tf_op jit(solution)/shard_map/ppermute | solution.py:612
  58.2 3.0 %left_roots.1.left_ref = bf16[2,2,256,256]{3,2,1,0:T(8,128)(2,1)S(1)} custom-call(f32[1024,256]{1,0:T(8,128)S(1)} %bitcast.18, f32[264,256]{1,0:T(8,128)S(1)} %left_grams.3.a_ref.rest_1_, f32[776,256]{1,0:T(8,128)S(1)} %collective-permute-done.9.rest_0_.b_ref.half_ref), custom_call_target="tpu_custom_call" | custom-call | flops 1 | bytes 1 | tf_op jit(solution)/shard_map/left_roots/pallas_call | solution.py:364
  61.2 9.7 %update.3 = (f32[512,4096]{1,0:T(8,128)}, f32[8,128]{1,0:T(8,128)S(1)}) custom-call(f32[1024,2048]{1,0:T(8,128)S(1)} %bitcast.14, bf16[2,2,256,256]{3,2,1,0:T(8,128)(2,1)S(1)} %left_roots.1.left_ref, bf16[8,2,256,256]{3,2,1,0:T(8,128)(2,1)S(1)} %get-tuple-element.26.right_ref), custom_call_target="tpu_custom_call" | custom-call | flops 1 | bytes 1 | tf_op jit(solution)/shard_map/update/pallas_call | solution.py:584
  71.6 8.4 %collective-permute-done.10.rest_0_.half_ref = f32[512,256]{1,0:T(8,128)S(1)} collective-permute-done((f32[512,256]{1,0:T(8,128)S(1)}, f32[512,256]{1,0:T(8,128)S(1)}, u32[]{:S(2)}, u32[]{:S(2)}) %collective-permute-start.10) | collective-permute-done | bytes 524320 | tf_op jit(solution)/shard_map/ppermute | solution.py:612
  80.5 1.8 %collective-permute-start.13 = (f32[512,128]{1,0:T(8,128)S(1)}, f32[512,128]{1,0:T(8,128)S(1)}, u32[]{:S(2)}, u32[]{:S(2)}) collective-permute-start(f32[512,128]{1,0:T(8,128)S(1)} %get-tuple-element.29.rest_1_), channel_id=1, source_target_pairs={{0,4},{4,0},{1,5},{5,1},{2,6},{6,2},{3,7},{7,3},{8,12},{12,8},{9,1... | collective-permute-start | bytes 786440 | tf_op jit(solution)/shard_map/ppermute | solution.py:612
  84.3 2.3 %collective-permute-done.17.x_ref = f32[72,256]{1,0:T(8,128)S(1)} collective-permute-done((f32[72,256]{1,0:T(8,128)S(1)}, f32[72,256]{1,0:T(8,128)S(1)}, u32[]{:S(2)}, u32[]{:S(2)}) %collective-permute-start.17) | collective-permute-done | bytes 73760 | tf_op jit(solution)/shard_map/ppermute | solution.py:614
  89.5 1.8 %update.4 = (f32[512,4096]{1,0:T(8,128)}, f32[8,128]{1,0:T(8,128)}) custom-call(f32[512,256]{1,0:T(8,128)S(1)} %collective-permute-done.1.rest_1_.g_ref, bf16[2,2,256,256]{3,2,1,0:T(8,128)(2,1)S(1)} %left_roots.1.left_ref, bf16[2,2,256,256]{3,2,1,0:T(8,128)(2,1)S(1)} %join_roots.1.right_ref, ...), custom_call_target="tpu_custom_call", output_to_operand_aliasing={{0}: (3, {})} | custom-call | flops 1 | bytes 1 | tf_op jit(solution)/shard_map/update/pallas_call | solution.py:584
  91.3 1.8 %update.5 = (f32[512,4096]{1,0:T(8,128)}, f32[8,128]{1,0:T(8,128)}) custom-call(f32[512,256]{1,0:T(8,128)S(1)} %collective-permute-done.4.rest_0_.g_ref, bf16[2,2,256,256]{3,2,1,0:T(8,128)(2,1)S(1)} %left_roots.1.left_ref, bf16[2,2,256,256]{3,2,1,0:T(8,128)(2,1)S(1)} %join_roots.1.right_ref, ...), custom_call_target="tpu_custom_call", output_to_operand_aliasing={{0}: (3, {})} | custom-call | flops 1 | bytes 1 | tf_op jit(solution)/shard_map/update/pallas_call | solution.py:584
  98.0 1.8 %collective-permute-done.12.half_ref = f32[256,128]{1,0:T(8,128)S(1)} collective-permute-done((f32[256,128]{1,0:T(8,128)S(1)}, f32[256,128]{1,0:T(8,128)S(1)}, u32[]{:S(2)}, u32[]{:S(2)}) %collective-permute-start.12) | collective-permute-done | bytes 131104 | tf_op jit(solution)/shard_map/ppermute | solution.py:612
  100.7 1.5 %collective-permute-done.11.half_ref = f32[256,128]{1,0:T(8,128)S(1)} collective-permute-done((f32[256,128]{1,0:T(8,128)S(1)}, f32[256,128]{1,0:T(8,128)S(1)}, u32[]{:S(2)}, u32[]{:S(2)}) %collective-permute-start.11) | collective-permute-done | bytes 131104 | tf_op jit(solution)/shard_map/ppermute | solution.py:612
  (50 shorter events, 19.3 us)
Async XLA Ops:
  0.0 4.2 %copy-start = (f32[1,1024,2048]{2,1,0:T(8,128)S(1)}, f32[1,1024,2048]{2,1,0:T(8,128)}, u32[]{:S(2)}) copy-start(f32[1,1024,2048]{2,1,0:T(8,128)} %param.3) | copy-start | bytes 25165828
  1.2 15.8 %collective-permute-start.1 = (f32[512,256]{1,0:T(8,128)S(1)}, f32[512,256]{1,0:T(8,128)S(1)}, u32[]{:S(2)}, u32[]{:S(2)}) collective-permute-start(f32[512,256]{1,0:T(8,128)S(1)} %take.2.rest_0_), channel_id=1, source_target_pairs={{0,4},{4,0},{1,5},{5,1},{2,6},{6,2},{3,7},{7,3},{8,12},{12,8},{9,1... | collective-permute-start | bytes 1572872 | tf_op jit(solution)/shard_map/ppermute | solution.py:612
  6.3 14.4 %copy-start.1 = (f32[1,2048,256]{2,1,0:T(8,128)S(1)}, f32[1,2048,256]{2,1,0:T(8,128)}, u32[]{:S(2)}) copy-start(f32[1,2048,256]{2,1,0:T(8,128)} %param.5) | copy-start | bytes 6291460
  6.3 2.5 %collective-permute-start = (f32[264,256]{1,0:T(8,128)S(1)}, f32[264,256]{1,0:T(8,128)S(1)}, u32[]{:S(2)}, u32[]{:S(2)}) collective-permute-start(f32[264,256]{1,0:T(8,128)S(1)} %get-tuple-element.21.rest_0_), channel_id=1, source_target_pairs={{0,8},{8,0},{16,24},{24,16},{1,9},{9,1},{17,25},{25,17},{2,10},{10... | collective-permute-start | bytes 811016 | tf_op jit(solution)/shard_map/ppermute | solution.py:614
  6.5 22.4 %collective-permute-start.4 = (f32[512,256]{1,0:T(8,128)S(1)}, f32[512,256]{1,0:T(8,128)S(1)}, u32[]{:S(2)}, u32[]{:S(2)}) collective-permute-start(f32[512,256]{1,0:T(8,128)S(1)} %take.3), channel_id=1, source_target_pairs={{0,4},{4,0},{1,5},{5,1},{2,6},{6,2},{3,7},{7,3},{8,12},{12,8},{9,1... | collective-permute-start | bytes 1572872 | tf_op jit(solution)/shard_map/ppermute | solution.py:612
  8.9 10.3 %collective-permute-start.3 = (f32[264,256]{1,0:T(8,128)S(1)}, f32[264,256]{1,0:T(8,128)S(1)}, u32[]{:S(2)}, u32[]{:S(2)}) collective-permute-start(f32[264,256]{1,0:T(8,128)S(1)} %fold.1.rest_0_), channel_id=1, source_target_pairs={{0,16},{8,24},{16,0},{24,8},{1,17},{9,25},{17,1},{25,9},{2,18},{10... | collective-permute-start | bytes 811016 | tf_op jit(solution)/shard_map/ppermute | solution.py:614
  19.0 1.6 %collective-permute-start.2 = (f32[264,256]{1,0:T(8,128)S(1)}, f32[264,256]{1,0:T(8,128)S(1)}, u32[]{:S(2)}, u32[]{:S(2)}) collective-permute-start(f32[264,256]{1,0:T(8,128)S(1)} %get-tuple-element.23), channel_id=1, source_target_pairs={{0,8},{8,0},{16,24},{24,16},{1,9},{9,1},{17,25},{25,17},{2,10},{10... | collective-permute-start | bytes 811016 | tf_op jit(solution)/shard_map/ppermute | solution.py:614
  23.9 15.1 %collective-permute-start.7 = (f32[512,256]{1,0:T(8,128)S(1)}, f32[512,256]{1,0:T(8,128)S(1)}, u32[]{:S(2)}, u32[]{:S(2)}) collective-permute-start(f32[512,256]{1,0:T(8,128)S(1)} %get-tuple-element.25.after_ref), channel_id=1, source_target_pairs={{0,4},{4,0},{1,5},{5,1},{2,6},{6,2},{3,7},{7,3},{8,12},{12,8},{9,1... | collective-permute-start | bytes 1572872 | tf_op jit(solution)/shard_map/ppermute | solution.py:612
  28.9 1.6 %collective-permute-start.5 = (f32[264,256]{1,0:T(8,128)S(1)}, f32[264,256]{1,0:T(8,128)S(1)}, u32[]{:S(2)}, u32[]{:S(2)}) collective-permute-start(f32[264,256]{1,0:T(8,128)S(1)} %hold.2.own_ref), channel_id=1, source_target_pairs={{0,8},{8,0},{16,24},{24,16},{1,9},{9,1},{17,25},{25,17},{2,10},{10... | collective-permute-start | bytes 811016 | tf_op jit(solution)/shard_map/ppermute | solution.py:614
  29.0 8.9 %collective-permute-start.6 = (f32[264,256]{1,0:T(8,128)S(1)}, f32[264,256]{1,0:T(8,128)S(1)}, u32[]{:S(2)}, u32[]{:S(2)}) collective-permute-start(f32[264,256]{1,0:T(8,128)S(1)} %hold.2.own_ref), channel_id=1, source_target_pairs={{0,16},{8,24},{16,0},{24,8},{1,17},{9,25},{17,1},{25,9},{2,18},{10... | collective-permute-start | bytes 811016 | tf_op jit(solution)/shard_map/ppermute | solution.py:614
  31.0 25.0 %collective-permute-start.9 = (f32[776,256]{1,0:T(8,128)S(1)}, f32[776,256]{1,0:T(8,128)S(1)}, u32[]{:S(2)}, u32[]{:S(2)}) collective-permute-start(f32[776,256]{1,0:T(8,128)S(1)} %core_apply.1.rest_0_.after_ref), channel_id=1, source_target_pairs={{0,4},{4,0},{1,5},{5,1},{2,6},{6,2},{3,7},{7,3},{8,12},{12,8},{9,1... | collective-permute-start | bytes 2383880 | tf_op jit(solution)/shard_map/ppermute | solution.py:612
  39.0 3.0 %collective-permute-start.8 = (f32[264,256]{1,0:T(8,128)S(1)}, f32[264,256]{1,0:T(8,128)S(1)}, u32[]{:S(2)}, u32[]{:S(2)}) collective-permute-start(f32[264,256]{1,0:T(8,128)S(1)} %hold.3.x_ref), channel_id=1, source_target_pairs={{0,8},{8,0},{16,24},{24,16},{1,9},{9,1},{17,25},{25,17},{2,10},{10... | collective-permute-start | bytes 811016 | tf_op jit(solution)/shard_map/ppermute | solution.py:614
  42.9 15.3 %copy-start.2 = (f32[1,1024,256]{2,1,0:T(8,128)S(1)}, f32[1,1024,256]{2,1,0:T(8,128)}, u32[]{:S(2)}) copy-start(f32[1,1024,256]{2,1,0:T(8,128)} %param.4) | copy-start | bytes 3145732
  42.9 28.0 %collective-permute-start.14 = (f32[584,256]{1,0:T(8,128)S(1)}, f32[584,256]{1,0:T(8,128)S(1)}, u32[]{:S(2)}, u32[]{:S(2)}) collective-permute-start(f32[584,256]{1,0:T(8,128)S(1)} %right_apply.6), channel_id=1, source_target_pairs={{0,4},{4,0},{1,5},{5,1},{2,6},{6,2},{3,7},{7,3},{8,12},{12,8},{9,1... | collective-permute-start | bytes 1794056 | tf_op jit(solution)/shard_map/ppermute | solution.py:612
  56.4 23.7 %collective-permute-start.10 = (f32[512,256]{1,0:T(8,128)S(1)}, f32[512,256]{1,0:T(8,128)S(1)}, u32[]{:S(2)}, u32[]{:S(2)}) collective-permute-start(f32[512,256]{1,0:T(8,128)S(1)} %right_apply.4), channel_id=1, source_target_pairs={{0,4},{4,0},{1,5},{5,1},{2,6},{6,2},{3,7},{7,3},{8,12},{12,8},{9,1... | collective-permute-start | bytes 1572872 | tf_op jit(solution)/shard_map/ppermute | solution.py:612
  71.3 24.2 %collective-permute-start.15 = (f32[512,256]{1,0:T(8,128)S(1)}, f32[512,256]{1,0:T(8,128)S(1)}, u32[]{:S(2)}, u32[]{:S(2)}) collective-permute-start(f32[512,256]{1,0:T(8,128)S(1)} %right_apply.7), channel_id=1, source_target_pairs={{0,4},{4,0},{1,5},{5,1},{2,6},{6,2},{3,7},{7,3},{8,12},{12,8},{9,1... | collective-permute-start | bytes 1572872 | tf_op jit(solution)/shard_map/ppermute | solution.py:612
  80.5 16.5 %collective-permute-start.13 = (f32[512,128]{1,0:T(8,128)S(1)}, f32[512,128]{1,0:T(8,128)S(1)}, u32[]{:S(2)}, u32[]{:S(2)}) collective-permute-start(f32[512,128]{1,0:T(8,128)S(1)} %get-tuple-element.29.rest_1_), channel_id=1, source_target_pairs={{0,4},{4,0},{1,5},{5,1},{2,6},{6,2},{3,7},{7,3},{8,12},{12,8},{9,1... | collective-permute-start | bytes 786440 | tf_op jit(solution)/shard_map/ppermute | solution.py:612
  82.3 4.4 %collective-permute-start.17 = (f32[72,256]{1,0:T(8,128)S(1)}, f32[72,256]{1,0:T(8,128)S(1)}, u32[]{:S(2)}, u32[]{:S(2)}) collective-permute-start(f32[72,256]{1,0:T(8,128)S(1)} %rest_of.1.own_ref), channel_id=1, source_target_pairs={{0,16},{8,24},{16,0},{24,8},{1,17},{9,25},{17,1},{25,9},{2,18},{10... | collective-permute-start | bytes 221192 | tf_op jit(solution)/shard_map/ppermute | solution.py:614
  83.8 3.1 %collective-permute-start.16 = (f32[72,256]{1,0:T(8,128)S(1)}, f32[72,256]{1,0:T(8,128)S(1)}, u32[]{:S(2)}, u32[]{:S(2)}) collective-permute-start(f32[72,256]{1,0:T(8,128)S(1)} %rest_of.1.own_ref), channel_id=1, source_target_pairs={{0,8},{8,0},{16,24},{24,16},{1,9},{9,1},{17,25},{25,17},{2,10},{10... | collective-permute-start | bytes 221192 | tf_op jit(solution)/shard_map/ppermute | solution.py:614
  83.8 15.9 %collective-permute-start.12 = (f32[256,128]{1,0:T(8,128)S(1)}, f32[256,128]{1,0:T(8,128)S(1)}, u32[]{:S(2)}, u32[]{:S(2)}) collective-permute-start(f32[256,128]{1,0:T(8,128)S(1)} %get-tuple-element.28), channel_id=1, source_target_pairs={{0,4},{4,0},{1,5},{5,1},{2,6},{6,2},{3,7},{7,3},{8,12},{12,8},{9,1... | collective-permute-start | bytes 393224 | tf_op jit(solution)/shard_map/ppermute | solution.py:612
  86.6 15.5 %collective-permute-start.11 = (f32[256,128]{1,0:T(8,128)S(1)}, f32[256,128]{1,0:T(8,128)S(1)}, u32[]{:S(2)}, u32[]{:S(2)}) collective-permute-start(f32[256,128]{1,0:T(8,128)S(1)} %get-tuple-element.27), channel_id=1, source_target_pairs={{0,4},{4,0},{1,5},{5,1},{2,6},{6,2},{3,7},{7,3},{8,12},{12,8},{9,1... | collective-permute-start | bytes 393224 | tf_op jit(solution)/shard_map/ppermute | solution.py:612
  86.9 2.4 %collective-permute-start.18 = (f32[72,256]{1,0:T(8,128)S(1)}, f32[72,256]{1,0:T(8,128)S(1)}, u32[]{:S(2)}, u32[]{:S(2)}) collective-permute-start(f32[72,256]{1,0:T(8,128)S(1)} %collective-permute-done.17.x_ref), channel_id=1, source_target_pairs={{0,8},{8,0},{16,24},{24,16},{1,9},{9,1},{17,25},{25,17},{2,10},{10... | collective-permute-start | bytes 221192 | tf_op jit(solution)/shard_map/ppermute | solution.py:614

commit v8 on v7

--- a/solution.py
+++ b/solution.py
@@ -113,9 +113,18 @@
     return first, second
 
 
-def right_gram_kernel(g_ref, *rest):
-    out_refs = rest[-2:]
+def put_packed(refs, body, diag):
+    at = 0
+    for ref in refs:
+        rows = min(ref.shape[0], body.shape[0] - at)
+        ref[:rows, :] = body[at : at + rows, :]
+        at += rows
+    refs[-1][refs[-1].shape[0] - PAD :, :] = diag
+
+
+def right_gram_kernel(parts, g_ref, *rest):
     step = pl.program_id(0)
+    out_refs = rest[-1 - parts :]
     blk = g_ref.shape[1] // 2
     high, low = split(g_ref[...])
     grams = []
@@ -126,30 +135,28 @@
         cross = dot(hb, lb, ((0,), (0,)))
         grams.append(both + (cross + cross.T))
     body, diag = pack(*grams)
-
-    for at, ref in enumerate(out_refs):
+    for at, refs in enumerate((out_refs[:parts], out_refs[parts:])):
 
         @pl.when(step == at)
         def _():
-            ref[:blk, :] = body
-            ref[blk:, :] = diag
-
-
-def right_grams(tile, blk, flips, *after):
+            put_packed(refs, body, diag)
+
+
+def right_grams(tile, blk, flips, parts, *after):
     rows = tile.shape[0]
     tall = blk + PAD
     flip = lambda s: jnp.where(s == 0, flips[0], flips[1])
-    return pl.pallas_call(
-        right_gram_kernel,
-        out_shape=(jax.ShapeDtypeStruct((tall, blk), jnp.float32),) * 2,
+    sizes = ((tall + PAD) // 2, (tall - PAD) // 2) if parts == 2 else (tall,)
+    sizes += (tall,)
+    return pl.pallas_call(
+        functools.partial(right_gram_kernel, parts),
+        out_shape=tuple(jax.ShapeDtypeStruct((size, blk), jnp.float32) for size in sizes),
         grid_spec=pltpu.PrefetchScalarGridSpec(
             num_scalar_prefetch=0,
             grid=(2,),
-            in_specs=[
-                pl.BlockSpec((rows, 2 * blk), placed(lambda s, place: (0, place[0] ^ flip(s)))),
-            ]
+            in_specs=[pl.BlockSpec((rows, 2 * blk), placed(lambda s, place: (0, place[0] ^ flip(s))))]
             + [pl.BlockSpec(memory_space=pl.ANY)] * len(after),
-            out_specs=(pl.BlockSpec((tall, blk), lambda s: (0, 0)),) * 2,
+            out_specs=tuple(pl.BlockSpec((size, blk), lambda s: (0, 0)) for size in sizes),
         ),
         compiler_params=pltpu.CompilerParams(vmem_limit_bytes=VMEM_LIMIT),
         cost_estimate=SMALL,
@@ -210,7 +217,7 @@
     )(tile, after)
 
 
-RAW = (1, 3)
+RAW = 1
 
 
 def own_first(place):
@@ -222,7 +229,7 @@
 
 
 def later(k, place):
-    return jnp.where(place[0] < 2, 4 + k, jnp.where(k < 2, 2 * k, 2 * k + 1))
+    return jnp.where(place[0] < 2, 3 + k, jnp.where(k == 0, 0, jnp.where(k < 3, k + 1, 2 * k - 1)))
 
 
 def take_kernel(block, g_ref, *rest):
@@ -248,18 +255,40 @@
     )(tile, *after)
 
 
-def fold_kernel(a_ref, b_ref, out_ref):
-    out_ref[...] = a_ref[...] + b_ref[...]
-
-
-def fold(kept, near):
+def fold_kernel(a_ref, top_ref, rest_ref, after_ref, out_ref):
+    top = top_ref.shape[0]
+    out_ref[:top, :] = a_ref[:top, :] + top_ref[...]
+    out_ref[top:, :] = a_ref[top:, :] + rest_ref[...]
+
+
+def fold(kept, top, rest, after):
     return pl.pallas_call(
         fold_kernel,
         out_shape=jax.ShapeDtypeStruct(kept.shape, jnp.float32),
+        in_specs=[pl.BlockSpec(memory_space=pltpu.VMEM)] * 3 + [pl.BlockSpec(memory_space=pl.ANY)],
         compiler_params=pltpu.CompilerParams(vmem_limit_bytes=VMEM_LIMIT),
         cost_estimate=SMALL,
         name="fold",
-    )(kept, near)
+    )(kept, top, rest, after)
+
+
+def halve_kernel(a_ref, *rest):
+    top_ref, rest_ref = rest[-2:]
+    top_ref[...] = a_ref[: top_ref.shape[0], :]
+    rest_ref[...] = a_ref[top_ref.shape[0] :, :]
+
+
+def halve(value, *after):
+    tall, blk = value.shape
+    sizes = ((tall + PAD) // 2, (tall - PAD) // 2)
+    return pl.pallas_call(
+        halve_kernel,
+        out_shape=tuple(jax.ShapeDtypeStruct((size, blk), jnp.float32) for size in sizes),
+        in_specs=[pl.BlockSpec(memory_space=pltpu.VMEM)] + [pl.BlockSpec(memory_space=pl.ANY)] * len(after),
+        compiler_params=pltpu.CompilerParams(vmem_limit_bytes=VMEM_LIMIT),
+        cost_estimate=SMALL,
+        name="halve",
+    )(value, *after)
 
 
 def hold_kernel(a_ref, *rest):
@@ -307,9 +336,9 @@
     return [r * jnp.exp(-0.25 * jnp.log(s)) for r, s in zip(result, scales)]
 
 
-def right_kernel(full_dim, stats_ref, a_ref, b_ref, c_ref, g_ref, out_ref, half_ref):
+def right_kernel(full_dim, stats_ref, a_ref, top_ref, rest_ref, c_ref, g_ref, after_ref, out_ref, half_ref):
     blk = stats_ref.shape[1]
-    total = a_ref[...] + b_ref[...] + c_ref[...]
+    total = a_ref[...] + jnp.concatenate([top_ref[...], rest_ref[...]], axis=0) + c_ref[...]
     roots = pair_roots(full_dim, stats_ref, total[:blk], total[blk : blk + 1])
     half_ref[...] = product(split(g_ref[...]), split(roots[0]))
     body, diag = pack(*roots)
@@ -317,7 +346,7 @@
     out_ref[blk:, :] = diag
 
 
-def right_roots(full_dim, stats, kept, near, far, tile):
+def right_roots(full_dim, stats, kept, near, far, tile, after):
     blk = stats.shape[1]
     tall = blk + PAD
     rows = tile.shape[0] // 2
@@ -334,9 +363,10 @@
             in_specs=[
                 pl.BlockSpec((2 * blk, blk), placed(lambda s, place: (place[0], 0))),
                 flat,
-                flat,
+                *(pl.BlockSpec(part.shape, lambda s: (0, 0)) for part in near),
                 flat,
                 pl.BlockSpec((rows, blk), placed(lambda s, place: (1 - place[1], own_first(place)))),
+                pl.BlockSpec(memory_space=pl.ANY),
             ],
             out_specs=(
                 flat,
@@ -346,7 +376,7 @@
         compiler_params=pltpu.CompilerParams(vmem_limit_bytes=VMEM_LIMIT),
         cost_estimate=SMALL,
         name="right_roots",
-    )(stats, kept, near, far, tile)
+    )(stats, kept, *near, far, tile, after)
 
 
 def left_kernel(full_dim, stats_ref, a_ref, b_ref, out_ref):
@@ -387,29 +417,33 @@
         out_ref[at + b, 1] = low
 
 
-def spread_kernel(own_ref, c_ref, x_ref, xc_ref, out_ref, cut_ref, seconds, body):
+def spread_kernel(own_ref, c_ref, x_ref, top_ref, rest_ref, out_ref, cut_ref, seconds, body):
     blk = out_ref.shape[-1]
+    half = blk // 2
     r = here()[0]
-    for flip, ref in enumerate((own_ref, c_ref, x_ref, xc_ref)):
-        roots = unpack(ref[:blk, :], ref[blk : blk + 1, :])
+    last = jnp.concatenate([top_ref[...], rest_ref[...]], axis=0)
+    for flip, packed in enumerate((own_ref[...], c_ref[...], x_ref[...], last)):
+        roots = unpack(packed[:blk, :], packed[blk : blk + 1, :])
         put_roots(out_ref, 2 * (r ^ flip), roots)
         seconds[r ^ flip] = roots[1]
+    root = seconds[RAW // 2]
+    pair, diag = pack(root[:half, :half], root[half:, half:])
+    body[...] = jnp.concatenate([pair, root[:half, half:]], axis=1)
     part = cut_ref.shape[0] - PAD
-    body[...], diag = pack(seconds[RAW[0] // 2], seconds[RAW[1] // 2])
     cut_ref[:part, :] = body[pl.ds(pl.multiple_of(r * part, part), part), :]
-    cut_ref[part:, :] = diag
+    cut_ref[part:, :] = jnp.concatenate([diag, diag], axis=1)
 
 
 def spread_roots(*packed):
     blk = packed[0].shape[1]
-    count = len(packed)
+    count = len(packed) - 1
     return pl.pallas_call(
         spread_kernel,
         out_shape=(
             jax.ShapeDtypeStruct((2 * count, 2, blk, blk), jnp.bfloat16),
-            jax.ShapeDtypeStruct((blk // count + PAD, blk), jnp.float32),
-        ),
-        scratch_shapes=[pltpu.VMEM((count, blk, blk), jnp.float32), pltpu.VMEM((blk, blk), jnp.float32)],
+            jax.ShapeDtypeStruct((blk // (2 * count) + PAD, blk), jnp.float32),
+        ),
+        scratch_shapes=[pltpu.VMEM((count, blk, blk), jnp.float32), pltpu.VMEM((blk // 2, blk), jnp.float32)],
         compiler_params=pltpu.CompilerParams(vmem_limit_bytes=VMEM_LIMIT),
         cost_estimate=SMALL,
         name="spread_roots",
@@ -432,51 +466,54 @@
 
 def join_kernel(own_ref, c_ref, x_ref, xc_ref, out_ref, body):
     part = own_ref.shape[0] - PAD
+    half = body.shape[0]
     r = here()[0]
     for flip, ref in enumerate((own_ref, c_ref, x_ref, xc_ref)):
         body[pl.ds(pl.multiple_of((r ^ flip) * part, part), part), :] = ref[:part, :]
-    put_roots(out_ref, 0, unpack(body[...], own_ref[part : part + 1, :]))
-
-
-def join_roots(*parts):
+    first, second = unpack(body[:, :half], own_ref[part : part + 1, :half])
+    side = body[:, half:]
+    top = jnp.concatenate([first, side], axis=1)
+    bottom = jnp.concatenate([side.T, second], axis=1)
+    put_roots(out_ref, 0, [jnp.concatenate([top, bottom], axis=0)])
+
+
+def join_root(*parts):
     blk = parts[0].shape[1]
     return pl.pallas_call(
         join_kernel,
-        out_shape=jax.ShapeDtypeStruct((2, 2, blk, blk), jnp.bfloat16),
-        scratch_shapes=[pltpu.VMEM((blk, blk), jnp.float32)],
-        compiler_params=pltpu.CompilerParams(vmem_limit_bytes=VMEM_LIMIT),
-        cost_estimate=SMALL,
-        name="join_roots",
+        out_shape=jax.ShapeDtypeStruct((1, 2, blk, blk), jnp.bfloat16),
+        scratch_shapes=[pltpu.VMEM((blk // 2, blk), jnp.float32)],
+        compiler_params=pltpu.CompilerParams(vmem_limit_bytes=VMEM_LIMIT),
+        cost_estimate=SMALL,
+        name="join_root",
     )(*parts)
 
 
-def core_apply_kernel(g_ref, packed_ref, under_ref, out_ref):
-    rows, blk = g_ref.shape
+def core_apply_kernel(g_ref, packed_ref, out_ref):
+    blk = g_ref.shape[1]
     root = unpack(packed_ref[:blk, :], packed_ref[blk : blk + 1, :])[0]
-    out_ref[:rows, :] = product(split(g_ref[...]), split(root))
-    out_ref[rows:, :] = under_ref[...]
-
-
-def core_apply(tile, packed, under):
+    out_ref[...] = product(split(g_ref[...]), split(root))
+
+
+def core_apply(tile, packed):
     rows = tile.shape[0] // 2
     tall, blk = packed.shape
     return pl.pallas_call(
         core_apply_kernel,
-        out_shape=jax.ShapeDtypeStruct((rows + tall, blk), jnp.float32),
+        out_shape=jax.ShapeDtypeStruct((rows, blk), jnp.float32),
         grid_spec=pltpu.PrefetchScalarGridSpec(
             num_scalar_prefetch=0,
             grid=(1,),
             in_specs=[
                 pl.BlockSpec((rows, blk), placed(lambda s, place: (1 - place[1], core_first(place)))),
                 pl.BlockSpec((tall, blk), lambda s: (0, 0)),
-                pl.BlockSpec((tall, blk), lambda s: (0, 0)),
             ],
-            out_specs=pl.BlockSpec((rows + tall, blk), lambda s: (0, 0)),
+            out_specs=pl.BlockSpec((rows, blk), lambda s: (0, 0)),
         ),
         compiler_params=pltpu.CompilerParams(vmem_limit_bytes=VMEM_LIMIT),
         cost_estimate=SMALL,
         name="core_apply",
-    )(tile, packed, under)
+    )(tile, packed)
 
 
 def right_apply_kernel(pieces, carries, g_ref, right_ref, *rest):
@@ -566,13 +603,13 @@
     )(half, left, out)
 
 
-def update(source, left, right, out, out_shape, g_map, out_map, first=0, count=None, after=()):
+def update(source, left, right, out, out_shape, g_map, out_map, after=()):
     rows = out_shape[0]
     blk = left.shape[-1]
     in_specs = [
         pl.BlockSpec((rows, blk), placed(g_map)),
         pl.BlockSpec((2, 2, blk, blk), lambda s: (0, 0, 0, 0)),
-        pl.BlockSpec((1, 2, blk, blk), lambda s: (first + s, 0, 0, 0)),
+        pl.BlockSpec((1, 2, blk, blk), lambda s: (s, 0, 0, 0)),
     ]
     operands = [source, left, right]
     aliases = {}
@@ -586,7 +623,7 @@
         out_shape=(jax.ShapeDtypeStruct(out_shape, jnp.float32), jax.ShapeDtypeStruct((8, 128), jnp.float32)),
         grid_spec=pltpu.PrefetchScalarGridSpec(
             num_scalar_prefetch=0,
-            grid=(count or right.shape[0],),
+            grid=(right.shape[0],),
             in_specs=in_specs,
             out_specs=(pl.BlockSpec((rows, blk), placed(out_map)), pl.BlockSpec((8, 128), lambda s: (0, 0))),
         ),
@@ -613,37 +650,37 @@
         flip = {"core": 1, "x": 2}[axis]
         return lax.ppermute(value, "row", [(i, i ^ flip) for i in range(n_row)])
 
-    first = take(pltpu.with_memory_space_constraint(tile, pltpu.HBM), blk, RAW[0])
-    raw = [over("y", first)]
-
-    send_on, keep_on = right_grams(tile, blk, (3, 2), first)
-    far = fold(keep_on, over("core", send_on))
-    raw.append(over("y", take(tile, blk, RAW[1], send_on)))
-    send, keep = right_grams(tile, blk, (1, 0), far, raw[0])
-    near = over("core", send)
+    first = take(pltpu.with_memory_space_constraint(tile, pltpu.HBM), blk, RAW)
+    raw = over("y", first)
+
+    *send_on, keep_on = right_grams(tile, blk, (3, 2), 2, first)
+    lsend = left_grams(tile, blk, lambda place: 1 - place[1], send_on[0])
+    lcame = over("y", lsend)
+    far = fold(keep_on, *(over("core", part) for part in send_on), lsend)
+    *send, keep = right_grams(tile, blk, (1, 0), 2, far)
+    near = [over("core", part) for part in send]
     far = over("x", far)
 
-    own, half = right_roots(full_dim, rstats, keep, near, far, tile)
+    own, half = right_roots(full_dim, rstats, keep, near, far, tile, raw)
     came_a = over("y", half)
-    lsend = left_grams(tile, blk, lambda place: 1 - place[1], half)
-    own = hold(own, raw[1], lsend)
+    own = hold(own, lcame)
     own_c = over("core", own)
     own_x = over("x", own)
-    half = core_apply(tile, own_c, lsend)
+    half = core_apply(tile, own_c)
     came_b = over("y", half)
-    own_x = hold(own_x, half, came_a)
+    parts = halve(own_x, half, came_a)
     lkeep = left_grams(tile, blk, lambda place: place[1], half)
-    roots, part = spread_roots(own, own_c, own_x, over("core", own_x))
+    roots, part = spread_roots(own, own_c, own_x, *(over("core", value) for value in parts))
 
     (half,) = right_apply(tile, roots, 0, None, part, (lkeep,))
     came_c = over("y", half)
-    (half,) = right_apply(tile, roots, 1, None, None, (came_b,))
+    left = left_roots(full_dim, lstats, lkeep, lcame)
+    (half,) = right_apply(tile, roots, 1, None, None, (came_b, left))
     came_d = over("y", half)
 
     def crossed(block, start=0):
         return lambda place: (1 - place[1]) * tile_cols + block(place) * blk + start
 
-    left = left_roots(full_dim, lstats, lkeep, came_b)
     out, done = update(
         tile, left, roots, None, shape,
         lambda s, place: (place[1], s),
@@ -651,26 +688,26 @@
     )
     (half,) = right_apply(tile, roots, 2, None, None, (came_c, done))
     came_e = over("y", half)
-    wide = blk // 2
-    last = ((0, rows, 0, wide), (0, blk, wide, wide), (blk, blk, wide, wide))
-    held = right_apply(tile, roots, 3, last, None, (came_d,))
-    came_last = [over("y", half) for half in held]
+    (half,) = right_apply(tile, roots, 3, None, None, (came_d,))
+    came_f = over("y", half)
     out = finish(came_a, left, out, crossed(own_first))
     out = finish(came_b, left, out, crossed(core_first))
     part = rest_of(came_c, rows)
     part_x = over("x", part)
-    roots_raw = join_roots(part, over("core", part), part_x, over("core", part_x))
-    for k, (block, value) in enumerate(zip(RAW, raw)):
-        out, done = update(
-            value, left, roots_raw, out, shape,
-            lambda s, place: (0, 0),
-            lambda s, place, block=block: (0, (1 - place[1]) * halves + block),
-            k, 1, held[:1],
-        )
-    for k, value in enumerate((came_c, came_d, came_e)):
+    root_raw = join_root(part, over("core", part), part_x, over("core", part_x))
+    out, done = update(
+        raw, left, root_raw, out, shape,
+        lambda s, place: (0, 0),
+        lambda s, place: (0, (1 - place[1]) * halves + RAW),
+        (half,),
+    )
+    wide = blk // 2
+    last = ((0, rows, 0, wide), (0, blk, wide, wide), (blk, blk, wide, wide))
+    came_last = [over("y", half) for half in right_apply(tile, roots, 4, last, None, (came_e,))]
+    for k, value in enumerate((came_c, came_d, came_e, came_f)):
         out = finish(value, left, out, crossed(functools.partial(later, k)))
     for (top, tall, start, _), value in zip(last, came_last):
-        out = finish(value, left, out, crossed(functools.partial(later, 3), start), top // blk, tall // blk)
+        out = finish(value, left, out, crossed(functools.partial(later, 4), start), top // blk, tall // blk)
     return out.reshape(1, rows, 2 * tile_cols)
 
 

time: 103 us -> 105 us (1.019)
  starting transfers between devices: 19.7 us -> 25.9 us
  waiting for transfers between devices: 40.9 us -> 36.9 us
    ppermute x10 -> x11, waiting for transfers between devices: 30.8 us -> 24.6 us  [over(): return lax.ppermute(value, 'col', [(0, 1), (1, 0)])]
    ppermute x10 -> x11, starting transfers between devices: 14.8 us -> 18.6 us  [over(): return lax.ppermute(value, 'col', [(0, 1), (1, 0)])]
    ppermute x9 -> x12, starting transfers between devices: 4.89 us -> 7.32 us  [over(): return lax.ppermute(value, 'row', [(i, i ^ flip) for i in range(n_row)])]
    ppermute x9 -> x12, waiting for transfers between devices: 10.1 us -> 12.2 us  [over(): return lax.ppermute(value, 'row', [(i, i ^ flip) for i in range(n_row)])]
    pallas_call x3 -> x2, Pallas kernels: 13.3 us -> 11.3 us  [update(): pl.pallas_call(update_kernel, out_shape=(jax.ShapeDtypeStruct(out_shape,...]
    pallas_call x8 -> x9, Pallas kernels: 8.84 us -> 10 us  [finish(): pl.pallas_call(functools.partial(finish_kernel, column, first), out_shape...]
    pallas_call x4 -> x5, Pallas kernels: 4.74 us -> 4.7 us  [the longest x2 4.08 us: right_grams(): pl.pallas_call(functools.partial(right_gram_kernel, parts), out_shape=tup...]
  transfers between devices with their start and end apart: 19 -> 23, of which waited for: 10 -> 10; matrix products, arithmetic and copies ran while one was open for 0% -> 0% of each run, Pallas kernels for 39% -> 38%
where the time goes in v8:
time: 105 us
  Pallas kernels  41.6 us (40%)
  waiting for transfers between devices  36.9 us (35%)
  starting transfers between devices  25.9 us (25%)
    ppermute x11, waiting for transfers between devices, over(): return lax.ppermute(value, 'col', [(0, 1), (1, 0)])  24.6 us
    ppermute x11, starting transfers between devices, over(): return lax.ppermute(value, 'col', [(0, 1), (1, 0)])  18.6 us
    ppermute x12, waiting for transfers between devices, over(): return lax.ppermute(value, 'row', [(i, i ^ flip) for i in range(n_row)])  12.2 us
    pallas_call x2, Pallas kernels, update(): pl.pallas_call(update_kernel, out_shape=(jax.ShapeDtypeStruct(out_shape,...  11.3 us
    pallas_call x9, Pallas kernels, finish(): pl.pallas_call(functools.partial(finish_kernel, column, first), out_shape...  10 us
    ppermute x12, starting transfers between devices, over(): return lax.ppermute(value, 'row', [(i, i ^ flip) for i in range(n_row)])  7.32 us
    pallas_call x2, Pallas kernels, left_grams(): pl.pallas_call(left_gram_kernel, out_shape=jax.ShapeDtypeStruct((tall, bl...  5.78 us
    pallas_call x2, Pallas kernels, right_grams(): pl.pallas_call(functools.partial(right_gram_kernel, parts), out_shape=tup...  4.08 us
  transfers between devices with their start and end apart: 23, of which 10 were waited for; matrix products, arithmetic and copies ran while one was open for 0% of the time, Pallas kernels for 38%

profile of v8, /device:TPU:0, one launch (start us, length us, event | category | flops | bytes accessed | tf_op | source)
XLA Modules:
  0.0 104.9 jit_solution(16481604256923438714)
XLA Ops:
  1.2 3.0 %collective-permute-start.5 = (f32[512,256]{1,0:T(8,128)S(1)}, f32[512,256]{1,0:T(8,128)S(1)}, u32[]{:S(2)}, u32[]{:S(2)}) collective-permute-start(f32[512,256]{1,0:T(8,128)S(1)} %take.1.rest_0_), channel_id=1, source_target_pairs={{0,4},{4,0},{1,5},{5,1},{2,6},{6,2},{3,7},{7,3},{8,12},{12,8},{9,1... | collective-permute-start | bytes 1572872 | tf_op jit(solution)/shard_map/ppermute | solution.py:649
  4.2 2.0 %right_grams.2 = (f32[136,256]{1,0:T(8,128)S(1)}, f32[128,256]{1,0:T(8,128)S(1)}, f32[264,256]{1,0:T(8,128)S(1)}) custom-call(f32[1024,2048]{1,0:T(8,128)S(1)} %bitcast.5, f32[512,256]{1,0:T(8,128)S(1)} %take.1.rest_0_), custom_call_target="tpu_custom_call" | custom-call | flops 1 | bytes 1 | tf_op jit(solution)/shard_map/right_grams/pallas_call | solution.py:151
  6.9 2.9 %left_grams.2.after_ref = f32[264,256]{1,0:T(8,128)S(1)} custom-call(f32[1024,2048]{1,0:T(8,128)S(1)} %bitcast.6, f32[136,256]{1,0:T(8,128)S(1)} %get-tuple-element.24.after_ref), custom_call_target="tpu_custom_call" | custom-call | flops 1 | bytes 1 | tf_op jit(solution)/shard_map/left_grams/pallas_call | solution.py:198
  9.8 2.3 %collective-permute-start.4 = (f32[264,256]{1,0:T(8,128)S(1)}, f32[264,256]{1,0:T(8,128)S(1)}, u32[]{:S(2)}, u32[]{:S(2)}) collective-permute-start(f32[264,256]{1,0:T(8,128)S(1)} %fold.1.rest_0_), channel_id=1, source_target_pairs={{0,16},{8,24},{16,0},{24,8},{1,17},{9,25},{17,1},{25,9},{2,18},{10... | collective-permute-start | bytes 811016 | tf_op jit(solution)/shard_map/ppermute | solution.py:651
  12.1 2.0 %right_grams.3 = (f32[136,256]{1,0:T(8,128)S(1)}, f32[128,256]{1,0:T(8,128)S(1)}, f32[264,256]{1,0:T(8,128)S(1)}) custom-call(f32[1024,2048]{1,0:T(8,128)S(1)} %bitcast.7, f32[264,256]{1,0:T(8,128)S(1)} %fold.1.rest_0_), custom_call_target="tpu_custom_call" | custom-call | flops 1 | bytes 1 | tf_op jit(solution)/shard_map/right_grams/pallas_call | solution.py:151
  16.3 2.6 %collective-permute-done.4.c_ref = f32[264,256]{1,0:T(8,128)S(1)} collective-permute-done((f32[264,256]{1,0:T(8,128)S(1)}, f32[264,256]{1,0:T(8,128)S(1)}, u32[]{:S(2)}, u32[]{:S(2)}) %collective-permute-start.4) | collective-permute-done | bytes 270368 | tf_op jit(solution)/shard_map/ppermute | solution.py:651
  18.9 3.2 %right_roots.1 = (f32[264,256]{1,0:T(8,128)S(1)}, f32[512,256]{1,0:T(8,128)S(1)}) custom-call(f32[2048,256]{1,0:T(8,128)S(1)} %bitcast.17, f32[264,256]{1,0:T(8,128)S(1)} %get-tuple-element.26.a_ref, f32[136,256]{1,0:T(8,128)S(1)} %collective-permute-done.2.top_ref, f32[128,256]{1,0:T(8,128)S(1)} %collective-permute-done.3.rest_ref, ...), custom_call_target="tpu_custom_call" | custom-call | flops 1 | bytes 1 | tf_op jit(solution)/shard_map/right_roots/pallas_call | solution.py:354
  22.1 1.8 %collective-permute-start.9 = (f32[512,256]{1,0:T(8,128)S(1)}, f32[512,256]{1,0:T(8,128)S(1)}, u32[]{:S(2)}, u32[]{:S(2)}) collective-permute-start(f32[512,256]{1,0:T(8,128)S(1)} %get-tuple-element.30), channel_id=1, source_target_pairs={{0,4},{4,0},{1,5},{5,1},{2,6},{6,2},{3,7},{7,3},{8,12},{12,8},{9,1... | collective-permute-start | bytes 1572872 | tf_op jit(solution)/shard_map/ppermute | solution.py:649
  26.9 6.0 %collective-permute-done.8.a_ref.x_ref = f32[264,256]{1,0:T(8,128)S(1)} collective-permute-done((f32[264,256]{1,0:T(8,128)S(1)}, f32[264,256]{1,0:T(8,128)S(1)}, u32[]{:S(2)}, u32[]{:S(2)}) %collective-permute-start.8) | collective-permute-done | bytes 270368 | tf_op jit(solution)/shard_map/ppermute | solution.py:651
  32.9 4.1 %collective-permute-done.9.rest_1_.half_ref = f32[512,256]{1,0:T(8,128)S(1)} collective-permute-done((f32[512,256]{1,0:T(8,128)S(1)}, f32[512,256]{1,0:T(8,128)S(1)}, u32[]{:S(2)}, u32[]{:S(2)}) %collective-permute-start.9) | collective-permute-done | bytes 524320 | tf_op jit(solution)/shard_map/ppermute | solution.py:649
  37.6 2.9 %left_grams.3.rest_1_.a_ref = f32[264,256]{1,0:T(8,128)S(1)} custom-call(f32[1024,2048]{1,0:T(8,128)S(1)} %bitcast.10, f32[512,256]{1,0:T(8,128)S(1)} %core_apply.1.rest_0_.after_ref), custom_call_target="tpu_custom_call" | custom-call | flops 1 | bytes 1 | tf_op jit(solution)/shard_map/left_grams/pallas_call | solution.py:198
  41.4 1.8 %collective-permute-start.12 = (f32[552,256]{1,0:T(8,128)S(1)}, f32[552,256]{1,0:T(8,128)S(1)}, u32[]{:S(2)}, u32[]{:S(2)}) collective-permute-start(f32[552,256]{1,0:T(8,128)S(1)} %right_apply.5), channel_id=1, source_target_pairs={{0,4},{4,0},{1,5},{5,1},{2,6},{6,2},{3,7},{7,3},{8,12},{12,8},{9,1... | collective-permute-start | bytes 1695752 | tf_op jit(solution)/shard_map/ppermute | solution.py:649
  43.3 3.0 %left_roots.1.left_ref.rest_1_ = bf16[2,2,256,256]{3,2,1,0:T(8,128)(2,1)S(1)} custom-call(f32[1024,256]{1,0:T(8,128)S(1)} %bitcast.18, f32[264,256]{1,0:T(8,128)S(1)} %left_grams.3.rest_1_.a_ref, f32[264,256]{1,0:T(8,128)S(1)} %collective-permute-done.6.rest_0_.b_ref), custom_call_target="tpu_custom_call" | custom-call | flops 1 | bytes 1 | tf_op jit(solution)/shard_map/left_roots/pallas_call | solution.py:394
  46.3 1.9 %collective-permute-done.17.rest_0_.half_ref = f32[512,256]{1,0:T(8,128)S(1)} collective-permute-done((f32[512,256]{1,0:T(8,128)S(1)}, f32[512,256]{1,0:T(8,128)S(1)}, u32[]{:S(2)}, u32[]{:S(2)}) %collective-permute-start.17) | collective-permute-done | bytes 524320 | tf_op jit(solution)/shard_map/ppermute | solution.py:649
  48.6 1.9 %collective-permute-start.18 = (f32[512,256]{1,0:T(8,128)S(1)}, f32[512,256]{1,0:T(8,128)S(1)}, u32[]{:S(2)}, u32[]{:S(2)}) collective-permute-start(f32[512,256]{1,0:T(8,128)S(1)} %right_apply.8), channel_id=1, source_target_pairs={{0,4},{4,0},{1,5},{5,1},{2,6},{6,2},{3,7},{7,3},{8,12},{12,8},{9,1... | collective-permute-start | bytes 1572872 | tf_op jit(solution)/shard_map/ppermute | solution.py:649
  50.4 9.5 %update.2 = (f32[512,4096]{1,0:T(8,128)}, f32[8,128]{1,0:T(8,128)S(1)}) custom-call(f32[1024,2048]{1,0:T(8,128)S(1)} %bitcast.13, bf16[2,2,256,256]{3,2,1,0:T(8,128)(2,1)S(1)} %left_roots.1.left_ref.rest_1_, bf16[8,2,256,256]{3,2,1,0:T(8,128)(2,1)S(1)} %get-tuple-element.33.right_ref), custom_call_target="tpu_custom_call" | custom-call | flops 1 | bytes 1 | tf_op jit(solution)/shard_map/update/pallas_call | solution.py:621
  60.7 1.9 %collective-permute-start.13 = (f32[512,256]{1,0:T(8,128)S(1)}, f32[512,256]{1,0:T(8,128)S(1)}, u32[]{:S(2)}, u32[]{:S(2)}) collective-permute-start(f32[512,256]{1,0:T(8,128)S(1)} %right_apply.6), channel_id=1, source_target_pairs={{0,4},{4,0},{1,5},{5,1},{2,6},{6,2},{3,7},{7,3},{8,12},{12,8},{9,1... | collective-permute-start | bytes 1572872 | tf_op jit(solution)/shard_map/ppermute | solution.py:649
  62.5 9.0 %collective-permute-done.18.rest_0_.half_ref = f32[512,256]{1,0:T(8,128)S(1)} collective-permute-done((f32[512,256]{1,0:T(8,128)S(1)}, f32[512,256]{1,0:T(8,128)S(1)}, u32[]{:S(2)}, u32[]{:S(2)}) %collective-permute-start.18) | collective-permute-done | bytes 524320 | tf_op jit(solution)/shard_map/ppermute | solution.py:649
  71.9 1.9 %collective-permute-start.19 = (f32[512,256]{1,0:T(8,128)S(1)}, f32[512,256]{1,0:T(8,128)S(1)}, u32[]{:S(2)}, u32[]{:S(2)}) collective-permute-start(f32[512,256]{1,0:T(8,128)S(1)} %right_apply.9.rest_1_), channel_id=1, source_target_pairs={{0,4},{4,0},{1,5},{5,1},{2,6},{6,2},{3,7},{7,3},{8,12},{12,8},{9,1... | collective-permute-start | bytes 1572872 | tf_op jit(solution)/shard_map/ppermute | solution.py:649
  73.8 9.0 %collective-permute-done.13.rest_0_.half_ref = f32[512,256]{1,0:T(8,128)S(1)} collective-permute-done((f32[512,256]{1,0:T(8,128)S(1)}, f32[512,256]{1,0:T(8,128)S(1)}, u32[]{:S(2)}, u32[]{:S(2)}) %collective-permute-start.13) | collective-permute-done | bytes 524320 | tf_op jit(solution)/shard_map/ppermute | solution.py:649
  83.2 1.9 %collective-permute-start.16 = (f32[512,128]{1,0:T(8,128)S(1)}, f32[512,128]{1,0:T(8,128)S(1)}, u32[]{:S(2)}, u32[]{:S(2)}) collective-permute-start(f32[512,128]{1,0:T(8,128)S(1)} %get-tuple-element.38), channel_id=1, source_target_pairs={{0,4},{4,0},{1,5},{5,1},{2,6},{6,2},{3,7},{7,3},{8,12},{12,8},{9,1... | collective-permute-start | bytes 786440 | tf_op jit(solution)/shard_map/ppermute | solution.py:649
  85.3 1.8 %collective-permute-start.14 = (f32[256,128]{1,0:T(8,128)S(1)}, f32[256,128]{1,0:T(8,128)S(1)}, u32[]{:S(2)}, u32[]{:S(2)}) collective-permute-start(f32[256,128]{1,0:T(8,128)S(1)} %get-tuple-element.36), channel_id=1, source_target_pairs={{0,4},{4,0},{1,5},{5,1},{2,6},{6,2},{3,7},{7,3},{8,12},{12,8},{9,1... | collective-permute-start | bytes 393224 | tf_op jit(solution)/shard_map/ppermute | solution.py:649
  88.6 2.5 %collective-permute-done.21.x_ref = f32[40,256]{1,0:T(8,128)S(1)} collective-permute-done((f32[40,256]{1,0:T(8,128)S(1)}, f32[40,256]{1,0:T(8,128)S(1)}, u32[]{:S(2)}, u32[]{:S(2)}) %collective-permute-start.21) | collective-permute-done | bytes 40992 | tf_op jit(solution)/shard_map/ppermute | solution.py:651
  95.0 1.8 %update.3 = (f32[512,4096]{1,0:T(8,128)}, f32[8,128]{1,0:T(8,128)}) custom-call(f32[512,256]{1,0:T(8,128)S(1)} %collective-permute-done.5.after_ref.g_ref, bf16[2,2,256,256]{3,2,1,0:T(8,128)(2,1)S(1)} %left_roots.1.left_ref.rest_1_, bf16[1,2,256,256]{3,2,1,0:T(8,128)(2,1)S(1)} %join_root.1.right_ref, ...), custom_call_target="tpu_custom_call", output_to_operand_aliasing={{0}: (3, {})} | custom-call | flops 1 | bytes 1 | tf_op jit(solution)/shard_map/update/pallas_call | solution.py:621
  (58 shorter events, 23.9 us)
Async XLA Ops:
  1.2 17.6 %collective-permute-start.5 = (f32[512,256]{1,0:T(8,128)S(1)}, f32[512,256]{1,0:T(8,128)S(1)}, u32[]{:S(2)}, u32[]{:S(2)}) collective-permute-start(f32[512,256]{1,0:T(8,128)S(1)} %take.1.rest_0_), channel_id=1, source_target_pairs={{0,4},{4,0},{1,5},{5,1},{2,6},{6,2},{3,7},{7,3},{8,12},{12,8},{9,1... | collective-permute-start | bytes 1572872 | tf_op jit(solution)/shard_map/ppermute | solution.py:649
  6.3 3.5 %collective-permute-start = (f32[136,256]{1,0:T(8,128)S(1)}, f32[136,256]{1,0:T(8,128)S(1)}, u32[]{:S(2)}, u32[]{:S(2)}) collective-permute-start(f32[136,256]{1,0:T(8,128)S(1)} %get-tuple-element.24.after_ref), channel_id=1, source_target_pairs={{0,8},{8,0},{16,24},{24,16},{1,9},{9,1},{17,25},{25,17},{2,10},{10... | collective-permute-start | bytes 417800 | tf_op jit(solution)/shard_map/ppermute | solution.py:651
  6.4 12.5 %copy-start.1 = (f32[1,2048,256]{2,1,0:T(8,128)S(1)}, f32[1,2048,256]{2,1,0:T(8,128)}, u32[]{:S(2)}) copy-start(f32[1,2048,256]{2,1,0:T(8,128)} %param.5) | copy-start | bytes 6291460
  6.4 3.4 %collective-permute-start.1 = (f32[128,256]{1,0:T(8,128)S(1)}, f32[128,256]{1,0:T(8,128)S(1)}, u32[]{:S(2)}, u32[]{:S(2)}) collective-permute-start(f32[128,256]{1,0:T(8,128)S(1)} %get-tuple-element.25), channel_id=1, source_target_pairs={{0,8},{8,0},{16,24},{24,16},{1,9},{9,1},{17,25},{25,17},{2,10},{10... | collective-permute-start | bytes 393224 | tf_op jit(solution)/shard_map/ppermute | solution.py:651
  9.8 9.0 %collective-permute-start.4 = (f32[264,256]{1,0:T(8,128)S(1)}, f32[264,256]{1,0:T(8,128)S(1)}, u32[]{:S(2)}, u32[]{:S(2)}) collective-permute-start(f32[264,256]{1,0:T(8,128)S(1)} %fold.1.rest_0_), channel_id=1, source_target_pairs={{0,16},{8,24},{16,0},{24,8},{1,17},{9,25},{17,1},{25,9},{2,18},{10... | collective-permute-start | bytes 811016 | tf_op jit(solution)/shard_map/ppermute | solution.py:651
  14.2 2.1 %collective-permute-start.2 = (f32[136,256]{1,0:T(8,128)S(1)}, f32[136,256]{1,0:T(8,128)S(1)}, u32[]{:S(2)}, u32[]{:S(2)}) collective-permute-start(f32[136,256]{1,0:T(8,128)S(1)} %get-tuple-element.27), channel_id=1, source_target_pairs={{0,8},{8,0},{16,24},{24,16},{1,9},{9,1},{17,25},{25,17},{2,10},{10... | collective-permute-start | bytes 417800 | tf_op jit(solution)/shard_map/ppermute | solution.py:651
  14.2 2.0 %collective-permute-start.3 = (f32[128,256]{1,0:T(8,128)S(1)}, f32[128,256]{1,0:T(8,128)S(1)}, u32[]{:S(2)}, u32[]{:S(2)}) collective-permute-start(f32[128,256]{1,0:T(8,128)S(1)} %get-tuple-element.28), channel_id=1, source_target_pairs={{0,8},{8,0},{16,24},{24,16},{1,9},{9,1},{17,25},{25,17},{2,10},{10... | collective-permute-start | bytes 393224 | tf_op jit(solution)/shard_map/ppermute | solution.py:651
  14.7 9.2 %collective-permute-start.6 = (f32[264,256]{1,0:T(8,128)S(1)}, f32[264,256]{1,0:T(8,128)S(1)}, u32[]{:S(2)}, u32[]{:S(2)}) collective-permute-start(f32[264,256]{1,0:T(8,128)S(1)} %left_grams.2.after_ref), channel_id=1, source_target_pairs={{0,4},{4,0},{1,5},{5,1},{2,6},{6,2},{3,7},{7,3},{8,12},{12,8},{9,1... | collective-permute-start | bytes 811016 | tf_op jit(solution)/shard_map/ppermute | solution.py:649
  22.1 14.9 %collective-permute-start.9 = (f32[512,256]{1,0:T(8,128)S(1)}, f32[512,256]{1,0:T(8,128)S(1)}, u32[]{:S(2)}, u32[]{:S(2)}) collective-permute-start(f32[512,256]{1,0:T(8,128)S(1)} %get-tuple-element.30), channel_id=1, source_target_pairs={{0,4},{4,0},{1,5},{5,1},{2,6},{6,2},{3,7},{7,3},{8,12},{12,8},{9,1... | collective-permute-start | bytes 1572872 | tf_op jit(solution)/shard_map/ppermute | solution.py:649
  23.9 1.7 %collective-permute-start.7 = (f32[264,256]{1,0:T(8,128)S(1)}, f32[264,256]{1,0:T(8,128)S(1)}, u32[]{:S(2)}, u32[]{:S(2)}) collective-permute-start(f32[264,256]{1,0:T(8,128)S(1)} %hold.1.own_ref), channel_id=1, source_target_pairs={{0,8},{8,0},{16,24},{24,16},{1,9},{9,1},{17,25},{25,17},{2,10},{10... | collective-permute-start | bytes 811016 | tf_op jit(solution)/shard_map/ppermute | solution.py:651
  24.0 8.9 %collective-permute-start.8 = (f32[264,256]{1,0:T(8,128)S(1)}, f32[264,256]{1,0:T(8,128)S(1)}, u32[]{:S(2)}, u32[]{:S(2)}) collective-permute-start(f32[264,256]{1,0:T(8,128)S(1)} %hold.1.own_ref), channel_id=1, source_target_pairs={{0,16},{8,24},{16,0},{24,8},{1,17},{9,25},{17,1},{25,9},{2,18},{10... | collective-permute-start | bytes 811016 | tf_op jit(solution)/shard_map/ppermute | solution.py:651
  26.1 22.1 %collective-permute-start.17 = (f32[512,256]{1,0:T(8,128)S(1)}, f32[512,256]{1,0:T(8,128)S(1)}, u32[]{:S(2)}, u32[]{:S(2)}) collective-permute-start(f32[512,256]{1,0:T(8,128)S(1)} %core_apply.1.rest_0_.after_ref), channel_id=1, source_target_pairs={{0,4},{4,0},{1,5},{5,1},{2,6},{6,2},{3,7},{7,3},{8,12},{12,8},{9,1... | collective-permute-start | bytes 1572872 | tf_op jit(solution)/shard_map/ppermute | solution.py:649
  37.0 3.5 %collective-permute-start.10 = (f32[136,256]{1,0:T(8,128)S(1)}, f32[136,256]{1,0:T(8,128)S(1)}, u32[]{:S(2)}, u32[]{:S(2)}) collective-permute-start(f32[136,256]{1,0:T(8,128)S(1)} %get-tuple-element.31), channel_id=1, source_target_pairs={{0,8},{8,0},{16,24},{24,16},{1,9},{9,1},{17,25},{25,17},{2,10},{10... | collective-permute-start | bytes 417800 | tf_op jit(solution)/shard_map/ppermute | solution.py:651
  37.1 3.4 %collective-permute-start.11 = (f32[128,256]{1,0:T(8,128)S(1)}, f32[128,256]{1,0:T(8,128)S(1)}, u32[]{:S(2)}, u32[]{:S(2)}) collective-permute-start(f32[128,256]{1,0:T(8,128)S(1)} %get-tuple-element.32), channel_id=1, source_target_pairs={{0,8},{8,0},{16,24},{24,16},{1,9},{9,1},{17,25},{25,17},{2,10},{10... | collective-permute-start | bytes 393224 | tf_op jit(solution)/shard_map/ppermute | solution.py:651
  41.4 18.9 %collective-permute-start.12 = (f32[552,256]{1,0:T(8,128)S(1)}, f32[552,256]{1,0:T(8,128)S(1)}, u32[]{:S(2)}, u32[]{:S(2)}) collective-permute-start(f32[552,256]{1,0:T(8,128)S(1)} %right_apply.5), channel_id=1, source_target_pairs={{0,4},{4,0},{1,5},{5,1},{2,6},{6,2},{3,7},{7,3},{8,12},{12,8},{9,1... | collective-permute-start | bytes 1695752 | tf_op jit(solution)/shard_map/ppermute | solution.py:649
  48.6 23.0 %collective-permute-start.18 = (f32[512,256]{1,0:T(8,128)S(1)}, f32[512,256]{1,0:T(8,128)S(1)}, u32[]{:S(2)}, u32[]{:S(2)}) collective-permute-start(f32[512,256]{1,0:T(8,128)S(1)} %right_apply.8), channel_id=1, source_target_pairs={{0,4},{4,0},{1,5},{5,1},{2,6},{6,2},{3,7},{7,3},{8,12},{12,8},{9,1... | collective-permute-start | bytes 1572872 | tf_op jit(solution)/shard_map/ppermute | solution.py:649
  60.7 22.1 %collective-permute-start.13 = (f32[512,256]{1,0:T(8,128)S(1)}, f32[512,256]{1,0:T(8,128)S(1)}, u32[]{:S(2)}, u32[]{:S(2)}) collective-permute-start(f32[512,256]{1,0:T(8,128)S(1)} %right_apply.6), channel_id=1, source_target_pairs={{0,4},{4,0},{1,5},{5,1},{2,6},{6,2},{3,7},{7,3},{8,12},{12,8},{9,1... | collective-permute-start | bytes 1572872 | tf_op jit(solution)/shard_map/ppermute | solution.py:649
  71.9 28.5 %collective-permute-start.19 = (f32[512,256]{1,0:T(8,128)S(1)}, f32[512,256]{1,0:T(8,128)S(1)}, u32[]{:S(2)}, u32[]{:S(2)}) collective-permute-start(f32[512,256]{1,0:T(8,128)S(1)} %right_apply.9.rest_1_), channel_id=1, source_target_pairs={{0,4},{4,0},{1,5},{5,1},{2,6},{6,2},{3,7},{7,3},{8,12},{12,8},{9,1... | collective-permute-start | bytes 1572872 | tf_op jit(solution)/shard_map/ppermute | solution.py:649
  83.2 18.5 %collective-permute-start.16 = (f32[512,128]{1,0:T(8,128)S(1)}, f32[512,128]{1,0:T(8,128)S(1)}, u32[]{:S(2)}, u32[]{:S(2)}) collective-permute-start(f32[512,128]{1,0:T(8,128)S(1)} %get-tuple-element.38), channel_id=1, source_target_pairs={{0,4},{4,0},{1,5},{5,1},{2,6},{6,2},{3,7},{7,3},{8,12},{12,8},{9,1... | collective-permute-start | bytes 786440 | tf_op jit(solution)/shard_map/ppermute | solution.py:649
  85.0 17.7 %collective-permute-start.15 = (f32[256,128]{1,0:T(8,128)S(1)}, f32[256,128]{1,0:T(8,128)S(1)}, u32[]{:S(2)}, u32[]{:S(2)}) collective-permute-start(f32[256,128]{1,0:T(8,128)S(1)} %get-tuple-element.37), channel_id=1, source_target_pairs={{0,4},{4,0},{1,5},{5,1},{2,6},{6,2},{3,7},{7,3},{8,12},{12,8},{9,1... | collective-permute-start | bytes 393224 | tf_op jit(solution)/shard_map/ppermute | solution.py:649
  85.3 18.6 %collective-permute-start.14 = (f32[256,128]{1,0:T(8,128)S(1)}, f32[256,128]{1,0:T(8,128)S(1)}, u32[]{:S(2)}, u32[]{:S(2)}) collective-permute-start(f32[256,128]{1,0:T(8,128)S(1)} %get-tuple-element.36), channel_id=1, source_target_pairs={{0,4},{4,0},{1,5},{5,1},{2,6},{6,2},{3,7},{7,3},{8,12},{12,8},{9,1... | collective-permute-start | bytes 393224 | tf_op jit(solution)/shard_map/ppermute | solution.py:649
  87.1 4.0 %collective-permute-start.21 = (f32[40,256]{1,0:T(8,128)S(1)}, f32[40,256]{1,0:T(8,128)S(1)}, u32[]{:S(2)}, u32[]{:S(2)}) collective-permute-start(f32[40,256]{1,0:T(8,128)S(1)} %rest_of.1.own_ref), channel_id=1, source_target_pairs={{0,16},{8,24},{16,0},{24,8},{1,17},{9,25},{17,1},{25,9},{2,18},{10... | collective-permute-start | bytes 122888 | tf_op jit(solution)/shard_map/ppermute | solution.py:651
  91.1 1.2 %collective-permute-start.20 = (f32[40,256]{1,0:T(8,128)S(1)}, f32[40,256]{1,0:T(8,128)S(1)}, u32[]{:S(2)}, u32[]{:S(2)}) collective-permute-start(f32[40,256]{1,0:T(8,128)S(1)} %rest_of.1.own_ref), channel_id=1, source_target_pairs={{0,8},{8,0},{16,24},{24,16},{1,9},{9,1},{17,25},{25,17},{2,10},{10... | collective-permute-start | bytes 122888 | tf_op jit(solution)/shard_map/ppermute | solution.py:651
  92.3 2.6 %collective-permute-start.22 = (f32[40,256]{1,0:T(8,128)S(1)}, f32[40,256]{1,0:T(8,128)S(1)}, u32[]{:S(2)}, u32[]{:S(2)}) collective-permute-start(f32[40,256]{1,0:T(8,128)S(1)} %collective-permute-done.21.x_ref), channel_id=1, source_target_pairs={{0,8},{8,0},{16,24},{24,16},{1,9},{9,1},{17,25},{25,17},{2,10},{10... | collective-permute-start | bytes 122888 | tf_op jit(solution)/shard_map/ppermute | solution.py:651
  (2 other events, 7.0 us)

commit v9 on v7

--- a/solution.py
+++ b/solution.py
@@ -226,26 +226,58 @@
 
 
 def take_kernel(block, g_ref, *rest):
-    out_ref, sem = rest[-2:]
+    out_ref, sems = rest[-2:]
     rows, blk = out_ref.shape
-    top = pl.multiple_of((1 - here()[1]) * rows, rows)
-    copy = pltpu.make_async_copy(g_ref.at[pl.ds(top, rows), pl.ds(block * blk, blk)], out_ref, sem)
-    copy.start()
-    copy.wait()
-
-
-def take(tile, blk, block, *after):
+    count = sems.shape[0]
+    part = rows // count
+    copies = []
+    for k in range(count):
+        top = pl.multiple_of((1 - here()[1]) * rows + k * part, part)
+        source = g_ref.at[pl.ds(top, part), pl.ds(block * blk, blk)]
+        copies.append(pltpu.make_async_copy(source, out_ref.at[pl.ds(k * part, part), :], sems.at[k]))
+        copies[k].start()
+    for copy in copies:
+        copy.wait()
+
+
+def take(tile, blk, block, count, *after):
     anywhere = pl.BlockSpec(memory_space=pl.ANY)
     return pl.pallas_call(
         functools.partial(take_kernel, block),
         out_shape=jax.ShapeDtypeStruct((tile.shape[0] // 2, blk), jnp.float32),
         in_specs=[anywhere] * (1 + len(after)),
         out_specs=anywhere,
-        scratch_shapes=[pltpu.SemaphoreType.DMA],
+        scratch_shapes=[pltpu.SemaphoreType.DMA((count,))],
         compiler_params=pltpu.CompilerParams(vmem_limit_bytes=VMEM_LIMIT),
         cost_estimate=SMALL,
         name="take",
     )(tile, *after)
+
+
+def load_kernel(g_ref, after_ref, out_ref, sems):
+    count = sems.shape[0]
+    part = g_ref.shape[0] // count
+    copies = []
+    for k in range(count):
+        rows = pl.ds(k * part, part)
+        copies.append(pltpu.make_async_copy(g_ref.at[rows, :], out_ref.at[rows, :], sems.at[k]))
+        copies[k].start()
+    for copy in copies:
+        copy.wait()
+
+
+def load(tile, after):
+    anywhere = pl.BlockSpec(memory_space=pl.ANY)
+    return pl.pallas_call(
+        load_kernel,
+        out_shape=jax.ShapeDtypeStruct(tile.shape, jnp.float32),
+        in_specs=[anywhere, anywhere],
+        out_specs=anywhere,
+        scratch_shapes=[pltpu.SemaphoreType.DMA((4,))],
+        compiler_params=pltpu.CompilerParams(vmem_limit_bytes=VMEM_LIMIT),
+        cost_estimate=SMALL,
+        name="load",
+    )(tile, after)
 
 
 def fold_kernel(a_ref, b_ref, out_ref):
@@ -600,7 +632,7 @@
 def exchange_device(full_dim, n_row, grads, left_stats, right_stats):
     tile_rows, tile_cols = grads.shape[1:]
     blk = left_stats.shape[2]
-    tile = grads.reshape(tile_rows, tile_cols)
+    tile = pltpu.with_memory_space_constraint(grads.reshape(tile_rows, tile_cols), pltpu.HBM)
     lstats = left_stats.reshape(tile_rows, blk)
     rstats = right_stats.reshape(tile_cols, blk)
     rows = tile_rows // 2
@@ -613,12 +645,13 @@
         flip = {"core": 1, "x": 2}[axis]
         return lax.ppermute(value, "row", [(i, i ^ flip) for i in range(n_row)])
 
-    first = take(pltpu.with_memory_space_constraint(tile, pltpu.HBM), blk, RAW[0])
+    first = take(tile, blk, RAW[0], 1)
     raw = [over("y", first)]
+    tile = load(tile, first)
 
     send_on, keep_on = right_grams(tile, blk, (3, 2), first)
     far = fold(keep_on, over("core", send_on))
-    raw.append(over("y", take(tile, blk, RAW[1], send_on)))
+    raw.append(over("y", take(tile, blk, RAW[1], 16, send_on)))
     send, keep = right_grams(tile, blk, (1, 0), far, raw[0])
     near = over("core", send)
     far = over("x", far)

time: 103 us -> 103 us (level)
  Pallas kernels: 42.3 us -> 45.9 us
  waiting for transfers between devices: 40.9 us -> 38 us
    pallas_call x0 -> x1, Pallas kernels: none -> 3.5 us  [load(): pl.pallas_call(load_kernel, out_shape=jax.ShapeDtypeStruct(tile.shape, jn...]
    ppermute x10, waiting for transfers between devices: 30.8 us -> 28.1 us  [over(): return lax.ppermute(value, 'col', [(0, 1), (1, 0)])]
  transfers between devices with their start and end apart: 19 -> 19, of which waited for: 10 -> 12; matrix products, arithmetic and copies ran while one was open for 0% -> 0% of each run, Pallas kernels for 39% -> 43%
where the time goes in v9:
time: 103 us
  Pallas kernels  45.9 us (45%)
  waiting for transfers between devices  38 us (37%)
  starting transfers between devices  18.7 us (18%)
    ppermute x10, waiting for transfers between devices, over(): return lax.ppermute(value, 'col', [(0, 1), (1, 0)])  28.1 us
    ppermute x10, starting transfers between devices, over(): return lax.ppermute(value, 'col', [(0, 1), (1, 0)])  13.7 us
    pallas_call x3, Pallas kernels, update(): pl.pallas_call(update_kernel, out_shape=(jax.ShapeDtypeStruct(out_shape,...  13.3 us
    ppermute x9, waiting for transfers between devices, over(): return lax.ppermute(value, 'row', [(i, i ^ flip) for i in range(n_row)])  9.87 us
    pallas_call x8, Pallas kernels, finish(): pl.pallas_call(functools.partial(finish_kernel, column, first), out_shape...  8.83 us
    pallas_call x2, Pallas kernels, left_grams(): pl.pallas_call(left_gram_kernel, out_shape=jax.ShapeDtypeStruct((tall, bl...  5.78 us
    ppermute x9, starting transfers between devices, over(): return lax.ppermute(value, 'row', [(i, i ^ flip) for i in range(n_row)])  4.96 us
    pallas_call x2, Pallas kernels, right_grams(): pl.pallas_call(right_gram_kernel, out_shape=(jax.ShapeDtypeStruct((tall,...  4.12 us
  transfers between devices with their start and end apart: 19, of which 12 were waited for; matrix products, arithmetic and copies ran while one was open for 0% of the time, Pallas kernels for 43%

profile of v9, /device:TPU:0, one launch (start us, length us, event | category | flops | bytes accessed | tf_op | source)
XLA Modules:
  0.0 103.1 jit_solution(4236640736062817213)
XLA Ops:
  1.1 3.0 %collective-permute-start.1 = (f32[512,256]{1,0:T(8,128)S(1)}, f32[512,256]{1,0:T(8,128)S(1)}, u32[]{:S(2)}, u32[]{:S(2)}) collective-permute-start(f32[512,256]{1,0:T(8,128)S(1)} %take.2.after_ref.rest_0_), channel_id=1, source_target_pairs={{0,4},{4,0},{1,5},{5,1},{2,6},{6,2},{3,7},{7,3},{8,12},{12,8},{9,1... | collective-permute-start | bytes 1572872 | tf_op jit(solution)/shard_map/ppermute | solution.py:644
  4.1 3.5 %load.1.g_ref = f32[1024,2048]{1,0:T(8,128)S(1)} custom-call(f32[1024,2048]{1,0:T(8,128)} %bitcast.7, f32[512,256]{1,0:T(8,128)S(1)} %take.2.after_ref.rest_0_), custom_call_target="tpu_custom_call" | custom-call | flops 1 | bytes 1 | tf_op jit(solution)/shard_map/load/pallas_call | solution.py:271
  7.6 2.1 %right_grams.2 = (f32[264,256]{1,0:T(8,128)S(1)}, f32[264,256]{1,0:T(8,128)S(1)}) custom-call(f32[1024,2048]{1,0:T(8,128)S(1)} %load.1.g_ref, f32[512,256]{1,0:T(8,128)S(1)} %take.2.after_ref.rest_0_), custom_call_target="tpu_custom_call" | custom-call | flops 1 | bytes 1 | tf_op jit(solution)/shard_map/right_grams/pallas_call | solution.py:142
  11.3 1.5 %collective-permute-start.3 = (f32[264,256]{1,0:T(8,128)S(1)}, f32[264,256]{1,0:T(8,128)S(1)}, u32[]{:S(2)}, u32[]{:S(2)}) collective-permute-start(f32[264,256]{1,0:T(8,128)S(1)} %fold.1.rest_0_), channel_id=1, source_target_pairs={{0,16},{8,24},{16,0},{24,8},{1,17},{9,25},{17,1},{25,9},{2,18},{10... | collective-permute-start | bytes 811016 | tf_op jit(solution)/shard_map/ppermute | solution.py:646
  12.9 4.0 %collective-permute-done.1.rest_1_.g_ref = f32[512,256]{1,0:T(8,128)S(1)} collective-permute-done((f32[512,256]{1,0:T(8,128)S(1)}, f32[512,256]{1,0:T(8,128)S(1)}, u32[]{:S(2)}, u32[]{:S(2)}) %collective-permute-start.1) | collective-permute-done | bytes 524320 | tf_op jit(solution)/shard_map/ppermute | solution.py:644
  16.8 2.0 %right_grams.3 = (f32[264,256]{1,0:T(8,128)S(1)}, f32[264,256]{1,0:T(8,128)S(1)}) custom-call(f32[1024,2048]{1,0:T(8,128)S(1)} %load.1.g_ref, f32[264,256]{1,0:T(8,128)S(1)} %fold.1.rest_0_, f32[512,256]{1,0:T(8,128)S(1)} %collective-permute-done.1.rest_1_.g_ref), custom_call_target="tpu_custom_call" | custom-call | flops 1 | bytes 1 | tf_op jit(solution)/shard_map/right_grams/pallas_call | solution.py:142
  20.5 3.2 %right_roots.1 = (f32[264,256]{1,0:T(8,128)S(1)}, f32[512,256]{1,0:T(8,128)S(1)}) custom-call(f32[2048,256]{1,0:T(8,128)S(1)} %bitcast.4, f32[264,256]{1,0:T(8,128)S(1)} %get-tuple-element.22.a_ref, f32[264,256]{1,0:T(8,128)S(1)} %collective-permute-done.2.b_ref, f32[264,256]{1,0:T(8,128)S(1)} %collective-permute-done.3.c_ref, f32[1024,2048]{1,0:T(8,128)S(1)} %load.1.g_ref), custom_call_target="tpu_custom_call" | custom-call | flops 1 | bytes 1 | tf_op jit(solution)/shard_map/right_roots/pallas_call | solution.py:357
  23.7 2.1 %collective-permute-start.7 = (f32[512,256]{1,0:T(8,128)S(1)}, f32[512,256]{1,0:T(8,128)S(1)}, u32[]{:S(2)}, u32[]{:S(2)}) collective-permute-start(f32[512,256]{1,0:T(8,128)S(1)} %get-tuple-element.25.after_ref), channel_id=1, source_target_pairs={{0,4},{4,0},{1,5},{5,1},{2,6},{6,2},{3,7},{7,3},{8,12},{12,8},{9,1... | collective-permute-start | bytes 1572872 | tf_op jit(solution)/shard_map/ppermute | solution.py:644
  25.8 2.9 %left_grams.2.rest_1_.under_ref = f32[264,256]{1,0:T(8,128)S(1)} custom-call(f32[1024,2048]{1,0:T(8,128)S(1)} %load.1.g_ref, f32[512,256]{1,0:T(8,128)S(1)} %get-tuple-element.25.after_ref), custom_call_target="tpu_custom_call" | custom-call | flops 1 | bytes 1 | tf_op jit(solution)/shard_map/left_grams/pallas_call | solution.py:191
  28.8 1.6 %collective-permute-start.6 = (f32[264,256]{1,0:T(8,128)S(1)}, f32[264,256]{1,0:T(8,128)S(1)}, u32[]{:S(2)}, u32[]{:S(2)}) collective-permute-start(f32[264,256]{1,0:T(8,128)S(1)} %hold.2.own_ref), channel_id=1, source_target_pairs={{0,16},{8,24},{16,0},{24,8},{1,17},{9,25},{17,1},{25,9},{2,18},{10... | collective-permute-start | bytes 811016 | tf_op jit(solution)/shard_map/ppermute | solution.py:646
  31.5 6.2 %collective-permute-done.6.a_ref = f32[264,256]{1,0:T(8,128)S(1)} collective-permute-done((f32[264,256]{1,0:T(8,128)S(1)}, f32[264,256]{1,0:T(8,128)S(1)}, u32[]{:S(2)}, u32[]{:S(2)}) %collective-permute-start.6) | collective-permute-done | bytes 270368 | tf_op jit(solution)/shard_map/ppermute | solution.py:646
  38.9 2.9 %left_grams.3.a_ref.rest_1_ = f32[264,256]{1,0:T(8,128)S(1)} custom-call(f32[1024,2048]{1,0:T(8,128)S(1)} %load.1.g_ref, f32[776,256]{1,0:T(8,128)S(1)} %core_apply.1.rest_0_.after_ref), custom_call_target="tpu_custom_call" | custom-call | flops 1 | bytes 1 | tf_op jit(solution)/shard_map/left_grams/pallas_call | solution.py:191
  42.8 1.8 %collective-permute-start.14 = (f32[584,256]{1,0:T(8,128)S(1)}, f32[584,256]{1,0:T(8,128)S(1)}, u32[]{:S(2)}, u32[]{:S(2)}) collective-permute-start(f32[584,256]{1,0:T(8,128)S(1)} %right_apply.6), channel_id=1, source_target_pairs={{0,4},{4,0},{1,5},{5,1},{2,6},{6,2},{3,7},{7,3},{8,12},{12,8},{9,1... | collective-permute-start | bytes 1794056 | tf_op jit(solution)/shard_map/ppermute | solution.py:644
  44.6 11.2 %collective-permute-done.9.rest_0_.b_ref.half_ref = f32[776,256]{1,0:T(8,128)S(1)} collective-permute-done((f32[776,256]{1,0:T(8,128)S(1)}, f32[776,256]{1,0:T(8,128)S(1)}, u32[]{:S(2)}, u32[]{:S(2)}) %collective-permute-start.9) | collective-permute-done | bytes 794656 | tf_op jit(solution)/shard_map/ppermute | solution.py:644
  56.3 1.8 %collective-permute-start.10 = (f32[512,256]{1,0:T(8,128)S(1)}, f32[512,256]{1,0:T(8,128)S(1)}, u32[]{:S(2)}, u32[]{:S(2)}) collective-permute-start(f32[512,256]{1,0:T(8,128)S(1)} %right_apply.4), channel_id=1, source_target_pairs={{0,4},{4,0},{1,5},{5,1},{2,6},{6,2},{3,7},{7,3},{8,12},{12,8},{9,1... | collective-permute-start | bytes 1572872 | tf_op jit(solution)/shard_map/ppermute | solution.py:644
  58.1 3.0 %left_roots.1.left_ref = bf16[2,2,256,256]{3,2,1,0:T(8,128)(2,1)S(1)} custom-call(f32[1024,256]{1,0:T(8,128)S(1)} %bitcast.5, f32[264,256]{1,0:T(8,128)S(1)} %left_grams.3.a_ref.rest_1_, f32[776,256]{1,0:T(8,128)S(1)} %collective-permute-done.9.rest_0_.b_ref.half_ref), custom_call_target="tpu_custom_call" | custom-call | flops 1 | bytes 1 | tf_op jit(solution)/shard_map/left_roots/pallas_call | solution.py:396
  61.1 9.7 %update.3 = (f32[512,4096]{1,0:T(8,128)}, f32[8,128]{1,0:T(8,128)S(1)}) custom-call(f32[1024,2048]{1,0:T(8,128)S(1)} %load.1.g_ref, bf16[2,2,256,256]{3,2,1,0:T(8,128)(2,1)S(1)} %left_roots.1.left_ref, bf16[8,2,256,256]{3,2,1,0:T(8,128)(2,1)S(1)} %get-tuple-element.26.right_ref), custom_call_target="tpu_custom_call" | custom-call | flops 1 | bytes 1 | tf_op jit(solution)/shard_map/update/pallas_call | solution.py:616
  71.5 8.4 %collective-permute-done.10.rest_0_.half_ref = f32[512,256]{1,0:T(8,128)S(1)} collective-permute-done((f32[512,256]{1,0:T(8,128)S(1)}, f32[512,256]{1,0:T(8,128)S(1)}, u32[]{:S(2)}, u32[]{:S(2)}) %collective-permute-start.10) | collective-permute-done | bytes 524320 | tf_op jit(solution)/shard_map/ppermute | solution.py:644
  80.3 1.8 %collective-permute-start.13 = (f32[512,128]{1,0:T(8,128)S(1)}, f32[512,128]{1,0:T(8,128)S(1)}, u32[]{:S(2)}, u32[]{:S(2)}) collective-permute-start(f32[512,128]{1,0:T(8,128)S(1)} %get-tuple-element.29.rest_1_), channel_id=1, source_target_pairs={{0,4},{4,0},{1,5},{5,1},{2,6},{6,2},{3,7},{7,3},{8,12},{12,8},{9,1... | collective-permute-start | bytes 786440 | tf_op jit(solution)/shard_map/ppermute | solution.py:644
  82.2 1.6 %collective-permute-start.17 = (f32[72,256]{1,0:T(8,128)S(1)}, f32[72,256]{1,0:T(8,128)S(1)}, u32[]{:S(2)}, u32[]{:S(2)}) collective-permute-start(f32[72,256]{1,0:T(8,128)S(1)} %rest_of.1.own_ref), channel_id=1, source_target_pairs={{0,16},{8,24},{16,0},{24,8},{1,17},{9,25},{17,1},{25,9},{2,18},{10... | collective-permute-start | bytes 221192 | tf_op jit(solution)/shard_map/ppermute | solution.py:646
  84.2 1.5 %collective-permute-start.11 = (f32[256,128]{1,0:T(8,128)S(1)}, f32[256,128]{1,0:T(8,128)S(1)}, u32[]{:S(2)}, u32[]{:S(2)}) collective-permute-start(f32[256,128]{1,0:T(8,128)S(1)} %get-tuple-element.27), channel_id=1, source_target_pairs={{0,4},{4,0},{1,5},{5,1},{2,6},{6,2},{3,7},{7,3},{8,12},{12,8},{9,1... | collective-permute-start | bytes 393224 | tf_op jit(solution)/shard_map/ppermute | solution.py:644
  89.4 1.8 %update.4 = (f32[512,4096]{1,0:T(8,128)}, f32[8,128]{1,0:T(8,128)}) custom-call(f32[512,256]{1,0:T(8,128)S(1)} %collective-permute-done.1.rest_1_.g_ref, bf16[2,2,256,256]{3,2,1,0:T(8,128)(2,1)S(1)} %left_roots.1.left_ref, bf16[2,2,256,256]{3,2,1,0:T(8,128)(2,1)S(1)} %join_roots.1.right_ref, ...), custom_call_target="tpu_custom_call", output_to_operand_aliasing={{0}: (3, {})} | custom-call | flops 1 | bytes 1 | tf_op jit(solution)/shard_map/update/pallas_call | solution.py:616
  91.2 1.8 %update.5 = (f32[512,4096]{1,0:T(8,128)}, f32[8,128]{1,0:T(8,128)}) custom-call(f32[512,256]{1,0:T(8,128)S(1)} %collective-permute-done.4.rest_0_.g_ref, bf16[2,2,256,256]{3,2,1,0:T(8,128)(2,1)S(1)} %left_roots.1.left_ref, bf16[2,2,256,256]{3,2,1,0:T(8,128)(2,1)S(1)} %join_roots.1.right_ref, ...), custom_call_target="tpu_custom_call", output_to_operand_aliasing={{0}: (3, {})} | custom-call | flops 1 | bytes 1 | tf_op jit(solution)/shard_map/update/pallas_call | solution.py:616
  97.8 1.8 %collective-permute-done.12.half_ref = f32[256,128]{1,0:T(8,128)S(1)} collective-permute-done((f32[256,128]{1,0:T(8,128)S(1)}, f32[256,128]{1,0:T(8,128)S(1)}, u32[]{:S(2)}, u32[]{:S(2)}) %collective-permute-start.12) | collective-permute-done | bytes 131104 | tf_op jit(solution)/shard_map/ppermute | solution.py:644
  (49 shorter events, 21.3 us)
Async XLA Ops:
  1.1 15.8 %collective-permute-start.1 = (f32[512,256]{1,0:T(8,128)S(1)}, f32[512,256]{1,0:T(8,128)S(1)}, u32[]{:S(2)}, u32[]{:S(2)}) collective-permute-start(f32[512,256]{1,0:T(8,128)S(1)} %take.2.after_ref.rest_0_), channel_id=1, source_target_pairs={{0,4},{4,0},{1,5},{5,1},{2,6},{6,2},{3,7},{7,3},{8,12},{12,8},{9,1... | collective-permute-start | bytes 1572872 | tf_op jit(solution)/shard_map/ppermute | solution.py:644
  9.7 10.8 %copy-start = (f32[1,2048,256]{2,1,0:T(8,128)S(1)}, f32[1,2048,256]{2,1,0:T(8,128)}, u32[]{:S(2)}) copy-start(f32[1,2048,256]{2,1,0:T(8,128)} %param.5) | copy-start | bytes 6291460
  9.7 1.6 %collective-permute-start = (f32[264,256]{1,0:T(8,128)S(1)}, f32[264,256]{1,0:T(8,128)S(1)}, u32[]{:S(2)}, u32[]{:S(2)}) collective-permute-start(f32[264,256]{1,0:T(8,128)S(1)} %get-tuple-element.21.rest_0_), channel_id=1, source_target_pairs={{0,8},{8,0},{16,24},{24,16},{1,9},{9,1},{17,25},{25,17},{2,10},{10... | collective-permute-start | bytes 811016 | tf_op jit(solution)/shard_map/ppermute | solution.py:646
  10.2 18.6 %collective-permute-start.4 = (f32[512,256]{1,0:T(8,128)S(1)}, f32[512,256]{1,0:T(8,128)S(1)}, u32[]{:S(2)}, u32[]{:S(2)}) collective-permute-start(f32[512,256]{1,0:T(8,128)S(1)} %take.3), channel_id=1, source_target_pairs={{0,4},{4,0},{1,5},{5,1},{2,6},{6,2},{3,7},{7,3},{8,12},{12,8},{9,1... | collective-permute-start | bytes 1572872 | tf_op jit(solution)/shard_map/ppermute | solution.py:644
  11.3 8.6 %collective-permute-start.3 = (f32[264,256]{1,0:T(8,128)S(1)}, f32[264,256]{1,0:T(8,128)S(1)}, u32[]{:S(2)}, u32[]{:S(2)}) collective-permute-start(f32[264,256]{1,0:T(8,128)S(1)} %fold.1.rest_0_), channel_id=1, source_target_pairs={{0,16},{8,24},{16,0},{24,8},{1,17},{9,25},{17,1},{25,9},{2,18},{10... | collective-permute-start | bytes 811016 | tf_op jit(solution)/shard_map/ppermute | solution.py:646
  18.9 1.6 %collective-permute-start.2 = (f32[264,256]{1,0:T(8,128)S(1)}, f32[264,256]{1,0:T(8,128)S(1)}, u32[]{:S(2)}, u32[]{:S(2)}) collective-permute-start(f32[264,256]{1,0:T(8,128)S(1)} %get-tuple-element.23), channel_id=1, source_target_pairs={{0,8},{8,0},{16,24},{24,16},{1,9},{9,1},{17,25},{25,17},{2,10},{10... | collective-permute-start | bytes 811016 | tf_op jit(solution)/shard_map/ppermute | solution.py:646
  23.7 15.1 %collective-permute-start.7 = (f32[512,256]{1,0:T(8,128)S(1)}, f32[512,256]{1,0:T(8,128)S(1)}, u32[]{:S(2)}, u32[]{:S(2)}) collective-permute-start(f32[512,256]{1,0:T(8,128)S(1)} %get-tuple-element.25.after_ref), channel_id=1, source_target_pairs={{0,4},{4,0},{1,5},{5,1},{2,6},{6,2},{3,7},{7,3},{8,12},{12,8},{9,1... | collective-permute-start | bytes 1572872 | tf_op jit(solution)/shard_map/ppermute | solution.py:644
  28.8 1.6 %collective-permute-start.5 = (f32[264,256]{1,0:T(8,128)S(1)}, f32[264,256]{1,0:T(8,128)S(1)}, u32[]{:S(2)}, u32[]{:S(2)}) collective-permute-start(f32[264,256]{1,0:T(8,128)S(1)} %hold.2.own_ref), channel_id=1, source_target_pairs={{0,8},{8,0},{16,24},{24,16},{1,9},{9,1},{17,25},{25,17},{2,10},{10... | collective-permute-start | bytes 811016 | tf_op jit(solution)/shard_map/ppermute | solution.py:646
  28.8 8.9 %collective-permute-start.6 = (f32[264,256]{1,0:T(8,128)S(1)}, f32[264,256]{1,0:T(8,128)S(1)}, u32[]{:S(2)}, u32[]{:S(2)}) collective-permute-start(f32[264,256]{1,0:T(8,128)S(1)} %hold.2.own_ref), channel_id=1, source_target_pairs={{0,16},{8,24},{16,0},{24,8},{1,17},{9,25},{17,1},{25,9},{2,18},{10... | collective-permute-start | bytes 811016 | tf_op jit(solution)/shard_map/ppermute | solution.py:646
  30.9 25.0 %collective-permute-start.9 = (f32[776,256]{1,0:T(8,128)S(1)}, f32[776,256]{1,0:T(8,128)S(1)}, u32[]{:S(2)}, u32[]{:S(2)}) collective-permute-start(f32[776,256]{1,0:T(8,128)S(1)} %core_apply.1.rest_0_.after_ref), channel_id=1, source_target_pairs={{0,4},{4,0},{1,5},{5,1},{2,6},{6,2},{3,7},{7,3},{8,12},{12,8},{9,1... | collective-permute-start | bytes 2383880 | tf_op jit(solution)/shard_map/ppermute | solution.py:644
  38.9 3.0 %collective-permute-start.8 = (f32[264,256]{1,0:T(8,128)S(1)}, f32[264,256]{1,0:T(8,128)S(1)}, u32[]{:S(2)}, u32[]{:S(2)}) collective-permute-start(f32[264,256]{1,0:T(8,128)S(1)} %hold.3.x_ref), channel_id=1, source_target_pairs={{0,8},{8,0},{16,24},{24,16},{1,9},{9,1},{17,25},{25,17},{2,10},{10... | collective-permute-start | bytes 811016 | tf_op jit(solution)/shard_map/ppermute | solution.py:646
  42.8 15.3 %copy-start.1 = (f32[1,1024,256]{2,1,0:T(8,128)S(1)}, f32[1,1024,256]{2,1,0:T(8,128)}, u32[]{:S(2)}) copy-start(f32[1,1024,256]{2,1,0:T(8,128)} %param.4) | copy-start | bytes 3145732
  42.8 28.0 %collective-permute-start.14 = (f32[584,256]{1,0:T(8,128)S(1)}, f32[584,256]{1,0:T(8,128)S(1)}, u32[]{:S(2)}, u32[]{:S(2)}) collective-permute-start(f32[584,256]{1,0:T(8,128)S(1)} %right_apply.6), channel_id=1, source_target_pairs={{0,4},{4,0},{1,5},{5,1},{2,6},{6,2},{3,7},{7,3},{8,12},{12,8},{9,1... | collective-permute-start | bytes 1794056 | tf_op jit(solution)/shard_map/ppermute | solution.py:644
  56.3 23.7 %collective-permute-start.10 = (f32[512,256]{1,0:T(8,128)S(1)}, f32[512,256]{1,0:T(8,128)S(1)}, u32[]{:S(2)}, u32[]{:S(2)}) collective-permute-start(f32[512,256]{1,0:T(8,128)S(1)} %right_apply.4), channel_id=1, source_target_pairs={{0,4},{4,0},{1,5},{5,1},{2,6},{6,2},{3,7},{7,3},{8,12},{12,8},{9,1... | collective-permute-start | bytes 1572872 | tf_op jit(solution)/shard_map/ppermute | solution.py:644
  71.2 24.3 %collective-permute-start.15 = (f32[512,256]{1,0:T(8,128)S(1)}, f32[512,256]{1,0:T(8,128)S(1)}, u32[]{:S(2)}, u32[]{:S(2)}) collective-permute-start(f32[512,256]{1,0:T(8,128)S(1)} %right_apply.7), channel_id=1, source_target_pairs={{0,4},{4,0},{1,5},{5,1},{2,6},{6,2},{3,7},{7,3},{8,12},{12,8},{9,1... | collective-permute-start | bytes 1572872 | tf_op jit(solution)/shard_map/ppermute | solution.py:644
  80.3 16.5 %collective-permute-start.13 = (f32[512,128]{1,0:T(8,128)S(1)}, f32[512,128]{1,0:T(8,128)S(1)}, u32[]{:S(2)}, u32[]{:S(2)}) collective-permute-start(f32[512,128]{1,0:T(8,128)S(1)} %get-tuple-element.29.rest_1_), channel_id=1, source_target_pairs={{0,4},{4,0},{1,5},{5,1},{2,6},{6,2},{3,7},{7,3},{8,12},{12,8},{9,1... | collective-permute-start | bytes 786440 | tf_op jit(solution)/shard_map/ppermute | solution.py:644
  82.1 2.1 %collective-permute-start.16 = (f32[72,256]{1,0:T(8,128)S(1)}, f32[72,256]{1,0:T(8,128)S(1)}, u32[]{:S(2)}, u32[]{:S(2)}) collective-permute-start(f32[72,256]{1,0:T(8,128)S(1)} %rest_of.1.own_ref), channel_id=1, source_target_pairs={{0,8},{8,0},{16,24},{24,16},{1,9},{9,1},{17,25},{25,17},{2,10},{10... | collective-permute-start | bytes 221192 | tf_op jit(solution)/shard_map/ppermute | solution.py:646
  82.2 4.7 %collective-permute-start.17 = (f32[72,256]{1,0:T(8,128)S(1)}, f32[72,256]{1,0:T(8,128)S(1)}, u32[]{:S(2)}, u32[]{:S(2)}) collective-permute-start(f32[72,256]{1,0:T(8,128)S(1)} %rest_of.1.own_ref), channel_id=1, source_target_pairs={{0,16},{8,24},{16,0},{24,8},{1,17},{9,25},{17,1},{25,9},{2,18},{10... | collective-permute-start | bytes 221192 | tf_op jit(solution)/shard_map/ppermute | solution.py:646
  83.7 15.9 %collective-permute-start.12 = (f32[256,128]{1,0:T(8,128)S(1)}, f32[256,128]{1,0:T(8,128)S(1)}, u32[]{:S(2)}, u32[]{:S(2)}) collective-permute-start(f32[256,128]{1,0:T(8,128)S(1)} %get-tuple-element.28), channel_id=1, source_target_pairs={{0,4},{4,0},{1,5},{5,1},{2,6},{6,2},{3,7},{7,3},{8,12},{12,8},{9,1... | collective-permute-start | bytes 393224 | tf_op jit(solution)/shard_map/ppermute | solution.py:644
  84.2 17.8 %collective-permute-start.11 = (f32[256,128]{1,0:T(8,128)S(1)}, f32[256,128]{1,0:T(8,128)S(1)}, u32[]{:S(2)}, u32[]{:S(2)}) collective-permute-start(f32[256,128]{1,0:T(8,128)S(1)} %get-tuple-element.27), channel_id=1, source_target_pairs={{0,4},{4,0},{1,5},{5,1},{2,6},{6,2},{3,7},{7,3},{8,12},{12,8},{9,1... | collective-permute-start | bytes 393224 | tf_op jit(solution)/shard_map/ppermute | solution.py:644
  86.8 2.4 %collective-permute-start.18 = (f32[72,256]{1,0:T(8,128)S(1)}, f32[72,256]{1,0:T(8,128)S(1)}, u32[]{:S(2)}, u32[]{:S(2)}) collective-permute-start(f32[72,256]{1,0:T(8,128)S(1)} %collective-permute-done.17.x_ref), channel_id=1, source_target_pairs={{0,8},{8,0},{16,24},{24,16},{1,9},{9,1},{17,25},{25,17},{2,10},{10... | collective-permute-start | bytes 221192 | tf_op jit(solution)/shard_map/ppermute | solution.py:646

commit v10 on v9

--- a/solution.py
+++ b/solution.py
@@ -104,6 +104,16 @@
     return body, jnp.broadcast_to(diag, (PAD, blk))
 
 
+def put_diag(ref, diag):
+    wide = ref.shape[1]
+    for k in range(ref.shape[0]):
+        ref[k : k + 1, :] = diag[:1, k * wide : (k + 1) * wide]
+
+
+def get_diag(ref):
+    return jnp.concatenate([ref[k : k + 1, :] for k in range(ref.shape[0])], axis=1)
+
+
 def unpack(body, diag):
     blk = body.shape[0]
     rows, cols = places(blk)
@@ -157,7 +167,7 @@
     )(tile, *after)
 
 
-def left_gram_kernel(g_ref, after_ref, out_ref, lhh, lcross):
+def left_gram_kernel(g_ref, after_ref, out_ref, diag_ref, lhh, lcross):
     step = pl.program_id(0)
     last = pl.num_programs(0) - 1
     blk = lhh.shape[-1]
@@ -181,16 +191,19 @@
     @pl.when(step == last)
     def _():
         body, diag = pack(*(lhh[b] + (lcross[b] + lcross[b].T) for b in range(2)))
-        out_ref[:blk, :] = body
-        out_ref[blk:, :] = diag
+        out_ref[...] = body
+        put_diag(diag_ref, diag)
 
 
 def left_grams(tile, blk, at, after):
     width = tile.shape[1]
-    tall = blk + PAD
+    half = blk // 2
     return pl.pallas_call(
         left_gram_kernel,
-        out_shape=jax.ShapeDtypeStruct((tall, blk), jnp.float32),
+        out_shape=(
+            jax.ShapeDtypeStruct((blk, blk), jnp.float32),
+            jax.ShapeDtypeStruct((2, half), jnp.float32),
+        ),
         grid_spec=pltpu.PrefetchScalarGridSpec(
             num_scalar_prefetch=0,
             grid=(width // (4 * blk),),
@@ -198,7 +211,7 @@
                 pl.BlockSpec((2 * blk, 4 * blk), placed(lambda s, place: (at(place), s))),
                 pl.BlockSpec(memory_space=pl.ANY),
             ],
-            out_specs=pl.BlockSpec((tall, blk), lambda s: (0, 0)),
+            out_specs=(pl.BlockSpec((blk, blk), lambda s: (0, 0)), pl.BlockSpec((2, half), lambda s: (0, 0))),
             scratch_shapes=[
                 pltpu.VMEM((2, blk, blk), jnp.float32),
                 pltpu.VMEM((2, blk, blk), jnp.float32),
@@ -381,35 +394,33 @@
     )(stats, kept, near, far, tile)
 
 
-def left_kernel(full_dim, stats_ref, a_ref, b_ref, out_ref):
+def left_kernel(full_dim, stats_ref, a_ref, a_diag, b_ref, rest_ref, after_ref, out_ref):
     blk = stats_ref.shape[1]
-    total = a_ref[...] + b_ref[b_ref.shape[0] - a_ref.shape[0] :, :]
-    for b, root in enumerate(pair_roots(full_dim, stats_ref, total[:blk], total[blk : blk + 1])):
+    at = rest_ref.shape[0] - PAD + 1
+    body = a_ref[...] + b_ref[b_ref.shape[0] - blk :, :]
+    for b, root in enumerate(pair_roots(full_dim, stats_ref, body, get_diag(a_diag) + rest_ref[at : at + 1, :])):
         high, low = split(root)
         out_ref[b, 0] = high
         out_ref[b, 1] = low
 
 
-def left_roots(full_dim, stats, kept, came):
+def left_roots(full_dim, stats, after, *parts):
     blk = stats.shape[1]
-    tall = blk + PAD
     return pl.pallas_call(
         functools.partial(left_kernel, full_dim),
         out_shape=jax.ShapeDtypeStruct((2, 2, blk, blk), jnp.bfloat16),
         grid_spec=pltpu.PrefetchScalarGridSpec(
             num_scalar_prefetch=0,
             grid=(1,),
-            in_specs=[
-                pl.BlockSpec((2 * blk, blk), placed(lambda s, place: (place[1], 0))),
-                pl.BlockSpec((tall, blk), lambda s: (0, 0)),
-                pl.BlockSpec(came.shape, lambda s: (0, 0)),
-            ],
+            in_specs=[pl.BlockSpec((2 * blk, blk), placed(lambda s, place: (place[1], 0)))]
+            + [pl.BlockSpec(part.shape, lambda s: (0, 0)) for part in parts]
+            + [pl.BlockSpec(memory_space=pl.ANY)],
             out_specs=pl.BlockSpec((2, 2, blk, blk), lambda s: (0, 0, 0, 0)),
         ),
         compiler_params=pltpu.CompilerParams(vmem_limit_bytes=VMEM_LIMIT),
         cost_estimate=SMALL,
         name="left_roots",
-    )(stats, kept, came)
+    )(stats, *parts, after)
 
 
 def put_roots(out_ref, at, roots):
@@ -419,7 +430,7 @@
         out_ref[at + b, 1] = low
 
 
-def spread_kernel(own_ref, c_ref, x_ref, xc_ref, out_ref, cut_ref, seconds, body):
+def spread_kernel(own_ref, c_ref, x_ref, xc_ref, ldiag_ref, out_ref, cut_ref, seconds, body):
     blk = out_ref.shape[-1]
     r = here()[0]
     for flip, ref in enumerate((own_ref, c_ref, x_ref, xc_ref)):
@@ -429,10 +440,11 @@
     part = cut_ref.shape[0] - PAD
     body[...], diag = pack(seconds[RAW[0] // 2], seconds[RAW[1] // 2])
     cut_ref[:part, :] = body[pl.ds(pl.multiple_of(r * part, part), part), :]
-    cut_ref[part:, :] = diag
-
-
-def spread_roots(*packed):
+    which = lax.broadcasted_iota(jnp.int32, diag.shape, 0)
+    cut_ref[part:, :] = jnp.where(which == 1, get_diag(ldiag_ref), diag)
+
+
+def spread_roots(ldiag, *packed):
     blk = packed[0].shape[1]
     count = len(packed)
     return pl.pallas_call(
@@ -445,7 +457,7 @@
         compiler_params=pltpu.CompilerParams(vmem_limit_bytes=VMEM_LIMIT),
         cost_estimate=SMALL,
         name="spread_roots",
-    )(*packed)
+    )(*packed, ldiag)
 
 
 def rest_kernel(a_ref, out_ref):
@@ -494,16 +506,16 @@
     tall, blk = packed.shape
     return pl.pallas_call(
         core_apply_kernel,
-        out_shape=jax.ShapeDtypeStruct((rows + tall, blk), jnp.float32),
+        out_shape=jax.ShapeDtypeStruct((rows + blk, blk), jnp.float32),
         grid_spec=pltpu.PrefetchScalarGridSpec(
             num_scalar_prefetch=0,
             grid=(1,),
             in_specs=[
                 pl.BlockSpec((rows, blk), placed(lambda s, place: (1 - place[1], core_first(place)))),
                 pl.BlockSpec((tall, blk), lambda s: (0, 0)),
-                pl.BlockSpec((tall, blk), lambda s: (0, 0)),
+                pl.BlockSpec((blk, blk), lambda s: (0, 0)),
             ],
-            out_specs=pl.BlockSpec((rows + tall, blk), lambda s: (0, 0)),
+            out_specs=pl.BlockSpec((rows + blk, blk), lambda s: (0, 0)),
         ),
         compiler_params=pltpu.CompilerParams(vmem_limit_bytes=VMEM_LIMIT),
         cost_estimate=SMALL,
@@ -658,15 +670,15 @@
 
     own, half = right_roots(full_dim, rstats, keep, near, far, tile)
     came_a = over("y", half)
-    lsend = left_grams(tile, blk, lambda place: 1 - place[1], half)
+    lsend, ldiag = left_grams(tile, blk, lambda place: 1 - place[1], half)
     own = hold(own, raw[1], lsend)
     own_c = over("core", own)
     own_x = over("x", own)
     half = core_apply(tile, own_c, lsend)
     came_b = over("y", half)
     own_x = hold(own_x, half, came_a)
-    lkeep = left_grams(tile, blk, lambda place: place[1], half)
-    roots, part = spread_roots(own, own_c, own_x, over("core", own_x))
+    lkeep, kdiag = left_grams(tile, blk, lambda place: place[1], half)
+    roots, part = spread_roots(ldiag, own, own_c, own_x, over("core", own_x))
 
     (half,) = right_apply(tile, roots, 0, None, part, (lkeep,))
     came_c = over("y", half)
@@ -676,17 +688,17 @@
     def crossed(block, start=0):
         return lambda place: (1 - place[1]) * tile_cols + block(place) * blk + start
 
-    left = left_roots(full_dim, lstats, lkeep, came_b)
+    (half,) = right_apply(tile, roots, 2, None, None, (came_c,))
+    came_e = over("y", half)
+    left = left_roots(full_dim, lstats, half, lkeep, kdiag, came_b, came_c)
     out, done = update(
         tile, left, roots, None, shape,
         lambda s, place: (place[1], s),
         lambda s, place: (0, place[1] * halves + s),
     )
-    (half,) = right_apply(tile, roots, 2, None, None, (came_c, done))
-    came_e = over("y", half)
     wide = blk // 2
     last = ((0, rows, 0, wide), (0, blk, wide, wide), (blk, blk, wide, wide))
-    held = right_apply(tile, roots, 3, last, None, (came_d,))
+    held = right_apply(tile, roots, 3, last, None, (came_d, done))
     came_last = [over("y", half) for half in held]
     out = finish(came_a, left, out, crossed(own_first))
     out = finish(came_b, left, out, crossed(core_first))

time: 103 us -> 103 us (level)
  transfers between devices with their start and end apart: 19 -> 19, of which waited for: 12 -> 10; matrix products, arithmetic and copies ran while one was open for 0% -> 0% of each run, Pallas kernels for 43% -> 43%
where the time goes in v10:
time: 103 us
  Pallas kernels  46 us (45%)
  waiting for transfers between devices  37.5 us (36%)
  starting transfers between devices  18.9 us (18%)
    ppermute x10, waiting for transfers between devices, over(): return lax.ppermute(value, 'col', [(0, 1), (1, 0)])  27.8 us
    ppermute x10, starting transfers between devices, over(): return lax.ppermute(value, 'col', [(0, 1), (1, 0)])  13.7 us
    pallas_call x3, Pallas kernels, update(): pl.pallas_call(update_kernel, out_shape=(jax.ShapeDtypeStruct(out_shape,...  13.3 us
    ppermute x9, waiting for transfers between devices, over(): return lax.ppermute(value, 'row', [(i, i ^ flip) for i in range(n_row)])  9.65 us
    pallas_call x8, Pallas kernels, finish(): pl.pallas_call(functools.partial(finish_kernel, column, first), out_shape...  8.9 us
    pallas_call x2, Pallas kernels, left_grams(): pl.pallas_call(left_gram_kernel, out_shape=(jax.ShapeDtypeStruct((blk, bl...  5.78 us
    ppermute x9, starting transfers between devices, over(): return lax.ppermute(value, 'row', [(i, i ^ flip) for i in range(n_row)])  5.2 us
    pallas_call x2, Pallas kernels, right_grams(): pl.pallas_call(right_gram_kernel, out_shape=(jax.ShapeDtypeStruct((tall,...  4.12 us
  transfers between devices with their start and end apart: 19, of which 10 were waited for; matrix products, arithmetic and copies ran while one was open for 0% of the time, Pallas kernels for 43%

profile of v10, /device:TPU:0, one launch (start us, length us, event | category | flops | bytes accessed | tf_op | source)
XLA Modules:
  0.0 102.9 jit_solution(15359234570420633739)
XLA Ops:
  1.1 3.0 %collective-permute-start.1 = (f32[512,256]{1,0:T(8,128)S(1)}, f32[512,256]{1,0:T(8,128)S(1)}, u32[]{:S(2)}, u32[]{:S(2)}) collective-permute-start(f32[512,256]{1,0:T(8,128)S(1)} %take.2.after_ref.rest_0_), channel_id=1, source_target_pairs={{0,4},{4,0},{1,5},{5,1},{2,6},{6,2},{3,7},{7,3},{8,12},{12,8},{9,1... | collective-permute-start | bytes 1572872 | tf_op jit(solution)/shard_map/ppermute | solution.py:656
  4.1 3.5 %load.1.g_ref = f32[1024,2048]{1,0:T(8,128)S(1)} custom-call(f32[1024,2048]{1,0:T(8,128)} %bitcast.7, f32[512,256]{1,0:T(8,128)S(1)} %take.2.after_ref.rest_0_), custom_call_target="tpu_custom_call" | custom-call | flops 1 | bytes 1 | tf_op jit(solution)/shard_map/load/pallas_call | solution.py:284
  7.6 2.1 %right_grams.2 = (f32[264,256]{1,0:T(8,128)S(1)}, f32[264,256]{1,0:T(8,128)S(1)}) custom-call(f32[1024,2048]{1,0:T(8,128)S(1)} %load.1.g_ref, f32[512,256]{1,0:T(8,128)S(1)} %take.2.after_ref.rest_0_), custom_call_target="tpu_custom_call" | custom-call | flops 1 | bytes 1 | tf_op jit(solution)/shard_map/right_grams/pallas_call | solution.py:152
  11.3 1.5 %collective-permute-start.3 = (f32[264,256]{1,0:T(8,128)S(1)}, f32[264,256]{1,0:T(8,128)S(1)}, u32[]{:S(2)}, u32[]{:S(2)}) collective-permute-start(f32[264,256]{1,0:T(8,128)S(1)} %fold.1.rest_0_), channel_id=1, source_target_pairs={{0,16},{8,24},{16,0},{24,8},{1,17},{9,25},{17,1},{25,9},{2,18},{10... | collective-permute-start | bytes 811016 | tf_op jit(solution)/shard_map/ppermute | solution.py:658
  12.9 4.0 %collective-permute-done.1.rest_1_.g_ref = f32[512,256]{1,0:T(8,128)S(1)} collective-permute-done((f32[512,256]{1,0:T(8,128)S(1)}, f32[512,256]{1,0:T(8,128)S(1)}, u32[]{:S(2)}, u32[]{:S(2)}) %collective-permute-start.1) | collective-permute-done | bytes 524320 | tf_op jit(solution)/shard_map/ppermute | solution.py:656
  16.8 2.0 %right_grams.3 = (f32[264,256]{1,0:T(8,128)S(1)}, f32[264,256]{1,0:T(8,128)S(1)}) custom-call(f32[1024,2048]{1,0:T(8,128)S(1)} %load.1.g_ref, f32[264,256]{1,0:T(8,128)S(1)} %fold.1.rest_0_, f32[512,256]{1,0:T(8,128)S(1)} %collective-permute-done.1.rest_1_.g_ref), custom_call_target="tpu_custom_call" | custom-call | flops 1 | bytes 1 | tf_op jit(solution)/shard_map/right_grams/pallas_call | solution.py:152
  20.5 3.2 %right_roots.1 = (f32[264,256]{1,0:T(8,128)S(1)}, f32[512,256]{1,0:T(8,128)S(1)}) custom-call(f32[2048,256]{1,0:T(8,128)S(1)} %bitcast.4, f32[264,256]{1,0:T(8,128)S(1)} %get-tuple-element.26.a_ref, f32[264,256]{1,0:T(8,128)S(1)} %collective-permute-done.2.b_ref, f32[264,256]{1,0:T(8,128)S(1)} %collective-permute-done.3.c_ref, f32[1024,2048]{1,0:T(8,128)S(1)} %load.1.g_ref), custom_call_target="tpu_custom_call" | custom-call | flops 1 | bytes 1 | tf_op jit(solution)/shard_map/right_roots/pallas_call | solution.py:370
  23.7 2.1 %collective-permute-start.7 = (f32[512,256]{1,0:T(8,128)S(1)}, f32[512,256]{1,0:T(8,128)S(1)}, u32[]{:S(2)}, u32[]{:S(2)}) collective-permute-start(f32[512,256]{1,0:T(8,128)S(1)} %get-tuple-element.29.after_ref), channel_id=1, source_target_pairs={{0,4},{4,0},{1,5},{5,1},{2,6},{6,2},{3,7},{7,3},{8,12},{12,8},{9,1... | collective-permute-start | bytes 1572872 | tf_op jit(solution)/shard_map/ppermute | solution.py:656
  25.8 2.9 %left_grams.2 = (f32[256,256]{1,0:T(8,128)S(1)}, f32[2,128]{1,0:T(2,128)S(1)}) custom-call(f32[1024,2048]{1,0:T(8,128)S(1)} %load.1.g_ref, f32[512,256]{1,0:T(8,128)S(1)} %get-tuple-element.29.after_ref), custom_call_target="tpu_custom_call" | custom-call | flops 1 | bytes 1 | tf_op jit(solution)/shard_map/left_grams/pallas_call | solution.py:201
  28.8 1.6 %collective-permute-start.6 = (f32[264,256]{1,0:T(8,128)S(1)}, f32[264,256]{1,0:T(8,128)S(1)}, u32[]{:S(2)}, u32[]{:S(2)}) collective-permute-start(f32[264,256]{1,0:T(8,128)S(1)} %hold.2.own_ref), channel_id=1, source_target_pairs={{0,16},{8,24},{16,0},{24,8},{1,17},{9,25},{17,1},{25,9},{2,18},{10... | collective-permute-start | bytes 811016 | tf_op jit(solution)/shard_map/ppermute | solution.py:658
  31.5 6.2 %collective-permute-done.6.a_ref = f32[264,256]{1,0:T(8,128)S(1)} collective-permute-done((f32[264,256]{1,0:T(8,128)S(1)}, f32[264,256]{1,0:T(8,128)S(1)}, u32[]{:S(2)}, u32[]{:S(2)}) %collective-permute-start.6) | collective-permute-done | bytes 270368 | tf_op jit(solution)/shard_map/ppermute | solution.py:658
  38.9 2.9 %left_grams.3 = (f32[256,256]{1,0:T(8,128)S(1)}, f32[2,128]{1,0:T(2,128)S(1)}) custom-call(f32[1024,2048]{1,0:T(8,128)S(1)} %load.1.g_ref, f32[768,256]{1,0:T(8,128)S(1)} %core_apply.1.rest_0_.after_ref), custom_call_target="tpu_custom_call" | custom-call | flops 1 | bytes 1 | tf_op jit(solution)/shard_map/left_grams/pallas_call | solution.py:201
  42.8 1.8 %collective-permute-start.11 = (f32[584,256]{1,0:T(8,128)S(1)}, f32[584,256]{1,0:T(8,128)S(1)}, u32[]{:S(2)}, u32[]{:S(2)}) collective-permute-start(f32[584,256]{1,0:T(8,128)S(1)} %right_apply.5), channel_id=1, source_target_pairs={{0,4},{4,0},{1,5},{5,1},{2,6},{6,2},{3,7},{7,3},{8,12},{12,8},{9,1... | collective-permute-start | bytes 1794056 | tf_op jit(solution)/shard_map/ppermute | solution.py:656
  44.6 11.1 %collective-permute-done.9.rest_0_.b_ref.half_ref = f32[768,256]{1,0:T(8,128)S(1)} collective-permute-done((f32[768,256]{1,0:T(8,128)S(1)}, f32[768,256]{1,0:T(8,128)S(1)}, u32[]{:S(2)}, u32[]{:S(2)}) %collective-permute-start.9) | collective-permute-done | bytes 786464 | tf_op jit(solution)/shard_map/ppermute | solution.py:656
  56.1 1.8 %collective-permute-start.10 = (f32[512,256]{1,0:T(8,128)S(1)}, f32[512,256]{1,0:T(8,128)S(1)}, u32[]{:S(2)}, u32[]{:S(2)}) collective-permute-start(f32[512,256]{1,0:T(8,128)S(1)} %right_apply.4), channel_id=1, source_target_pairs={{0,4},{4,0},{1,5},{5,1},{2,6},{6,2},{3,7},{7,3},{8,12},{12,8},{9,1... | collective-permute-start | bytes 1572872 | tf_op jit(solution)/shard_map/ppermute | solution.py:656
  57.9 10.6 %collective-permute-done.11.rest_0_.rest_ref.a_ref.half_ref = f32[584,256]{1,0:T(8,128)S(1)} collective-permute-done((f32[584,256]{1,0:T(8,128)S(1)}, f32[584,256]{1,0:T(8,128)S(1)}, u32[]{:S(2)}, u32[]{:S(2)}) %collective-permute-start.11) | collective-permute-done | bytes 598048 | tf_op jit(solution)/shard_map/ppermute | solution.py:656
  68.9 1.8 %collective-permute-start.15 = (f32[512,256]{1,0:T(8,128)S(1)}, f32[512,256]{1,0:T(8,128)S(1)}, u32[]{:S(2)}, u32[]{:S(2)}) collective-permute-start(f32[512,256]{1,0:T(8,128)S(1)} %right_apply.6.after_ref), channel_id=1, source_target_pairs={{0,4},{4,0},{1,5},{5,1},{2,6},{6,2},{3,7},{7,3},{8,12},{12,8},{9,1... | collective-permute-start | bytes 1572872 | tf_op jit(solution)/shard_map/ppermute | solution.py:656
  70.7 3.0 %left_roots.1.left_ref = bf16[2,2,256,256]{3,2,1,0:T(8,128)(2,1)S(1)} custom-call(f32[1024,256]{1,0:T(8,128)S(1)} %bitcast.5, f32[256,256]{1,0:T(8,128)S(1)} %get-tuple-element.33.rest_1_.a_ref, f32[2,128]{1,0:T(2,128)S(1)} %get-tuple-element.34.a_diag, f32[768,256]{1,0:T(8,128)S(1)} %collective-permute-done.9.rest_0_.b_ref.half_ref, ...), custom_call_target="tpu_custom_call" | custom-call | flops 1 | bytes 1 | tf_op jit(solution)/shard_map/left_roots/pallas_call | solution.py:409
  73.7 9.7 %update.3 = (f32[512,4096]{1,0:T(8,128)}, f32[8,128]{1,0:T(8,128)S(1)}) custom-call(f32[1024,2048]{1,0:T(8,128)S(1)} %load.1.g_ref, bf16[2,2,256,256]{3,2,1,0:T(8,128)(2,1)S(1)} %left_roots.1.left_ref, bf16[8,2,256,256]{3,2,1,0:T(8,128)(2,1)S(1)} %get-tuple-element.32.right_ref), custom_call_target="tpu_custom_call" | custom-call | flops 1 | bytes 1 | tf_op jit(solution)/shard_map/update/pallas_call | solution.py:628
  84.2 1.8 %collective-permute-start.17 = (f32[72,256]{1,0:T(8,128)S(1)}, f32[72,256]{1,0:T(8,128)S(1)}, u32[]{:S(2)}, u32[]{:S(2)}) collective-permute-start(f32[72,256]{1,0:T(8,128)S(1)} %rest_of.1.own_ref), channel_id=1, source_target_pairs={{0,16},{8,24},{16,0},{24,8},{1,17},{9,25},{17,1},{25,9},{2,18},{10... | collective-permute-start | bytes 221192 | tf_op jit(solution)/shard_map/ppermute | solution.py:658
  86.0 1.5 %collective-permute-start.13 = (f32[256,128]{1,0:T(8,128)S(1)}, f32[256,128]{1,0:T(8,128)S(1)}, u32[]{:S(2)}, u32[]{:S(2)}) collective-permute-start(f32[256,128]{1,0:T(8,128)S(1)} %get-tuple-element.38), channel_id=1, source_target_pairs={{0,4},{4,0},{1,5},{5,1},{2,6},{6,2},{3,7},{7,3},{8,12},{12,8},{9,1... | collective-permute-start | bytes 393224 | tf_op jit(solution)/shard_map/ppermute | solution.py:656
  88.8 1.2 %finish.8.out_before = f32[512,4096]{1,0:T(8,128)} custom-call(f32[512,256]{1,0:T(8,128)S(1)} %collective-permute-done.7.rest_1_.half_ref, bf16[2,2,256,256]{3,2,1,0:T(8,128)(2,1)S(1)} %left_roots.1.left_ref, f32[512,4096]{1,0:T(8,128)} %get-tuple-element.40.out_before), custom_call_target="tpu_custom_call", output_to_operand_aliasing={{}: (2, {})} | custom-call | flops 1 | bytes 1 | tf_op jit(solution)/shard_map/finish/pallas_call | solution.py:600
  91.5 1.8 %update.4 = (f32[512,4096]{1,0:T(8,128)}, f32[8,128]{1,0:T(8,128)}) custom-call(f32[512,256]{1,0:T(8,128)S(1)} %collective-permute-done.1.rest_1_.g_ref, bf16[2,2,256,256]{3,2,1,0:T(8,128)(2,1)S(1)} %left_roots.1.left_ref, bf16[2,2,256,256]{3,2,1,0:T(8,128)(2,1)S(1)} %join_roots.1.right_ref, ...), custom_call_target="tpu_custom_call", output_to_operand_aliasing={{0}: (3, {})} | custom-call | flops 1 | bytes 1 | tf_op jit(solution)/shard_map/update/pallas_call | solution.py:628
  93.3 1.8 %update.5 = (f32[512,4096]{1,0:T(8,128)}, f32[8,128]{1,0:T(8,128)}) custom-call(f32[512,256]{1,0:T(8,128)S(1)} %collective-permute-done.4.rest_0_.g_ref, bf16[2,2,256,256]{3,2,1,0:T(8,128)(2,1)S(1)} %left_roots.1.left_ref, bf16[2,2,256,256]{3,2,1,0:T(8,128)(2,1)S(1)} %join_roots.1.right_ref, ...), custom_call_target="tpu_custom_call", output_to_operand_aliasing={{0}: (3, {})} | custom-call | flops 1 | bytes 1 | tf_op jit(solution)/shard_map/update/pallas_call | solution.py:628
  (49 shorter events, 19.4 us)
Async XLA Ops:
  1.1 15.8 %collective-permute-start.1 = (f32[512,256]{1,0:T(8,128)S(1)}, f32[512,256]{1,0:T(8,128)S(1)}, u32[]{:S(2)}, u32[]{:S(2)}) collective-permute-start(f32[512,256]{1,0:T(8,128)S(1)} %take.2.after_ref.rest_0_), channel_id=1, source_target_pairs={{0,4},{4,0},{1,5},{5,1},{2,6},{6,2},{3,7},{7,3},{8,12},{12,8},{9,1... | collective-permute-start | bytes 1572872 | tf_op jit(solution)/shard_map/ppermute | solution.py:656
  9.7 10.8 %copy-start = (f32[1,2048,256]{2,1,0:T(8,128)S(1)}, f32[1,2048,256]{2,1,0:T(8,128)}, u32[]{:S(2)}) copy-start(f32[1,2048,256]{2,1,0:T(8,128)} %param.5) | copy-start | bytes 6291460
  9.7 1.6 %collective-permute-start = (f32[264,256]{1,0:T(8,128)S(1)}, f32[264,256]{1,0:T(8,128)S(1)}, u32[]{:S(2)}, u32[]{:S(2)}) collective-permute-start(f32[264,256]{1,0:T(8,128)S(1)} %get-tuple-element.25.rest_0_), channel_id=1, source_target_pairs={{0,8},{8,0},{16,24},{24,16},{1,9},{9,1},{17,25},{25,17},{2,10},{10... | collective-permute-start | bytes 811016 | tf_op jit(solution)/shard_map/ppermute | solution.py:658
  10.2 18.6 %collective-permute-start.4 = (f32[512,256]{1,0:T(8,128)S(1)}, f32[512,256]{1,0:T(8,128)S(1)}, u32[]{:S(2)}, u32[]{:S(2)}) collective-permute-start(f32[512,256]{1,0:T(8,128)S(1)} %take.3), channel_id=1, source_target_pairs={{0,4},{4,0},{1,5},{5,1},{2,6},{6,2},{3,7},{7,3},{8,12},{12,8},{9,1... | collective-permute-start | bytes 1572872 | tf_op jit(solution)/shard_map/ppermute | solution.py:656
  11.3 8.6 %collective-permute-start.3 = (f32[264,256]{1,0:T(8,128)S(1)}, f32[264,256]{1,0:T(8,128)S(1)}, u32[]{:S(2)}, u32[]{:S(2)}) collective-permute-start(f32[264,256]{1,0:T(8,128)S(1)} %fold.1.rest_0_), channel_id=1, source_target_pairs={{0,16},{8,24},{16,0},{24,8},{1,17},{9,25},{17,1},{25,9},{2,18},{10... | collective-permute-start | bytes 811016 | tf_op jit(solution)/shard_map/ppermute | solution.py:658
  18.9 1.6 %collective-permute-start.2 = (f32[264,256]{1,0:T(8,128)S(1)}, f32[264,256]{1,0:T(8,128)S(1)}, u32[]{:S(2)}, u32[]{:S(2)}) collective-permute-start(f32[264,256]{1,0:T(8,128)S(1)} %get-tuple-element.27), channel_id=1, source_target_pairs={{0,8},{8,0},{16,24},{24,16},{1,9},{9,1},{17,25},{25,17},{2,10},{10... | collective-permute-start | bytes 811016 | tf_op jit(solution)/shard_map/ppermute | solution.py:658
  23.7 15.1 %collective-permute-start.7 = (f32[512,256]{1,0:T(8,128)S(1)}, f32[512,256]{1,0:T(8,128)S(1)}, u32[]{:S(2)}, u32[]{:S(2)}) collective-permute-start(f32[512,256]{1,0:T(8,128)S(1)} %get-tuple-element.29.after_ref), channel_id=1, source_target_pairs={{0,4},{4,0},{1,5},{5,1},{2,6},{6,2},{3,7},{7,3},{8,12},{12,8},{9,1... | collective-permute-start | bytes 1572872 | tf_op jit(solution)/shard_map/ppermute | solution.py:656
  28.8 1.6 %collective-permute-start.5 = (f32[264,256]{1,0:T(8,128)S(1)}, f32[264,256]{1,0:T(8,128)S(1)}, u32[]{:S(2)}, u32[]{:S(2)}) collective-permute-start(f32[264,256]{1,0:T(8,128)S(1)} %hold.2.own_ref), channel_id=1, source_target_pairs={{0,8},{8,0},{16,24},{24,16},{1,9},{9,1},{17,25},{25,17},{2,10},{10... | collective-permute-start | bytes 811016 | tf_op jit(solution)/shard_map/ppermute | solution.py:658
  28.8 8.9 %collective-permute-start.6 = (f32[264,256]{1,0:T(8,128)S(1)}, f32[264,256]{1,0:T(8,128)S(1)}, u32[]{:S(2)}, u32[]{:S(2)}) collective-permute-start(f32[264,256]{1,0:T(8,128)S(1)} %hold.2.own_ref), channel_id=1, source_target_pairs={{0,16},{8,24},{16,0},{24,8},{1,17},{9,25},{17,1},{25,9},{2,18},{10... | collective-permute-start | bytes 811016 | tf_op jit(solution)/shard_map/ppermute | solution.py:658
  30.9 24.8 %collective-permute-start.9 = (f32[768,256]{1,0:T(8,128)S(1)}, f32[768,256]{1,0:T(8,128)S(1)}, u32[]{:S(2)}, u32[]{:S(2)}) collective-permute-start(f32[768,256]{1,0:T(8,128)S(1)} %core_apply.1.rest_0_.after_ref), channel_id=1, source_target_pairs={{0,4},{4,0},{1,5},{5,1},{2,6},{6,2},{3,7},{7,3},{8,12},{12,8},{9,1... | collective-permute-start | bytes 2359304 | tf_op jit(solution)/shard_map/ppermute | solution.py:656
  38.9 3.0 %collective-permute-start.8 = (f32[264,256]{1,0:T(8,128)S(1)}, f32[264,256]{1,0:T(8,128)S(1)}, u32[]{:S(2)}, u32[]{:S(2)}) collective-permute-start(f32[264,256]{1,0:T(8,128)S(1)} %hold.3.x_ref), channel_id=1, source_target_pairs={{0,8},{8,0},{16,24},{24,16},{1,9},{9,1},{17,25},{25,17},{2,10},{10... | collective-permute-start | bytes 811016 | tf_op jit(solution)/shard_map/ppermute | solution.py:658
  42.8 25.7 %collective-permute-start.11 = (f32[584,256]{1,0:T(8,128)S(1)}, f32[584,256]{1,0:T(8,128)S(1)}, u32[]{:S(2)}, u32[]{:S(2)}) collective-permute-start(f32[584,256]{1,0:T(8,128)S(1)} %right_apply.5), channel_id=1, source_target_pairs={{0,4},{4,0},{1,5},{5,1},{2,6},{6,2},{3,7},{7,3},{8,12},{12,8},{9,1... | collective-permute-start | bytes 1794056 | tf_op jit(solution)/shard_map/ppermute | solution.py:656
  56.1 14.6 %copy-start.1 = (f32[1,1024,256]{2,1,0:T(8,128)S(1)}, f32[1,1024,256]{2,1,0:T(8,128)}, u32[]{:S(2)}) copy-start(f32[1,1024,256]{2,1,0:T(8,128)} %param.4) | copy-start | bytes 3145732
  56.1 27.3 %collective-permute-start.10 = (f32[512,256]{1,0:T(8,128)S(1)}, f32[512,256]{1,0:T(8,128)S(1)}, u32[]{:S(2)}, u32[]{:S(2)}) collective-permute-start(f32[512,256]{1,0:T(8,128)S(1)} %right_apply.4), channel_id=1, source_target_pairs={{0,4},{4,0},{1,5},{5,1},{2,6},{6,2},{3,7},{7,3},{8,12},{12,8},{9,1... | collective-permute-start | bytes 1572872 | tf_op jit(solution)/shard_map/ppermute | solution.py:656
  68.9 28.6 %collective-permute-start.15 = (f32[512,256]{1,0:T(8,128)S(1)}, f32[512,256]{1,0:T(8,128)S(1)}, u32[]{:S(2)}, u32[]{:S(2)}) collective-permute-start(f32[512,256]{1,0:T(8,128)S(1)} %right_apply.6.after_ref), channel_id=1, source_target_pairs={{0,4},{4,0},{1,5},{5,1},{2,6},{6,2},{3,7},{7,3},{8,12},{12,8},{9,1... | collective-permute-start | bytes 1572872 | tf_op jit(solution)/shard_map/ppermute | solution.py:656
  83.8 14.9 %collective-permute-start.14 = (f32[512,128]{1,0:T(8,128)S(1)}, f32[512,128]{1,0:T(8,128)S(1)}, u32[]{:S(2)}, u32[]{:S(2)}) collective-permute-start(f32[512,128]{1,0:T(8,128)S(1)} %get-tuple-element.39.rest_1_), channel_id=1, source_target_pairs={{0,4},{4,0},{1,5},{5,1},{2,6},{6,2},{3,7},{7,3},{8,12},{12,8},{9,1... | collective-permute-start | bytes 786440 | tf_op jit(solution)/shard_map/ppermute | solution.py:656
  84.1 3.4 %collective-permute-start.16 = (f32[72,256]{1,0:T(8,128)S(1)}, f32[72,256]{1,0:T(8,128)S(1)}, u32[]{:S(2)}, u32[]{:S(2)}) collective-permute-start(f32[72,256]{1,0:T(8,128)S(1)} %rest_of.1.own_ref), channel_id=1, source_target_pairs={{0,8},{8,0},{16,24},{24,16},{1,9},{9,1},{17,25},{25,17},{2,10},{10... | collective-permute-start | bytes 221192 | tf_op jit(solution)/shard_map/ppermute | solution.py:658
  84.2 4.7 %collective-permute-start.17 = (f32[72,256]{1,0:T(8,128)S(1)}, f32[72,256]{1,0:T(8,128)S(1)}, u32[]{:S(2)}, u32[]{:S(2)}) collective-permute-start(f32[72,256]{1,0:T(8,128)S(1)} %rest_of.1.own_ref), channel_id=1, source_target_pairs={{0,16},{8,24},{16,0},{24,8},{1,17},{9,25},{17,1},{25,9},{2,18},{10... | collective-permute-start | bytes 221192 | tf_op jit(solution)/shard_map/ppermute | solution.py:658
  86.0 13.8 %collective-permute-start.13 = (f32[256,128]{1,0:T(8,128)S(1)}, f32[256,128]{1,0:T(8,128)S(1)}, u32[]{:S(2)}, u32[]{:S(2)}) collective-permute-start(f32[256,128]{1,0:T(8,128)S(1)} %get-tuple-element.38), channel_id=1, source_target_pairs={{0,4},{4,0},{1,5},{5,1},{2,6},{6,2},{3,7},{7,3},{8,12},{12,8},{9,1... | collective-permute-start | bytes 393224 | tf_op jit(solution)/shard_map/ppermute | solution.py:656
  87.5 14.4 %collective-permute-start.12 = (f32[256,128]{1,0:T(8,128)S(1)}, f32[256,128]{1,0:T(8,128)S(1)}, u32[]{:S(2)}, u32[]{:S(2)}) collective-permute-start(f32[256,128]{1,0:T(8,128)S(1)} %get-tuple-element.37), channel_id=1, source_target_pairs={{0,4},{4,0},{1,5},{5,1},{2,6},{6,2},{3,7},{7,3},{8,12},{12,8},{9,1... | collective-permute-start | bytes 393224 | tf_op jit(solution)/shard_map/ppermute | solution.py:656
  88.8 2.4 %collective-permute-start.18 = (f32[72,256]{1,0:T(8,128)S(1)}, f32[72,256]{1,0:T(8,128)S(1)}, u32[]{:S(2)}, u32[]{:S(2)}) collective-permute-start(f32[72,256]{1,0:T(8,128)S(1)} %collective-permute-done.17.x_ref), channel_id=1, source_target_pairs={{0,8},{8,0},{16,24},{24,16},{1,9},{9,1},{17,25},{25,17},{2,10},{10... | collective-permute-start | bytes 221192 | tf_op jit(solution)/shard_map/ppermute | solution.py:658

commit v11 on v9

--- a/solution.py
+++ b/solution.py
@@ -566,16 +566,18 @@
 def finish_kernel(column, first, half_ref, left_ref, out_before, out_ref, stage, sems):
     blk = left_ref.shape[-1]
     width = stage.shape[1]
+    part = blk // 2
     cols = pl.ds(pl.multiple_of(column(here()), width), width)
     copies = []
     for i in range(stage.shape[0] // blk):
-        rows = pl.ds(i * blk, blk)
-        root = (left_ref[first + i, 0], left_ref[first + i, 1])
-        stage[rows, :] = product(root, split(half_ref[rows, :]))
-        copies.append(
-            pltpu.make_async_copy(stage.at[rows, :], out_ref.at[pl.ds((first + i) * blk, blk), cols], sems.at[i])
-        )
-        copies[i].start()
+        value = split(half_ref[pl.ds(i * blk, blk), :])
+        for k in range(2):
+            root = tuple(left_ref[first + i, h, pl.ds(k * part, part), :] for h in range(2))
+            rows = pl.ds(i * blk + k * part, part)
+            stage[rows, :] = product(root, value)
+            there = out_ref.at[pl.ds((first + i) * blk + k * part, part), cols]
+            copies.append(pltpu.make_async_copy(stage.at[rows, :], there, sems.at[len(copies)]))
+            copies[-1].start()
     for copy in copies:
         copy.wait()
 
@@ -590,7 +592,7 @@
         out_shape=jax.ShapeDtypeStruct(out.shape, jnp.float32),
         in_specs=[vmem, vmem, anywhere],
         out_specs=anywhere,
-        scratch_shapes=[pltpu.VMEM((count * blk, width), jnp.float32), pltpu.SemaphoreType.DMA((count,))],
+        scratch_shapes=[pltpu.VMEM((count * blk, width), jnp.float32), pltpu.SemaphoreType.DMA((2 * count,))],
         input_output_aliases={2: 0},
         compiler_params=pltpu.CompilerParams(vmem_limit_bytes=VMEM_LIMIT),
         cost_estimate=SMALL,

time: 103 us -> 103 us (level)
  transfers between devices with their start and end apart: 19 -> 19, of which waited for: 12 -> 12; matrix products, arithmetic and copies ran while one was open for 0% -> 0% of each run, Pallas kernels for 43% -> 42%
where the time goes in v11:
time: 103 us
  Pallas kernels  45.5 us (44%)
  waiting for transfers between devices  38.4 us (37%)
  starting transfers between devices  18.7 us (18%)
    ppermute x10, waiting for transfers between devices, over(): return lax.ppermute(value, 'col', [(0, 1), (1, 0)])  28.6 us
    ppermute x10, starting transfers between devices, over(): return lax.ppermute(value, 'col', [(0, 1), (1, 0)])  13.7 us
    pallas_call x3, Pallas kernels, update(): pl.pallas_call(update_kernel, out_shape=(jax.ShapeDtypeStruct(out_shape,...  13.3 us
    ppermute x9, waiting for transfers between devices, over(): return lax.ppermute(value, 'row', [(i, i ^ flip) for i in range(n_row)])  9.87 us
    pallas_call x8, Pallas kernels, finish(): pl.pallas_call(functools.partial(finish_kernel, column, first), out_shape...  8.39 us
    pallas_call x2, Pallas kernels, left_grams(): pl.pallas_call(left_gram_kernel, out_shape=jax.ShapeDtypeStruct((tall, bl...  5.78 us
    ppermute x9, starting transfers between devices, over(): return lax.ppermute(value, 'row', [(i, i ^ flip) for i in range(n_row)])  4.96 us
    pallas_call x2, Pallas kernels, right_grams(): pl.pallas_call(right_gram_kernel, out_shape=(jax.ShapeDtypeStruct((tall,...  4.12 us
  transfers between devices with their start and end apart: 19, of which 12 were waited for; matrix products, arithmetic and copies ran while one was open for 0% of the time, Pallas kernels for 42%

profile of v11, /device:TPU:0, one launch (start us, length us, event | category | flops | bytes accessed | tf_op | source)
XLA Modules:
  0.0 103.1 jit_solution(7870063597982952073)
XLA Ops:
  1.1 3.0 %collective-permute-start.1 = (f32[512,256]{1,0:T(8,128)S(1)}, f32[512,256]{1,0:T(8,128)S(1)}, u32[]{:S(2)}, u32[]{:S(2)}) collective-permute-start(f32[512,256]{1,0:T(8,128)S(1)} %take.2.after_ref.rest_0_), channel_id=1, source_target_pairs={{0,4},{4,0},{1,5},{5,1},{2,6},{6,2},{3,7},{7,3},{8,12},{12,8},{9,1... | collective-permute-start | bytes 1572872 | tf_op jit(solution)/shard_map/ppermute | solution.py:646
  4.1 3.5 %load.1.g_ref = f32[1024,2048]{1,0:T(8,128)S(1)} custom-call(f32[1024,2048]{1,0:T(8,128)} %bitcast.7, f32[512,256]{1,0:T(8,128)S(1)} %take.2.after_ref.rest_0_), custom_call_target="tpu_custom_call" | custom-call | flops 1 | bytes 1 | tf_op jit(solution)/shard_map/load/pallas_call | solution.py:271
  7.6 2.1 %right_grams.2 = (f32[264,256]{1,0:T(8,128)S(1)}, f32[264,256]{1,0:T(8,128)S(1)}) custom-call(f32[1024,2048]{1,0:T(8,128)S(1)} %load.1.g_ref, f32[512,256]{1,0:T(8,128)S(1)} %take.2.after_ref.rest_0_), custom_call_target="tpu_custom_call" | custom-call | flops 1 | bytes 1 | tf_op jit(solution)/shard_map/right_grams/pallas_call | solution.py:142
  11.3 1.5 %collective-permute-start.3 = (f32[264,256]{1,0:T(8,128)S(1)}, f32[264,256]{1,0:T(8,128)S(1)}, u32[]{:S(2)}, u32[]{:S(2)}) collective-permute-start(f32[264,256]{1,0:T(8,128)S(1)} %fold.1.rest_0_), channel_id=1, source_target_pairs={{0,16},{8,24},{16,0},{24,8},{1,17},{9,25},{17,1},{25,9},{2,18},{10... | collective-permute-start | bytes 811016 | tf_op jit(solution)/shard_map/ppermute | solution.py:648
  12.9 4.0 %collective-permute-done.1.rest_1_.g_ref = f32[512,256]{1,0:T(8,128)S(1)} collective-permute-done((f32[512,256]{1,0:T(8,128)S(1)}, f32[512,256]{1,0:T(8,128)S(1)}, u32[]{:S(2)}, u32[]{:S(2)}) %collective-permute-start.1) | collective-permute-done | bytes 524320 | tf_op jit(solution)/shard_map/ppermute | solution.py:646
  16.8 2.0 %right_grams.3 = (f32[264,256]{1,0:T(8,128)S(1)}, f32[264,256]{1,0:T(8,128)S(1)}) custom-call(f32[1024,2048]{1,0:T(8,128)S(1)} %load.1.g_ref, f32[264,256]{1,0:T(8,128)S(1)} %fold.1.rest_0_, f32[512,256]{1,0:T(8,128)S(1)} %collective-permute-done.1.rest_1_.g_ref), custom_call_target="tpu_custom_call" | custom-call | flops 1 | bytes 1 | tf_op jit(solution)/shard_map/right_grams/pallas_call | solution.py:142
  20.5 3.2 %right_roots.1 = (f32[264,256]{1,0:T(8,128)S(1)}, f32[512,256]{1,0:T(8,128)S(1)}) custom-call(f32[2048,256]{1,0:T(8,128)S(1)} %bitcast.4, f32[264,256]{1,0:T(8,128)S(1)} %get-tuple-element.22.a_ref, f32[264,256]{1,0:T(8,128)S(1)} %collective-permute-done.2.b_ref, f32[264,256]{1,0:T(8,128)S(1)} %collective-permute-done.3.c_ref, f32[1024,2048]{1,0:T(8,128)S(1)} %load.1.g_ref), custom_call_target="tpu_custom_call" | custom-call | flops 1 | bytes 1 | tf_op jit(solution)/shard_map/right_roots/pallas_call | solution.py:357
  23.7 2.1 %collective-permute-start.7 = (f32[512,256]{1,0:T(8,128)S(1)}, f32[512,256]{1,0:T(8,128)S(1)}, u32[]{:S(2)}, u32[]{:S(2)}) collective-permute-start(f32[512,256]{1,0:T(8,128)S(1)} %get-tuple-element.25.after_ref), channel_id=1, source_target_pairs={{0,4},{4,0},{1,5},{5,1},{2,6},{6,2},{3,7},{7,3},{8,12},{12,8},{9,1... | collective-permute-start | bytes 1572872 | tf_op jit(solution)/shard_map/ppermute | solution.py:646
  25.8 2.9 %left_grams.2.rest_1_.under_ref = f32[264,256]{1,0:T(8,128)S(1)} custom-call(f32[1024,2048]{1,0:T(8,128)S(1)} %load.1.g_ref, f32[512,256]{1,0:T(8,128)S(1)} %get-tuple-element.25.after_ref), custom_call_target="tpu_custom_call" | custom-call | flops 1 | bytes 1 | tf_op jit(solution)/shard_map/left_grams/pallas_call | solution.py:191
  28.8 1.6 %collective-permute-start.6 = (f32[264,256]{1,0:T(8,128)S(1)}, f32[264,256]{1,0:T(8,128)S(1)}, u32[]{:S(2)}, u32[]{:S(2)}) collective-permute-start(f32[264,256]{1,0:T(8,128)S(1)} %hold.2.own_ref), channel_id=1, source_target_pairs={{0,16},{8,24},{16,0},{24,8},{1,17},{9,25},{17,1},{25,9},{2,18},{10... | collective-permute-start | bytes 811016 | tf_op jit(solution)/shard_map/ppermute | solution.py:648
  31.5 6.2 %collective-permute-done.6.a_ref = f32[264,256]{1,0:T(8,128)S(1)} collective-permute-done((f32[264,256]{1,0:T(8,128)S(1)}, f32[264,256]{1,0:T(8,128)S(1)}, u32[]{:S(2)}, u32[]{:S(2)}) %collective-permute-start.6) | collective-permute-done | bytes 270368 | tf_op jit(solution)/shard_map/ppermute | solution.py:648
  38.9 2.9 %left_grams.3.a_ref.rest_1_ = f32[264,256]{1,0:T(8,128)S(1)} custom-call(f32[1024,2048]{1,0:T(8,128)S(1)} %load.1.g_ref, f32[776,256]{1,0:T(8,128)S(1)} %core_apply.1.rest_0_.after_ref), custom_call_target="tpu_custom_call" | custom-call | flops 1 | bytes 1 | tf_op jit(solution)/shard_map/left_grams/pallas_call | solution.py:191
  42.8 1.8 %collective-permute-start.14 = (f32[584,256]{1,0:T(8,128)S(1)}, f32[584,256]{1,0:T(8,128)S(1)}, u32[]{:S(2)}, u32[]{:S(2)}) collective-permute-start(f32[584,256]{1,0:T(8,128)S(1)} %right_apply.6), channel_id=1, source_target_pairs={{0,4},{4,0},{1,5},{5,1},{2,6},{6,2},{3,7},{7,3},{8,12},{12,8},{9,1... | collective-permute-start | bytes 1794056 | tf_op jit(solution)/shard_map/ppermute | solution.py:646
  44.6 11.2 %collective-permute-done.9.rest_0_.b_ref.half_ref = f32[776,256]{1,0:T(8,128)S(1)} collective-permute-done((f32[776,256]{1,0:T(8,128)S(1)}, f32[776,256]{1,0:T(8,128)S(1)}, u32[]{:S(2)}, u32[]{:S(2)}) %collective-permute-start.9) | collective-permute-done | bytes 794656 | tf_op jit(solution)/shard_map/ppermute | solution.py:646
  56.3 1.8 %collective-permute-start.10 = (f32[512,256]{1,0:T(8,128)S(1)}, f32[512,256]{1,0:T(8,128)S(1)}, u32[]{:S(2)}, u32[]{:S(2)}) collective-permute-start(f32[512,256]{1,0:T(8,128)S(1)} %right_apply.4), channel_id=1, source_target_pairs={{0,4},{4,0},{1,5},{5,1},{2,6},{6,2},{3,7},{7,3},{8,12},{12,8},{9,1... | collective-permute-start | bytes 1572872 | tf_op jit(solution)/shard_map/ppermute | solution.py:646
  58.1 3.0 %left_roots.1.left_ref = bf16[2,2,256,256]{3,2,1,0:T(8,128)(2,1)S(1)} custom-call(f32[1024,256]{1,0:T(8,128)S(1)} %bitcast.5, f32[264,256]{1,0:T(8,128)S(1)} %left_grams.3.a_ref.rest_1_, f32[776,256]{1,0:T(8,128)S(1)} %collective-permute-done.9.rest_0_.b_ref.half_ref), custom_call_target="tpu_custom_call" | custom-call | flops 1 | bytes 1 | tf_op jit(solution)/shard_map/left_roots/pallas_call | solution.py:396
  61.1 9.7 %update.3 = (f32[512,4096]{1,0:T(8,128)}, f32[8,128]{1,0:T(8,128)S(1)}) custom-call(f32[1024,2048]{1,0:T(8,128)S(1)} %load.1.g_ref, bf16[2,2,256,256]{3,2,1,0:T(8,128)(2,1)S(1)} %left_roots.1.left_ref, bf16[8,2,256,256]{3,2,1,0:T(8,128)(2,1)S(1)} %get-tuple-element.26.right_ref), custom_call_target="tpu_custom_call" | custom-call | flops 1 | bytes 1 | tf_op jit(solution)/shard_map/update/pallas_call | solution.py:618
  71.5 8.4 %collective-permute-done.10.rest_0_.half_ref = f32[512,256]{1,0:T(8,128)S(1)} collective-permute-done((f32[512,256]{1,0:T(8,128)S(1)}, f32[512,256]{1,0:T(8,128)S(1)}, u32[]{:S(2)}, u32[]{:S(2)}) %collective-permute-start.10) | collective-permute-done | bytes 524320 | tf_op jit(solution)/shard_map/ppermute | solution.py:646
  80.3 1.8 %collective-permute-start.13 = (f32[512,128]{1,0:T(8,128)S(1)}, f32[512,128]{1,0:T(8,128)S(1)}, u32[]{:S(2)}, u32[]{:S(2)}) collective-permute-start(f32[512,128]{1,0:T(8,128)S(1)} %get-tuple-element.29.rest_1_), channel_id=1, source_target_pairs={{0,4},{4,0},{1,5},{5,1},{2,6},{6,2},{3,7},{7,3},{8,12},{12,8},{9,1... | collective-permute-start | bytes 786440 | tf_op jit(solution)/shard_map/ppermute | solution.py:646
  82.2 1.6 %collective-permute-start.17 = (f32[72,256]{1,0:T(8,128)S(1)}, f32[72,256]{1,0:T(8,128)S(1)}, u32[]{:S(2)}, u32[]{:S(2)}) collective-permute-start(f32[72,256]{1,0:T(8,128)S(1)} %rest_of.1.own_ref), channel_id=1, source_target_pairs={{0,16},{8,24},{16,0},{24,8},{1,17},{9,25},{17,1},{25,9},{2,18},{10... | collective-permute-start | bytes 221192 | tf_op jit(solution)/shard_map/ppermute | solution.py:648
  84.2 1.5 %collective-permute-start.11 = (f32[256,128]{1,0:T(8,128)S(1)}, f32[256,128]{1,0:T(8,128)S(1)}, u32[]{:S(2)}, u32[]{:S(2)}) collective-permute-start(f32[256,128]{1,0:T(8,128)S(1)} %get-tuple-element.27), channel_id=1, source_target_pairs={{0,4},{4,0},{1,5},{5,1},{2,6},{6,2},{3,7},{7,3},{8,12},{12,8},{9,1... | collective-permute-start | bytes 393224 | tf_op jit(solution)/shard_map/ppermute | solution.py:646
  89.3 1.8 %update.4 = (f32[512,4096]{1,0:T(8,128)}, f32[8,128]{1,0:T(8,128)}) custom-call(f32[512,256]{1,0:T(8,128)S(1)} %collective-permute-done.1.rest_1_.g_ref, bf16[2,2,256,256]{3,2,1,0:T(8,128)(2,1)S(1)} %left_roots.1.left_ref, bf16[2,2,256,256]{3,2,1,0:T(8,128)(2,1)S(1)} %join_roots.1.right_ref, ...), custom_call_target="tpu_custom_call", output_to_operand_aliasing={{0}: (3, {})} | custom-call | flops 1 | bytes 1 | tf_op jit(solution)/shard_map/update/pallas_call | solution.py:618
  91.1 1.8 %update.5 = (f32[512,4096]{1,0:T(8,128)}, f32[8,128]{1,0:T(8,128)}) custom-call(f32[512,256]{1,0:T(8,128)S(1)} %collective-permute-done.4.rest_0_.g_ref, bf16[2,2,256,256]{3,2,1,0:T(8,128)(2,1)S(1)} %left_roots.1.left_ref, bf16[2,2,256,256]{3,2,1,0:T(8,128)(2,1)S(1)} %join_roots.1.right_ref, ...), custom_call_target="tpu_custom_call", output_to_operand_aliasing={{0}: (3, {})} | custom-call | flops 1 | bytes 1 | tf_op jit(solution)/shard_map/update/pallas_call | solution.py:618
  97.8 1.8 %collective-permute-done.12.half_ref = f32[256,128]{1,0:T(8,128)S(1)} collective-permute-done((f32[256,128]{1,0:T(8,128)S(1)}, f32[256,128]{1,0:T(8,128)S(1)}, u32[]{:S(2)}, u32[]{:S(2)}) %collective-permute-start.12) | collective-permute-done | bytes 131104 | tf_op jit(solution)/shard_map/ppermute | solution.py:646
  (49 shorter events, 21.3 us)
Async XLA Ops:
  1.1 15.8 %collective-permute-start.1 = (f32[512,256]{1,0:T(8,128)S(1)}, f32[512,256]{1,0:T(8,128)S(1)}, u32[]{:S(2)}, u32[]{:S(2)}) collective-permute-start(f32[512,256]{1,0:T(8,128)S(1)} %take.2.after_ref.rest_0_), channel_id=1, source_target_pairs={{0,4},{4,0},{1,5},{5,1},{2,6},{6,2},{3,7},{7,3},{8,12},{12,8},{9,1... | collective-permute-start | bytes 1572872 | tf_op jit(solution)/shard_map/ppermute | solution.py:646
  9.7 10.8 %copy-start = (f32[1,2048,256]{2,1,0:T(8,128)S(1)}, f32[1,2048,256]{2,1,0:T(8,128)}, u32[]{:S(2)}) copy-start(f32[1,2048,256]{2,1,0:T(8,128)} %param.5) | copy-start | bytes 6291460
  9.7 1.6 %collective-permute-start = (f32[264,256]{1,0:T(8,128)S(1)}, f32[264,256]{1,0:T(8,128)S(1)}, u32[]{:S(2)}, u32[]{:S(2)}) collective-permute-start(f32[264,256]{1,0:T(8,128)S(1)} %get-tuple-element.21.rest_0_), channel_id=1, source_target_pairs={{0,8},{8,0},{16,24},{24,16},{1,9},{9,1},{17,25},{25,17},{2,10},{10... | collective-permute-start | bytes 811016 | tf_op jit(solution)/shard_map/ppermute | solution.py:648
  10.2 18.6 %collective-permute-start.4 = (f32[512,256]{1,0:T(8,128)S(1)}, f32[512,256]{1,0:T(8,128)S(1)}, u32[]{:S(2)}, u32[]{:S(2)}) collective-permute-start(f32[512,256]{1,0:T(8,128)S(1)} %take.3), channel_id=1, source_target_pairs={{0,4},{4,0},{1,5},{5,1},{2,6},{6,2},{3,7},{7,3},{8,12},{12,8},{9,1... | collective-permute-start | bytes 1572872 | tf_op jit(solution)/shard_map/ppermute | solution.py:646
  11.3 8.6 %collective-permute-start.3 = (f32[264,256]{1,0:T(8,128)S(1)}, f32[264,256]{1,0:T(8,128)S(1)}, u32[]{:S(2)}, u32[]{:S(2)}) collective-permute-start(f32[264,256]{1,0:T(8,128)S(1)} %fold.1.rest_0_), channel_id=1, source_target_pairs={{0,16},{8,24},{16,0},{24,8},{1,17},{9,25},{17,1},{25,9},{2,18},{10... | collective-permute-start | bytes 811016 | tf_op jit(solution)/shard_map/ppermute | solution.py:648
  18.9 1.6 %collective-permute-start.2 = (f32[264,256]{1,0:T(8,128)S(1)}, f32[264,256]{1,0:T(8,128)S(1)}, u32[]{:S(2)}, u32[]{:S(2)}) collective-permute-start(f32[264,256]{1,0:T(8,128)S(1)} %get-tuple-element.23), channel_id=1, source_target_pairs={{0,8},{8,0},{16,24},{24,16},{1,9},{9,1},{17,25},{25,17},{2,10},{10... | collective-permute-start | bytes 811016 | tf_op jit(solution)/shard_map/ppermute | solution.py:648
  23.7 15.1 %collective-permute-start.7 = (f32[512,256]{1,0:T(8,128)S(1)}, f32[512,256]{1,0:T(8,128)S(1)}, u32[]{:S(2)}, u32[]{:S(2)}) collective-permute-start(f32[512,256]{1,0:T(8,128)S(1)} %get-tuple-element.25.after_ref), channel_id=1, source_target_pairs={{0,4},{4,0},{1,5},{5,1},{2,6},{6,2},{3,7},{7,3},{8,12},{12,8},{9,1... | collective-permute-start | bytes 1572872 | tf_op jit(solution)/shard_map/ppermute | solution.py:646
  28.8 1.6 %collective-permute-start.5 = (f32[264,256]{1,0:T(8,128)S(1)}, f32[264,256]{1,0:T(8,128)S(1)}, u32[]{:S(2)}, u32[]{:S(2)}) collective-permute-start(f32[264,256]{1,0:T(8,128)S(1)} %hold.2.own_ref), channel_id=1, source_target_pairs={{0,8},{8,0},{16,24},{24,16},{1,9},{9,1},{17,25},{25,17},{2,10},{10... | collective-permute-start | bytes 811016 | tf_op jit(solution)/shard_map/ppermute | solution.py:648
  28.8 8.9 %collective-permute-start.6 = (f32[264,256]{1,0:T(8,128)S(1)}, f32[264,256]{1,0:T(8,128)S(1)}, u32[]{:S(2)}, u32[]{:S(2)}) collective-permute-start(f32[264,256]{1,0:T(8,128)S(1)} %hold.2.own_ref), channel_id=1, source_target_pairs={{0,16},{8,24},{16,0},{24,8},{1,17},{9,25},{17,1},{25,9},{2,18},{10... | collective-permute-start | bytes 811016 | tf_op jit(solution)/shard_map/ppermute | solution.py:648
  30.9 25.0 %collective-permute-start.9 = (f32[776,256]{1,0:T(8,128)S(1)}, f32[776,256]{1,0:T(8,128)S(1)}, u32[]{:S(2)}, u32[]{:S(2)}) collective-permute-start(f32[776,256]{1,0:T(8,128)S(1)} %core_apply.1.rest_0_.after_ref), channel_id=1, source_target_pairs={{0,4},{4,0},{1,5},{5,1},{2,6},{6,2},{3,7},{7,3},{8,12},{12,8},{9,1... | collective-permute-start | bytes 2383880 | tf_op jit(solution)/shard_map/ppermute | solution.py:646
  38.9 3.0 %collective-permute-start.8 = (f32[264,256]{1,0:T(8,128)S(1)}, f32[264,256]{1,0:T(8,128)S(1)}, u32[]{:S(2)}, u32[]{:S(2)}) collective-permute-start(f32[264,256]{1,0:T(8,128)S(1)} %hold.3.x_ref), channel_id=1, source_target_pairs={{0,8},{8,0},{16,24},{24,16},{1,9},{9,1},{17,25},{25,17},{2,10},{10... | collective-permute-start | bytes 811016 | tf_op jit(solution)/shard_map/ppermute | solution.py:648
  42.8 15.3 %copy-start.1 = (f32[1,1024,256]{2,1,0:T(8,128)S(1)}, f32[1,1024,256]{2,1,0:T(8,128)}, u32[]{:S(2)}) copy-start(f32[1,1024,256]{2,1,0:T(8,128)} %param.4) | copy-start | bytes 3145732
  42.8 28.0 %collective-permute-start.14 = (f32[584,256]{1,0:T(8,128)S(1)}, f32[584,256]{1,0:T(8,128)S(1)}, u32[]{:S(2)}, u32[]{:S(2)}) collective-permute-start(f32[584,256]{1,0:T(8,128)S(1)} %right_apply.6), channel_id=1, source_target_pairs={{0,4},{4,0},{1,5},{5,1},{2,6},{6,2},{3,7},{7,3},{8,12},{12,8},{9,1... | collective-permute-start | bytes 1794056 | tf_op jit(solution)/shard_map/ppermute | solution.py:646
  56.3 23.7 %collective-permute-start.10 = (f32[512,256]{1,0:T(8,128)S(1)}, f32[512,256]{1,0:T(8,128)S(1)}, u32[]{:S(2)}, u32[]{:S(2)}) collective-permute-start(f32[512,256]{1,0:T(8,128)S(1)} %right_apply.4), channel_id=1, source_target_pairs={{0,4},{4,0},{1,5},{5,1},{2,6},{6,2},{3,7},{7,3},{8,12},{12,8},{9,1... | collective-permute-start | bytes 1572872 | tf_op jit(solution)/shard_map/ppermute | solution.py:646
  71.2 24.0 %collective-permute-start.15 = (f32[512,256]{1,0:T(8,128)S(1)}, f32[512,256]{1,0:T(8,128)S(1)}, u32[]{:S(2)}, u32[]{:S(2)}) collective-permute-start(f32[512,256]{1,0:T(8,128)S(1)} %right_apply.7), channel_id=1, source_target_pairs={{0,4},{4,0},{1,5},{5,1},{2,6},{6,2},{3,7},{7,3},{8,12},{12,8},{9,1... | collective-permute-start | bytes 1572872 | tf_op jit(solution)/shard_map/ppermute | solution.py:646
  80.3 16.5 %collective-permute-start.13 = (f32[512,128]{1,0:T(8,128)S(1)}, f32[512,128]{1,0:T(8,128)S(1)}, u32[]{:S(2)}, u32[]{:S(2)}) collective-permute-start(f32[512,128]{1,0:T(8,128)S(1)} %get-tuple-element.29.rest_1_), channel_id=1, source_target_pairs={{0,4},{4,0},{1,5},{5,1},{2,6},{6,2},{3,7},{7,3},{8,12},{12,8},{9,1... | collective-permute-start | bytes 786440 | tf_op jit(solution)/shard_map/ppermute | solution.py:646
  82.1 2.1 %collective-permute-start.16 = (f32[72,256]{1,0:T(8,128)S(1)}, f32[72,256]{1,0:T(8,128)S(1)}, u32[]{:S(2)}, u32[]{:S(2)}) collective-permute-start(f32[72,256]{1,0:T(8,128)S(1)} %rest_of.1.own_ref), channel_id=1, source_target_pairs={{0,8},{8,0},{16,24},{24,16},{1,9},{9,1},{17,25},{25,17},{2,10},{10... | collective-permute-start | bytes 221192 | tf_op jit(solution)/shard_map/ppermute | solution.py:648
  82.2 4.7 %collective-permute-start.17 = (f32[72,256]{1,0:T(8,128)S(1)}, f32[72,256]{1,0:T(8,128)S(1)}, u32[]{:S(2)}, u32[]{:S(2)}) collective-permute-start(f32[72,256]{1,0:T(8,128)S(1)} %rest_of.1.own_ref), channel_id=1, source_target_pairs={{0,16},{8,24},{16,0},{24,8},{1,17},{9,25},{17,1},{25,9},{2,18},{10... | collective-permute-start | bytes 221192 | tf_op jit(solution)/shard_map/ppermute | solution.py:648
  83.7 15.9 %collective-permute-start.12 = (f32[256,128]{1,0:T(8,128)S(1)}, f32[256,128]{1,0:T(8,128)S(1)}, u32[]{:S(2)}, u32[]{:S(2)}) collective-permute-start(f32[256,128]{1,0:T(8,128)S(1)} %get-tuple-element.28), channel_id=1, source_target_pairs={{0,4},{4,0},{1,5},{5,1},{2,6},{6,2},{3,7},{7,3},{8,12},{12,8},{9,1... | collective-permute-start | bytes 393224 | tf_op jit(solution)/shard_map/ppermute | solution.py:646
  84.2 17.8 %collective-permute-start.11 = (f32[256,128]{1,0:T(8,128)S(1)}, f32[256,128]{1,0:T(8,128)S(1)}, u32[]{:S(2)}, u32[]{:S(2)}) collective-permute-start(f32[256,128]{1,0:T(8,128)S(1)} %get-tuple-element.27), channel_id=1, source_target_pairs={{0,4},{4,0},{1,5},{5,1},{2,6},{6,2},{3,7},{7,3},{8,12},{12,8},{9,1... | collective-permute-start | bytes 393224 | tf_op jit(solution)/shard_map/ppermute | solution.py:646
  86.8 2.2 %collective-permute-start.18 = (f32[72,256]{1,0:T(8,128)S(1)}, f32[72,256]{1,0:T(8,128)S(1)}, u32[]{:S(2)}, u32[]{:S(2)}) collective-permute-start(f32[72,256]{1,0:T(8,128)S(1)} %collective-permute-done.17.x_ref), channel_id=1, source_target_pairs={{0,8},{8,0},{16,24},{24,16},{1,9},{9,1},{17,25},{25,17},{2,10},{10... | collective-permute-start | bytes 221192 | tf_op jit(solution)/shard_map/ppermute | solution.py:648

commit v12 on v10

--- a/solution.py
+++ b/solution.py
@@ -578,16 +578,18 @@
 def finish_kernel(column, first, half_ref, left_ref, out_before, out_ref, stage, sems):
     blk = left_ref.shape[-1]
     width = stage.shape[1]
+    part = blk // 2
     cols = pl.ds(pl.multiple_of(column(here()), width), width)
     copies = []
     for i in range(stage.shape[0] // blk):
-        rows = pl.ds(i * blk, blk)
-        root = (left_ref[first + i, 0], left_ref[first + i, 1])
-        stage[rows, :] = product(root, split(half_ref[rows, :]))
-        copies.append(
-            pltpu.make_async_copy(stage.at[rows, :], out_ref.at[pl.ds((first + i) * blk, blk), cols], sems.at[i])
-        )
-        copies[i].start()
+        value = split(half_ref[pl.ds(i * blk, blk), :])
+        for k in range(2):
+            root = tuple(left_ref[first + i, h, pl.ds(k * part, part), :] for h in range(2))
+            rows = pl.ds(i * blk + k * part, part)
+            stage[rows, :] = product(root, value)
+            there = out_ref.at[pl.ds((first + i) * blk + k * part, part), cols]
+            copies.append(pltpu.make_async_copy(stage.at[rows, :], there, sems.at[len(copies)]))
+            copies[-1].start()
     for copy in copies:
         copy.wait()
 
@@ -602,7 +604,7 @@
         out_shape=jax.ShapeDtypeStruct(out.shape, jnp.float32),
         in_specs=[vmem, vmem, anywhere],
         out_specs=anywhere,
-        scratch_shapes=[pltpu.VMEM((count * blk, width), jnp.float32), pltpu.SemaphoreType.DMA((count,))],
+        scratch_shapes=[pltpu.VMEM((count * blk, width), jnp.float32), pltpu.SemaphoreType.DMA((2 * count,))],
         input_output_aliases={2: 0},
         compiler_params=pltpu.CompilerParams(vmem_limit_bytes=VMEM_LIMIT),
         cost_estimate=SMALL,

time: 103 us -> 103 us (level)
  transfers between devices with their start and end apart: 19 -> 19, of which waited for: 10 -> 10; matrix products, arithmetic and copies ran while one was open for 0% -> 0% of each run, Pallas kernels for 43% -> 42%
where the time goes in v12:
time: 103 us
  Pallas kernels  45.6 us (44%)
  waiting for transfers between devices  37.9 us (37%)
  starting transfers between devices  18.9 us (18%)
    ppermute x10, waiting for transfers between devices, over(): return lax.ppermute(value, 'col', [(0, 1), (1, 0)])  28.2 us
    ppermute x10, starting transfers between devices, over(): return lax.ppermute(value, 'col', [(0, 1), (1, 0)])  13.7 us
    pallas_call x3, Pallas kernels, update(): pl.pallas_call(update_kernel, out_shape=(jax.ShapeDtypeStruct(out_shape,...  13.3 us
    ppermute x9, waiting for transfers between devices, over(): return lax.ppermute(value, 'row', [(i, i ^ flip) for i in range(n_row)])  9.65 us
    pallas_call x8, Pallas kernels, finish(): pl.pallas_call(functools.partial(finish_kernel, column, first), out_shape...  8.5 us
    pallas_call x2, Pallas kernels, left_grams(): pl.pallas_call(left_gram_kernel, out_shape=(jax.ShapeDtypeStruct((blk, bl...  5.78 us
    ppermute x9, starting transfers between devices, over(): return lax.ppermute(value, 'row', [(i, i ^ flip) for i in range(n_row)])  5.2 us
    pallas_call x2, Pallas kernels, right_grams(): pl.pallas_call(right_gram_kernel, out_shape=(jax.ShapeDtypeStruct((tall,...  4.12 us
  transfers between devices with their start and end apart: 19, of which 10 were waited for; matrix products, arithmetic and copies ran while one was open for 0% of the time, Pallas kernels for 42%

profile of v12, /device:TPU:0, one launch (start us, length us, event | category | flops | bytes accessed | tf_op | source)
XLA Modules:
  0.0 102.9 jit_solution(11705642689263229108)
XLA Ops:
  1.1 3.0 %collective-permute-start.1 = (f32[512,256]{1,0:T(8,128)S(1)}, f32[512,256]{1,0:T(8,128)S(1)}, u32[]{:S(2)}, u32[]{:S(2)}) collective-permute-start(f32[512,256]{1,0:T(8,128)S(1)} %take.2.after_ref.rest_0_), channel_id=1, source_target_pairs={{0,4},{4,0},{1,5},{5,1},{2,6},{6,2},{3,7},{7,3},{8,12},{12,8},{9,1... | collective-permute-start | bytes 1572872 | tf_op jit(solution)/shard_map/ppermute | solution.py:658
  4.1 3.5 %load.1.g_ref = f32[1024,2048]{1,0:T(8,128)S(1)} custom-call(f32[1024,2048]{1,0:T(8,128)} %bitcast.7, f32[512,256]{1,0:T(8,128)S(1)} %take.2.after_ref.rest_0_), custom_call_target="tpu_custom_call" | custom-call | flops 1 | bytes 1 | tf_op jit(solution)/shard_map/load/pallas_call | solution.py:284
  7.6 2.1 %right_grams.2 = (f32[264,256]{1,0:T(8,128)S(1)}, f32[264,256]{1,0:T(8,128)S(1)}) custom-call(f32[1024,2048]{1,0:T(8,128)S(1)} %load.1.g_ref, f32[512,256]{1,0:T(8,128)S(1)} %take.2.after_ref.rest_0_), custom_call_target="tpu_custom_call" | custom-call | flops 1 | bytes 1 | tf_op jit(solution)/shard_map/right_grams/pallas_call | solution.py:152
  11.3 1.5 %collective-permute-start.3 = (f32[264,256]{1,0:T(8,128)S(1)}, f32[264,256]{1,0:T(8,128)S(1)}, u32[]{:S(2)}, u32[]{:S(2)}) collective-permute-start(f32[264,256]{1,0:T(8,128)S(1)} %fold.1.rest_0_), channel_id=1, source_target_pairs={{0,16},{8,24},{16,0},{24,8},{1,17},{9,25},{17,1},{25,9},{2,18},{10... | collective-permute-start | bytes 811016 | tf_op jit(solution)/shard_map/ppermute | solution.py:660
  12.9 4.0 %collective-permute-done.1.rest_1_.g_ref = f32[512,256]{1,0:T(8,128)S(1)} collective-permute-done((f32[512,256]{1,0:T(8,128)S(1)}, f32[512,256]{1,0:T(8,128)S(1)}, u32[]{:S(2)}, u32[]{:S(2)}) %collective-permute-start.1) | collective-permute-done | bytes 524320 | tf_op jit(solution)/shard_map/ppermute | solution.py:658
  16.8 2.0 %right_grams.3 = (f32[264,256]{1,0:T(8,128)S(1)}, f32[264,256]{1,0:T(8,128)S(1)}) custom-call(f32[1024,2048]{1,0:T(8,128)S(1)} %load.1.g_ref, f32[264,256]{1,0:T(8,128)S(1)} %fold.1.rest_0_, f32[512,256]{1,0:T(8,128)S(1)} %collective-permute-done.1.rest_1_.g_ref), custom_call_target="tpu_custom_call" | custom-call | flops 1 | bytes 1 | tf_op jit(solution)/shard_map/right_grams/pallas_call | solution.py:152
  20.5 3.2 %right_roots.1 = (f32[264,256]{1,0:T(8,128)S(1)}, f32[512,256]{1,0:T(8,128)S(1)}) custom-call(f32[2048,256]{1,0:T(8,128)S(1)} %bitcast.4, f32[264,256]{1,0:T(8,128)S(1)} %get-tuple-element.26.a_ref, f32[264,256]{1,0:T(8,128)S(1)} %collective-permute-done.2.b_ref, f32[264,256]{1,0:T(8,128)S(1)} %collective-permute-done.3.c_ref, f32[1024,2048]{1,0:T(8,128)S(1)} %load.1.g_ref), custom_call_target="tpu_custom_call" | custom-call | flops 1 | bytes 1 | tf_op jit(solution)/shard_map/right_roots/pallas_call | solution.py:370
  23.7 2.1 %collective-permute-start.7 = (f32[512,256]{1,0:T(8,128)S(1)}, f32[512,256]{1,0:T(8,128)S(1)}, u32[]{:S(2)}, u32[]{:S(2)}) collective-permute-start(f32[512,256]{1,0:T(8,128)S(1)} %get-tuple-element.29.after_ref), channel_id=1, source_target_pairs={{0,4},{4,0},{1,5},{5,1},{2,6},{6,2},{3,7},{7,3},{8,12},{12,8},{9,1... | collective-permute-start | bytes 1572872 | tf_op jit(solution)/shard_map/ppermute | solution.py:658
  25.8 2.9 %left_grams.2 = (f32[256,256]{1,0:T(8,128)S(1)}, f32[2,128]{1,0:T(2,128)S(1)}) custom-call(f32[1024,2048]{1,0:T(8,128)S(1)} %load.1.g_ref, f32[512,256]{1,0:T(8,128)S(1)} %get-tuple-element.29.after_ref), custom_call_target="tpu_custom_call" | custom-call | flops 1 | bytes 1 | tf_op jit(solution)/shard_map/left_grams/pallas_call | solution.py:201
  28.8 1.6 %collective-permute-start.6 = (f32[264,256]{1,0:T(8,128)S(1)}, f32[264,256]{1,0:T(8,128)S(1)}, u32[]{:S(2)}, u32[]{:S(2)}) collective-permute-start(f32[264,256]{1,0:T(8,128)S(1)} %hold.2.own_ref), channel_id=1, source_target_pairs={{0,16},{8,24},{16,0},{24,8},{1,17},{9,25},{17,1},{25,9},{2,18},{10... | collective-permute-start | bytes 811016 | tf_op jit(solution)/shard_map/ppermute | solution.py:660
  31.5 6.2 %collective-permute-done.6.a_ref = f32[264,256]{1,0:T(8,128)S(1)} collective-permute-done((f32[264,256]{1,0:T(8,128)S(1)}, f32[264,256]{1,0:T(8,128)S(1)}, u32[]{:S(2)}, u32[]{:S(2)}) %collective-permute-start.6) | collective-permute-done | bytes 270368 | tf_op jit(solution)/shard_map/ppermute | solution.py:660
  38.9 2.9 %left_grams.3 = (f32[256,256]{1,0:T(8,128)S(1)}, f32[2,128]{1,0:T(2,128)S(1)}) custom-call(f32[1024,2048]{1,0:T(8,128)S(1)} %load.1.g_ref, f32[768,256]{1,0:T(8,128)S(1)} %core_apply.1.rest_0_.after_ref), custom_call_target="tpu_custom_call" | custom-call | flops 1 | bytes 1 | tf_op jit(solution)/shard_map/left_grams/pallas_call | solution.py:201
  42.8 1.8 %collective-permute-start.11 = (f32[584,256]{1,0:T(8,128)S(1)}, f32[584,256]{1,0:T(8,128)S(1)}, u32[]{:S(2)}, u32[]{:S(2)}) collective-permute-start(f32[584,256]{1,0:T(8,128)S(1)} %right_apply.5), channel_id=1, source_target_pairs={{0,4},{4,0},{1,5},{5,1},{2,6},{6,2},{3,7},{7,3},{8,12},{12,8},{9,1... | collective-permute-start | bytes 1794056 | tf_op jit(solution)/shard_map/ppermute | solution.py:658
  44.6 11.1 %collective-permute-done.9.rest_0_.b_ref.half_ref = f32[768,256]{1,0:T(8,128)S(1)} collective-permute-done((f32[768,256]{1,0:T(8,128)S(1)}, f32[768,256]{1,0:T(8,128)S(1)}, u32[]{:S(2)}, u32[]{:S(2)}) %collective-permute-start.9) | collective-permute-done | bytes 786464 | tf_op jit(solution)/shard_map/ppermute | solution.py:658
  56.1 1.8 %collective-permute-start.10 = (f32[512,256]{1,0:T(8,128)S(1)}, f32[512,256]{1,0:T(8,128)S(1)}, u32[]{:S(2)}, u32[]{:S(2)}) collective-permute-start(f32[512,256]{1,0:T(8,128)S(1)} %right_apply.4), channel_id=1, source_target_pairs={{0,4},{4,0},{1,5},{5,1},{2,6},{6,2},{3,7},{7,3},{8,12},{12,8},{9,1... | collective-permute-start | bytes 1572872 | tf_op jit(solution)/shard_map/ppermute | solution.py:658
  57.9 10.6 %collective-permute-done.11.rest_0_.rest_ref.a_ref.half_ref = f32[584,256]{1,0:T(8,128)S(1)} collective-permute-done((f32[584,256]{1,0:T(8,128)S(1)}, f32[584,256]{1,0:T(8,128)S(1)}, u32[]{:S(2)}, u32[]{:S(2)}) %collective-permute-start.11) | collective-permute-done | bytes 598048 | tf_op jit(solution)/shard_map/ppermute | solution.py:658
  68.9 1.8 %collective-permute-start.15 = (f32[512,256]{1,0:T(8,128)S(1)}, f32[512,256]{1,0:T(8,128)S(1)}, u32[]{:S(2)}, u32[]{:S(2)}) collective-permute-start(f32[512,256]{1,0:T(8,128)S(1)} %right_apply.6.after_ref), channel_id=1, source_target_pairs={{0,4},{4,0},{1,5},{5,1},{2,6},{6,2},{3,7},{7,3},{8,12},{12,8},{9,1... | collective-permute-start | bytes 1572872 | tf_op jit(solution)/shard_map/ppermute | solution.py:658
  70.7 3.0 %left_roots.1.left_ref = bf16[2,2,256,256]{3,2,1,0:T(8,128)(2,1)S(1)} custom-call(f32[1024,256]{1,0:T(8,128)S(1)} %bitcast.5, f32[256,256]{1,0:T(8,128)S(1)} %get-tuple-element.33.rest_1_.a_ref, f32[2,128]{1,0:T(2,128)S(1)} %get-tuple-element.34.a_diag, f32[768,256]{1,0:T(8,128)S(1)} %collective-permute-done.9.rest_0_.b_ref.half_ref, ...), custom_call_target="tpu_custom_call" | custom-call | flops 1 | bytes 1 | tf_op jit(solution)/shard_map/left_roots/pallas_call | solution.py:409
  73.7 9.7 %update.3 = (f32[512,4096]{1,0:T(8,128)}, f32[8,128]{1,0:T(8,128)S(1)}) custom-call(f32[1024,2048]{1,0:T(8,128)S(1)} %load.1.g_ref, bf16[2,2,256,256]{3,2,1,0:T(8,128)(2,1)S(1)} %left_roots.1.left_ref, bf16[8,2,256,256]{3,2,1,0:T(8,128)(2,1)S(1)} %get-tuple-element.32.right_ref), custom_call_target="tpu_custom_call" | custom-call | flops 1 | bytes 1 | tf_op jit(solution)/shard_map/update/pallas_call | solution.py:630
  84.2 1.8 %collective-permute-start.17 = (f32[72,256]{1,0:T(8,128)S(1)}, f32[72,256]{1,0:T(8,128)S(1)}, u32[]{:S(2)}, u32[]{:S(2)}) collective-permute-start(f32[72,256]{1,0:T(8,128)S(1)} %rest_of.1.own_ref), channel_id=1, source_target_pairs={{0,16},{8,24},{16,0},{24,8},{1,17},{9,25},{17,1},{25,9},{2,18},{10... | collective-permute-start | bytes 221192 | tf_op jit(solution)/shard_map/ppermute | solution.py:660
  86.0 1.5 %collective-permute-start.13 = (f32[256,128]{1,0:T(8,128)S(1)}, f32[256,128]{1,0:T(8,128)S(1)}, u32[]{:S(2)}, u32[]{:S(2)}) collective-permute-start(f32[256,128]{1,0:T(8,128)S(1)} %get-tuple-element.38), channel_id=1, source_target_pairs={{0,4},{4,0},{1,5},{5,1},{2,6},{6,2},{3,7},{7,3},{8,12},{12,8},{9,1... | collective-permute-start | bytes 393224 | tf_op jit(solution)/shard_map/ppermute | solution.py:658
  91.3 1.8 %update.4 = (f32[512,4096]{1,0:T(8,128)}, f32[8,128]{1,0:T(8,128)}) custom-call(f32[512,256]{1,0:T(8,128)S(1)} %collective-permute-done.1.rest_1_.g_ref, bf16[2,2,256,256]{3,2,1,0:T(8,128)(2,1)S(1)} %left_roots.1.left_ref, bf16[2,2,256,256]{3,2,1,0:T(8,128)(2,1)S(1)} %join_roots.1.right_ref, ...), custom_call_target="tpu_custom_call", output_to_operand_aliasing={{0}: (3, {})} | custom-call | flops 1 | bytes 1 | tf_op jit(solution)/shard_map/update/pallas_call | solution.py:630
  93.1 1.8 %update.5 = (f32[512,4096]{1,0:T(8,128)}, f32[8,128]{1,0:T(8,128)}) custom-call(f32[512,256]{1,0:T(8,128)S(1)} %collective-permute-done.4.rest_0_.g_ref, bf16[2,2,256,256]{3,2,1,0:T(8,128)(2,1)S(1)} %left_roots.1.left_ref, bf16[2,2,256,256]{3,2,1,0:T(8,128)(2,1)S(1)} %join_roots.1.right_ref, ...), custom_call_target="tpu_custom_call", output_to_operand_aliasing={{0}: (3, {})} | custom-call | flops 1 | bytes 1 | tf_op jit(solution)/shard_map/update/pallas_call | solution.py:630
  100.3 1.5 %collective-permute-done.12.half_ref = f32[256,128]{1,0:T(8,128)S(1)} collective-permute-done((f32[256,128]{1,0:T(8,128)S(1)}, f32[256,128]{1,0:T(8,128)S(1)}, u32[]{:S(2)}, u32[]{:S(2)}) %collective-permute-start.12) | collective-permute-done | bytes 131104 | tf_op jit(solution)/shard_map/ppermute | solution.py:658
  (49 shorter events, 19.1 us)
Async XLA Ops:
  1.1 15.8 %collective-permute-start.1 = (f32[512,256]{1,0:T(8,128)S(1)}, f32[512,256]{1,0:T(8,128)S(1)}, u32[]{:S(2)}, u32[]{:S(2)}) collective-permute-start(f32[512,256]{1,0:T(8,128)S(1)} %take.2.after_ref.rest_0_), channel_id=1, source_target_pairs={{0,4},{4,0},{1,5},{5,1},{2,6},{6,2},{3,7},{7,3},{8,12},{12,8},{9,1... | collective-permute-start | bytes 1572872 | tf_op jit(solution)/shard_map/ppermute | solution.py:658
  9.7 10.8 %copy-start = (f32[1,2048,256]{2,1,0:T(8,128)S(1)}, f32[1,2048,256]{2,1,0:T(8,128)}, u32[]{:S(2)}) copy-start(f32[1,2048,256]{2,1,0:T(8,128)} %param.5) | copy-start | bytes 6291460
  9.7 1.6 %collective-permute-start = (f32[264,256]{1,0:T(8,128)S(1)}, f32[264,256]{1,0:T(8,128)S(1)}, u32[]{:S(2)}, u32[]{:S(2)}) collective-permute-start(f32[264,256]{1,0:T(8,128)S(1)} %get-tuple-element.25.rest_0_), channel_id=1, source_target_pairs={{0,8},{8,0},{16,24},{24,16},{1,9},{9,1},{17,25},{25,17},{2,10},{10... | collective-permute-start | bytes 811016 | tf_op jit(solution)/shard_map/ppermute | solution.py:660
  10.2 18.6 %collective-permute-start.4 = (f32[512,256]{1,0:T(8,128)S(1)}, f32[512,256]{1,0:T(8,128)S(1)}, u32[]{:S(2)}, u32[]{:S(2)}) collective-permute-start(f32[512,256]{1,0:T(8,128)S(1)} %take.3), channel_id=1, source_target_pairs={{0,4},{4,0},{1,5},{5,1},{2,6},{6,2},{3,7},{7,3},{8,12},{12,8},{9,1... | collective-permute-start | bytes 1572872 | tf_op jit(solution)/shard_map/ppermute | solution.py:658
  11.3 8.6 %collective-permute-start.3 = (f32[264,256]{1,0:T(8,128)S(1)}, f32[264,256]{1,0:T(8,128)S(1)}, u32[]{:S(2)}, u32[]{:S(2)}) collective-permute-start(f32[264,256]{1,0:T(8,128)S(1)} %fold.1.rest_0_), channel_id=1, source_target_pairs={{0,16},{8,24},{16,0},{24,8},{1,17},{9,25},{17,1},{25,9},{2,18},{10... | collective-permute-start | bytes 811016 | tf_op jit(solution)/shard_map/ppermute | solution.py:660
  18.9 1.6 %collective-permute-start.2 = (f32[264,256]{1,0:T(8,128)S(1)}, f32[264,256]{1,0:T(8,128)S(1)}, u32[]{:S(2)}, u32[]{:S(2)}) collective-permute-start(f32[264,256]{1,0:T(8,128)S(1)} %get-tuple-element.27), channel_id=1, source_target_pairs={{0,8},{8,0},{16,24},{24,16},{1,9},{9,1},{17,25},{25,17},{2,10},{10... | collective-permute-start | bytes 811016 | tf_op jit(solution)/shard_map/ppermute | solution.py:660
  23.7 15.1 %collective-permute-start.7 = (f32[512,256]{1,0:T(8,128)S(1)}, f32[512,256]{1,0:T(8,128)S(1)}, u32[]{:S(2)}, u32[]{:S(2)}) collective-permute-start(f32[512,256]{1,0:T(8,128)S(1)} %get-tuple-element.29.after_ref), channel_id=1, source_target_pairs={{0,4},{4,0},{1,5},{5,1},{2,6},{6,2},{3,7},{7,3},{8,12},{12,8},{9,1... | collective-permute-start | bytes 1572872 | tf_op jit(solution)/shard_map/ppermute | solution.py:658
  28.8 1.6 %collective-permute-start.5 = (f32[264,256]{1,0:T(8,128)S(1)}, f32[264,256]{1,0:T(8,128)S(1)}, u32[]{:S(2)}, u32[]{:S(2)}) collective-permute-start(f32[264,256]{1,0:T(8,128)S(1)} %hold.2.own_ref), channel_id=1, source_target_pairs={{0,8},{8,0},{16,24},{24,16},{1,9},{9,1},{17,25},{25,17},{2,10},{10... | collective-permute-start | bytes 811016 | tf_op jit(solution)/shard_map/ppermute | solution.py:660
  28.8 8.9 %collective-permute-start.6 = (f32[264,256]{1,0:T(8,128)S(1)}, f32[264,256]{1,0:T(8,128)S(1)}, u32[]{:S(2)}, u32[]{:S(2)}) collective-permute-start(f32[264,256]{1,0:T(8,128)S(1)} %hold.2.own_ref), channel_id=1, source_target_pairs={{0,16},{8,24},{16,0},{24,8},{1,17},{9,25},{17,1},{25,9},{2,18},{10... | collective-permute-start | bytes 811016 | tf_op jit(solution)/shard_map/ppermute | solution.py:660
  30.9 24.8 %collective-permute-start.9 = (f32[768,256]{1,0:T(8,128)S(1)}, f32[768,256]{1,0:T(8,128)S(1)}, u32[]{:S(2)}, u32[]{:S(2)}) collective-permute-start(f32[768,256]{1,0:T(8,128)S(1)} %core_apply.1.rest_0_.after_ref), channel_id=1, source_target_pairs={{0,4},{4,0},{1,5},{5,1},{2,6},{6,2},{3,7},{7,3},{8,12},{12,8},{9,1... | collective-permute-start | bytes 2359304 | tf_op jit(solution)/shard_map/ppermute | solution.py:658
  38.9 3.0 %collective-permute-start.8 = (f32[264,256]{1,0:T(8,128)S(1)}, f32[264,256]{1,0:T(8,128)S(1)}, u32[]{:S(2)}, u32[]{:S(2)}) collective-permute-start(f32[264,256]{1,0:T(8,128)S(1)} %hold.3.x_ref), channel_id=1, source_target_pairs={{0,8},{8,0},{16,24},{24,16},{1,9},{9,1},{17,25},{25,17},{2,10},{10... | collective-permute-start | bytes 811016 | tf_op jit(solution)/shard_map/ppermute | solution.py:660
  42.8 25.7 %collective-permute-start.11 = (f32[584,256]{1,0:T(8,128)S(1)}, f32[584,256]{1,0:T(8,128)S(1)}, u32[]{:S(2)}, u32[]{:S(2)}) collective-permute-start(f32[584,256]{1,0:T(8,128)S(1)} %right_apply.5), channel_id=1, source_target_pairs={{0,4},{4,0},{1,5},{5,1},{2,6},{6,2},{3,7},{7,3},{8,12},{12,8},{9,1... | collective-permute-start | bytes 1794056 | tf_op jit(solution)/shard_map/ppermute | solution.py:658
  56.1 14.6 %copy-start.1 = (f32[1,1024,256]{2,1,0:T(8,128)S(1)}, f32[1,1024,256]{2,1,0:T(8,128)}, u32[]{:S(2)}) copy-start(f32[1,1024,256]{2,1,0:T(8,128)} %param.4) | copy-start | bytes 3145732
  56.1 27.3 %collective-permute-start.10 = (f32[512,256]{1,0:T(8,128)S(1)}, f32[512,256]{1,0:T(8,128)S(1)}, u32[]{:S(2)}, u32[]{:S(2)}) collective-permute-start(f32[512,256]{1,0:T(8,128)S(1)} %right_apply.4), channel_id=1, source_target_pairs={{0,4},{4,0},{1,5},{5,1},{2,6},{6,2},{3,7},{7,3},{8,12},{12,8},{9,1... | collective-permute-start | bytes 1572872 | tf_op jit(solution)/shard_map/ppermute | solution.py:658
  68.9 28.3 %collective-permute-start.15 = (f32[512,256]{1,0:T(8,128)S(1)}, f32[512,256]{1,0:T(8,128)S(1)}, u32[]{:S(2)}, u32[]{:S(2)}) collective-permute-start(f32[512,256]{1,0:T(8,128)S(1)} %right_apply.6.after_ref), channel_id=1, source_target_pairs={{0,4},{4,0},{1,5},{5,1},{2,6},{6,2},{3,7},{7,3},{8,12},{12,8},{9,1... | collective-permute-start | bytes 1572872 | tf_op jit(solution)/shard_map/ppermute | solution.py:658
  83.8 14.6 %collective-permute-start.14 = (f32[512,128]{1,0:T(8,128)S(1)}, f32[512,128]{1,0:T(8,128)S(1)}, u32[]{:S(2)}, u32[]{:S(2)}) collective-permute-start(f32[512,128]{1,0:T(8,128)S(1)} %get-tuple-element.39.rest_1_), channel_id=1, source_target_pairs={{0,4},{4,0},{1,5},{5,1},{2,6},{6,2},{3,7},{7,3},{8,12},{12,8},{9,1... | collective-permute-start | bytes 786440 | tf_op jit(solution)/shard_map/ppermute | solution.py:658
  84.1 3.4 %collective-permute-start.16 = (f32[72,256]{1,0:T(8,128)S(1)}, f32[72,256]{1,0:T(8,128)S(1)}, u32[]{:S(2)}, u32[]{:S(2)}) collective-permute-start(f32[72,256]{1,0:T(8,128)S(1)} %rest_of.1.own_ref), channel_id=1, source_target_pairs={{0,8},{8,0},{16,24},{24,16},{1,9},{9,1},{17,25},{25,17},{2,10},{10... | collective-permute-start | bytes 221192 | tf_op jit(solution)/shard_map/ppermute | solution.py:660
  84.2 4.7 %collective-permute-start.17 = (f32[72,256]{1,0:T(8,128)S(1)}, f32[72,256]{1,0:T(8,128)S(1)}, u32[]{:S(2)}, u32[]{:S(2)}) collective-permute-start(f32[72,256]{1,0:T(8,128)S(1)} %rest_of.1.own_ref), channel_id=1, source_target_pairs={{0,16},{8,24},{16,0},{24,8},{1,17},{9,25},{17,1},{25,9},{2,18},{10... | collective-permute-start | bytes 221192 | tf_op jit(solution)/shard_map/ppermute | solution.py:660
  86.0 13.5 %collective-permute-start.13 = (f32[256,128]{1,0:T(8,128)S(1)}, f32[256,128]{1,0:T(8,128)S(1)}, u32[]{:S(2)}, u32[]{:S(2)}) collective-permute-start(f32[256,128]{1,0:T(8,128)S(1)} %get-tuple-element.38), channel_id=1, source_target_pairs={{0,4},{4,0},{1,5},{5,1},{2,6},{6,2},{3,7},{7,3},{8,12},{12,8},{9,1... | collective-permute-start | bytes 393224 | tf_op jit(solution)/shard_map/ppermute | solution.py:658
  87.5 14.4 %collective-permute-start.12 = (f32[256,128]{1,0:T(8,128)S(1)}, f32[256,128]{1,0:T(8,128)S(1)}, u32[]{:S(2)}, u32[]{:S(2)}) collective-permute-start(f32[256,128]{1,0:T(8,128)S(1)} %get-tuple-element.37), channel_id=1, source_target_pairs={{0,4},{4,0},{1,5},{5,1},{2,6},{6,2},{3,7},{7,3},{8,12},{12,8},{9,1... | collective-permute-start | bytes 393224 | tf_op jit(solution)/shard_map/ppermute | solution.py:658
  88.8 2.3 %collective-permute-start.18 = (f32[72,256]{1,0:T(8,128)S(1)}, f32[72,256]{1,0:T(8,128)S(1)}, u32[]{:S(2)}, u32[]{:S(2)}) collective-permute-start(f32[72,256]{1,0:T(8,128)S(1)} %collective-permute-done.17.x_ref), channel_id=1, source_target_pairs={{0,8},{8,0},{16,24},{24,16},{1,9},{9,1},{17,25},{25,17},{2,10},{10... | collective-permute-start | bytes 221192 | tf_op jit(solution)/shard_map/ppermute | solution.py:660
